TPU v7x, 32 devices: a whole 2x2x4 slice. The times are simulated.
32 devices in a mesh: sess: 4 (over z), tile: 8 (over y, x, core).
Axes of the slice: x: 2, y: 2, z: 4, core: 2. Of those that a mesh axis runs over, the one named last changes fastest.
Arguments:
- features: bfloat16 [24, 16, 320, 128], P('sess', 'tile'), parts along dimension 0, may hold values from -6 to 6
- dec_weight: bfloat16 [9, 128, 128], replicated, may hold values from -0.1875 to 0.1875
- dec_bias: float32 [128], replicated, may hold values from -3 to 3
- first_weight: bfloat16 [9, 128, 128], replicated, may hold values from -0.1875 to 0.1875
- first_bias: float32 [128], replicated, may hold values from -3 to 3
- second_weight: bfloat16 [9, 128, 128], replicated, may hold values from -0.1875 to 0.1875
- second_bias: float32 [128], replicated, may hold values from -3 to 3
- boxes: int32 [3, 32], P(None, 'sess'), parts along dimension 1, may hold values from 0 to 272, as said below
- slots: int32 [64], P('sess'), parts along dimension 0, may hold values from -1 to 7, as said below
Outputs:
- finished: bfloat16 [24, 16, 320, 128], P('sess', 'tile'), parts along dimension 0
- restorations: bfloat16 [64, 64, 64, 128], P(('sess', 'tile')), parts along dimension 0
There are 4 independent parts, one for each index of `sess`. A program takes and returns all parts, laid end to end along the dimension named above; an argument that names none is the same for every part. Nothing has to cross between parts.
Inputs may be any that keep to these rules, and one draw needn't show every extreme that they name: Column k of boxes is crop k: its first row r, its first column w and its size class c; the box has side 12 * (c + 2), and the square of side 48 at rows r, columns w lies inside the frame; some crop has class 3 - 1. `slots`: entries w * 2 to w * 2 + 1 are the crops that worker w restores, -1 marking an empty entry; each crop appears exactly once; some worker has 2 crops.
All inputs are finite; a program needn't handle non-finite values.
Results may differ from a plain program's by a relative error of at most 0.0057.
Values may be sent and summed in bfloat16 or wider, within the bound.
No kernel may reach another device: no remote copies, remote signals or barrier semaphores. Data moves between devices by JAX's collectives and lax.ppermute only.
A program may use at most 64 MiB of HBM per device.

v0:
```python
import jax
import jax.numpy as jnp
from jax import lax
from jax.sharding import PartitionSpec as P

S = 64
UNIT = 12
NCLS = 3
CAP = 2


def extended_2(x, sides, width):
    for axis, dim in sides:
        peers, length = (lax.axis_size(axis), x.shape[dim])
        up = [(i, (i + 1) % peers) for i in range(peers)]
        down = [(j, i) for i, j in up]
        last = lax.slice_in_dim(x, length - width, length, axis=dim)
        leading = lax.slice_in_dim(x, 0, width, axis=dim)
        before = lax.ppermute(last, axis, up)
        after = lax.ppermute(leading, axis, down)
        x = jnp.concatenate([before, x, after], axis=dim)
    return x


def hat_down(length, cells, size_out):
    spots = (jnp.arange(size_out, dtype=jnp.float32) + 0.5) * length / size_out - 0.5
    spots = jnp.clip(spots, 0.0, length - 1.0)
    return jnp.maximum(0.0, 1.0 - jnp.abs(spots[:, None] - cells[None, :]))


def hat_up(length, cells, size_in):
    spots = (cells + 0.5) * size_in / length - 0.5
    spots = jnp.clip(spots, 0.0, size_in - 1.0)
    inside = ((cells >= 0.0) & (cells < length)).astype(jnp.float32)
    grid = jnp.arange(size_in, dtype=jnp.float32)
    return jnp.maximum(0.0, 1.0 - jnp.abs(spots[:, None] - grid[None, :])) * inside[:, None]


def conv_taps(padded, weight):
    height = padded.shape[-3] - 2
    width = padded.shape[-2] - 2
    chans = padded.shape[-1]
    wide = jnp.concatenate(
        [padded[..., 0:width, :], padded[..., 1 : width + 1, :], padded[..., 2 : width + 2, :]],
        axis=-1,
    )
    stacked = weight.reshape(3, 3 * chans, weight.shape[-1])
    total = None
    for offset in range(3):
        term = jnp.einsum(
            "...hwk,kd->...hwd",
            wide[..., offset : offset + height, :, :],
            stacked[offset],
            preferred_element_type=jnp.float32,
        )
        total = term if total is None else total + term
    return total


def shards(
    features,
    dec_weight,
    dec_bias,
    first_weight,
    first_bias,
    second_weight,
    second_bias,
    boxes,
    slots,
):
    bands, band_rows, cols, chans = features.shape
    tile_count = lax.axis_size("tile")
    position = lax.axis_index("tile")
    span = UNIT * (NCLS + 1)
    stride = tile_count * band_rows
    piece = band_rows * (span // stride + 1)
    local_rows = bands * band_rows
    highest = lax.Precision.HIGHEST
    anchor = jnp.zeros((), jnp.int32)
    grown = extended_2(features, (("tile", 1),), 1)
    upper_rim = grown[:, 0]
    lower_rim = grown[:, band_rows + 1]
    blank_rim = jnp.zeros_like(upper_rim[:1])
    upper_rim = jnp.where(position == 0, jnp.concatenate([blank_rim, upper_rim[:-1]], 0), upper_rim)
    lower_rim = jnp.where(
        position == tile_count - 1, jnp.concatenate([lower_rim[1:], blank_rim], 0), lower_rim
    )
    extended = jnp.concatenate([upper_rim[:, None], features, lower_rim[:, None]], axis=1)
    extended = jnp.pad(extended, ((0, 0), (0, 0), (1, 1), (0, 0)))
    decoded = (
        features.astype(jnp.float32) + jax.nn.silu(conv_taps(extended, dec_weight) + dec_bias)
    ).astype(jnp.bfloat16)
    decoded = decoded.reshape(local_rows, cols, chans)
    widened = jnp.pad(decoded, ((0, piece), (0, span), (0, 0)))
    band_index = jnp.arange(bands, dtype=jnp.int32)[:, None] * stride
    within = position * band_rows + jnp.arange(band_rows, dtype=jnp.int32)[None, :]
    global_rows = (band_index + within).reshape(local_rows)
    padded_rows = jnp.concatenate(
        [global_rows, jnp.full((piece,), stride * bands + span, jnp.int32)]
    )
    box_cells = jnp.arange(span, dtype=jnp.float32)

    def locate(slot):
        crop = jnp.maximum(slot, 0)
        row0 = boxes[0, crop]
        col0 = boxes[1, crop]
        length = UNIT * (boxes[2, crop] + 2)
        start = jnp.sum((global_rows < row0).astype(jnp.int32))
        offsets = lax.dynamic_slice_in_dim(padded_rows, start, piece) - row0
        valid = (offsets < span) & (slot >= 0)
        return (start, col0, length, offsets, valid)

    def outgoing(slot):
        start, col0, length, offsets, valid = locate(slot)
        block = lax.dynamic_slice(widened, (start, col0, anchor), (piece, span, chans))
        block = jnp.where(valid[:, None, None], block, jnp.zeros_like(block))
        places = jnp.where(valid, offsets, -1).astype(jnp.float32)
        size_entry = jnp.where(slot >= 0, length, span).astype(jnp.float32)
        meta = jnp.concatenate([places, size_entry[None]]).astype(jnp.bfloat16)
        return (block, meta)

    sent, meta = lax.map(outgoing, slots)
    sent = sent.reshape((tile_count, CAP) + sent.shape[1:])
    meta = meta.reshape(tile_count, CAP, piece + 1)

    def restore_one(crop):
        padded = jnp.pad(crop, ((1, 1), (1, 1), (0, 0)))
        inner = jax.nn.silu(conv_taps(padded, first_weight) + first_bias).astype(jnp.bfloat16)
        padded = jnp.pad(inner, ((1, 1), (1, 1), (0, 0)))
        return (conv_taps(padded, second_weight) + second_bias).astype(jnp.bfloat16)

    got_rows = lax.all_to_all(sent, "tile", split_axis=0, concat_axis=0, tiled=True)
    got_meta = lax.all_to_all(meta, "tile", split_axis=0, concat_axis=0, tiled=True)
    sources = got_rows.shape[0]
    count = got_rows.shape[1]
    places = jnp.transpose(got_meta[:, :, :piece].astype(jnp.float32), (1, 0, 2)).reshape(
        count, sources * piece
    )
    lengths = got_meta[0, :, piece].astype(jnp.float32)
    down_rows = jax.vmap(lambda size_one, cell_one: hat_down(size_one, cell_one, S))(
        lengths, places
    )
    down_rows = down_rows.reshape(count, S, sources, piece)
    down_cols = jax.vmap(lambda size_one: hat_down(size_one, box_cells, S))(lengths)
    colcut = jnp.einsum(
        "mtw,emrwc->emrtc", down_cols, got_rows.astype(jnp.float32), precision=highest
    ).astype(jnp.bfloat16)
    crops = jnp.einsum(
        "mser,emrtc->mstc", down_rows, colcut.astype(jnp.float32), precision=highest
    ).astype(jnp.bfloat16)
    delta = lax.map(restore_one, crops)
    lifts = jax.vmap(lambda size_one, cell_one: hat_up(size_one, cell_one, S))(lengths, places)
    lifts = lifts.reshape(count, sources, piece, S)
    upper = jnp.einsum(
        "mers,mstc->emrtc", lifts, delta.astype(jnp.float32), precision=highest
    ).astype(jnp.bfloat16)
    lift_cols = jax.vmap(lambda size_one: hat_up(size_one, box_cells, S))(lengths)
    outbound = jnp.einsum(
        "mwt,emrtc->emrwc", lift_cols, upper.astype(jnp.float32), precision=highest
    ).astype(jnp.bfloat16)
    finish_returned = lax.all_to_all(outbound, "tile", split_axis=0, concat_axis=0, tiled=True)
    returned = finish_returned
    deltas = delta[None]
    returned = returned.reshape((tile_count * CAP,) + returned.shape[2:])
    owned = lax.dynamic_slice_in_dim(slots, position * CAP, CAP)
    keep = (owned >= 0)[:, None, None, None]
    restorations = jnp.where(keep, deltas[0], jnp.zeros_like(deltas[0]))

    def paste_slot(index, canvas):
        start, col0, length, offsets, valid = locate(slots[index])
        incoming = returned[index]
        old = lax.dynamic_slice(canvas, (start, col0, anchor), (piece, span, chans))
        return lax.dynamic_update_slice(
            canvas, old + incoming.astype(jnp.float32), (start, col0, anchor)
        )

    canvas = lax.fori_loop(
        0,
        tile_count * CAP,
        paste_slot,
        jnp.zeros((local_rows + piece, cols + span, chans), jnp.float32),
    )
    finished = (decoded.astype(jnp.float32) + canvas[:local_rows, :cols]).astype(jnp.bfloat16)
    return (finished.reshape(bands, band_rows, cols, chans), restorations)


def solution(mesh):
    return jax.shard_map(
        shards,
        mesh=mesh,
        in_specs=(
            P("sess", "tile", None, None),
            P(),
            P(),
            P(),
            P(),
            P(),
            P(),
            P(None, "sess"),
            P("sess"),
        ),
        out_specs=(P("sess", "tile", None, None), P(("sess", "tile"), None, None, None)),
        check_vma=False,
    )
```

profile of v0, /device:TPU:0, one launch (start us, length us, event | category | flops | bytes accessed | tf_op | source)
XLA Modules:
  0.0 459.3 jit_solution(3556774509860764584)
XLA Ops:
  1.9 3.4 collective-permute-start.1
  5.5 10.5 %collective-permute-done.1 = bf16[6,1,320,128]{3,2,0,1:T(8,128)(2,1)S(1)} collective-permute-done((bf16[6,1,320,128]{3,2,0,1:T(8,128)(2,1)S(1)}, bf16[6,1,320,128]{3,2,0,1:T(8,128)(2,1)S(1)}, u32[]{:S(2)}, u32[]{:S(2)}) %collective-permute-start.1) | collective-permute-done | bytes 491552 | tf_op jit(solution)/shard_map/ppermute | solution.py:20
  16.1 1.9 collective-permute-done
  22.7 1.3 add_convert_fusion.2
  25.2 181.5 %while.43 = (s32[]{:T(128)}, bf16[16,8,48,128]{3,2,1,0:T(8,128)(2,1)}, bf16[16,9]{1,0:T(8,128)(2,1)}, s32[16]{0:T(128)S(1)}, s32[3,8]{1,0:T(4,128)S(1)}, /*index...) while((s32[]{:T(128)}, ...), condition=%wide.region_2.3_spmd.clone.clone, body=%wide.region_0.2_spmd.clone.sunk.clone | while | flops 49297 | bytes 197798 | solution.py:122
  27.3 1.3 fusion.141
  49.9 1.3 fusion.141
  83.9 1.3 fusion.141
  95.2 1.3 fusion.141
  206.7 3.3 all-to-all-start
  210.1 4.6 all-to-all-done
  214.6 3.6 all-to-all-start.1
  218.8 20.4 %all-to-all-done.1 = bf16[8,2,8,48,128]{4,3,2,1,0:T(8,128)(2,1)S(1)} async-done(((bf16[8,2,8,48,128]{4,3,2,1,0:T(8,128)(2,1)}), bf16[8,2,8,48,128]{4,3,2,1,0:T(8,128)(2,1)S(1)}, u32[]{:S(2)}, u32[]{:S(2)}) %all-to-all-start.1) | async-done | bytes 1572896 | tf_op jit(solution)/shard_map/all_to_all | solution.py:132
  239.2 1.9 convert_bitcast_fusion.2
  241.1 2.7 bitcast_convert_fusion
  243.8 22.6 %while.42 = (s32[]{:T(128)}, bf16[2,64,64,128]{3,2,1,0:T(8,128)(2,1)}, bf16[2,64,64,128]{3,1,2,0:T(8,128)(2,1)S(1)}, bf16[9,128,128]{2,1,0:T(8,128)(2,1)S(1)}, f...) while((s32[]{:T(128)}, bf16[2,64,64,128]{3,2,1,0:T(8,128)(2,1)}, ...), condition=%wide.region_4.5_spmd.clone, body=%wide.region_3.4_spmd.sunk.clone | while | flops 2480603136 | bytes 52889168 | solution.py:151
  244.8 1.5 pad_slice_fusion.10
  248.3 1.5 multiply_convert_fusion.3
  249.7 1.5 pad_slice_fusion.11
  253.2 2.0 fusion.140
  256.0 1.5 pad_slice_fusion.10
  259.5 1.5 multiply_convert_fusion.3
  260.9 1.5 pad_slice_fusion.11
  264.4 2.0 fusion.140
  266.4 4.2 convert_bitcast_fusion.1
  270.6 2.4 fusion.29
  274.4 3.6 all-to-all-start.2
  278.0 3.1 broadcast_select_fusion
  281.2 17.8 %all-to-all-done.2 = bf16[8,2,8,48,128]{4,3,2,1,0:T(8,128)(2,1)S(1)} async-done(((bf16[8,2,8,48,128]{4,3,2,1,0:T(8,128)(2,1)}), bf16[8,2,8,48,128]{4,3,2,1,0:T(8,128)(2,1)S(1)}, u32[]{:S(2)}, u32[]{:S(2)}) %all-to-all-start.2) | async-done | bytes 1572896 | tf_op jit(solution)/shard_map/all_to_all | solution.py:161
  298.9 2.1 broadcast_in_dim.49
  301.0 155.6 %while.44 = (s32[]{:T(128)}, f32[20,368,128]{2,1,0:T(8,128)}, s32[16]{0:T(128)S(1)}, s32[3,8]{1,0:T(4,128)S(1)}, bf16[16,8,48,128]{3,2,1,0:T(8,128)(2,1)S(1)}, /*index=5*/s32[2]{0:T(128)S(1)}, s32[6]{0:T(128)S(1)}, s32[1]{0:T(128)}) while((s32[]{:T(128)}, f32[20,368,128]{2,1,0:T(8,128)}, s32[16]{0:T(128)S(1)}, ...), condition=%wide.region_7.8_spmd.clone.clone, body=%wide.region_5.7_spmd.clone.sunk.clone | while | flops 98360 | bytes 885181 | solution.py:177
  308.9 1.8 dynamic_update_slice.38
  318.6 1.8 dynamic_update_slice.38
  328.3 1.8 dynamic_update_slice.38
  338.1 1.8 dynamic_update_slice.38
  347.8 1.8 dynamic_update_slice.38
  357.5 1.8 dynamic_update_slice.38
  367.2 1.8 dynamic_update_slice.38
  377.0 1.8 dynamic_update_slice.38
  386.7 1.8 dynamic_update_slice.38
  396.4 1.8 dynamic_update_slice.38
  406.2 1.8 dynamic_update_slice.38
  415.9 1.8 dynamic_update_slice.38
  425.6 1.8 dynamic_update_slice.38
  435.3 1.8 dynamic_update_slice.38
  445.1 1.8 dynamic_update_slice.38
  454.8 1.8 dynamic_update_slice.38
  456.6 2.7 add_convert_fusion.1
  (305 shorter events, 159.3 us)
Async XLA Ops:
  0.6 4.9 %copy-start.5 = (bf16[9,128,128]{2,1,0:T(8,128)(2,1)S(1)}, bf16[9,128,128]{2,1,0:T(8,128)(2,1)}, u32[]{:S(2)}) copy-start(bf16[9,128,128]{2,1,0:T(8,128)(2,1)} %param.16) | copy-start | bytes 884740
  1.9 14.1 %collective-permute-start.1 = (bf16[6,1,320,128]{3,2,0,1:T(8,128)(2,1)S(1)}, bf16[6,1,320,128]{3,2,0,1:T(8,128)(2,1)S(1)}, u32[]{:S(2)}, u32[]{:S(2)}) collective-permute-start(bf16[6,1,320,128]{3,2,0,1:T(8,128)(2,1)S(1)} %get-tuple-element.400), channel_id=1, source_target_pairs={{1,0},{2,1},{3,2},{4,3},{5,4},{6,5},{7,6},{0,7},{9,8},{10,9},{11,1... | collective-permute-start | bytes 1474568 | tf_op jit(solution)/shard_map/ppermute | solution.py:20
  5.3 12.6 %collective-permute-start = (bf16[6,1,320,128]{3,2,0,1:T(8,128)(2,1)S(1)}, bf16[6,1,320,128]{3,2,0,1:T(8,128)(2,1)S(1)}, u32[]{:S(2)}, u32[]{:S(2)}) collective-permute-start(bf16[6,1,320,128]{3,2,0,1:T(8,128)(2,1)S(1)} %get-tuple-element.399), channel_id=1, source_target_pairs={{0,1},{1,2},{2,3},{3,4},{4,5},{5,6},{6,7},{7,0},{8,9},{9,10},{10,1... | collective-permute-start | bytes 1474568 | tf_op jit(solution)/shard_map/ppermute | solution.py:19
  5.5 12.6 %copy-start = (bf16[6,2,320,128]{3,2,1,0:T(8,128)(2,1)S(1)}, bf16[6,2,320,128]{3,2,1,0:T(8,128)(2,1)}, u32[]{:S(2)}) copy-start(bf16[6,2,320,128]{3,2,1,0:T(8,128)(2,1)} %param.15) | copy-start | bytes 2949124
  21.7 1.0 copy-start.7
  24.0 0.9 copy-start.3
  24.0 1.1 copy-start.6
  24.0 1.1 copy-start.10
  206.7 7.9 %all-to-all-start = ((bf16[8,2,9]{2,1,0:T(2,128)(2,1)}), bf16[8,2,9]{2,1,0:T(2,128)(2,1)S(1)}, u32[]{:S(2)}, u32[]{:S(2)}) async-start(bf16[8,2,9]{2,1,0:T(2,128)(2,1)} %bitcast.30), calls=%async_computation | async-start | bytes 8192 | tf_op jit(solution)/shard_map/all_to_all | solution.py:133
  214.6 24.5 %all-to-all-start.1 = ((bf16[8,2,8,48,128]{4,3,2,1,0:T(8,128)(2,1)}), bf16[8,2,8,48,128]{4,3,2,1,0:T(8,128)(2,1)S(1)}, u32[]{:S(2)}, u32[]{:S(2)}) async-start(bf16[8,2,8,48,128]{4,3,2,1,0:T(8,128)(2,1)} %bitcast.34), calls=%async_computation.1 | async-start | bytes 3145728 | tf_op jit(solution)/shard_map/all_to_all | solution.py:132
  241.0 2.7 copy-start.1
  241.0 2.7 copy-start.2
  241.1 2.7 copy-start.8
  241.1 2.7 copy-start.9
  274.4 24.5 %all-to-all-start.2 = ((bf16[8,2,8,48,128]{4,3,2,1,0:T(8,128)(2,1)}), bf16[8,2,8,48,128]{4,3,2,1,0:T(8,128)(2,1)S(1)}, u32[]{:S(2)}, u32[]{:S(2)}) async-start(bf16[8,2,8,48,128]{4,3,2,1,0:T(8,128)(2,1)} %copy.66), calls=%async_computation.2 | async-start | bytes 3145728 | tf_op jit(solution)/shard_map/all_to_all | solution.py:161
  298.9 157.7 %copy-start.4 = (bf16[6,2,320,128]{3,2,1,0:T(8,128)(2,1)S(1)}, bf16[6,2,320,128]{3,2,1,0:T(8,128)(2,1)}, u32[]{:S(2)}) copy-start(bf16[6,2,320,128]{3,2,1,0:T(8,128)(2,1)} %copy-done.3) | copy-start | bytes 2949124
where the time goes:
time: 464 us; the launch traced here: 459 us
  loops' own time  163 us (35%)
  local copies, waits for them, and re-layouts  106 us (23%)
  other arithmetic  91 us (20%)
  waiting for transfers between devices  55.1 us (12%)
  matrix products  29.2 us (6%)
  starting transfers between devices  13.9 us (3%)
    another operation x1, loops' own time, shards(): sent, meta = lax.map(outgoing, slots)  92.2 us
    another operation x1, loops' own time, shards(): lax.fori_loop(0, tile_count * CAP, paste_slot, jnp.zeros((local_rows + pi...  70.2 us
    reduce_sum x32, other arithmetic, locate(): start = jnp.sum((global_rows < row0).astype(jnp.int32))  40.4 us
    dynamic_update_slice x16, local copies, waits for them, and re-layouts, paste_slot(): lax.dynamic_update_slice(canvas, old + incoming.astype(jnp.float32), (sta...  28.7 us
    dynamic_update_slice x16, local copies, waits for them, and re-layouts, shards(): sent, meta = lax.map(outgoing, slots)  20.5 us
    all_to_all x1, waiting for transfers between devices, shards(): lax.all_to_all(sent, 'tile', split_axis=0, concat_axis=0, tiled=True)  20.4 us
    dot_general x15, matrix products, conv_taps(): jnp.einsum('...hwk,kd->...hwd', wide[..., offset:offset + height, :, :],...  18 us
    all_to_all x1, waiting for transfers between devices, shards(): lax.all_to_all(outbound, 'tile', split_axis=0, concat_axis=0, tiled=True)  17.8 us
  transfers between devices with their start and end apart: 5, of which 5 were waited for; matrix products, arithmetic and copies ran while one was open for 1% of the time, Pallas kernels for 0%

commit v1 on v0

v1 whole, which is shorter than its diff:
```python
import functools

import jax
import jax.numpy as jnp
from jax import lax
from jax.experimental import pallas as pl
from jax.experimental.pallas import tpu as pltpu
from jax.sharding import PartitionSpec as P

S = 64
UNIT = 12
NCLS = 3
CAP = 2
SPAN = UNIT * (NCLS + 1)
BF16 = jnp.bfloat16
F32 = jnp.float32
VMEM_LIMIT = 48 * 1024 * 1024


def rows_within(window, band_rows, stride):
    return band_rows * (window // stride) + min(band_rows, window % stride)


def first_local(row, tile, band_rows, stride):
    whole = lax.div(row, stride) * band_rows
    return whole + jnp.clip(lax.rem(row, stride) - tile * band_rows, 0, band_rows)


def global_row(local, tile, band_rows, stride):
    return lax.div(local, band_rows) * stride + tile * band_rows + lax.rem(local, band_rows)


def silu(v):
    half = 0.5 * v
    return half + half * jnp.tanh(half)


def doubled_weight(weight):
    chans = weight.shape[-1]
    taps = weight.reshape(3, 3, chans, chans)
    none = jnp.zeros_like(taps[:1])
    upper = jnp.concatenate([taps, none], 0)
    lower = jnp.concatenate([none, taps], 0)
    return jnp.concatenate([upper, lower], -1).reshape(12 * chans, 2 * chans)


def three_columns(x, width, left, right):
    count = x.shape[0]
    at = lax.rem(lax.broadcasted_iota(jnp.int32, x.shape, 0), width)
    before = jnp.where(at == 0, left, pltpu.roll(x, 1, 0))
    after = jnp.where(at == width - 1, right, pltpu.roll(x, count - 1, 0))
    return before.astype(BF16), x.astype(BF16), after.astype(BF16)


def conv_pairs(src, first, count, weight):
    parts = [
        src[pl.ds(first, count), 0],
        src[pl.ds(first, count), 1],
        src[pl.ds(first + 1, count), 0],
        src[pl.ds(first + 1, count), 1],
    ]
    wide = jnp.concatenate(parts, -1)
    wide = wide.reshape(wide.shape[0] * wide.shape[1], wide.shape[2])
    return jnp.dot(wide, weight[...], preferred_element_type=F32)


def pack_kernel(dims, boxes, slots, feat, sent_main, sent_extra, table, canvas, rim, seconds):
    tiles, band_rows, stride, local_rows, cols, chans, rows = dims
    me = lax.axis_index("tile")

    def first_pass(w, count):
        one = slots[CAP * w]
        two = slots[CAP * w + 1]
        both = (one >= 0) & (two >= 0)
        second = jnp.where(both, two, -1)
        table[0, w] = jnp.where(one >= 0, one, two)
        table[1, w] = second
        seconds[count] = second
        return count + both.astype(jnp.int32)

    lax.fori_loop(0, tiles, first_pass, jnp.int32(0))

    def second_pass(w, count):
        idle = table[0, w] < 0

        @pl.when(idle)
        def _():
            table[0, w] = seconds[count]

        return count + idle.astype(jnp.int32)

    lax.fori_loop(0, tiles, second_pass, jnp.int32(0))

    edge = jnp.zeros((8, chans), F32)
    for row in range(local_rows):
        canvas[row, 0:8, :] = edge
        canvas[row, 8 + cols : 16 + cols, :] = edge
        canvas[row, 8 : 8 + cols, :] = feat[row].astype(F32)
    rim[...] = jnp.zeros_like(rim)

    def pack(crop, w, out):
        row0 = boxes[0, crop]
        col0 = boxes[1, crop]
        start = first_local(jnp.maximum(row0 - 1, 0), me, band_rows, stride)
        for i in range(rows):
            row = jnp.minimum(start + i, local_rows - 1)
            out[w, i * SPAN : (i + 1) * SPAN, :] = canvas[row, pl.ds(col0 + 8, SPAN), :].astype(BF16)
            rim[2 * i : 2 * i + 1, :] = canvas[row, pl.ds(col0 + 7, 1), :]
            rim[2 * i + 1 : 2 * i + 2, :] = canvas[row, pl.ds(col0 + 8 + SPAN, 1), :]
        out[w, rows * SPAN :, :] = rim[...].astype(BF16)

    @pl.loop(0, tiles)
    def _(w):
        pack(table[0, w], w, sent_main)
        extra = table[1, w]

        @pl.when(extra >= 0)
        def _():
            pack(extra, w, sent_extra)


def restore(dims, crop, boxes, got, dec_w, dec_b, one_w, one_b, two_w, two_b, raw, cut, wide, inner, delta):
    tiles, band_rows, stride, local_rows, cols, chans, rows = dims
    row0 = boxes[0, crop]
    length = UNIT * (boxes[2, crop] + 2)
    above = row0 - 1
    pairs = SPAN // 2
    nothing = jnp.zeros((SPAN, 3 * chans), BF16)
    raw[0, 0] = nothing
    raw[pairs, 1] = nothing

    @pl.loop(0, tiles)
    def _(e):
        start = first_local(jnp.maximum(above, 0), e, band_rows, stride)
        rim = got[e, rows * SPAN :, :].astype(F32)
        for i in range(rows):
            local = start + i
            place = global_row(local, e, band_rows, stride) - above
            place = jnp.where((local < local_rows) & (place < SPAN + 2), place, SPAN + 2)
            main = got[e, i * SPAN : (i + 1) * SPAN, :].astype(F32)
            trio = three_columns(main, SPAN, rim[2 * i : 2 * i + 1], rim[2 * i + 1 : 2 * i + 2])
            for b in range(3):
                raw[lax.div(place, 2), lax.rem(place, 2), :, b * chans : (b + 1) * chans] = trio[b]

    lengthf = length.astype(F32)
    t = lax.broadcasted_iota(jnp.int32, (S, SPAN), 0).astype(F32)
    j = lax.broadcasted_iota(jnp.int32, (S, SPAN), 1).astype(F32)
    spots = jnp.clip((t + 0.5) * lengthf / S - 0.5, 0.0, lengthf - 1.0)
    across = jnp.maximum(0.0, 1.0 - jnp.abs(spots - j)).astype(BF16)

    n = 8
    for first in range(0, pairs, n):
        total = silu(conv_pairs(raw, first, n, dec_w) + dec_b[...])
        for k in range(n):
            feat = jnp.concatenate(
                [raw[first + k, 1, :, chans : 2 * chans], raw[first + k + 1, 0, :, chans : 2 * chans]], -1
            )
            decoded = (feat.astype(F32) + total[k * SPAN : (k + 1) * SPAN]).astype(BF16)
            both = jnp.dot(across, decoded, preferred_element_type=F32).astype(BF16)
            cut[2 * (first + k)] = both[:, :chans]
            cut[2 * (first + k) + 1] = both[:, chans:]

    empty = jnp.zeros((S, 3 * chans), BF16)
    for store in (wide, inner):
        store[0, 0] = empty
        store[S // 2, 1] = empty

    @pl.loop(0, S // 2)
    def _(m):
        for parity in range(2):
            s = 2 * m + parity
            spot = jnp.clip((2 * s + 1) * length - S, 0, (length - 1) * 2 * S)
            low = lax.div(spot, 2 * S)
            part = lax.rem(spot, 2 * S).astype(F32) * (1.0 / (2 * S))
            high = jnp.minimum(low + 1, SPAN - 1)
            line = (1.0 - part) * cut[low].astype(F32) + part * cut[high].astype(F32)
            trio = three_columns(line, S, 0.0, 0.0)
            for b in range(3):
                wide[m + parity, 1 - parity, :, b * chans : (b + 1) * chans] = trio[b]

    for first in range(0, S // 2, n):
        total = silu(conv_pairs(wide, first, n, one_w) + one_b[...])
        for half in range(2):
            trio = three_columns(total[:, half * chans : (half + 1) * chans], S, 0.0, 0.0)
            for b in range(3):
                inner[first + half : first + half + n, 1 - half, :, b * chans : (b + 1) * chans] = trio[b].reshape(
                    n, S, chans
                )

    for first in range(0, S // 2, n):
        total = (conv_pairs(inner, first, n, two_w) + two_b[...]).astype(BF16).reshape(n, S, 2 * chans)
        for k in range(n):
            delta[2 * (first + k)] = total[k, :, :chans]
            delta[2 * (first + k) + 1] = total[k, :, chans:]


def main_kernel(
    dims, table, boxes, slots, got, dec_w, dec_b, one_w, one_b, two_w, two_b,
    back, restored, raw, cut, wide, inner, delta, sem,
):
    tiles, band_rows, stride, local_rows, cols, chans, rows = dims
    me = lax.axis_index("tile")
    crop = table[0, me]
    restore(dims, crop, boxes, got, dec_w, dec_b, one_w, one_b, two_w, two_b, raw, cut, wide, inner, delta)
    place = jnp.where(slots[CAP * me] >= 0, 0, 1)
    own = (slots[CAP * me] >= 0) | (slots[CAP * me + 1] >= 0)

    @pl.when(own)
    def _():
        pltpu.make_async_copy(delta, restored.at[place], sem).start()

    row0 = boxes[0, crop]
    length = UNIT * (boxes[2, crop] + 2)
    lengthf = length.astype(F32)
    t = lax.broadcasted_iota(jnp.int32, (SPAN, S), 0).astype(F32)
    s = lax.broadcasted_iota(jnp.int32, (SPAN, S), 1).astype(F32)
    spots = jnp.clip((t + 0.5) * S / lengthf - 0.5, 0.0, S - 1.0)
    lift = jnp.where(t < lengthf, jnp.maximum(0.0, 1.0 - jnp.abs(spots - s)), 0.0)
    coarse = lift.astype(BF16)
    lift = jnp.concatenate([coarse, (lift - coarse.astype(F32)).astype(BF16)], 0)
    scale = 1.0 / (2.0 * lengthf)

    @pl.loop(0, SPAN // 2)
    def _(m):
        lines = []
        for parity in range(2):
            h = 2 * m + parity
            spot = jnp.clip((2 * h + 1) * S - length, 0, (S - 1) * 2 * length)
            low = ((spot.astype(F32) + 0.5) * scale).astype(jnp.int32)
            part = (spot - low * 2 * length).astype(F32) * scale
            high = jnp.minimum(low + 1, S - 1)
            lines.append(((1.0 - part) * delta[low].astype(F32) + part * delta[high].astype(F32)).astype(BF16))
        upper = jnp.concatenate(lines, -1)
        patch = jnp.dot(lift, upper, preferred_element_type=F32)
        patch = (patch[:SPAN] + patch[SPAN:]).astype(BF16)
        for parity in range(2):
            row = row0 + 2 * m + parity
            within = lax.rem(row, stride)
            dest = lax.div(within, band_rows)
            local = lax.div(row, stride) * band_rows + lax.rem(within, band_rows)
            place = local - first_local(row0, dest, band_rows, stride)
            back[dest, place] = patch[:, parity * chans : (parity + 1) * chans]

    @pl.when(own)
    def _():
        pltpu.make_async_copy(delta, restored.at[place], sem).wait()


def extra_kernel(
    dims, table, boxes, slots, got, dec_w, dec_b, one_w, one_b, two_w, two_b, partial,
    restored, raw, cut, wide, inner, delta, sem,
):
    me = lax.axis_index("tile")
    extra = table[1, me]
    one = slots[CAP * me] >= 0
    two = slots[CAP * me + 1] >= 0

    @pl.when(extra >= 0)
    def _():
        restore(dims, extra, boxes, got, dec_w, dec_b, one_w, one_b, two_w, two_b, raw, cut, wide, inner, delta)
        copy = pltpu.make_async_copy(delta, restored.at[1], sem)
        copy.start()
        copy.wait()

    @pl.when(extra < 0)
    def _():
        delta[...] = jnp.zeros_like(delta)

        @pl.when(jnp.logical_not(one))
        def _():
            copy = pltpu.make_async_copy(delta, restored.at[0], sem)
            copy.start()
            copy.wait()

        @pl.when(jnp.logical_not(two))
        def _():
            copy = pltpu.make_async_copy(delta, restored.at[1], sem)
            copy.start()
            copy.wait()


def decode_kernel(dims, feat, above, below, weight, bias, decoded, wide):
    tiles, band_rows, stride, local_rows, cols, chans, rows = dims
    me = lax.axis_index("tile")
    bands = local_rows // band_rows
    top = (me == 0).astype(jnp.int32)
    bottom = (me == tiles - 1).astype(jnp.int32)
    for j in range(bands):
        up = above[jnp.maximum(j - top, 0)].astype(F32)
        down = below[jnp.minimum(j + bottom, bands - 1)].astype(F32)
        if j == 0:
            up = jnp.where(top == 1, 0.0, up)
        if j == bands - 1:
            down = jnp.where(bottom == 1, 0.0, down)
        lines = [up, feat[2 * j].astype(F32), feat[2 * j + 1].astype(F32), down]
        for a in range(4):
            trio = three_columns(lines[a], cols, 0.0, 0.0)
            for b in range(3):
                at = (3 * a + b) * chans
                wide[j % 2, :, at : at + chans] = trio[b]
        total = silu(jnp.dot(wide[j % 2], weight[...], preferred_element_type=F32) + bias[...])
        decoded[2 * j] = (lines[1] + total[:, :chans]).astype(BF16)
        decoded[2 * j + 1] = (lines[2] + total[:, chans:]).astype(BF16)


def paste_kernel(dims, table, boxes, decoded, back, finished, canvas):
    tiles, band_rows, stride, local_rows, cols, chans, rows = dims
    me = lax.axis_index("tile")
    count = back.shape[1]
    for row in range(local_rows):
        canvas[row] = decoded[row].astype(F32)

    @pl.loop(0, tiles)
    def _(e):
        crop = table[0, e]
        row0 = boxes[0, crop]
        col0 = boxes[1, crop]
        length = UNIT * (boxes[2, crop] + 2)
        start = first_local(row0, me, band_rows, stride)
        for i in range(count):
            local = start + i

            @pl.when((local < local_rows) & (global_row(local, me, band_rows, stride) - row0 < length))
            def _():
                canvas[local, pl.ds(col0, SPAN), :] += back[e, i].astype(F32)

    for row in range(local_rows):
        finished[row] = canvas[row].astype(BF16)


def shards(features, dec_weight, dec_bias, first_weight, first_bias, second_weight, second_bias, boxes, slots):
    bands, band_rows, cols, chans = features.shape
    tiles = lax.axis_size("tile")
    assert band_rows == 2 and slots.shape[0] == CAP * tiles and boxes.shape[1] == tiles
    stride = tiles * band_rows
    local_rows = bands * band_rows
    rows = rows_within(SPAN + 2, band_rows, stride)
    back_rows = rows_within(SPAN, band_rows, stride)
    message = rows * SPAN + -(-2 * rows // 16) * 16
    dims = (tiles, band_rows, stride, local_rows, cols, chans, rows)
    frame = features.reshape(local_rows, cols, chans)

    smem = pl.BlockSpec(memory_space=pltpu.SMEM)
    vmem = pl.BlockSpec(memory_space=pltpu.VMEM)
    hbm = pl.BlockSpec(memory_space=pl.ANY)
    params = pltpu.CompilerParams(vmem_limit_bytes=VMEM_LIMIT)

    def cost(flops, moved):
        return pl.CostEstimate(flops=int(flops), bytes_accessed=int(moved), transcendentals=0)

    sent = jax.ShapeDtypeStruct((tiles, message, chans), BF16)
    sent_main, sent_extra, table = pl.pallas_call(
        functools.partial(pack_kernel, dims),
        out_shape=(sent, sent, jax.ShapeDtypeStruct((2, tiles), jnp.int32)),
        in_specs=[smem, smem, vmem],
        out_specs=(vmem, vmem, smem),
        scratch_shapes=[
            pltpu.VMEM((local_rows, cols + 16, chans), F32),
            pltpu.VMEM((message - rows * SPAN, chans), F32),
            pltpu.SMEM((tiles + 1,), jnp.int32),
        ],
        compiler_params=params,
        cost_estimate=cost(0, 6e6),
        name="pack",
    )(boxes, slots, frame)

    got_main = lax.all_to_all(sent_main, "tile", split_axis=0, concat_axis=0, tiled=True)
    got_extra = lax.all_to_all(sent_extra, "tile", split_axis=0, concat_axis=0, tiled=True)

    last = features[:, band_rows - 1]
    leading = features[:, 0]
    last, leading, got_main = lax.optimization_barrier((last, leading, got_main))
    up = [(i, (i + 1) % tiles) for i in range(tiles)]
    above = lax.ppermute(last, "tile", up)
    below = lax.ppermute(leading, "tile", [(j, i) for i, j in up])

    def twice(bias):
        return jnp.concatenate([bias, bias])[None]

    weights = (
        doubled_weight(dec_weight), twice(dec_bias),
        doubled_weight(first_weight), twice(first_bias),
        doubled_weight(second_weight), twice(second_bias),
    )
    scratch = [
        pltpu.VMEM((SPAN // 2 + 2, 2, SPAN, 3 * chans), BF16),
        pltpu.VMEM((SPAN, S, chans), BF16),
        pltpu.VMEM((S // 2 + 1, 2, S, 3 * chans), BF16),
        pltpu.VMEM((S // 2 + 1, 2, S, 3 * chans), BF16),
        pltpu.VMEM((S, S, chans), BF16),
        pltpu.SemaphoreType.DMA,
    ]
    restored_shape = jax.ShapeDtypeStruct((CAP, S, S, chans), BF16)
    back, partial = pl.pallas_call(
        functools.partial(main_kernel, dims),
        out_shape=(jax.ShapeDtypeStruct((tiles, back_rows, SPAN, chans), BF16), restored_shape),
        in_specs=[smem, smem, smem] + [vmem] * 7,
        out_specs=(vmem, hbm),
        scratch_shapes=scratch,
        compiler_params=params,
        cost_estimate=cost(7e9, 8e6),
        name="restore_main",
    )(table, boxes, slots, got_main, *weights)

    got_back = lax.all_to_all(back, "tile", split_axis=0, concat_axis=0, tiled=True)

    restorations = pl.pallas_call(
        functools.partial(extra_kernel, dims),
        out_shape=restored_shape,
        in_specs=[smem, smem, smem] + [vmem] * 7 + [hbm],
        out_specs=hbm,
        scratch_shapes=scratch,
        input_output_aliases={10: 0},
        compiler_params=params,
        cost_estimate=cost(6e9, 8e6),
        name="restore_extra",
    )(table, boxes, slots, got_extra, *weights, partial)

    decoded = pl.pallas_call(
        functools.partial(decode_kernel, dims),
        out_shape=jax.ShapeDtypeStruct((local_rows, cols, chans), BF16),
        in_specs=[vmem] * 5,
        out_specs=vmem,
        scratch_shapes=[pltpu.VMEM((2, cols, 12 * chans), BF16)],
        compiler_params=params,
        cost_estimate=cost(3e9, 6e6),
        name="decode",
    )(frame, above, below, weights[0], weights[1])

    finished = pl.pallas_call(
        functools.partial(paste_kernel, dims),
        out_shape=jax.ShapeDtypeStruct((local_rows, cols, chans), BF16),
        in_specs=[smem, smem, vmem, vmem],
        out_specs=vmem,
        scratch_shapes=[pltpu.VMEM((local_rows, cols, chans), F32)],
        compiler_params=params,
        cost_estimate=cost(0, 6e6),
        name="paste",
    )(table, boxes, decoded, got_back)
    return finished.reshape(bands, band_rows, cols, chans), restorations


def solution(mesh):
    return jax.shard_map(
        shards,
        mesh=mesh,
        in_specs=(
            P("sess", "tile", None, None),
            P(),
            P(),
            P(),
            P(),
            P(),
            P(),
            P(None, "sess"),
            P("sess"),
        ),
        out_specs=(P("sess", "tile", None, None), P(("sess", "tile"), None, None, None)),
        check_vma=False,
    )
```

time: 464 us -> 69.1 us (0.15)
  the two profiles are of different devices: /device:TPU:0 before, /device:TPU:1 now
where the time goes in v1:
time: 69.1 us; the launch traced here: 68.5 us
  Pallas kernels  31.8 us (46%)
  starting transfers between devices  18.5 us (27%)
  local copies, waits for them, and re-layouts  8.93 us (13%)
  waiting for transfers between devices  6.34 us (9%)
  other arithmetic  2.07 us (3%)
  between operations  0.81 us (1%)
    pallas_call x1, Pallas kernels, shards(): pl.pallas_call(functools.partial(main_kernel, dims), out_shape=(jax.Shape...  12.8 us
    pallas_call x1, Pallas kernels, shards(): pl.pallas_call(functools.partial(extra_kernel, dims), out_shape=restored_...  9.96 us
    unnamed x34, local copies, waits for them, and re-layouts  7.92 us
    all_to_all x1, starting transfers between devices, shards(): lax.all_to_all(sent_extra, 'tile', split_axis=0, concat_axis=0, tiled=True)  6.91 us
    all_to_all x1, waiting for transfers between devices, shards(): lax.all_to_all(sent_main, 'tile', split_axis=0, concat_axis=0, tiled=True)  6.33 us
    all_to_all x1, starting transfers between devices, shards(): lax.all_to_all(sent_main, 'tile', split_axis=0, concat_axis=0, tiled=True)  5.37 us
    all_to_all x1, starting transfers between devices, shards(): lax.all_to_all(back, 'tile', split_axis=0, concat_axis=0, tiled=True)  4.58 us
    pallas_call x1, Pallas kernels, shards(): pl.pallas_call(functools.partial(decode_kernel, dims), out_shape=jax.Shap...  4.18 us
  transfers between devices with their start and end apart: 5, of which 1 were waited for; matrix products, arithmetic and copies ran while one was open for 5% of the time, Pallas kernels for 39%

profile of v1, /device:TPU:1, one launch (start us, length us, event | category | flops | bytes accessed | tf_op | source)
XLA Modules:
  0.0 68.5 jit_solution(2741082415295131559)
XLA Ops:
  0.6 0.0 copy-start.14
  0.6 0.0 copy-start.15
  0.7 0.0 copy-start
  0.7 1.2 %copy-done = bf16[6,2,320,128]{3,2,1,0:T(8,128)(2,1)S(1)} copy-done((bf16[6,2,320,128]{3,2,1,0:T(8,128)(2,1)S(1)}, bf16[6,2,320,128]{3,2,1,0:T(8,128)(2,1)}, u32[]{:S(2)}) %copy-start) | copy-done | bytes 983064
  1.9 0.0 copy-start.7
  1.9 0.7 copy-done.7
  2.5 0.0 copy-start.9
  2.5 0.7 copy-done.9
  3.2 0.0 copy-start.11
  3.2 2.4 %pack.1 = (bf16[8,400,128]{2,1,0:T(8,128)(2,1)}, bf16[8,400,128]{2,1,0:T(8,128)(2,1)}, s32[2,8]{1,0:T(2,128)S(1)}) custom-call(s32[3,8]{1,0:T(4,128)S(1)} %copy-done.7, s32[16]{0:T(128)S(1)} %copy-done.9, bf16[12,320,128]{2,1,0:T(8,128)(2,1)S(1)} %bitcast.19), custom_call_target="tpu_custom_call" | custom-call | bytes 6000000 | tf_op jit(solution)/shard_map/pack/pallas_call | solution.py:352
  5.6 0.0 copy-start.12
  5.6 5.4 %all-to-all-start = ((bf16[8,400,128]{2,1,0:T(8,128)(2,1)}), bf16[8,400,128]{2,1,0:T(8,128)(2,1)S(1)}, u32[]{:S(2)}, u32[]{:S(2)}) async-start(bf16[8,400,128]{2,1,0:T(8,128)(2,1)} %get-tuple-element.11), calls=%async_computation | async-start | bytes 1638400 | tf_op jit(solution)/shard_map/all_to_all | solution.py:367
  11.0 0.0 copy-done.14
  11.0 0.0 copy-start.13
  11.0 0.0 copy-done.15
  11.0 0.0 copy-done.11
  11.0 0.0 copy-start.1
  11.0 0.1 fusion.6
  11.1 0.0 copy-done.12
  11.1 1.0 %fusion.8 = bf16[4,3,128,256]{3,2,1,0:T(8,128)(2,1)} fusion(bf16[3,3,128,128]{3,2,1,0:T(8,128)(2,1)S(1)} %bitcast.37), kind=kLoop, calls=%fused_computation.10 | loop fusion | flops 3145728 | bytes 1081344 | tf_op jit(solution)/shard_map/concatenate | solution.py:44
  12.1 0.0 copy-done.13
  12.1 1.0 %fusion.7 = bf16[4,3,128,256]{3,2,1,0:T(8,128)(2,1)} fusion(bf16[3,3,128,128]{3,2,1,0:T(8,128)(2,1)S(1)} %bitcast.38), kind=kLoop, calls=%fused_computation.9 | loop fusion | flops 3145728 | bytes 1081344 | tf_op jit(solution)/shard_map/concatenate | solution.py:44
  13.1 0.0 copy-done.1
  13.1 0.0 copy-start.16
  13.1 1.0 %slice_bitcast_fusion = (bf16[6,320,128]{2,1,0:T(8,128)(2,1)}, bf16[6,320,128]{2,1,0:T(8,128)(2,1)}) fusion(bf16[6,2,320,128]{3,2,1,0:T(8,128)(2,1)S(1)} %copy-done.1), kind=kLoop, calls=%fused_computation.11 | loop fusion | bytes 1966080 | tf_op jit(solution)/shard_map/squeeze | solution.py:371
  14.1 6.3 %all-to-all-done.got = bf16[8,400,128]{2,1,0:T(8,128)(2,1)S(1)} async-done(((bf16[8,400,128]{2,1,0:T(8,128)(2,1)}), bf16[8,400,128]{2,1,0:T(8,128)(2,1)S(1)}, u32[]{:S(2)}, u32[]{:S(2)}) %all-to-all-start) | async-done | bytes 819232 | tf_op jit(solution)/shard_map/all_to_all | solution.py:367
  20.5 6.9 %all-to-all-start.2 = ((bf16[8,400,128]{2,1,0:T(8,128)(2,1)}), bf16[8,400,128]{2,1,0:T(8,128)(2,1)S(1)}, u32[]{:S(2)}, u32[]{:S(2)}) async-start(bf16[8,400,128]{2,1,0:T(8,128)(2,1)} %get-tuple-element.16), calls=%async_computation.2 | async-start | bytes 1638400 | tf_op jit(solution)/shard_map/all_to_all | solution.py:368
  27.4 0.0 copy-done.16
  27.4 1.7 %collective-permute-start = (bf16[6,320,128]{2,1,0:T(8,128)(2,1)}, bf16[6,320,128]{2,1,0:T(8,128)(2,1)}, u32[]{:S(2)}, u32[]{:S(2)}) collective-permute-start(bf16[6,320,128]{2,1,0:T(8,128)(2,1)} %get-tuple-element.12), channel_id=1, source_target_pairs={{0,1},{1,2},{2,3},{3,4},{4,5},{5,6},{6,7},{7,0},{8,9},{9,10},{10,1... | collective-permute-start | bytes 1474568 | tf_op jit(solution)/shard_map/ppermute | solution.py:374
  29.1 0.0 collective-permute-start.1
  29.1 0.0 copy-done.8
  29.1 0.0 copy-done.10
  29.1 0.0 copy-start.2
  29.1 1.1 %copy-done.2 = bf16[4,3,128,256]{3,2,1,0:T(8,128)(2,1)S(1)} copy-done((bf16[4,3,128,256]{3,2,1,0:T(8,128)(2,1)S(1)}, bf16[4,3,128,256]{3,2,1,0:T(8,128)(2,1)}, u32[]{:S(2)}) %copy-start.2) | copy-done | bytes 786456
  30.2 1.1 %copy-done.4 = bf16[4,3,128,256]{3,2,1,0:T(8,128)(2,1)S(1)} copy-done((bf16[4,3,128,256]{3,2,1,0:T(8,128)(2,1)S(1)}, bf16[4,3,128,256]{3,2,1,0:T(8,128)(2,1)}, u32[]{:S(2)}) %copy-start.4) | copy-done | bytes 786456
  31.4 12.8 %restore_main.1 = (bf16[8,6,48,128]{3,2,1,0:T(8,128)(2,1)S(1)}, bf16[2,64,64,128]{3,2,1,0:T(8,128)(2,1)}) custom-call(s32[2,8]{1,0:T(2,128)S(1)} %get-tuple-element.10.table, s32[3,8]{1,0:T(4,128)S(1)} %copy-done.8, s32[16]{0:T(128)S(1)} %copy-done.10, bf16[8,400,128]{2,1,0:T(8,128)(2,1)S(1)} %all-to-all-done.got, bf16[1536,256]{1,0:T(8,128)(2,1)S(1)} %bitcast.21, ...), custom_call_target="tpu_custom_call" | custom-call | flops 7000000000 | bytes 8000000 | tf_op jit(solution)/shard_map/restore_main/pallas_call | solution.py:394
  44.2 0.0 copy-start.6
  44.2 0.8 %copy-done.6 = bf16[8,6,48,128]{3,2,1,0:T(8,128)(2,1)} copy-done((bf16[8,6,48,128]{3,2,1,0:T(8,128)(2,1)}, bf16[8,6,48,128]{3,2,1,0:T(8,128)(2,1)S(1)}, u32[]{:S(2)}) %copy-start.6) | copy-done | bytes 589848
  45.0 0.0 all-to-all-done.2.got
  45.0 4.6 %all-to-all-start.1 = ((bf16[8,6,48,128]{3,2,1,0:T(8,128)(2,1)}), bf16[8,6,48,128]{3,2,1,0:T(8,128)(2,1)S(1)}, u32[]{:S(2)}, u32[]{:S(2)}) async-start(bf16[8,6,48,128]{3,2,1,0:T(8,128)(2,1)} %copy-done.6), calls=%async_computation.1 | async-start | bytes 1179648 | tf_op jit(solution)/shard_map/all_to_all | solution.py:405
  49.6 1.1 %copy-done.3 = bf16[4,3,128,256]{3,2,1,0:T(8,128)(2,1)S(1)} copy-done((bf16[4,3,128,256]{3,2,1,0:T(8,128)(2,1)S(1)}, bf16[4,3,128,256]{3,2,1,0:T(8,128)(2,1)}, u32[]{:S(2)}) %copy-start.3) | copy-done | bytes 786456
  50.7 1.1 %copy-done.5 = bf16[4,3,128,256]{3,2,1,0:T(8,128)(2,1)S(1)} copy-done((bf16[4,3,128,256]{3,2,1,0:T(8,128)(2,1)S(1)}, bf16[4,3,128,256]{3,2,1,0:T(8,128)(2,1)}, u32[]{:S(2)}) %copy-start.5) | copy-done | bytes 786456
  51.8 10.0 %restore_extra.1 = bf16[2,64,64,128]{3,2,1,0:T(8,128)(2,1)} custom-call(s32[2,8]{1,0:T(2,128)S(1)} %get-tuple-element.10.table, s32[3,8]{1,0:T(4,128)S(1)} %copy-done.8, s32[16]{0:T(128)S(1)} %copy-done.10, bf16[8,400,128]{2,1,0:T(8,128)(2,1)S(1)} %all-to-all-done.2.got, bf16[1536,256]{1,0:T(8,128)(2,1)S(1)} %bitcast.22, ...), custom_call_target="tpu_custom_call", output_to_operand_aliasing={{}: (10, {})} | custom-call | flops 6000000000 | bytes 8000000 | tf_op jit(solution)/shard_map/restore_extra/pallas_call | solution.py:407
  61.8 0.0 collective-permute-done.above
  61.8 0.0 collective-permute-done.1.below
  61.8 4.2 %decode.1.decoded = bf16[12,320,128]{2,1,0:T(8,128)(2,1)S(1)} custom-call(bf16[12,320,128]{2,1,0:T(8,128)(2,1)S(1)} %bitcast.20, bf16[6,320,128]{2,1,0:T(8,128)(2,1)} %collective-permute-done.above, bf16[6,320,128]{2,1,0:T(8,128)(2,1)} %collective-permute-done.1.below, bf16[1536,256]{1,0:T(8,128)(2,1)S(1)} %bitcast.23, f32[1,256]{1,0:T(1,128)S(1)} %bitcast.30), custom_call_target="tpu_custom_call" | custom-call | flops 3000000000 | bytes 6000000 | tf_op jit(solution)/shard_map/decode/pallas_call | solution.py:419
  66.0 0.0 all-to-all-done.1.back
  66.0 2.5 %paste.1 = bf16[12,320,128]{2,1,0:T(8,128)(2,1)} custom-call(s32[2,8]{1,0:T(2,128)S(1)} %get-tuple-element.10.table, s32[3,8]{1,0:T(4,128)S(1)} %copy-done.8, bf16[12,320,128]{2,1,0:T(8,128)(2,1)S(1)} %decode.1.decoded, bf16[8,6,48,128]{3,2,1,0:T(8,128)(2,1)S(1)} %all-to-all-done.1.back), custom_call_target="tpu_custom_call" | custom-call | bytes 6000000 | tf_op jit(solution)/shard_map/paste/pallas_call | solution.py:430
  (8 shorter events, 0.0 us)
Async XLA Ops:
  0.6 10.4 %copy-start.14 = (f32[128]{0:T(128)S(1)}, f32[128]{0:T(128)}, u32[]{:S(2)}) copy-start(f32[128]{0:T(128)} %param.11) | copy-start | bytes 1540
  0.6 10.4 %copy-start.15 = (f32[128]{0:T(128)S(1)}, f32[128]{0:T(128)}, u32[]{:S(2)}) copy-start(f32[128]{0:T(128)} %param.15) | copy-start | bytes 1540
  0.7 1.2 %copy-start = (bf16[6,2,320,128]{3,2,1,0:T(8,128)(2,1)S(1)}, bf16[6,2,320,128]{3,2,1,0:T(8,128)(2,1)}, u32[]{:S(2)}) copy-start(bf16[6,2,320,128]{3,2,1,0:T(8,128)(2,1)} %param.9) | copy-start | bytes 2949124
  1.9 0.7 copy-start.7
  2.5 0.7 copy-start.9
  3.2 7.8 %copy-start.11 = (bf16[9,128,128]{2,1,0:T(8,128)(2,1)S(1)}, bf16[9,128,128]{2,1,0:T(8,128)(2,1)}, u32[]{:S(2)}) copy-start(bf16[9,128,128]{2,1,0:T(8,128)(2,1)} %param.10) | copy-start | bytes 884740
  5.6 5.5 %copy-start.12 = (bf16[9,128,128]{2,1,0:T(8,128)(2,1)S(1)}, bf16[9,128,128]{2,1,0:T(8,128)(2,1)}, u32[]{:S(2)}) copy-start(bf16[9,128,128]{2,1,0:T(8,128)(2,1)} %param.14) | copy-start | bytes 884740
  5.6 14.9 %all-to-all-start = ((bf16[8,400,128]{2,1,0:T(8,128)(2,1)}), bf16[8,400,128]{2,1,0:T(8,128)(2,1)S(1)}, u32[]{:S(2)}, u32[]{:S(2)}) async-start(bf16[8,400,128]{2,1,0:T(8,128)(2,1)} %get-tuple-element.11), calls=%async_computation | async-start | bytes 1638400 | tf_op jit(solution)/shard_map/all_to_all | solution.py:367
  11.0 1.1 %copy-start.13 = (bf16[9,128,128]{2,1,0:T(8,128)(2,1)S(1)}, bf16[9,128,128]{2,1,0:T(8,128)(2,1)}, u32[]{:S(2)}) copy-start(bf16[9,128,128]{2,1,0:T(8,128)(2,1)} %param.12) | copy-start | bytes 884740
  11.0 2.1 %copy-start.1 = (bf16[6,2,320,128]{3,2,1,0:T(8,128)(2,1)S(1)}, bf16[6,2,320,128]{3,2,1,0:T(8,128)(2,1)}, u32[]{:S(2)}) copy-start(bf16[6,2,320,128]{3,2,1,0:T(8,128)(2,1)} %param.9) | copy-start | bytes 2949124
  13.1 14.3 %copy-start.16 = (f32[128]{0:T(128)S(1)}, f32[128]{0:T(128)}, u32[]{:S(2)}) copy-start(f32[128]{0:T(128)} %param.13) | copy-start | bytes 1540
  13.1 16.0 %copy-start.8 = (s32[3,8]{1,0:T(4,128)S(1)}, s32[3,8]{1,0:T(4,128)}, u32[]{:S(2)}) copy-start(s32[3,8]{1,0:T(4,128)} %boxes.7) | copy-start | bytes 292
  13.1 16.0 %copy-start.10 = (s32[16]{0:T(128)S(1)}, s32[16]{0:T(128)}, u32[]{:S(2)}) copy-start(s32[16]{0:T(128)} %slots.5) | copy-start | bytes 196
  20.5 24.5 %all-to-all-start.2 = ((bf16[8,400,128]{2,1,0:T(8,128)(2,1)}), bf16[8,400,128]{2,1,0:T(8,128)(2,1)S(1)}, u32[]{:S(2)}, u32[]{:S(2)}) async-start(bf16[8,400,128]{2,1,0:T(8,128)(2,1)} %get-tuple-element.16), calls=%async_computation.2 | async-start | bytes 1638400 | tf_op jit(solution)/shard_map/all_to_all | solution.py:368
  27.4 34.4 %collective-permute-start = (bf16[6,320,128]{2,1,0:T(8,128)(2,1)}, bf16[6,320,128]{2,1,0:T(8,128)(2,1)}, u32[]{:S(2)}, u32[]{:S(2)}) collective-permute-start(bf16[6,320,128]{2,1,0:T(8,128)(2,1)} %get-tuple-element.12), channel_id=1, source_target_pairs={{0,1},{1,2},{2,3},{3,4},{4,5},{5,6},{6,7},{7,0},{8,9},{9,10},{10,1... | collective-permute-start | bytes 1474568 | tf_op jit(solution)/shard_map/ppermute | solution.py:374
  29.1 32.7 %collective-permute-start.1 = (bf16[6,320,128]{2,1,0:T(8,128)(2,1)}, bf16[6,320,128]{2,1,0:T(8,128)(2,1)}, u32[]{:S(2)}, u32[]{:S(2)}) collective-permute-start(bf16[6,320,128]{2,1,0:T(8,128)(2,1)} %get-tuple-element.13), channel_id=1, source_target_pairs={{1,0},{2,1},{3,2},{4,3},{5,4},{6,5},{7,6},{0,7},{9,8},{10,9},{11,1... | collective-permute-start | bytes 1474568 | tf_op jit(solution)/shard_map/ppermute | solution.py:375
  29.1 1.1 %copy-start.2 = (bf16[4,3,128,256]{3,2,1,0:T(8,128)(2,1)S(1)}, bf16[4,3,128,256]{3,2,1,0:T(8,128)(2,1)}, u32[]{:S(2)}) copy-start(bf16[4,3,128,256]{3,2,1,0:T(8,128)(2,1)} %fusion.8) | copy-start | bytes 2359300
  30.2 1.1 %copy-start.4 = (bf16[4,3,128,256]{3,2,1,0:T(8,128)(2,1)S(1)}, bf16[4,3,128,256]{3,2,1,0:T(8,128)(2,1)}, u32[]{:S(2)}) copy-start(bf16[4,3,128,256]{3,2,1,0:T(8,128)(2,1)} %fusion.7) | copy-start | bytes 2359300
  44.2 0.8 %copy-start.6 = (bf16[8,6,48,128]{3,2,1,0:T(8,128)(2,1)}, bf16[8,6,48,128]{3,2,1,0:T(8,128)(2,1)S(1)}, u32[]{:S(2)}) copy-start(bf16[8,6,48,128]{3,2,1,0:T(8,128)(2,1)S(1)} %get-tuple-element.15) | copy-start | bytes 1769476
  45.0 21.0 %all-to-all-start.1 = ((bf16[8,6,48,128]{3,2,1,0:T(8,128)(2,1)}), bf16[8,6,48,128]{3,2,1,0:T(8,128)(2,1)S(1)}, u32[]{:S(2)}, u32[]{:S(2)}) async-start(bf16[8,6,48,128]{3,2,1,0:T(8,128)(2,1)} %copy-done.6), calls=%async_computation.1 | async-start | bytes 1179648 | tf_op jit(solution)/shard_map/all_to_all | solution.py:405
  49.6 1.1 %copy-start.3 = (bf16[4,3,128,256]{3,2,1,0:T(8,128)(2,1)S(1)}, bf16[4,3,128,256]{3,2,1,0:T(8,128)(2,1)}, u32[]{:S(2)}) copy-start(bf16[4,3,128,256]{3,2,1,0:T(8,128)(2,1)} %fusion.8) | copy-start | bytes 2359300
  50.7 1.1 %copy-start.5 = (bf16[4,3,128,256]{3,2,1,0:T(8,128)(2,1)S(1)}, bf16[4,3,128,256]{3,2,1,0:T(8,128)(2,1)}, u32[]{:S(2)}) copy-start(bf16[4,3,128,256]{3,2,1,0:T(8,128)(2,1)} %fusion.7) | copy-start | bytes 2359300

commit v2 on v0

v2 whole, which is shorter than its diff:
```python
import functools

import jax
import jax.numpy as jnp
from jax import lax
from jax.experimental import pallas as pl
from jax.experimental.pallas import tpu as pltpu
from jax.sharding import PartitionSpec as P

S = 64
UNIT = 12
NCLS = 3
CAP = 2
SPAN = UNIT * (NCLS + 1)
BF16 = jnp.bfloat16
F32 = jnp.float32
I32 = jnp.int32
VMEM_LIMIT = 40 * 1024 * 1024
ROW, COL, SIDE, ROW2, COL2, SIDE2, PLACE = range(7)


def rows_within(window, band_rows, stride):
    return band_rows * (window // stride) + min(band_rows, window % stride)


def first_local(row, tile, dims):
    whole = lax.div(row, dims.stride) * dims.band_rows
    return whole + jnp.clip(lax.rem(row, dims.stride) - tile * dims.band_rows, 0, dims.band_rows)


def global_row(local, tile, dims):
    return lax.div(local, dims.band_rows) * dims.stride + tile * dims.band_rows + lax.rem(local, dims.band_rows)


class Dims:
    def __init__(self, features, tiles):
        self.bands, self.band_rows, self.cols, self.chans = features.shape
        self.tiles = tiles
        self.stride = tiles * self.band_rows
        self.local_rows = self.bands * self.band_rows
        self.rows = rows_within(SPAN + 2, self.band_rows, self.stride)
        self.back_rows = rows_within(SPAN, self.band_rows, self.stride)
        self.rim = -(-2 * self.rows // 16) * 16
        self.message = self.rows * SPAN + self.rim


def silu(v):
    half = 0.5 * v
    return half + half * jnp.tanh(half)


def three_columns(x, left, right):
    axis = x.ndim - 2
    width = x.shape[axis]
    at = lax.broadcasted_iota(I32, x.shape, axis)
    flat = x.reshape(-1, x.shape[-1])
    count = flat.shape[0]
    before = jnp.where(at == 0, left, pltpu.roll(flat, 1, 0).reshape(x.shape))
    after = jnp.where(at == width - 1, right, pltpu.roll(flat, count - 1, 0).reshape(x.shape))
    return before.astype(BF16), x.astype(BF16), after.astype(BF16)


def both(bias):
    return jnp.concatenate([bias[...], bias[...]], -1)


class Taps:
    def __init__(self, source, store, sems):
        chans = source.shape[-1]
        self.store = store
        self.copies = (
            pltpu.make_async_copy(source, store.at[0:9, :, 0:chans], sems.at[0]),
            pltpu.make_async_copy(source, store.at[3:12, :, chans : 2 * chans], sems.at[1]),
        )

    def start(self):
        for copy in self.copies:
            copy.start()
        chans = self.store.shape[1]
        none = jnp.zeros((3, chans, chans), BF16)
        self.store[9:12, :, 0:chans] = none
        self.store[0:3, :, chans : 2 * chans] = none

    def wait(self):
        for copy in self.copies:
            copy.wait()

    def value(self):
        shape = self.store.shape
        return self.store[...].reshape(shape[0] * shape[1], shape[2])


def conv_pairs(src, first, count, taps):
    parts = [
        src[first : first + count, 0],
        src[first : first + count, 1],
        src[first + 1 : first + count + 1, 0],
        src[first + 1 : first + count + 1, 1],
    ]
    wide = jnp.concatenate(parts, -1)
    wide = wide.reshape(wide.shape[0] * wide.shape[1], wide.shape[2])
    return jnp.dot(wide, taps.value(), preferred_element_type=F32)


def fill_canvas(dims, feat, held, canvas, sems):
    for band in range(dims.bands):
        at = pl.ds(band * dims.band_rows, dims.band_rows)
        pltpu.make_async_copy(feat.at[at], held.at[at], sems.at[band]).start()

    def finish():
        edge = jnp.zeros((8, dims.chans), F32)
        for band in range(dims.bands):
            at = pl.ds(band * dims.band_rows, dims.band_rows)
            pltpu.make_async_copy(feat.at[at], held.at[at], sems.at[band]).wait()
            for i in range(dims.band_rows):
                row = band * dims.band_rows + i
                canvas[row, 0:8, :] = edge
                canvas[row, 8 + dims.cols : 16 + dims.cols, :] = edge
                canvas[row, 8 : 8 + dims.cols, :] = held[row].astype(F32)

    return finish


def pack_crops(dims, table, row_at, col_at, canvas, rim, staged, sent, sems):
    me = lax.axis_index("tile")
    rim[...] = jnp.zeros_like(rim)
    for s in reversed(range(dims.tiles)):
        w = me ^ s
        row0 = table[row_at, w]
        col0 = table[col_at, w]
        start = first_local(jnp.maximum(row0 - 1, 0), me, dims)
        for i in range(dims.rows):
            row = jnp.minimum(start + i, dims.local_rows - 1)
            staged[s, i * SPAN : (i + 1) * SPAN, :] = canvas[row, pl.ds(col0 + 8, SPAN), :].astype(BF16)
            rim[2 * i : 2 * i + 1, :] = canvas[row, pl.ds(col0 + 7, 1), :]
            rim[2 * i + 1 : 2 * i + 2, :] = canvas[row, pl.ds(col0 + 8 + SPAN, 1), :]
        staged[s, dims.rows * SPAN :, :] = rim[...].astype(BF16)
        pltpu.make_async_copy(staged.at[s], sent[s], sems.at[s]).start()
    for s in range(dims.tiles):
        pltpu.make_async_copy(staged.at[s], sent[s], sems.at[s]).wait()


def pack_main_kernel(dims, boxes_in, slots_in, feat, *refs):
    sent, refs = refs[: dims.tiles], refs[dims.tiles :]
    table, boxes, slots, main, extra, seconds, held, canvas, rim, staged, sems, feat_sems, sent_sems = refs
    finish = fill_canvas(dims, feat, held, canvas, feat_sems)
    copies = (
        pltpu.make_async_copy(boxes_in, boxes, sems.at[0]),
        pltpu.make_async_copy(slots_in, slots, sems.at[1]),
    )
    for copy in copies:
        copy.start()
    for copy in copies:
        copy.wait()

    def first_pass(w, count):
        one = slots[CAP * w]
        two = slots[CAP * w + 1]
        full = (one >= 0) & (two >= 0)
        second = jnp.where(full, two, -1)
        main[w] = jnp.where(one >= 0, one, two)
        extra[w] = second
        seconds[count] = second
        return count + full.astype(I32)

    lax.fori_loop(0, dims.tiles, first_pass, jnp.int32(0))

    def second_pass(w, count):
        own = main[w]
        idle = own < 0
        crop = jnp.where(idle, seconds[count], own)
        table[ROW, w] = boxes[0, crop]
        table[COL, w] = boxes[1, crop]
        table[SIDE, w] = UNIT * (boxes[2, crop] + 2)
        other = jnp.maximum(extra[w], 0)
        table[ROW2, w] = boxes[0, other]
        table[COL2, w] = boxes[1, other]
        table[SIDE2, w] = jnp.where(extra[w] >= 0, UNIT * (boxes[2, other] + 2), 0)
        table[PLACE, w] = jnp.where(idle, 2, jnp.where(slots[CAP * w] >= 0, 0, 1))
        return count + idle.astype(I32)

    lax.fori_loop(0, dims.tiles, second_pass, jnp.int32(0))
    finish()
    pack_crops(dims, table, ROW, COL, canvas, rim, staged, sent, sent_sems)


def pack_extra_kernel(dims, table, feat, *refs):
    sent, refs = refs[: dims.tiles], refs[dims.tiles :]
    last, leading, held, canvas, rim, staged, sems, feat_sems, sent_sems = refs
    finish = fill_canvas(dims, feat, held, canvas, feat_sems)
    finish()
    copies = []
    for band in range(dims.bands):
        row = band * dims.band_rows
        copies.append(pltpu.make_async_copy(held.at[row + dims.band_rows - 1], last.at[band], sems.at[2 * band]))
        copies.append(pltpu.make_async_copy(held.at[row], leading.at[band], sems.at[2 * band + 1]))
    for copy in copies:
        copy.start()
    pack_crops(dims, table, ROW2, COL2, canvas, rim, staged, sent, sent_sems)
    for copy in copies:
        copy.wait()


def restore(dims, row0, length, arrivals, got, taps, biases, raw, decoded, wide, inner, delta):
    chans = dims.chans
    me = lax.axis_index("tile")
    above = row0 - 1
    pairs = SPAN // 2
    nothing = jnp.zeros((SPAN, 3 * chans), BF16)
    raw[0, 0] = nothing
    raw[pairs, 1] = nothing
    empty = jnp.zeros((S, 3 * chans), BF16)
    for store in (wide, inner):
        store[0, 0] = empty
        store[S // 2, 1] = empty

    for s in range(dims.tiles):
        arrivals[s].wait()
        e = me ^ s
        start = first_local(jnp.maximum(above, 0), e, dims)
        rim = got[s, dims.rows * SPAN :, :].astype(F32)
        for i in range(dims.rows):
            local = start + i
            place = global_row(local, e, dims) - above
            place = jnp.where((local < dims.local_rows) & (place < SPAN + 2), place, SPAN + 2)
            main = got[s, i * SPAN : (i + 1) * SPAN, :].astype(F32)
            trio = three_columns(main, rim[2 * i : 2 * i + 1], rim[2 * i + 1 : 2 * i + 2])
            for b in range(3):
                raw[place >> 1, place & 1, :, b * chans : (b + 1) * chans] = trio[b]

    lengthf = length.astype(F32)
    t = lax.broadcasted_iota(I32, (S, SPAN), 0)
    j = lax.broadcasted_iota(I32, (S, SPAN), 1).astype(F32)
    across = []
    for b in range(3):
        at = t + (b - 1)
        spots = jnp.clip((at.astype(F32) + 0.5) * lengthf / S - 0.5, 0.0, lengthf - 1.0)
        hat = jnp.maximum(0.0, 1.0 - jnp.abs(spots - j))
        across.append(jnp.where((at >= 0) & (at < S), hat, 0.0))
    across = jnp.concatenate(across, 0).astype(BF16)

    n = 8
    taps[0].wait()
    for first in range(0, pairs, n):
        total = silu(conv_pairs(raw, first, n, taps[0]) + both(biases[0]))
        for k in range(n):
            part = total[k * SPAN : (k + 1) * SPAN]
            at = 2 * (first + k)
            upper = raw[first + k, 1, :, chans : 2 * chans].astype(F32) + part[:, :chans]
            lower = raw[first + k + 1, 0, :, chans : 2 * chans].astype(F32) + part[:, chans:]
            decoded[at] = upper.astype(BF16).astype(F32)
            decoded[at + 1] = lower.astype(BF16).astype(F32)

    for m in range(S // 2):
        lines = []
        for parity in range(2):
            s = 2 * m + parity
            spot = jnp.clip((2 * s + 1) * length - S, 0, (length - 1) * 2 * S)
            low = spot >> 7
            part = (spot & 127).astype(F32) * (1.0 / (2 * S))
            high = jnp.minimum(low + 1, SPAN - 1)
            lines.append(((1.0 - part) * decoded[low] + part * decoded[high]).astype(BF16))
        cells = jnp.dot(across, jnp.concatenate(lines, -1), preferred_element_type=F32).astype(BF16)
        for parity in range(2):
            for b in range(3):
                wide[m + parity, 1 - parity, :, b * chans : (b + 1) * chans] = cells[
                    b * S : (b + 1) * S, parity * chans : (parity + 1) * chans
                ]

    taps[1].wait()
    for first in range(0, S // 2, n):
        total = silu(conv_pairs(wide, first, n, taps[1]) + both(biases[1])).reshape(n, S, 2 * chans)
        trio = three_columns(total, 0.0, 0.0)
        for half in range(2):
            for b in range(3):
                inner[first + half : first + half + n, 1 - half, :, b * chans : (b + 1) * chans] = trio[b][
                    :, :, half * chans : (half + 1) * chans
                ]

    taps[2].wait()
    for first in range(0, S // 2, n):
        total = (conv_pairs(inner, first, n, taps[2]) + both(biases[2])).astype(BF16).reshape(n, S, 2 * chans)
        for k in range(n):
            delta[2 * (first + k)] = total[k, :, :chans]
            delta[2 * (first + k) + 1] = total[k, :, chans:]


def begin(dims, arrived, weights, scratch):
    got, stores, got_sems, tap_sems = scratch
    arrivals = [pltpu.make_async_copy(arrived[s], got.at[s], got_sems.at[s]) for s in range(dims.tiles)]
    taps = [Taps(weights[i], stores.at[i], tap_sems.at[i]) for i in range(3)]
    for arrival in arrivals:
        arrival.start()
    for tap in taps:
        tap.start()
    return arrivals, taps


def main_kernel(dims, *refs):
    tiles, chans = dims.tiles, dims.chans
    arrived, refs = refs[:tiles], refs[tiles:]
    table, weights, biases, refs = refs[0], refs[1:4], refs[4:7], refs[7:]
    sent, refs = refs[:tiles], refs[tiles:]
    restored, got, stores, got_sems, tap_sems, raw, decoded, wide, inner, delta, sem, back, back_sems = refs
    me = lax.axis_index("tile")
    row0 = table[ROW, me]
    length = table[SIDE, me]
    place = table[PLACE, me]
    arrivals, taps = begin(dims, arrived, weights, (got, stores, got_sems, tap_sems))
    restore(dims, row0, length, arrivals, got, taps, biases, raw, decoded, wide, inner, delta)

    @pl.when(place < CAP)
    def _():
        pltpu.make_async_copy(delta, restored.at[place], sem).start()

    lengthf = length.astype(F32)
    t = lax.broadcasted_iota(I32, (SPAN, S), 0).astype(F32)
    s = lax.broadcasted_iota(I32, (SPAN, S), 1).astype(F32)
    spots = jnp.clip((t + 0.5) * S / lengthf - 0.5, 0.0, S - 1.0)
    lift = jnp.where(t < lengthf, jnp.maximum(0.0, 1.0 - jnp.abs(spots - s)), 0.0)
    coarse = lift.astype(BF16)
    lift = jnp.concatenate([coarse, (lift - coarse.astype(F32)).astype(BF16)], 0)
    scale = 1.0 / (2.0 * lengthf)

    for m in range(SPAN // 2):
        lines = []
        for parity in range(2):
            h = 2 * m + parity
            spot = jnp.clip((2 * h + 1) * S - length, 0, (S - 1) * 2 * length)
            low = ((spot.astype(F32) + 0.5) * scale).astype(I32)
            part = (spot - low * 2 * length).astype(F32) * scale
            high = jnp.minimum(low + 1, S - 1)
            lines.append(((1.0 - part) * delta[low].astype(F32) + part * delta[high].astype(F32)).astype(BF16))
        patch = jnp.dot(lift, jnp.concatenate(lines, -1), preferred_element_type=F32)
        patch = (patch[:SPAN] + patch[SPAN:]).astype(BF16)
        for parity in range(2):
            row = row0 + 2 * m + parity
            within = lax.rem(row, dims.stride)
            dest = lax.div(within, dims.band_rows)
            local = lax.div(row, dims.stride) * dims.band_rows + lax.rem(within, dims.band_rows)
            back[dest ^ me, local - first_local(row0, dest, dims)] = patch[:, parity * chans : (parity + 1) * chans]

    copies = [pltpu.make_async_copy(back.at[s], sent[s], back_sems.at[s]) for s in range(tiles)]
    for copy in copies:
        copy.start()
    for copy in copies:
        copy.wait()

    @pl.when(place < CAP)
    def _():
        pltpu.make_async_copy(delta, restored.at[place], sem).wait()


def extra_kernel(dims, *refs):
    tiles = dims.tiles
    arrived, refs = refs[:tiles], refs[tiles:]
    table, weights, biases, refs = refs[0], refs[1:4], refs[4:7], refs[8:]
    restored, got, stores, got_sems, tap_sems, raw, decoded, wide, inner, delta, sem = refs
    me = lax.axis_index("tile")
    row0 = table[ROW2, me]
    length = table[SIDE2, me]
    place = table[PLACE, me]

    def write(slot):
        copy = pltpu.make_async_copy(delta, restored.at[slot], sem)
        copy.start()
        copy.wait()

    @pl.when(length > 0)
    def _():
        arrivals, taps = begin(dims, arrived, weights, (got, stores, got_sems, tap_sems))
        restore(dims, row0, length, arrivals, got, taps, biases, raw, decoded, wide, inner, delta)
        write(1)

    @pl.when(length == 0)
    def _():
        delta[...] = jnp.zeros_like(delta)

        @pl.when(place != 0)
        def _():
            write(0)

        @pl.when(place != 1)
        def _():
            write(1)


def decode_kernel(dims, feat, above, below, weight, bias, decoded, held, up, down, store, wide, sems, tap_sems):
    me = lax.axis_index("tile")
    bands, chans = dims.bands, dims.chans
    taps = Taps(weight, store, tap_sems)
    copies = []
    for band in range(bands):
        at = pl.ds(band * 2, 2)
        copies.append(
            (
                pltpu.make_async_copy(feat.at[at], held.at[at], sems.at[3 * band]),
                pltpu.make_async_copy(above.at[band], up.at[band], sems.at[3 * band + 1]),
                pltpu.make_async_copy(below.at[band], down.at[band], sems.at[3 * band + 2]),
            )
        )
    for trio in copies:
        for copy in trio:
            copy.start()
    taps.start()
    for trio in copies:
        for copy in trio:
            copy.wait()
    taps.wait()
    top = (me == 0).astype(I32)
    bottom = (me == dims.tiles - 1).astype(I32)
    for j in range(bands):
        over = up[jnp.maximum(j - top, 0)].astype(F32)
        under = down[jnp.minimum(j + bottom, bands - 1)].astype(F32)
        if j == 0:
            over = jnp.where(top == 1, 0.0, over)
        if j == bands - 1:
            under = jnp.where(bottom == 1, 0.0, under)
        lines = [over, held[2 * j].astype(F32), held[2 * j + 1].astype(F32), under]
        for a in range(4):
            trio = three_columns(lines[a], 0.0, 0.0)
            for b in range(3):
                at = (3 * a + b) * chans
                wide[j % 2, :, at : at + chans] = trio[b]
        total = silu(jnp.dot(wide[j % 2], taps.value(), preferred_element_type=F32) + both(bias))
        decoded[2 * j] = (lines[1] + total[:, :chans]).astype(BF16)
        decoded[2 * j + 1] = (lines[2] + total[:, chans:]).astype(BF16)


def paste_kernel(dims, table, decoded, *refs):
    back, (finished, canvas, out, sems) = refs[: dims.tiles], refs[dims.tiles :]
    me = lax.axis_index("tile")
    for row in range(dims.local_rows):
        canvas[row] = decoded[row].astype(F32)

    for s in range(dims.tiles):
        e = me ^ s
        row0 = table[ROW, e]
        col0 = table[COL, e]
        length = table[SIDE, e]
        start = first_local(row0, me, dims)
        for i in range(dims.back_rows):
            local = start + i

            @pl.when((local < dims.local_rows) & (global_row(local, me, dims) - row0 < length))
            def _():
                canvas[local, pl.ds(col0, SPAN), :] += back[s][i].astype(F32)

    copies = [pltpu.make_async_copy(out.at[row], finished.at[row], sems.at[row]) for row in range(dims.local_rows)]
    for row in range(dims.local_rows):
        out[row] = canvas[row].astype(BF16)
        copies[row].start()
    for copy in copies:
        copy.wait()


def shards(features, dec_weight, dec_bias, first_weight, first_bias, second_weight, second_bias, boxes, slots):
    tiles = lax.axis_size("tile")
    dims = Dims(features, tiles)
    cols, chans, local_rows = dims.cols, dims.chans, dims.local_rows
    assert dims.band_rows == 2 and slots.shape[0] == CAP * tiles and boxes.shape[1] == tiles
    assert tiles & (tiles - 1) == 0
    frame = features.reshape(local_rows, cols, chans)

    smem = pl.BlockSpec(memory_space=pltpu.SMEM)
    vmem = pl.BlockSpec(memory_space=pltpu.VMEM)
    hbm = pl.BlockSpec(memory_space=pltpu.HBM)
    params = pltpu.CompilerParams(vmem_limit_bytes=VMEM_LIMIT)
    dma = pltpu.SemaphoreType.DMA

    def cost(flops, moved):
        return pl.CostEstimate(flops=int(flops), bytes_accessed=int(moved), transcendentals=0)

    def shaped(*shape, kind=BF16):
        return jax.ShapeDtypeStruct(shape, kind)

    def swap(arrays):
        moved = [arrays[0]] + [None] * (tiles - 1)
        for s in reversed(range(1, tiles)):
            moved[s] = lax.ppermute(arrays[s], "tile", [(i, i ^ s) for i in range(tiles)])
        return moved

    pack_scratch = [
        pltpu.VMEM((local_rows, cols, chans), BF16),
        pltpu.VMEM((local_rows, cols + 16, chans), F32),
        pltpu.VMEM((dims.rim, chans), F32),
        pltpu.VMEM((tiles, dims.message, chans), BF16),
        dma((2 * dims.bands,)),
        dma((dims.bands,)),
        dma((tiles,)),
    ]
    *sent_main, table = pl.pallas_call(
        functools.partial(pack_main_kernel, dims),
        out_shape=[shaped(dims.message, chans)] * tiles + [shaped(7, tiles, kind=I32)],
        in_specs=[hbm, hbm, hbm],
        out_specs=[hbm] * tiles + [smem],
        scratch_shapes=[
            pltpu.SMEM(boxes.shape, I32),
            pltpu.SMEM(slots.shape, I32),
            pltpu.SMEM((tiles,), I32),
            pltpu.SMEM((tiles,), I32),
            pltpu.SMEM((tiles + 1,), I32),
        ]
        + pack_scratch,
        compiler_params=params,
        cost_estimate=cost(0, 6e6),
        name="pack_main",
    )(boxes, slots, frame)
    got_main = swap(sent_main)

    *sent_extra, last, leading = pl.pallas_call(
        functools.partial(pack_extra_kernel, dims),
        out_shape=[shaped(dims.message, chans)] * tiles + [shaped(dims.bands, cols, chans)] * 2,
        in_specs=[smem, hbm],
        out_specs=[hbm] * (tiles + 2),
        scratch_shapes=pack_scratch,
        compiler_params=params,
        cost_estimate=cost(0, 6e6),
        name="pack_extra",
    )(table, frame)
    up = [(i, (i + 1) % tiles) for i in range(tiles)]
    above = lax.ppermute(last, "tile", up)
    below = lax.ppermute(leading, "tile", [(j, i) for i, j in up])
    got_extra = swap(sent_extra)

    weights = (dec_weight, first_weight, second_weight)
    biases = (dec_bias[None], first_bias[None], second_bias[None])
    restore_scratch = [
        pltpu.VMEM((tiles, dims.message, chans), BF16),
        pltpu.VMEM((3, 12, chans, 2 * chans), BF16),
        dma((tiles,)),
        dma((3, 2)),
        pltpu.VMEM((SPAN // 2 + 2, 2, SPAN, 3 * chans), BF16),
        pltpu.VMEM((SPAN, SPAN, chans), F32),
        pltpu.VMEM((S // 2 + 1, 2, S, 3 * chans), BF16),
        pltpu.VMEM((S // 2 + 1, 2, S, 3 * chans), BF16),
        pltpu.VMEM((S, S, chans), BF16),
        dma,
    ]
    *sent_back, partial = pl.pallas_call(
        functools.partial(main_kernel, dims),
        out_shape=[shaped(dims.back_rows, SPAN, chans)] * tiles + [shaped(CAP, S, S, chans)],
        in_specs=[hbm] * tiles + [smem] + [hbm] * 3 + [vmem] * 3,
        out_specs=[hbm] * (tiles + 1),
        scratch_shapes=restore_scratch
        + [pltpu.VMEM((tiles, dims.back_rows, SPAN, chans), BF16), dma((tiles,))],
        compiler_params=params,
        cost_estimate=cost(7e9, 8e6),
        name="restore_main",
    )(*got_main, table, *weights, *biases)
    got_back = swap(sent_back)

    restorations = pl.pallas_call(
        functools.partial(extra_kernel, dims),
        out_shape=shaped(CAP, S, S, chans),
        in_specs=[hbm] * tiles + [smem] + [hbm] * 3 + [vmem] * 3 + [hbm],
        out_specs=hbm,
        scratch_shapes=restore_scratch,
        input_output_aliases={tiles + 7: 0},
        compiler_params=params,
        cost_estimate=cost(6e9, 8e6),
        name="restore_extra",
    )(*got_extra, table, *weights, *biases, partial)

    above, below, _ = lax.optimization_barrier((above, below, sent_back[0]))
    decoded = pl.pallas_call(
        functools.partial(decode_kernel, dims),
        out_shape=shaped(local_rows, cols, chans),
        in_specs=[hbm] * 4 + [vmem],
        out_specs=vmem,
        scratch_shapes=[
            pltpu.VMEM((local_rows, cols, chans), BF16),
            pltpu.VMEM((dims.bands, cols, chans), BF16),
            pltpu.VMEM((dims.bands, cols, chans), BF16),
            pltpu.VMEM((12, chans, 2 * chans), BF16),
            pltpu.VMEM((2, cols, 12 * chans), BF16),
            dma((3 * dims.bands,)),
            dma((2,)),
        ],
        compiler_params=params,
        cost_estimate=cost(3e9, 6e6),
        name="decode",
    )(frame, above, below, weights[0], biases[0])

    finished = pl.pallas_call(
        functools.partial(paste_kernel, dims),
        out_shape=shaped(local_rows, cols, chans),
        in_specs=[smem, vmem] + [vmem] * tiles,
        out_specs=hbm,
        scratch_shapes=[
            pltpu.VMEM((local_rows, cols, chans), F32),
            pltpu.VMEM((local_rows, cols, chans), BF16),
            dma((local_rows,)),
        ],
        compiler_params=params,
        cost_estimate=cost(0, 6e6),
        name="paste",
    )(table, decoded, *got_back)
    return finished.reshape(features.shape), restorations


def solution(mesh):
    return jax.shard_map(
        shards,
        mesh=mesh,
        in_specs=(
            P("sess", "tile", None, None),
            P(),
            P(),
            P(),
            P(),
            P(),
            P(),
            P(None, "sess"),
            P("sess"),
        ),
        out_specs=(P("sess", "tile", None, None), P(("sess", "tile"), None, None, None)),
        check_vma=False,
    )
```

time: 464 us -> 76.4 us (0.16)
  loops' own time: 163 us -> 0 us
  local copies, waits for them, and re-layouts: 106 us -> 8.6 us
  other arithmetic: 91 us -> 0 us
  waiting for transfers between devices: 55.1 us -> 1.53 us
  Pallas kernels: 0 us -> 40.5 us
  matrix products: 29.2 us -> 0 us
  starting transfers between devices: 13.9 us -> 24.4 us
    another operation x3 -> x0, loops' own time: 163 us -> none  [the longest x1 92.2 us: shards(): sent, meta = lax.map(outgoing, slots)]
    dynamic_update_slice x32 -> x0, local copies, waits for them, and re-layouts: 49.2 us -> none  [the longest x16 28.7 us: paste_slot(): lax.dynamic_update_slice(canvas, old + incoming.astype(jnp.float32), (sta...]
    all_to_all x3 -> x0, waiting for transfers between devices: 42.7 us -> none  [the longest x1 20.4 us: shards(): lax.all_to_all(sent, 'tile', split_axis=0, concat_axis=0, tiled=True)]
    dynamic_slice x68 -> x0, local copies, waits for them, and re-layouts: 41.6 us -> none  [the longest x16 10.5 us: locate(): length = UNIT * (boxes[2, crop] + 2)]
    pallas_call x0 -> x6, Pallas kernels: none -> 40.5 us  [the longest x1 12.1 us: shards(): pl.pallas_call(functools.partial(main_kernel, dims), out_shape=[shaped(di...]
    reduce_sum x32 -> x0, other arithmetic: 40.4 us -> none  [locate(): start = jnp.sum((global_rows < row0).astype(jnp.int32))]
    dot_general x19 -> x0, matrix products: 29.2 us -> none  [the longest x15 18 us: conv_taps(): jnp.einsum('...hwk,kd->...hwd', wide[..., offset:offset + height, :, :],...]
    ppermute x2 -> x23, starting transfers between devices: 3.39 us -> 24.4 us  [the longest x21 21.7 us: swap(): lax.ppermute(arrays[s], 'tile', [(i, i ^ s) for i in range(tiles)])]
  transfers between devices with their start and end apart: 5 -> 23, of which waited for: 5 -> 2; matrix products, arithmetic and copies ran while one was open for 1% -> 0% of each run, Pallas kernels for 0% -> 44%
where the time goes in v2:
time: 76.4 us; the launch traced here: 76 us
  Pallas kernels  40.5 us (53%)
  starting transfers between devices  24.4 us (32%)
  local copies, waits for them, and re-layouts  8.6 us (11%)
  waiting for transfers between devices  1.53 us (2%)
  between operations  0.97 us (1%)
    ppermute x21, starting transfers between devices, swap(): lax.ppermute(arrays[s], 'tile', [(i, i ^ s) for i in range(tiles)])  21.7 us
    pallas_call x1, Pallas kernels, shards(): pl.pallas_call(functools.partial(main_kernel, dims), out_shape=[shaped(di...  12.1 us
    pallas_call x1, Pallas kernels, shards(): pl.pallas_call(functools.partial(extra_kernel, dims), out_shape=shaped(CA...  11.2 us
    unnamed x28, local copies, waits for them, and re-layouts  8.6 us
    pallas_call x1, Pallas kernels, shards(): pl.pallas_call(functools.partial(decode_kernel, dims), out_shape=shaped(l...  5.48 us
    pallas_call x1, Pallas kernels, shards(): pl.pallas_call(functools.partial(pack_extra_kernel, dims), out_shape=[sha...  4.86 us
    pallas_call x1, Pallas kernels, shards(): pl.pallas_call(functools.partial(pack_main_kernel, dims), out_shape=[shap...  4.4 us
    pallas_call x1, Pallas kernels, shards(): pl.pallas_call(functools.partial(paste_kernel, dims), out_shape=shaped(lo...  2.4 us
  transfers between devices with their start and end apart: 23, of which 2 were waited for; matrix products, arithmetic and copies ran while one was open for 0% of the time, Pallas kernels for 44%

profile of v2, /device:TPU:0, one launch (start us, length us, event | category | flops | bytes accessed | tf_op | source)
XLA Modules:
  0.0 76.0 jit_solution(2785558817099551868)
XLA Ops:
  0.6 0.0 copy-start
  0.6 1.2 %copy-done = bf16[6,2,320,128]{3,2,1,0:T(8,128)(2,1)S(1)} copy-done((bf16[6,2,320,128]{3,2,1,0:T(8,128)(2,1)S(1)}, bf16[6,2,320,128]{3,2,1,0:T(8,128)(2,1)}, u32[]{:S(2)}) %copy-start) | copy-done | bytes 983064
  1.8 0.7 copy-done.3
  2.5 0.7 copy-done.4
  3.2 4.4 %pack_main.1 = (bf16[400,128]{1,0:T(8,128)(2,1)S(1)}, bf16[400,128]{1,0:T(8,128)(2,1)S(1)}, bf16[400,128]{1,0:T(8,128)(2,1)S(1)}, bf16[400,128]{1,0:T(8,128)(2,1...) custom-call(s32[3,8]{1,0:T(4,128)S(1)} %copy-done.3, ...), custom_call_target="tpu_custom_call" | custom-call | bytes 6000000 | tf_op jit(solution)/shard_map/pack_main/pallas_call | solution.py:492
  7.6 0.5 collective-permute-start.2
  8.1 2.6 %collective-permute-start.3 = (bf16[400,128]{1,0:T(8,128)(2,1)S(1)}, bf16[400,128]{1,0:T(8,128)(2,1)S(1)}, u32[]{:S(2)}, u32[]{:S(2)}) collective-permute-start(bf16[400,128]{1,0:T(8,128)(2,1)S(1)} %get-tuple-element.37), channel_id=1, source_target_pairs={{0,2},{1,3},{2,0},{3,1},{4,6},{5,7},{6,4},{7,5},{8,10},{9,11},{10,... | collective-permute-start | bytes 307208 | tf_op jit(solution)/shard_map/ppermute | solution.py:480
  10.7 0.1 collective-permute-start.4
  10.7 1.8 %collective-permute-start.5 = (bf16[400,128]{1,0:T(8,128)(2,1)S(1)}, bf16[400,128]{1,0:T(8,128)(2,1)S(1)}, u32[]{:S(2)}, u32[]{:S(2)}) collective-permute-start(bf16[400,128]{1,0:T(8,128)(2,1)S(1)} %get-tuple-element.39), channel_id=1, source_target_pairs={{0,4},{1,5},{2,6},{3,7},{4,0},{5,1},{6,2},{7,3},{8,12},{9,13},{10,... | collective-permute-start | bytes 307208 | tf_op jit(solution)/shard_map/ppermute | solution.py:480
  12.5 0.0 collective-permute-start.6
  12.5 1.2 %copy-done.1 = bf16[6,2,320,128]{3,2,1,0:T(8,128)(2,1)S(1)} copy-done((bf16[6,2,320,128]{3,2,1,0:T(8,128)(2,1)S(1)}, bf16[6,2,320,128]{3,2,1,0:T(8,128)(2,1)}, u32[]{:S(2)}) %copy-start.1) | copy-done | bytes 983064
  13.7 4.9 %pack_extra.1 = (bf16[400,128]{1,0:T(8,128)(2,1)S(1)}, bf16[400,128]{1,0:T(8,128)(2,1)S(1)}, bf16[400,128]{1,0:T(8,128)(2,1)S(1)}, bf16[400,128]{1,0:T(8,128)(2,...) custom-call(s32[7,8]{1,0:T(8,128)S(1)} %get-tuple-element.32.table.r, ...), custom_call_target="tpu_custom_call" | custom-call | bytes 6000000 | tf_op jit(solution)/shard_map/pack_extra/pallas_call | solution.py:511
  18.6 0.0 collective-permute-done.2.refs_1_
  18.6 2.7 %collective-permute-start.7 = (bf16[400,128]{1,0:T(8,128)(2,1)S(1)}, bf16[400,128]{1,0:T(8,128)(2,1)S(1)}, u32[]{:S(2)}, u32[]{:S(2)}) collective-permute-start(bf16[400,128]{1,0:T(8,128)(2,1)S(1)} %get-tuple-element.41), channel_id=1, source_target_pairs={{0,6},{1,7},{2,4},{3,5},{4,2},{5,3},{6,0},{7,1},{8,14},{9,15},{10,... | collective-permute-start | bytes 307208 | tf_op jit(solution)/shard_map/ppermute | solution.py:480
  21.3 0.0 collective-permute-done.3.refs_2_
  21.3 0.1 collective-permute-start.8
  21.4 0.0 collective-permute-done.4.refs_3_
  21.4 0.3 collective-permute-start.16
  21.7 1.6 %collective-permute-start.17 = (bf16[400,128]{1,0:T(8,128)(2,1)S(1)}, bf16[400,128]{1,0:T(8,128)(2,1)S(1)}, u32[]{:S(2)}, u32[]{:S(2)}) collective-permute-start(bf16[400,128]{1,0:T(8,128)(2,1)S(1)} %get-tuple-element.55), channel_id=1, source_target_pairs={{0,2},{1,3},{2,0},{3,1},{4,6},{5,7},{6,4},{7,5},{8,10},{9,11},{10,... | collective-permute-start | bytes 307208 | tf_op jit(solution)/shard_map/ppermute | solution.py:480
  23.4 0.0 collective-permute-start.18
  23.4 1.4 %collective-permute-done.7.refs_6_ = bf16[400,128]{1,0:T(8,128)(2,1)S(1)} collective-permute-done((bf16[400,128]{1,0:T(8,128)(2,1)S(1)}, bf16[400,128]{1,0:T(8,128)(2,1)S(1)}, u32[]{:S(2)}, u32[]{:S(2)}) %collective-permute-start.7) | collective-permute-done | bytes 102432 | tf_op jit(solution)/shard_map/ppermute | solution.py:480
  24.8 2.2 %collective-permute-start.19 = (bf16[400,128]{1,0:T(8,128)(2,1)S(1)}, bf16[400,128]{1,0:T(8,128)(2,1)S(1)}, u32[]{:S(2)}, u32[]{:S(2)}) collective-permute-start(bf16[400,128]{1,0:T(8,128)(2,1)S(1)} %get-tuple-element.57), channel_id=1, source_target_pairs={{0,4},{1,5},{2,6},{3,7},{4,0},{5,1},{6,2},{7,3},{8,12},{9,13},{10,... | collective-permute-start | bytes 307208 | tf_op jit(solution)/shard_map/ppermute | solution.py:480
  26.9 0.1 collective-permute-done.8.refs_7_
  27.0 1.5 %collective-permute-start.20 = (bf16[400,128]{1,0:T(8,128)(2,1)S(1)}, bf16[400,128]{1,0:T(8,128)(2,1)S(1)}, u32[]{:S(2)}, u32[]{:S(2)}) collective-permute-start(bf16[400,128]{1,0:T(8,128)(2,1)S(1)} %get-tuple-element.58), channel_id=1, source_target_pairs={{0,5},{1,4},{2,7},{3,6},{4,1},{5,0},{6,3},{7,2},{8,13},{9,12},{10,... | collective-permute-start | bytes 307208 | tf_op jit(solution)/shard_map/ppermute | solution.py:480
  28.5 1.4 %collective-permute-start.21 = (bf16[400,128]{1,0:T(8,128)(2,1)S(1)}, bf16[400,128]{1,0:T(8,128)(2,1)S(1)}, u32[]{:S(2)}, u32[]{:S(2)}) collective-permute-start(bf16[400,128]{1,0:T(8,128)(2,1)S(1)} %get-tuple-element.59), channel_id=1, source_target_pairs={{0,6},{1,7},{2,4},{3,5},{4,2},{5,3},{6,0},{7,1},{8,14},{9,15},{10,... | collective-permute-start | bytes 307208 | tf_op jit(solution)/shard_map/ppermute | solution.py:480
  30.0 0.0 collective-permute-done.17.refs_2_
  30.0 0.6 collective-permute-start.22
  30.6 1.0 %copy-done.5 = bf16[9,128,128]{2,1,0:T(8,128)(2,1)S(1)} copy-done((bf16[9,128,128]{2,1,0:T(8,128)(2,1)S(1)}, bf16[9,128,128]{2,1,0:T(8,128)(2,1)}, u32[]{:S(2)}) %copy-start.5) | copy-done | bytes 294936
  31.6 1.0 %copy-done.7 = bf16[9,128,128]{2,1,0:T(8,128)(2,1)S(1)} copy-done((bf16[9,128,128]{2,1,0:T(8,128)(2,1)S(1)}, bf16[9,128,128]{2,1,0:T(8,128)(2,1)}, u32[]{:S(2)}) %copy-start.7) | copy-done | bytes 294936
  32.5 1.0 %copy-done.9 = bf16[9,128,128]{2,1,0:T(8,128)(2,1)S(1)} copy-done((bf16[9,128,128]{2,1,0:T(8,128)(2,1)S(1)}, bf16[9,128,128]{2,1,0:T(8,128)(2,1)}, u32[]{:S(2)}) %copy-start.9) | copy-done | bytes 294936
  33.5 0.7 copy-done.11
  34.2 0.7 copy-done.12
  34.8 0.7 copy-done.13
  35.5 12.1 %restore_main.1 = (bf16[6,48,128]{2,1,0:T(8,128)(2,1)S(1)}, bf16[6,48,128]{2,1,0:T(8,128)(2,1)S(1)}, bf16[6,48,128]{2,1,0:T(8,128)(2,1)S(1)}, bf16[6,48,128]{2,1...) custom-call(bf16[400,128]{1,0:T(8,128)(2,1)S(1)} %get-tuple-element., ...), custom_call_target="tpu_custom_call" | custom-call | flops 7000000000 | bytes 8000000 | tf_op jit(solution)/shard_map/restore_main/pallas_call | solution.py:540
  47.6 0.0 collective-permute-done.18.refs_3_
  47.6 1.0 %collective-permute-start = (bf16[6,320,128]{2,1,0:T(8,128)(2,1)S(1)}, bf16[6,320,128]{2,1,0:T(8,128)(2,1)S(1)}, u32[]{:S(2)}, u32[]{:S(2)}) collective-permute-start(bf16[6,320,128]{2,1,0:T(8,128)(2,1)S(1)} %get-tuple-element.33), channel_id=1, source_target_pairs={{0,1},{1,2},{2,3},{3,4},{4,5},{5,6},{6,7},{7,0},{8,9},{9,10},{10,1... | collective-permute-start | bytes 1474568 | tf_op jit(solution)/shard_map/ppermute | solution.py:522
  48.6 0.0 collective-permute-done.19.refs_4_
  48.6 1.7 %collective-permute-start.1 = (bf16[6,320,128]{2,1,0:T(8,128)(2,1)S(1)}, bf16[6,320,128]{2,1,0:T(8,128)(2,1)S(1)}, u32[]{:S(2)}, u32[]{:S(2)}) collective-permute-start(bf16[6,320,128]{2,1,0:T(8,128)(2,1)S(1)} %get-tuple-element.34), channel_id=1, source_target_pairs={{1,0},{2,1},{3,2},{4,3},{5,4},{6,5},{7,6},{0,7},{9,8},{10,9},{11,1... | collective-permute-start | bytes 1474568 | tf_op jit(solution)/shard_map/ppermute | solution.py:523
  50.3 0.6 collective-permute-start.10
  50.9 1.2 %collective-permute-start.11 = (bf16[6,48,128]{2,1,0:T(8,128)(2,1)S(1)}, bf16[6,48,128]{2,1,0:T(8,128)(2,1)S(1)}, u32[]{:S(2)}, u32[]{:S(2)}) collective-permute-start(bf16[6,48,128]{2,1,0:T(8,128)(2,1)S(1)} %get-tuple-element.48), channel_id=1, source_target_pairs={{0,3},{1,2},{2,1},{3,0},{4,7},{5,6},{6,5},{7,4},{8,11},{9,10},{10,... | collective-permute-start | bytes 221192 | tf_op jit(solution)/shard_map/ppermute | solution.py:480
  52.2 11.2 %restore_extra.1 = bf16[2,64,64,128]{3,2,1,0:T(8,128)(2,1)} custom-call(bf16[400,128]{1,0:T(8,128)(2,1)S(1)} %get-tuple-element.53.refs_0_, bf16[400,128]{1,0:T(8,128)(2,1)S(1)} %collective-permute-done.16.refs_1_, bf16[400,128]{1,0:T(8,128)(2,1)S(1)} %collective-permute-done.17.refs_2_, ...), custom_call_target="tpu_custom_call", output_to_operand_aliasing={{}: (15, {})} | custom-call | flops 6000000000 | bytes 8000000 | tf_op jit(solution)/shard_map/restore_extra/pallas_call | solution.py:553
  63.4 0.0 collective-permute-done.above
  63.4 0.1 collective-permute-start.12
  63.5 0.1 collective-permute-start.13
  63.6 1.8 %collective-permute-start.14 = (bf16[6,48,128]{2,1,0:T(8,128)(2,1)S(1)}, bf16[6,48,128]{2,1,0:T(8,128)(2,1)S(1)}, u32[]{:S(2)}, u32[]{:S(2)}) collective-permute-start(bf16[6,48,128]{2,1,0:T(8,128)(2,1)S(1)} %get-tuple-element.51), channel_id=1, source_target_pairs={{0,6},{1,7},{2,4},{3,5},{4,2},{5,3},{6,0},{7,1},{8,14},{9,15},{10,... | collective-permute-start | bytes 221192 | tf_op jit(solution)/shard_map/ppermute | solution.py:480
  65.4 2.5 %collective-permute-start.15 = (bf16[6,48,128]{2,1,0:T(8,128)(2,1)S(1)}, bf16[6,48,128]{2,1,0:T(8,128)(2,1)S(1)}, u32[]{:S(2)}, u32[]{:S(2)}) collective-permute-start(bf16[6,48,128]{2,1,0:T(8,128)(2,1)S(1)} %get-tuple-element.52), channel_id=1, source_target_pairs={{0,7},{1,6},{2,5},{3,4},{4,3},{5,2},{6,1},{7,0},{8,15},{9,14},{10,... | collective-permute-start | bytes 221192 | tf_op jit(solution)/shard_map/ppermute | solution.py:480
  67.9 5.5 %decode.1.decoded = bf16[12,320,128]{2,1,0:T(8,128)(2,1)S(1)} custom-call(bf16[12,320,128]{2,1,0:T(8,128)(2,1)S(1)} %bitcast.7, bf16[6,320,128]{2,1,0:T(8,128)(2,1)S(1)} %collective-permute-done.above, bf16[6,320,128]{2,1,0:T(8,128)(2,1)S(1)} %collective-permute-done.1.below, bf16[9,128,128]{2,1,0:T(8,128)(2,1)S(1)} %copy-done.10, f32[1,128]{1,0:T(1,128)S(1)} %bitcast.14), custom_call_target="tpu_custom_call" | custom-call | flops 3000000000 | bytes 6000000 | tf_op jit(solution)/shard_map/decode/pallas_call | solution.py:566
  73.4 2.4 %paste.1 = bf16[12,320,128]{2,1,0:T(8,128)(2,1)} custom-call(s32[7,8]{1,0:T(8,128)S(1)} %get-tuple-element.32.table.refs_8_, bf16[12,320,128]{2,1,0:T(8,128)(2,1)S(1)} %decode.1.decoded, bf16[6,48,128]{2,1,0:T(8,128)(2,1)S(1)} %get-tuple-element.43.refs_0_, bf16[6,48,128]{2,1,0:T(8,128)(2,1)S(1)} %collective-permute-done.9.refs_1_, ...), custom_call_target="tpu_custom_call" | custom-call | bytes 6000000 | tf_op jit(solution)/shard_map/paste/pallas_call | solution.py:585
  (32 shorter events, 0.1 us)
Async XLA Ops:
  0.6 1.2 %copy-start = (bf16[6,2,320,128]{3,2,1,0:T(8,128)(2,1)S(1)}, bf16[6,2,320,128]{3,2,1,0:T(8,128)(2,1)}, u32[]{:S(2)}) copy-start(bf16[6,2,320,128]{3,2,1,0:T(8,128)(2,1)} %param.9) | copy-start | bytes 2949124
  1.8 0.7 copy-start.3
  2.5 0.7 copy-start.4
  7.6 11.0 %collective-permute-start.2 = (bf16[400,128]{1,0:T(8,128)(2,1)S(1)}, bf16[400,128]{1,0:T(8,128)(2,1)S(1)}, u32[]{:S(2)}, u32[]{:S(2)}) collective-permute-start(bf16[400,128]{1,0:T(8,128)(2,1)S(1)} %get-tuple-element.36), channel_id=1, source_target_pairs={{0,1},{1,0},{2,3},{3,2},{4,5},{5,4},{6,7},{7,6},{8,9},{9,8},{10,11... | collective-permute-start | bytes 307208 | tf_op jit(solution)/shard_map/ppermute | solution.py:480
  8.1 13.2 %collective-permute-start.3 = (bf16[400,128]{1,0:T(8,128)(2,1)S(1)}, bf16[400,128]{1,0:T(8,128)(2,1)S(1)}, u32[]{:S(2)}, u32[]{:S(2)}) collective-permute-start(bf16[400,128]{1,0:T(8,128)(2,1)S(1)} %get-tuple-element.37), channel_id=1, source_target_pairs={{0,2},{1,3},{2,0},{3,1},{4,6},{5,7},{6,4},{7,5},{8,10},{9,11},{10,... | collective-permute-start | bytes 307208 | tf_op jit(solution)/shard_map/ppermute | solution.py:480
  10.7 10.7 %collective-permute-start.4 = (bf16[400,128]{1,0:T(8,128)(2,1)S(1)}, bf16[400,128]{1,0:T(8,128)(2,1)S(1)}, u32[]{:S(2)}, u32[]{:S(2)}) collective-permute-start(bf16[400,128]{1,0:T(8,128)(2,1)S(1)} %get-tuple-element.38), channel_id=1, source_target_pairs={{0,3},{1,2},{2,1},{3,0},{4,7},{5,6},{6,5},{7,4},{8,11},{9,10},{10,... | collective-permute-start | bytes 307208 | tf_op jit(solution)/shard_map/ppermute | solution.py:480
  10.7 11.0 %collective-permute-start.5 = (bf16[400,128]{1,0:T(8,128)(2,1)S(1)}, bf16[400,128]{1,0:T(8,128)(2,1)S(1)}, u32[]{:S(2)}, u32[]{:S(2)}) collective-permute-start(bf16[400,128]{1,0:T(8,128)(2,1)S(1)} %get-tuple-element.39), channel_id=1, source_target_pairs={{0,4},{1,5},{2,6},{3,7},{4,0},{5,1},{6,2},{7,3},{8,12},{9,13},{10,... | collective-permute-start | bytes 307208 | tf_op jit(solution)/shard_map/ppermute | solution.py:480
  12.5 10.9 %collective-permute-start.6 = (bf16[400,128]{1,0:T(8,128)(2,1)S(1)}, bf16[400,128]{1,0:T(8,128)(2,1)S(1)}, u32[]{:S(2)}, u32[]{:S(2)}) collective-permute-start(bf16[400,128]{1,0:T(8,128)(2,1)S(1)} %get-tuple-element.40), channel_id=1, source_target_pairs={{0,5},{1,4},{2,7},{3,6},{4,1},{5,0},{6,3},{7,2},{8,13},{9,12},{10,... | collective-permute-start | bytes 307208 | tf_op jit(solution)/shard_map/ppermute | solution.py:480
  12.5 1.2 %copy-start.1 = (bf16[6,2,320,128]{3,2,1,0:T(8,128)(2,1)S(1)}, bf16[6,2,320,128]{3,2,1,0:T(8,128)(2,1)}, u32[]{:S(2)}) copy-start(bf16[6,2,320,128]{3,2,1,0:T(8,128)(2,1)} %param.9) | copy-start | bytes 2949124
  18.6 6.2 %collective-permute-start.7 = (bf16[400,128]{1,0:T(8,128)(2,1)S(1)}, bf16[400,128]{1,0:T(8,128)(2,1)S(1)}, u32[]{:S(2)}, u32[]{:S(2)}) collective-permute-start(bf16[400,128]{1,0:T(8,128)(2,1)S(1)} %get-tuple-element.41), channel_id=1, source_target_pairs={{0,6},{1,7},{2,4},{3,5},{4,2},{5,3},{6,0},{7,1},{8,14},{9,15},{10,... | collective-permute-start | bytes 307208 | tf_op jit(solution)/shard_map/ppermute | solution.py:480
  21.3 5.7 %collective-permute-start.8 = (bf16[400,128]{1,0:T(8,128)(2,1)S(1)}, bf16[400,128]{1,0:T(8,128)(2,1)S(1)}, u32[]{:S(2)}, u32[]{:S(2)}) collective-permute-start(bf16[400,128]{1,0:T(8,128)(2,1)S(1)} %get-tuple-element.42), channel_id=1, source_target_pairs={{0,7},{1,6},{2,5},{3,4},{4,3},{5,2},{6,1},{7,0},{8,15},{9,14},{10,... | collective-permute-start | bytes 307208 | tf_op jit(solution)/shard_map/ppermute | solution.py:480
  21.4 7.1 %collective-permute-start.16 = (bf16[400,128]{1,0:T(8,128)(2,1)S(1)}, bf16[400,128]{1,0:T(8,128)(2,1)S(1)}, u32[]{:S(2)}, u32[]{:S(2)}) collective-permute-start(bf16[400,128]{1,0:T(8,128)(2,1)S(1)} %get-tuple-element.54), channel_id=1, source_target_pairs={{0,1},{1,0},{2,3},{3,2},{4,5},{5,4},{6,7},{7,6},{8,9},{9,8},{10,11... | collective-permute-start | bytes 307208 | tf_op jit(solution)/shard_map/ppermute | solution.py:480
  21.7 8.3 %collective-permute-start.17 = (bf16[400,128]{1,0:T(8,128)(2,1)S(1)}, bf16[400,128]{1,0:T(8,128)(2,1)S(1)}, u32[]{:S(2)}, u32[]{:S(2)}) collective-permute-start(bf16[400,128]{1,0:T(8,128)(2,1)S(1)} %get-tuple-element.55), channel_id=1, source_target_pairs={{0,2},{1,3},{2,0},{3,1},{4,6},{5,7},{6,4},{7,5},{8,10},{9,11},{10,... | collective-permute-start | bytes 307208 | tf_op jit(solution)/shard_map/ppermute | solution.py:480
  23.4 24.2 %collective-permute-start.18 = (bf16[400,128]{1,0:T(8,128)(2,1)S(1)}, bf16[400,128]{1,0:T(8,128)(2,1)S(1)}, u32[]{:S(2)}, u32[]{:S(2)}) collective-permute-start(bf16[400,128]{1,0:T(8,128)(2,1)S(1)} %get-tuple-element.56), channel_id=1, source_target_pairs={{0,3},{1,2},{2,1},{3,0},{4,7},{5,6},{6,5},{7,4},{8,11},{9,10},{10,... | collective-permute-start | bytes 307208 | tf_op jit(solution)/shard_map/ppermute | solution.py:480
  24.8 23.9 %collective-permute-start.19 = (bf16[400,128]{1,0:T(8,128)(2,1)S(1)}, bf16[400,128]{1,0:T(8,128)(2,1)S(1)}, u32[]{:S(2)}, u32[]{:S(2)}) collective-permute-start(bf16[400,128]{1,0:T(8,128)(2,1)S(1)} %get-tuple-element.57), channel_id=1, source_target_pairs={{0,4},{1,5},{2,6},{3,7},{4,0},{5,1},{6,2},{7,3},{8,12},{9,13},{10,... | collective-permute-start | bytes 307208 | tf_op jit(solution)/shard_map/ppermute | solution.py:480
  27.0 23.3 %collective-permute-start.20 = (bf16[400,128]{1,0:T(8,128)(2,1)S(1)}, bf16[400,128]{1,0:T(8,128)(2,1)S(1)}, u32[]{:S(2)}, u32[]{:S(2)}) collective-permute-start(bf16[400,128]{1,0:T(8,128)(2,1)S(1)} %get-tuple-element.58), channel_id=1, source_target_pairs={{0,5},{1,4},{2,7},{3,6},{4,1},{5,0},{6,3},{7,2},{8,13},{9,12},{10,... | collective-permute-start | bytes 307208 | tf_op jit(solution)/shard_map/ppermute | solution.py:480
  28.5 21.7 %collective-permute-start.21 = (bf16[400,128]{1,0:T(8,128)(2,1)S(1)}, bf16[400,128]{1,0:T(8,128)(2,1)S(1)}, u32[]{:S(2)}, u32[]{:S(2)}) collective-permute-start(bf16[400,128]{1,0:T(8,128)(2,1)S(1)} %get-tuple-element.59), channel_id=1, source_target_pairs={{0,6},{1,7},{2,4},{3,5},{4,2},{5,3},{6,0},{7,1},{8,14},{9,15},{10,... | collective-permute-start | bytes 307208 | tf_op jit(solution)/shard_map/ppermute | solution.py:480
  30.0 21.0 %collective-permute-start.22 = (bf16[400,128]{1,0:T(8,128)(2,1)S(1)}, bf16[400,128]{1,0:T(8,128)(2,1)S(1)}, u32[]{:S(2)}, u32[]{:S(2)}) collective-permute-start(bf16[400,128]{1,0:T(8,128)(2,1)S(1)} %get-tuple-element.60), channel_id=1, source_target_pairs={{0,7},{1,6},{2,5},{3,4},{4,3},{5,2},{6,1},{7,0},{8,15},{9,14},{10,... | collective-permute-start | bytes 307208 | tf_op jit(solution)/shard_map/ppermute | solution.py:480
  30.6 1.0 %copy-start.5 = (bf16[9,128,128]{2,1,0:T(8,128)(2,1)S(1)}, bf16[9,128,128]{2,1,0:T(8,128)(2,1)}, u32[]{:S(2)}) copy-start(bf16[9,128,128]{2,1,0:T(8,128)(2,1)} %refs_10_.3) | copy-start | bytes 884740
  31.6 1.0 %copy-start.7 = (bf16[9,128,128]{2,1,0:T(8,128)(2,1)S(1)}, bf16[9,128,128]{2,1,0:T(8,128)(2,1)}, u32[]{:S(2)}) copy-start(bf16[9,128,128]{2,1,0:T(8,128)(2,1)} %refs_11_.3) | copy-start | bytes 884740
  32.5 1.0 %copy-start.9 = (bf16[9,128,128]{2,1,0:T(8,128)(2,1)S(1)}, bf16[9,128,128]{2,1,0:T(8,128)(2,1)}, u32[]{:S(2)}) copy-start(bf16[9,128,128]{2,1,0:T(8,128)(2,1)} %refs_9_.3) | copy-start | bytes 884740
  33.5 0.7 copy-start.11
  34.2 0.7 copy-start.12
  34.8 0.7 copy-start.13
  35.5 16.7 %copy-start.6 = (bf16[9,128,128]{2,1,0:T(8,128)(2,1)S(1)}, bf16[9,128,128]{2,1,0:T(8,128)(2,1)}, u32[]{:S(2)}) copy-start(bf16[9,128,128]{2,1,0:T(8,128)(2,1)} %refs_10_.3) | copy-start | bytes 884740
  35.5 16.7 %copy-start.8 = (bf16[9,128,128]{2,1,0:T(8,128)(2,1)S(1)}, bf16[9,128,128]{2,1,0:T(8,128)(2,1)}, u32[]{:S(2)}) copy-start(bf16[9,128,128]{2,1,0:T(8,128)(2,1)} %refs_11_.3) | copy-start | bytes 884740
  35.5 16.7 %copy-start.10 = (bf16[9,128,128]{2,1,0:T(8,128)(2,1)S(1)}, bf16[9,128,128]{2,1,0:T(8,128)(2,1)}, u32[]{:S(2)}) copy-start(bf16[9,128,128]{2,1,0:T(8,128)(2,1)} %refs_9_.3) | copy-start | bytes 884740
  47.6 15.8 %collective-permute-start = (bf16[6,320,128]{2,1,0:T(8,128)(2,1)S(1)}, bf16[6,320,128]{2,1,0:T(8,128)(2,1)S(1)}, u32[]{:S(2)}, u32[]{:S(2)}) collective-permute-start(bf16[6,320,128]{2,1,0:T(8,128)(2,1)S(1)} %get-tuple-element.33), channel_id=1, source_target_pairs={{0,1},{1,2},{2,3},{3,4},{4,5},{5,6},{6,7},{7,0},{8,9},{9,10},{10,1... | collective-permute-start | bytes 1474568 | tf_op jit(solution)/shard_map/ppermute | solution.py:522
  48.6 14.9 %collective-permute-start.1 = (bf16[6,320,128]{2,1,0:T(8,128)(2,1)S(1)}, bf16[6,320,128]{2,1,0:T(8,128)(2,1)S(1)}, u32[]{:S(2)}, u32[]{:S(2)}) collective-permute-start(bf16[6,320,128]{2,1,0:T(8,128)(2,1)S(1)} %get-tuple-element.34), channel_id=1, source_target_pairs={{1,0},{2,1},{3,2},{4,3},{5,4},{6,5},{7,6},{0,7},{9,8},{10,9},{11,1... | collective-permute-start | bytes 1474568 | tf_op jit(solution)/shard_map/ppermute | solution.py:523
  50.3 13.3 %collective-permute-start.9 = (bf16[6,48,128]{2,1,0:T(8,128)(2,1)S(1)}, bf16[6,48,128]{2,1,0:T(8,128)(2,1)S(1)}, u32[]{:S(2)}, u32[]{:S(2)}) collective-permute-start(bf16[6,48,128]{2,1,0:T(8,128)(2,1)S(1)} %get-tuple-element.46), channel_id=1, source_target_pairs={{0,1},{1,0},{2,3},{3,2},{4,5},{5,4},{6,7},{7,6},{8,9},{9,8},{10,11... | collective-permute-start | bytes 221192 | tf_op jit(solution)/shard_map/ppermute | solution.py:480
  50.3 15.1 %collective-permute-start.10 = (bf16[6,48,128]{2,1,0:T(8,128)(2,1)S(1)}, bf16[6,48,128]{2,1,0:T(8,128)(2,1)S(1)}, u32[]{:S(2)}, u32[]{:S(2)}) collective-permute-start(bf16[6,48,128]{2,1,0:T(8,128)(2,1)S(1)} %get-tuple-element.47), channel_id=1, source_target_pairs={{0,2},{1,3},{2,0},{3,1},{4,6},{5,7},{6,4},{7,5},{8,10},{9,11},{10,... | collective-permute-start | bytes 221192 | tf_op jit(solution)/shard_map/ppermute | solution.py:480
  50.9 22.4 %collective-permute-start.11 = (bf16[6,48,128]{2,1,0:T(8,128)(2,1)S(1)}, bf16[6,48,128]{2,1,0:T(8,128)(2,1)S(1)}, u32[]{:S(2)}, u32[]{:S(2)}) collective-permute-start(bf16[6,48,128]{2,1,0:T(8,128)(2,1)S(1)} %get-tuple-element.48), channel_id=1, source_target_pairs={{0,3},{1,2},{2,1},{3,0},{4,7},{5,6},{6,5},{7,4},{8,11},{9,10},{10,... | collective-permute-start | bytes 221192 | tf_op jit(solution)/shard_map/ppermute | solution.py:480
  52.2 15.7 %copy-start.2 = (bf16[6,2,320,128]{3,2,1,0:T(8,128)(2,1)S(1)}, bf16[6,2,320,128]{3,2,1,0:T(8,128)(2,1)}, u32[]{:S(2)}) copy-start(bf16[6,2,320,128]{3,2,1,0:T(8,128)(2,1)} %param.9) | copy-start | bytes 2949124
  63.4 10.0 %collective-permute-start.12 = (bf16[6,48,128]{2,1,0:T(8,128)(2,1)S(1)}, bf16[6,48,128]{2,1,0:T(8,128)(2,1)S(1)}, u32[]{:S(2)}, u32[]{:S(2)}) collective-permute-start(bf16[6,48,128]{2,1,0:T(8,128)(2,1)S(1)} %get-tuple-element.49), channel_id=1, source_target_pairs={{0,4},{1,5},{2,6},{3,7},{4,0},{5,1},{6,2},{7,3},{8,12},{9,13},{10,... | collective-permute-start | bytes 221192 | tf_op jit(solution)/shard_map/ppermute | solution.py:480
  63.5 9.9 %collective-permute-start.13 = (bf16[6,48,128]{2,1,0:T(8,128)(2,1)S(1)}, bf16[6,48,128]{2,1,0:T(8,128)(2,1)S(1)}, u32[]{:S(2)}, u32[]{:S(2)}) collective-permute-start(bf16[6,48,128]{2,1,0:T(8,128)(2,1)S(1)} %get-tuple-element.50), channel_id=1, source_target_pairs={{0,5},{1,4},{2,7},{3,6},{4,1},{5,0},{6,3},{7,2},{8,13},{9,12},{10,... | collective-permute-start | bytes 221192 | tf_op jit(solution)/shard_map/ppermute | solution.py:480
  63.6 9.8 %collective-permute-start.14 = (bf16[6,48,128]{2,1,0:T(8,128)(2,1)S(1)}, bf16[6,48,128]{2,1,0:T(8,128)(2,1)S(1)}, u32[]{:S(2)}, u32[]{:S(2)}) collective-permute-start(bf16[6,48,128]{2,1,0:T(8,128)(2,1)S(1)} %get-tuple-element.51), channel_id=1, source_target_pairs={{0,6},{1,7},{2,4},{3,5},{4,2},{5,3},{6,0},{7,1},{8,14},{9,15},{10,... | collective-permute-start | bytes 221192 | tf_op jit(solution)/shard_map/ppermute | solution.py:480
  65.4 8.0 %collective-permute-start.15 = (bf16[6,48,128]{2,1,0:T(8,128)(2,1)S(1)}, bf16[6,48,128]{2,1,0:T(8,128)(2,1)S(1)}, u32[]{:S(2)}, u32[]{:S(2)}) collective-permute-start(bf16[6,48,128]{2,1,0:T(8,128)(2,1)S(1)} %get-tuple-element.52), channel_id=1, source_target_pairs={{0,7},{1,6},{2,5},{3,4},{4,3},{5,2},{6,1},{7,0},{8,15},{9,14},{10,... | collective-permute-start | bytes 221192 | tf_op jit(solution)/shard_map/ppermute | solution.py:480

commit v3 on v2

v3 whole, which is shorter than its diff:
```python
import functools

import jax
import jax.numpy as jnp
from jax import lax
from jax.experimental import pallas as pl
from jax.experimental.pallas import tpu as pltpu
from jax.sharding import PartitionSpec as P

S = 64
UNIT = 12
NCLS = 3
CAP = 2
SPAN = UNIT * (NCLS + 1)
BF16 = jnp.bfloat16
F32 = jnp.float32
I32 = jnp.int32
FULL_GRANT = 62 * 1024 * 1024
SMALL_GRANT = 32 * 1024 * 1024
ROW, COL, SIDE, ROW2, COL2, SIDE2, PLACE = range(7)


def rows_within(window, band_rows, stride):
    return band_rows * (window // stride) + min(band_rows, window % stride)


class Dims:
    def __init__(self, features, tiles):
        self.bands, self.band_rows, self.cols, self.chans = features.shape
        self.tiles = tiles
        self.stride = tiles * self.band_rows
        self.shift = self.stride.bit_length() - 1
        self.local_rows = self.bands * self.band_rows
        self.rows = rows_within(SPAN + 2, self.band_rows, self.stride)
        self.back_rows = rows_within(SPAN, self.band_rows, self.stride)
        self.rim = -(-2 * self.rows // 16) * 16
        self.message = self.rows * SPAN + self.rim


def first_local(row, tile, dims):
    return ((row >> dims.shift) << 1) + jnp.clip((row & (dims.stride - 1)) - 2 * tile, 0, 2)


def global_row(local, tile, dims):
    return ((local >> 1) << dims.shift) + 2 * tile + (local & 1)


def silu(v):
    half = 0.5 * v
    return half + half * jnp.tanh(half)


def both(bias):
    return jnp.concatenate([bias[...], bias[...]], -1)


class RowTaps:
    def __init__(self, source, store, sems):
        chans = source.shape[-1]
        self.store = store
        self.copies = (
            pltpu.make_async_copy(source, store.at[0:3, :, :, 0:chans], sems.at[0]),
            pltpu.make_async_copy(source, store.at[1:4, :, :, chans : 2 * chans], sems.at[1]),
        )

    def start(self):
        for copy in self.copies:
            copy.start()
        chans = self.store.shape[2]
        none = jnp.zeros((3, chans, chans), BF16)
        self.store[3, :, :, 0:chans] = none
        self.store[0, :, :, chans : 2 * chans] = none

    def wait(self):
        for copy in self.copies:
            copy.wait()

    def value(self):
        return self.store[...].reshape(-1, self.store.shape[-1])


class ColumnTaps(RowTaps):
    def __init__(self, source, store, sems):
        chans = source.shape[-1]
        self.store = store
        self.copies = (
            pltpu.make_async_copy(source, store.at[:, 0:3, :, 0:chans], sems.at[0]),
            pltpu.make_async_copy(source, store.at[:, 1:4, :, chans : 2 * chans], sems.at[1]),
        )

    def start(self):
        for copy in self.copies:
            copy.start()
        chans = self.store.shape[2]
        none = jnp.zeros((3, chans, chans), BF16)
        self.store[:, 3, :, 0:chans] = none
        self.store[:, 0, :, chans : 2 * chans] = none


def row_pairs(src, first, count, taps):
    parts = [
        src[pl.ds(first, count), 0],
        src[pl.ds(first, count), 1],
        src[pl.ds(first + 1, count), 0],
        src[pl.ds(first + 1, count), 1],
    ]
    wide = jnp.concatenate(parts, -1)
    return jnp.dot(wide.reshape(-1, wide.shape[-1]), taps.value(), preferred_element_type=F32)


def column_pairs(src, first, count, taps):
    wide = jnp.concatenate([src[pl.ds(first + a, count)] for a in range(3)], -1)
    return jnp.dot(wide.reshape(-1, wide.shape[-1]), taps.value(), preferred_element_type=F32)


def fill_canvas(dims, feat, held, canvas, sems):
    def copy(band):
        return pltpu.make_async_copy(feat.at[band], held.at[band], sems.at[band])

    for band in range(dims.bands):
        copy(band).start()

    def finish():
        edge = jnp.zeros((8, dims.chans), F32)
        for band in range(dims.bands):
            copy(band).wait()
            for i in range(2):
                row = 2 * band + i
                canvas[row, 0:8, :] = edge
                canvas[row, 8 + dims.cols : 16 + dims.cols, :] = edge
                canvas[row, 8 : 8 + dims.cols, :] = held[band, i].astype(F32)

    return finish


def pack_crops(dims, table, row_at, col_at, canvas, rim, staged, sent, sems):
    me = lax.axis_index("tile")
    rim[...] = jnp.zeros_like(rim)

    @pl.loop(0, dims.tiles)
    def _(w):
        row0 = table[row_at, w]
        col0 = table[col_at, w]
        start = first_local(jnp.maximum(row0 - 1, 0), me, dims)
        for i in range(dims.rows):
            row = jnp.minimum(start + i, dims.local_rows - 1)
            staged[w, i * SPAN : (i + 1) * SPAN, :] = canvas[row, pl.ds(col0 + 8, SPAN), :].astype(BF16)
            rim[2 * i : 2 * i + 1, :] = canvas[row, pl.ds(col0 + 7, 1), :]
            rim[2 * i + 1 : 2 * i + 2, :] = canvas[row, pl.ds(col0 + 8 + SPAN, 1), :]
        staged[w, dims.rows * SPAN :, :] = rim[...].astype(BF16)
        pltpu.make_async_copy(staged.at[w], sent.at[w], sems.at[w]).start()

    @pl.loop(0, dims.tiles)
    def _(w):
        pltpu.make_async_copy(staged.at[w], sent.at[w], sems.at[w]).wait()


def pack_main_kernel(
    dims, boxes_in, slots_in, feat, sent, table, last, leading,
    boxes, slots, main, extra, seconds, held, canvas, rim, staged, sems, feat_sems, sent_sems,
):
    copies = (
        pltpu.make_async_copy(boxes_in, boxes, sems.at[0]),
        pltpu.make_async_copy(slots_in, slots, sems.at[1]),
    )
    for copy in copies:
        copy.start()
    finish = fill_canvas(dims, feat, held, canvas, feat_sems)
    edges = (
        pltpu.make_async_copy(feat.at[:, 1], last, sems.at[2]),
        pltpu.make_async_copy(feat.at[:, 0], leading, sems.at[3]),
    )
    for edge in edges:
        edge.start()
    for copy in copies:
        copy.wait()

    def first_pass(w, count):
        one = slots[CAP * w]
        two = slots[CAP * w + 1]
        full = (one >= 0) & (two >= 0)
        second = jnp.where(full, two, -1)
        main[w] = jnp.where(one >= 0, one, two)
        extra[w] = second
        seconds[count] = second
        return count + full.astype(I32)

    lax.fori_loop(0, dims.tiles, first_pass, jnp.int32(0))

    def second_pass(w, count):
        own = main[w]
        idle = own < 0
        crop = jnp.where(idle, seconds[count], own)
        table[ROW, w] = boxes[0, crop]
        table[COL, w] = boxes[1, crop]
        table[SIDE, w] = UNIT * (boxes[2, crop] + 2)
        other = jnp.maximum(extra[w], 0)
        table[ROW2, w] = boxes[0, other]
        table[COL2, w] = boxes[1, other]
        table[SIDE2, w] = jnp.where(extra[w] >= 0, UNIT * (boxes[2, other] + 2), 0)
        table[PLACE, w] = jnp.where(idle, 2, jnp.where(slots[CAP * w] >= 0, 0, 1))
        return count + idle.astype(I32)

    lax.fori_loop(0, dims.tiles, second_pass, jnp.int32(0))
    finish()
    pack_crops(dims, table, ROW, COL, canvas, rim, staged, sent, sent_sems)
    for edge in edges:
        edge.wait()


def pack_extra_kernel(dims, table, feat, sent, held, canvas, rim, staged, sems, feat_sems, sent_sems):
    fill_canvas(dims, feat, held, canvas, feat_sems)()
    pack_crops(dims, table, ROW2, COL2, canvas, rim, staged, sent, sent_sems)


def restore(dims, row0, length, arrival, got, taps, biases, raw, decoded, wide, inner, mixed, delta):
    chans = dims.chans
    above = row0 - 1
    pairs = SPAN // 2
    half = S // 2
    nothing = jnp.zeros((SPAN, 3 * chans), BF16)
    raw[0, 0] = nothing
    raw[pairs, 1] = nothing
    empty = jnp.zeros((half, 4 * chans), BF16)
    for store in (wide, inner):
        store[0] = empty
        store[S + 1] = empty

    @pl.loop(0, dims.tiles)
    def _(e):
        arrival(e).wait()
        start = first_local(jnp.maximum(above, 0), e, dims)
        rim = got[e, dims.rows * SPAN :, :].astype(F32)
        at = lax.broadcasted_iota(I32, (SPAN, chans), 0)
        for i in range(dims.rows):
            local = start + i
            place = global_row(local, e, dims) - above
            place = jnp.where((local < dims.local_rows) & (place < SPAN + 2), place, SPAN + 2)
            line = got[e, i * SPAN : (i + 1) * SPAN, :]
            wider = line.astype(F32)
            left = jnp.where(at == 0, rim[2 * i : 2 * i + 1], pltpu.roll(wider, 1, 0))
            right = jnp.where(at == SPAN - 1, rim[2 * i + 1 : 2 * i + 2], pltpu.roll(wider, SPAN - 1, 0))
            raw[place >> 1, place & 1] = jnp.concatenate([left.astype(BF16), line, right.astype(BF16)], -1)

    taps[0].wait()
    n = 8

    @pl.loop(0, pairs // n)
    def _(step):
        first = step * n
        total = silu(row_pairs(raw, first, n, taps[0]) + both(biases[0]))
        for k in range(n):
            part = total[k * SPAN : (k + 1) * SPAN]
            at = 2 * (first + k)
            upper = raw[first + k, 1, :, chans : 2 * chans].astype(F32) + part[:, :chans]
            lower = raw[first + k + 1, 0, :, chans : 2 * chans].astype(F32) + part[:, chans:]
            decoded[at] = upper.astype(BF16).astype(F32)
            decoded[at + 1] = lower.astype(BF16).astype(F32)

    lengthf = length.astype(F32)
    block = lax.broadcasted_iota(I32, (4, half, SPAN), 0)
    t = 2 * lax.broadcasted_iota(I32, (4, half, SPAN), 1) + block - 1
    j = lax.broadcasted_iota(I32, (4, half, SPAN), 2).astype(F32)
    spots = jnp.clip((t.astype(F32) + 0.5) * lengthf / S - 0.5, 0.0, lengthf - 1.0)
    across = jnp.where((t >= 0) & (t < S), jnp.maximum(0.0, 1.0 - jnp.abs(spots - j)), 0.0)
    across = across.reshape(4 * half, SPAN).astype(BF16)
    group = 4

    @pl.loop(0, S // 2 // group)
    def _(step):
        for k in range(group):
            lines = []
            for parity in range(2):
                s = 2 * (step * group + k) + parity
                spot = jnp.clip((2 * s + 1) * length - S, 0, (length - 1) * 2 * S)
                low = spot >> 7
                part = (spot & 127).astype(F32) * (1.0 / (2 * S))
                high = jnp.minimum(low + 1, SPAN - 1)
                lines.append(((1.0 - part) * decoded[low] + part * decoded[high]).astype(BF16))
            cells = jnp.dot(across, jnp.concatenate(lines, -1), preferred_element_type=F32).astype(BF16)
            for parity in range(2):
                at = 2 * (step * group + k) + parity + 1
                for b in range(4):
                    wide[at, :, b * chans : (b + 1) * chans] = cells[
                        b * half : (b + 1) * half, parity * chans : (parity + 1) * chans
                    ]

    n = 16
    taps[1].wait()

    @pl.loop(0, S // n)
    def _(step):
        first = step * n
        total = silu(column_pairs(wide, first, n, taps[1]) + both(biases[1]))
        at = lax.broadcasted_iota(I32, (n, half, chans), 1)
        even = pltpu.roll(total[:, :chans], n * half - 1, 0).reshape(n, half, chans)
        odd = pltpu.roll(total[:, chans:], 1, 0).reshape(n, half, chans)
        rows = pl.ds(first + 1, n)
        inner[rows, :, 0:chans] = jnp.where(at == 0, 0.0, odd).astype(BF16)
        inner[rows, :, chans : 3 * chans] = total.astype(BF16).reshape(n, half, 2 * chans)
        inner[rows, :, 3 * chans :] = jnp.where(at == half - 1, 0.0, even).astype(BF16)

    taps[2].wait()

    @pl.loop(0, S // n)
    def _(step):
        first = step * n
        total = column_pairs(inner, first, n, taps[2]) + both(biases[2])
        for k in range(n):
            mixed[k, pl.ds(0, half, stride=2), :] = total[k * half : (k + 1) * half, :chans]
            mixed[k, pl.ds(1, half, stride=2), :] = total[k * half : (k + 1) * half, chans:]
        delta[pl.ds(first, n)] = mixed[...].astype(BF16)


def begin(dims, arrived, weights, scratch):
    got, row_store, column_store, got_sems, tap_sems = scratch

    def arrival(e):
        return pltpu.make_async_copy(arrived.at[e], got.at[e], got_sems.at[e])

    for e in range(dims.tiles):
        arrival(e).start()
    taps = (
        RowTaps(weights[0], row_store, tap_sems.at[0]),
        ColumnTaps(weights[1], column_store.at[0], tap_sems.at[1]),
        ColumnTaps(weights[2], column_store.at[1], tap_sems.at[2]),
    )
    for tap in taps:
        tap.start()
    return arrival, taps


def main_kernel(
    dims, table, arrived, dec_w, one_w, two_w, dec_b, one_b, two_b, sent, restored,
    got, row_store, column_store, got_sems, tap_sems, raw, decoded, wide, inner, mixed, delta, sem, back, back_sems,
):
    tiles, chans = dims.tiles, dims.chans
    me = lax.axis_index("tile")
    row0 = table[ROW, me]
    length = table[SIDE, me]
    place = table[PLACE, me]
    scratch = (got, row_store, column_store, got_sems, tap_sems)
    arrival, taps = begin(dims, arrived, (dec_w, one_w, two_w), scratch)
    restore(dims, row0, length, arrival, got, taps, (dec_b, one_b, two_b), raw, decoded, wide, inner, mixed, delta)

    @pl.when(place < CAP)
    def _():
        pltpu.make_async_copy(delta, restored.at[place], sem).start()

    lengthf = length.astype(F32)
    t = lax.broadcasted_iota(I32, (SPAN, S), 0).astype(F32)
    s = lax.broadcasted_iota(I32, (SPAN, S), 1).astype(F32)
    spots = jnp.clip((t + 0.5) * S / lengthf - 0.5, 0.0, S - 1.0)
    lift = jnp.where(t < lengthf, jnp.maximum(0.0, 1.0 - jnp.abs(spots - s)), 0.0)
    coarse = lift.astype(BF16)
    lift = jnp.concatenate([coarse, (lift - coarse.astype(F32)).astype(BF16)], 0)
    scale = 1.0 / (2.0 * lengthf)
    group = 4

    @pl.loop(0, SPAN // 2 // group)
    def _(step):
        for k in range(group):
            lines = []
            for parity in range(2):
                h = 2 * (step * group + k) + parity
                spot = jnp.clip((2 * h + 1) * S - length, 0, (S - 1) * 2 * length)
                low = ((spot.astype(F32) + 0.5) * scale).astype(I32)
                part = (spot - low * 2 * length).astype(F32) * scale
                high = jnp.minimum(low + 1, S - 1)
                lines.append(((1.0 - part) * delta[low].astype(F32) + part * delta[high].astype(F32)).astype(BF16))
            patch = jnp.dot(lift, jnp.concatenate(lines, -1), preferred_element_type=F32)
            patch = (patch[:SPAN] + patch[SPAN:]).astype(BF16)
            for parity in range(2):
                row = row0 + 2 * (step * group + k) + parity
                dest = (row & (dims.stride - 1)) >> 1
                local = ((row >> dims.shift) << 1) + (row & 1)
                back[dest, local - first_local(row0, dest, dims)] = patch[:, parity * chans : (parity + 1) * chans]

    def leave(e):
        return pltpu.make_async_copy(back.at[e], sent.at[e], back_sems.at[e])

    for e in range(tiles):
        leave(e).start()
    for e in range(tiles):
        leave(e).wait()

    @pl.when(place < CAP)
    def _():
        pltpu.make_async_copy(delta, restored.at[place], sem).wait()


def extra_kernel(
    dims, table, arrived, dec_w, one_w, two_w, dec_b, one_b, two_b, partial, restored,
    got, row_store, column_store, got_sems, tap_sems, raw, decoded, wide, inner, mixed, delta, sem,
):
    me = lax.axis_index("tile")
    row0 = table[ROW2, me]
    length = table[SIDE2, me]
    place = table[PLACE, me]

    def write(slot):
        copy = pltpu.make_async_copy(delta, restored.at[slot], sem)
        copy.start()
        copy.wait()

    @pl.when(length > 0)
    def _():
        scratch = (got, row_store, column_store, got_sems, tap_sems)
        arrival, taps = begin(dims, arrived, (dec_w, one_w, two_w), scratch)
        restore(dims, row0, length, arrival, got, taps, (dec_b, one_b, two_b), raw, decoded, wide, inner, mixed, delta)
        write(1)

    @pl.when(length == 0)
    def _():
        delta[...] = jnp.zeros_like(delta)

        @pl.when(place != 0)
        def _():
            write(0)

        @pl.when(place != 1)
        def _():
            write(1)


def decode_kernel(dims, feat, above, below, weight, bias, decoded, held, up, down, store, lines, wide, mixed, sems, tap_sems):
    me = lax.axis_index("tile")
    bands, chans, cols = dims.bands, dims.chans, dims.cols
    half = cols // 2
    taps = ColumnTaps(weight, store, tap_sems)

    def fetch(band):
        return (
            pltpu.make_async_copy(feat.at[band], held.at[band], sems.at[0, band]),
            pltpu.make_async_copy(above.at[band], up.at[band], sems.at[1, band]),
            pltpu.make_async_copy(below.at[band], down.at[band], sems.at[2, band]),
        )

    for band in range(bands):
        for copy in fetch(band):
            copy.start()
    taps.start()
    top = (me == 0).astype(I32)
    bottom = (me == dims.tiles - 1).astype(I32)
    edge = jnp.zeros((8, chans), F32)
    for a in range(4):
        lines[a, 0:8] = edge
        lines[a, 8 + cols :] = edge
    for band in range(bands):
        for copy in fetch(band):
            copy.wait()
    taps.wait()

    @pl.loop(0, bands)
    def _(j):
        no_top = (top == 1) & (j == 0)
        no_bottom = (bottom == 1) & (j == bands - 1)
        over = up[jnp.maximum(j - top, 0)].astype(F32)
        under = down[jnp.minimum(j + bottom, bands - 1)].astype(F32)
        middle = slice(8, 8 + cols)
        lines[0, middle] = jnp.where(no_top, 0.0, over)
        lines[1, middle] = held[j, 0].astype(F32)
        lines[2, middle] = held[j, 1].astype(F32)
        lines[3, middle] = jnp.where(no_bottom, 0.0, under)
        for a in range(4):
            for b in range(4):
                wide[a, :, b * chans : (b + 1) * chans] = lines[a, pl.ds(7 + b, half, stride=2), :].astype(BF16)
        total = silu(column_pairs(wide, 0, 2, taps) + both(bias))
        for i in range(2):
            part = total[i * half : (i + 1) * half]
            for b in range(2):
                here = lines[i + 1, pl.ds(8 + b, half, stride=2), :]
                mixed[i, pl.ds(b, half, stride=2), :] = here + part[:, b * chans : (b + 1) * chans]
            decoded[2 * j + i] = mixed[i].astype(BF16)


def paste_kernel(dims, table, decoded, back, finished, canvas, out, sems):
    me = lax.axis_index("tile")
    for row in range(dims.local_rows):
        canvas[row] = decoded[row].astype(F32)

    @pl.loop(0, dims.tiles)
    def _(e):
        row0 = table[ROW, e]
        col0 = table[COL, e]
        length = table[SIDE, e]
        start = first_local(row0, me, dims)
        for i in range(dims.back_rows):
            local = start + i

            @pl.when((local < dims.local_rows) & (global_row(local, me, dims) - row0 < length))
            def _():
                canvas[local, pl.ds(col0, SPAN), :] += back[e, i].astype(F32)

    copies = [pltpu.make_async_copy(out.at[row], finished.at[row], sems.at[row]) for row in range(dims.local_rows)]
    for row in range(dims.local_rows):
        out[row] = canvas[row].astype(BF16)
        copies[row].start()
    for copy in copies:
        copy.wait()


def shards(features, dec_weight, dec_bias, first_weight, first_bias, second_weight, second_bias, boxes, slots):
    tiles = lax.axis_size("tile")
    dims = Dims(features, tiles)
    bands, cols, chans, local_rows = dims.bands, dims.cols, dims.chans, dims.local_rows
    assert dims.band_rows == 2 and slots.shape[0] == CAP * tiles and boxes.shape[1] == tiles
    assert tiles & (tiles - 1) == 0

    smem = pl.BlockSpec(memory_space=pltpu.SMEM)
    vmem = pl.BlockSpec(memory_space=pltpu.VMEM)
    hbm = pl.BlockSpec(memory_space=pl.ANY)
    full = pltpu.CompilerParams(vmem_limit_bytes=FULL_GRANT)
    small = pltpu.CompilerParams(vmem_limit_bytes=SMALL_GRANT)
    dma = pltpu.SemaphoreType.DMA

    def cost(flops, moved):
        return pl.CostEstimate(flops=int(flops), bytes_accessed=int(moved), transcendentals=0)

    def shaped(*shape, kind=BF16):
        return jax.ShapeDtypeStruct(shape, kind)

    def swap(array):
        return lax.all_to_all(array, "tile", split_axis=0, concat_axis=0, tiled=True)

    pack_scratch = [
        pltpu.VMEM((bands, 2, cols, chans), BF16),
        pltpu.VMEM((local_rows, cols + 16, chans), F32),
        pltpu.VMEM((dims.rim, chans), F32),
        pltpu.VMEM((tiles, dims.message, chans), BF16),
        dma((4,)),
        dma((bands,)),
        dma((tiles,)),
    ]
    message = shaped(tiles, dims.message, chans)
    sent_main, table, last, leading = pl.pallas_call(
        functools.partial(pack_main_kernel, dims),
        out_shape=[message, shaped(7, tiles, kind=I32), shaped(bands, cols, chans), shaped(bands, cols, chans)],
        in_specs=[hbm, hbm, hbm],
        out_specs=[hbm, smem, hbm, hbm],
        scratch_shapes=[
            pltpu.SMEM(boxes.shape, I32),
            pltpu.SMEM(slots.shape, I32),
            pltpu.SMEM((tiles,), I32),
            pltpu.SMEM((tiles,), I32),
            pltpu.SMEM((tiles + 1,), I32),
        ]
        + pack_scratch,
        compiler_params=full,
        cost_estimate=cost(0, 6e6),
        name="pack_main",
    )(boxes, slots, features)
    got_main = swap(sent_main)
    up = [(i, (i + 1) % tiles) for i in range(tiles)]
    above = lax.ppermute(last, "tile", up)
    below = lax.ppermute(leading, "tile", [(j, i) for i, j in up])

    sent_extra = pl.pallas_call(
        functools.partial(pack_extra_kernel, dims),
        out_shape=message,
        in_specs=[smem, hbm],
        out_specs=hbm,
        scratch_shapes=pack_scratch,
        compiler_params=full,
        cost_estimate=cost(0, 6e6),
        name="pack_extra",
    )(table, features)
    got_extra = swap(sent_extra)

    weights = tuple(w.reshape(3, 3, chans, chans) for w in (dec_weight, first_weight, second_weight))
    biases = (dec_bias[None], first_bias[None], second_bias[None])
    restore_scratch = [
        pltpu.VMEM((tiles, dims.message, chans), BF16),
        pltpu.VMEM((4, 3, chans, 2 * chans), BF16),
        pltpu.VMEM((2, 3, 4, chans, 2 * chans), BF16),
        dma((tiles,)),
        dma((3, 2)),
        pltpu.VMEM((SPAN // 2 + 2, 2, SPAN, 3 * chans), BF16),
        pltpu.VMEM((SPAN, SPAN, chans), F32),
        pltpu.VMEM((S + 2, S // 2, 4 * chans), BF16),
        pltpu.VMEM((S + 2, S // 2, 4 * chans), BF16),
        pltpu.VMEM((16, S, chans), F32),
        pltpu.VMEM((S, S, chans), BF16),
        dma,
    ]
    restored_shape = shaped(CAP, S, S, chans)
    sent_back, partial = pl.pallas_call(
        functools.partial(main_kernel, dims),
        out_shape=[shaped(tiles, dims.back_rows, SPAN, chans), restored_shape],
        in_specs=[smem] + [hbm] * 4 + [vmem] * 3,
        out_specs=[hbm, hbm],
        scratch_shapes=restore_scratch
        + [pltpu.VMEM((tiles, dims.back_rows, SPAN, chans), BF16), dma((tiles,))],
        compiler_params=full,
        cost_estimate=cost(7e9, 8e6),
        name="restore_main",
    )(table, got_main, *weights, *biases)
    got_back = swap(sent_back)

    restorations = pl.pallas_call(
        functools.partial(extra_kernel, dims),
        out_shape=restored_shape,
        in_specs=[smem] + [hbm] * 4 + [vmem] * 3 + [hbm],
        out_specs=hbm,
        scratch_shapes=restore_scratch,
        input_output_aliases={8: 0},
        compiler_params=full,
        cost_estimate=cost(6e9, 8e6),
        name="restore_extra",
    )(table, got_extra, *weights, *biases, partial)

    above, below, restorations = lax.optimization_barrier((above, below, restorations))
    decoded = pl.pallas_call(
        functools.partial(decode_kernel, dims),
        out_shape=shaped(local_rows, cols, chans),
        in_specs=[hbm] * 4 + [vmem],
        out_specs=vmem,
        scratch_shapes=[
            pltpu.VMEM((bands, 2, cols, chans), BF16),
            pltpu.VMEM((bands, cols, chans), BF16),
            pltpu.VMEM((bands, cols, chans), BF16),
            pltpu.VMEM((3, 4, chans, 2 * chans), BF16),
            pltpu.VMEM((4, cols + 16, chans), F32),
            pltpu.VMEM((4, cols // 2, 4 * chans), BF16),
            pltpu.VMEM((2, cols, chans), F32),
            dma((3, bands)),
            dma((2,)),
        ],
        compiler_params=small,
        cost_estimate=cost(3e9, 6e6),
        name="decode",
    )(features, above, below, weights[0], biases[0])

    finished = pl.pallas_call(
        functools.partial(paste_kernel, dims),
        out_shape=shaped(local_rows, cols, chans),
        in_specs=[smem, vmem, vmem],
        out_specs=hbm,
        scratch_shapes=[
            pltpu.VMEM((local_rows, cols, chans), F32),
            pltpu.VMEM((local_rows, cols, chans), BF16),
            dma((local_rows,)),
        ],
        compiler_params=small,
        cost_estimate=cost(0, 6e6),
        name="paste",
    )(table, decoded, got_back)
    return finished.reshape(features.shape), restorations


def solution(mesh):
    return jax.shard_map(
        shards,
        mesh=mesh,
        in_specs=(
            P("sess", "tile", None, None),
            P(),
            P(),
            P(),
            P(),
            P(),
            P(),
            P(None, "sess"),
            P("sess"),
        ),
        out_specs=(P("sess", "tile", None, None), P(("sess", "tile"), None, None, None)),
        check_vma=False,
    )
```

time: 76.4 us -> 95.2 us (1.25)
  the two profiles are of different devices: /device:TPU:0 before, /device:TPU:4 now
where the time goes in v3:
time: 95.2 us; the launch traced here: 93.6 us
  Pallas kernels  68.2 us (72%)
  starting transfers between devices  15.4 us (16%)
  waiting for transfers between devices  8.35 us (9%)
    pallas_call x1, Pallas kernels, shards(): pl.pallas_call(functools.partial(pack_main_kernel, dims), out_shape=[mess...  31.7 us
    pallas_call x1, Pallas kernels, shards(): pl.pallas_call(functools.partial(main_kernel, dims), out_shape=[shaped(ti...  13.3 us
    all_to_all x3, starting transfers between devices, swap(): lax.all_to_all(array, 'tile', split_axis=0, concat_axis=0, tiled=True)  12.8 us
    pallas_call x1, Pallas kernels, shards(): pl.pallas_call(functools.partial(extra_kernel, dims), out_shape=restored_...  12 us
    all_to_all x3, waiting for transfers between devices, swap(): lax.all_to_all(array, 'tile', split_axis=0, concat_axis=0, tiled=True)  8.35 us
    pallas_call x1, Pallas kernels, shards(): pl.pallas_call(functools.partial(decode_kernel, dims), out_shape=shaped(l...  5.68 us
    pallas_call x1, Pallas kernels, shards(): pl.pallas_call(functools.partial(pack_extra_kernel, dims), out_shape=mess...  3.14 us
    ppermute x1, starting transfers between devices, shards(): below = lax.ppermute(leading, 'tile', [(j, i) for i, j in up])  2.5 us
  transfers between devices with their start and end apart: 5, of which 1 were waited for; matrix products, arithmetic and copies ran while one was open for 0% of the time, Pallas kernels for 36%

profile of v3, /device:TPU:4, one launch (start us, length us, event | category | flops | bytes accessed | tf_op | source)
XLA Modules:
  0.0 93.6 jit_solution(13330638935850385393)
XLA Ops:
  0.6 31.7 %pack_main.1 = (bf16[8,400,128]{2,1,0:T(8,128)(2,1)}, s32[7,8]{1,0:T(8,128)}, bf16[6,320,128]{2,1,0:T(8,128)(2,1)}, bf16[6,320,128]{2,1,0:T(8,128)(2,1)}) custom-call(s32[3,8]{1,0:T(4,128)} %boxes_in.1, s32[16]{0:T(128)} %slots_in.1, bf16[6,2,320,128]{3,2,1,0:T(8,128)(2,1)} %feat.5), custom_call_target="tpu_custom_call" | custom-call | bytes 6000000 | tf_op jit(solution)/shard_map/pack_main/pallas_call | solution.py:536
  32.3 4.2 %all-to-all-start.1 = ((bf16[8,400,128]{2,1,0:T(8,128)(2,1)}), bf16[8,400,128]{2,1,0:T(8,128)(2,1)S(1)}, u32[]{:S(2)}, u32[]{:S(2)}) async-start(bf16[8,400,128]{2,1,0:T(8,128)(2,1)} %get-tuple-element.14), calls=%async_computation.1 | async-start | bytes 1638400 | tf_op jit(solution)/shard_map/all_to_all | solution.py:524
  36.5 3.1 %pack_extra.1 = bf16[8,400,128]{2,1,0:T(8,128)(2,1)} custom-call(s32[7,8]{1,0:T(8,128)} %get-tuple-element.11.table, bf16[6,2,320,128]{3,2,1,0:T(8,128)(2,1)} %feat.5), custom_call_target="tpu_custom_call" | custom-call | bytes 6000000 | tf_op jit(solution)/shard_map/pack_extra/pallas_call | solution.py:558
  39.7 8.3 %all-to-all-done.1.arrived = bf16[8,400,128]{2,1,0:T(8,128)(2,1)S(1)} async-done(((bf16[8,400,128]{2,1,0:T(8,128)(2,1)}), bf16[8,400,128]{2,1,0:T(8,128)(2,1)S(1)}, u32[]{:S(2)}, u32[]{:S(2)}) %all-to-all-start.1) | async-done | bytes 819232 | tf_op jit(solution)/shard_map/all_to_all | solution.py:524
  48.0 0.0 copy-start.5
  48.0 4.9 %all-to-all-start = ((bf16[8,400,128]{2,1,0:T(8,128)(2,1)}), bf16[8,400,128]{2,1,0:T(8,128)(2,1)S(1)}, u32[]{:S(2)}, u32[]{:S(2)}) async-start(bf16[8,400,128]{2,1,0:T(8,128)(2,1)} %pack_extra.1), calls=%async_computation | async-start | bytes 1638400 | tf_op jit(solution)/shard_map/all_to_all | solution.py:524
  53.0 0.1 collective-permute-start
  53.1 2.5 %collective-permute-start.1 = (bf16[6,320,128]{2,1,0:T(8,128)(2,1)}, bf16[6,320,128]{2,1,0:T(8,128)(2,1)}, u32[]{:S(2)}, u32[]{:S(2)}) collective-permute-start(bf16[6,320,128]{2,1,0:T(8,128)(2,1)} %get-tuple-element.13), channel_id=1, source_target_pairs={{1,0},{2,1},{3,2},{4,3},{5,4},{6,5},{7,6},{0,7},{9,8},{10,9},{11,1... | collective-permute-start | bytes 1474568 | tf_op jit(solution)/shard_map/ppermute | solution.py:556
  55.6 0.0 copy-done.5
  55.6 13.3 %restore_main.1 = (bf16[8,6,48,128]{3,2,1,0:T(8,128)(2,1)}, bf16[2,64,64,128]{3,2,1,0:T(8,128)(2,1)}) custom-call(s32[7,8]{1,0:T(8,128)} %get-tuple-element.11.table, bf16[8,400,128]{2,1,0:T(8,128)(2,1)} %copy-done.5, bf16[3,3,128,128]{3,2,1,0:T(8,128)(2,1)} %bitcast.7, bf16[3,3,128,128]{3,2,1,0:T(8,128)(2,1)} %bitcast.14, ...), custom_call_target="tpu_custom_call" | custom-call | flops 7000000000 | bytes 8000000 | tf_op jit(solution)/shard_map/restore_main/pallas_call | solution.py:587
  68.9 0.0 all-to-all-done.arrived
  68.9 0.0 copy-start.4
  68.9 0.9 copy-done.4
  69.8 3.6 %all-to-all-start.2 = ((bf16[8,6,48,128]{3,2,1,0:T(8,128)(2,1)}), bf16[8,6,48,128]{3,2,1,0:T(8,128)(2,1)S(1)}, u32[]{:S(2)}, u32[]{:S(2)}) async-start(bf16[8,6,48,128]{3,2,1,0:T(8,128)(2,1)} %get-tuple-element.18), calls=%async_computation.2 | async-start | bytes 1179648 | tf_op jit(solution)/shard_map/all_to_all | solution.py:524
  73.4 0.0 copy-start
  73.4 0.0 copy-start.2
  73.4 0.0 copy-start.3
  73.4 12.0 %restore_extra.1 = bf16[2,64,64,128]{3,2,1,0:T(8,128)(2,1)} custom-call(s32[7,8]{1,0:T(8,128)} %get-tuple-element.11.table, bf16[8,400,128]{2,1,0:T(8,128)(2,1)} %copy-done.4, bf16[3,3,128,128]{3,2,1,0:T(8,128)(2,1)} %bitcast.8, bf16[3,3,128,128]{3,2,1,0:T(8,128)(2,1)} %bitcast.15, ...), custom_call_target="tpu_custom_call", output_to_operand_aliasing={{}: (8, {})} | custom-call | flops 6000000000 | bytes 8000000 | tf_op jit(solution)/shard_map/restore_extra/pallas_call | solution.py:600
  85.4 0.0 copy-start.1
  85.4 0.0 collective-permute-done.above
  85.5 0.0 collective-permute-done.1.below
  85.5 0.0 copy-done
  85.5 0.0 copy-done.2
  85.5 0.0 copy-done.3
  85.5 5.7 %decode.1.decoded = bf16[12,320,128]{2,1,0:T(8,128)(2,1)S(1)} custom-call(bf16[6,2,320,128]{3,2,1,0:T(8,128)(2,1)S(1)} %copy-done, bf16[6,320,128]{2,1,0:T(8,128)(2,1)} %collective-permute-done.above, bf16[6,320,128]{2,1,0:T(8,128)(2,1)} %collective-permute-done.1.below, bf16[3,3,128,128]{3,2,1,0:T(8,128)(2,1)S(1)} %bitcast.9, f32[1,128]{1,0:T(1,128)S(1)} %bitcast.12), custom_call_target="tpu_custom_call" | custom-call | flops 3000000000 | bytes 6000000 | tf_op jit(solution)/shard_map/decode/pallas_call | solution.py:613
  91.2 0.0 all-to-all-done.2.back
  91.2 0.0 copy-done.1
  91.2 2.4 %paste.1 = bf16[12,320,128]{2,1,0:T(8,128)(2,1)} custom-call(s32[7,8]{1,0:T(8,128)S(1)} %copy-done.1, bf16[12,320,128]{2,1,0:T(8,128)(2,1)S(1)} %decode.1.decoded, bf16[8,6,48,128]{3,2,1,0:T(8,128)(2,1)S(1)} %all-to-all-done.2.back), custom_call_target="tpu_custom_call" | custom-call | bytes 6000000 | tf_op jit(solution)/shard_map/paste/pallas_call | solution.py:634
Async XLA Ops:
  32.3 15.7 %all-to-all-start.1 = ((bf16[8,400,128]{2,1,0:T(8,128)(2,1)}), bf16[8,400,128]{2,1,0:T(8,128)(2,1)S(1)}, u32[]{:S(2)}, u32[]{:S(2)}) async-start(bf16[8,400,128]{2,1,0:T(8,128)(2,1)} %get-tuple-element.14), calls=%async_computation.1 | async-start | bytes 1638400 | tf_op jit(solution)/shard_map/all_to_all | solution.py:524
  48.0 7.6 %copy-start.5 = (bf16[8,400,128]{2,1,0:T(8,128)(2,1)}, bf16[8,400,128]{2,1,0:T(8,128)(2,1)S(1)}, u32[]{:S(2)}) copy-start(bf16[8,400,128]{2,1,0:T(8,128)(2,1)S(1)} %all-to-all-done.1.arrived) | copy-start | bytes 2457604
  48.0 20.9 %all-to-all-start = ((bf16[8,400,128]{2,1,0:T(8,128)(2,1)}), bf16[8,400,128]{2,1,0:T(8,128)(2,1)S(1)}, u32[]{:S(2)}, u32[]{:S(2)}) async-start(bf16[8,400,128]{2,1,0:T(8,128)(2,1)} %pack_extra.1), calls=%async_computation | async-start | bytes 1638400 | tf_op jit(solution)/shard_map/all_to_all | solution.py:524
  53.0 32.5 %collective-permute-start = (bf16[6,320,128]{2,1,0:T(8,128)(2,1)}, bf16[6,320,128]{2,1,0:T(8,128)(2,1)}, u32[]{:S(2)}, u32[]{:S(2)}) collective-permute-start(bf16[6,320,128]{2,1,0:T(8,128)(2,1)} %get-tuple-element.12), channel_id=1, source_target_pairs={{0,1},{1,2},{2,3},{3,4},{4,5},{5,6},{6,7},{7,0},{8,9},{9,10},{10,1... | collective-permute-start | bytes 1474568 | tf_op jit(solution)/shard_map/ppermute | solution.py:555
  53.1 32.3 %collective-permute-start.1 = (bf16[6,320,128]{2,1,0:T(8,128)(2,1)}, bf16[6,320,128]{2,1,0:T(8,128)(2,1)}, u32[]{:S(2)}, u32[]{:S(2)}) collective-permute-start(bf16[6,320,128]{2,1,0:T(8,128)(2,1)} %get-tuple-element.13), channel_id=1, source_target_pairs={{1,0},{2,1},{3,2},{4,3},{5,4},{6,5},{7,6},{0,7},{9,8},{10,9},{11,1... | collective-permute-start | bytes 1474568 | tf_op jit(solution)/shard_map/ppermute | solution.py:556
  68.9 0.9 copy-start.4
  69.8 21.4 %all-to-all-start.2 = ((bf16[8,6,48,128]{3,2,1,0:T(8,128)(2,1)}), bf16[8,6,48,128]{3,2,1,0:T(8,128)(2,1)S(1)}, u32[]{:S(2)}, u32[]{:S(2)}) async-start(bf16[8,6,48,128]{3,2,1,0:T(8,128)(2,1)} %get-tuple-element.18), calls=%async_computation.2 | async-start | bytes 1179648 | tf_op jit(solution)/shard_map/all_to_all | solution.py:524
  73.4 12.1 %copy-start = (bf16[6,2,320,128]{3,2,1,0:T(8,128)(2,1)S(1)}, bf16[6,2,320,128]{3,2,1,0:T(8,128)(2,1)}, u32[]{:S(2)}) copy-start(bf16[6,2,320,128]{3,2,1,0:T(8,128)(2,1)} %feat.5) | copy-start | bytes 2949124
  73.4 12.1 %copy-start.2 = (bf16[9,128,128]{2,1,0:T(8,128)(2,1)S(1)}, bf16[9,128,128]{2,1,0:T(8,128)(2,1)}, u32[]{:S(2)}) copy-start(bf16[9,128,128]{2,1,0:T(8,128)(2,1)} %param.10) | copy-start | bytes 884740
  73.4 12.1 %copy-start.3 = (f32[128]{0:T(128)S(1)}, f32[128]{0:T(128)}, u32[]{:S(2)}) copy-start(f32[128]{0:T(128)} %param.11) | copy-start | bytes 1540
  85.4 5.8 %copy-start.1 = (s32[7,8]{1,0:T(8,128)S(1)}, s32[7,8]{1,0:T(8,128)}, u32[]{:S(2)}) copy-start(s32[7,8]{1,0:T(8,128)} %get-tuple-element.11.table) | copy-start | bytes 676

commit v4 on v3

--- a/solution.py
+++ b/solution.py
@@ -97,6 +97,15 @@
         self.store[:, 0, :, chans : 2 * chans] = none
 
 
+def two_chains(wide, taps):
+    wide = wide.reshape(-1, wide.shape[-1])
+    weight = taps.value()
+    middle = weight.shape[0] // 2
+    one = jnp.dot(wide[:, :middle], weight[:middle], preferred_element_type=F32)
+    two = jnp.dot(wide[:, middle:], weight[middle:], preferred_element_type=F32)
+    return one + two
+
+
 def row_pairs(src, first, count, taps):
     parts = [
         src[pl.ds(first, count), 0],
@@ -104,13 +113,11 @@
         src[pl.ds(first + 1, count), 0],
         src[pl.ds(first + 1, count), 1],
     ]
-    wide = jnp.concatenate(parts, -1)
-    return jnp.dot(wide.reshape(-1, wide.shape[-1]), taps.value(), preferred_element_type=F32)
+    return two_chains(jnp.concatenate(parts, -1), taps)
 
 
 def column_pairs(src, first, count, taps):
-    wide = jnp.concatenate([src[pl.ds(first + a, count)] for a in range(3)], -1)
-    return jnp.dot(wide.reshape(-1, wide.shape[-1]), taps.value(), preferred_element_type=F32)
+    return two_chains(jnp.concatenate([src[pl.ds(first + a, count)] for a in range(3)], -1), taps)
 
 
 def fill_canvas(dims, feat, held, canvas, sems):
@@ -166,12 +173,6 @@
     for copy in copies:
         copy.start()
     finish = fill_canvas(dims, feat, held, canvas, feat_sems)
-    edges = (
-        pltpu.make_async_copy(feat.at[:, 1], last, sems.at[2]),
-        pltpu.make_async_copy(feat.at[:, 0], leading, sems.at[3]),
-    )
-    for edge in edges:
-        edge.start()
     for copy in copies:
         copy.wait()
 
@@ -203,6 +204,12 @@
 
     lax.fori_loop(0, dims.tiles, second_pass, jnp.int32(0))
     finish()
+    edges = (
+        pltpu.make_async_copy(held.at[:, 1], last, sems.at[2]),
+        pltpu.make_async_copy(held.at[:, 0], leading, sems.at[3]),
+    )
+    for edge in edges:
+        edge.start()
     pack_crops(dims, table, ROW, COL, canvas, rim, staged, sent, sent_sems)
     for edge in edges:
         edge.wait()
@@ -243,7 +250,7 @@
             raw[place >> 1, place & 1] = jnp.concatenate([left.astype(BF16), line, right.astype(BF16)], -1)
 
     taps[0].wait()
-    n = 8
+    n = 12
 
     @pl.loop(0, pairs // n)
     def _(step):
@@ -285,7 +292,7 @@
                         b * half : (b + 1) * half, parity * chans : (parity + 1) * chans
                     ]
 
-    n = 16
+    n = 32
     taps[1].wait()
 
     @pl.loop(0, S // n)
@@ -579,7 +586,7 @@
         pltpu.VMEM((SPAN, SPAN, chans), F32),
         pltpu.VMEM((S + 2, S // 2, 4 * chans), BF16),
         pltpu.VMEM((S + 2, S // 2, 4 * chans), BF16),
-        pltpu.VMEM((16, S, chans), F32),
+        pltpu.VMEM((32, S, chans), F32),
         pltpu.VMEM((S, S, chans), BF16),
         dma,
     ]

time: 95.2 us -> 65.1 us (0.68)
  the two profiles are of different devices: /device:TPU:4 before, /device:TPU:13 now
where the time goes in v4:
time: 65.1 us; the launch traced here: 63.8 us
  Pallas kernels  38 us (58%)
  starting transfers between devices  18 us (28%)
  waiting for transfers between devices  6.06 us (9%)
  local copies, waits for them, and re-layouts  0.9 us (1%)
  between operations  0.76 us (1%)
    all_to_all x3, starting transfers between devices, swap(): lax.all_to_all(array, 'tile', split_axis=0, concat_axis=0, tiled=True)  16.6 us
    pallas_call x1, Pallas kernels, shards(): pl.pallas_call(functools.partial(main_kernel, dims), out_shape=[shaped(ti...  12.4 us
    pallas_call x1, Pallas kernels, shards(): pl.pallas_call(functools.partial(extra_kernel, dims), out_shape=restored_...  11.2 us
    all_to_all x3, waiting for transfers between devices, swap(): lax.all_to_all(array, 'tile', split_axis=0, concat_axis=0, tiled=True)  6.05 us
    pallas_call x1, Pallas kernels, shards(): pl.pallas_call(functools.partial(decode_kernel, dims), out_shape=shaped(l...  5.65 us
    pallas_call x1, Pallas kernels, shards(): pl.pallas_call(functools.partial(pack_main_kernel, dims), out_shape=[mess...  3.25 us
    pallas_call x1, Pallas kernels, shards(): pl.pallas_call(functools.partial(pack_extra_kernel, dims), out_shape=mess...  3.14 us
    pallas_call x1, Pallas kernels, shards(): pl.pallas_call(functools.partial(paste_kernel, dims), out_shape=shaped(lo...  2.4 us
  transfers between devices with their start and end apart: 5, of which 1 were waited for; matrix products, arithmetic and copies ran while one was open for 0% of the time, Pallas kernels for 51%

profile of v4, /device:TPU:13, one launch (start us, length us, event | category | flops | bytes accessed | tf_op | source)
XLA Modules:
  0.0 63.8 jit_solution(15233983627870968019)
XLA Ops:
  0.6 3.3 %pack_main.1 = (bf16[8,400,128]{2,1,0:T(8,128)(2,1)}, s32[7,8]{1,0:T(8,128)}, bf16[6,320,128]{2,1,0:T(8,128)(2,1)}, bf16[6,320,128]{2,1,0:T(8,128)(2,1)}) custom-call(s32[3,8]{1,0:T(4,128)} %boxes_in.1, s32[16]{0:T(128)} %slots_in.1, bf16[6,2,320,128]{3,2,1,0:T(8,128)(2,1)} %feat.5), custom_call_target="tpu_custom_call" | custom-call | bytes 6000000 | tf_op jit(solution)/shard_map/pack_main/pallas_call | solution.py:543
  3.9 4.6 %all-to-all-start.1 = ((bf16[8,400,128]{2,1,0:T(8,128)(2,1)}), bf16[8,400,128]{2,1,0:T(8,128)(2,1)S(1)}, u32[]{:S(2)}, u32[]{:S(2)}) async-start(bf16[8,400,128]{2,1,0:T(8,128)(2,1)} %get-tuple-element.14), calls=%async_computation.1 | async-start | bytes 1638400 | tf_op jit(solution)/shard_map/all_to_all | solution.py:531
  8.4 3.1 %pack_extra.1 = bf16[8,400,128]{2,1,0:T(8,128)(2,1)} custom-call(s32[7,8]{1,0:T(8,128)} %get-tuple-element.11.table, bf16[6,2,320,128]{3,2,1,0:T(8,128)(2,1)} %feat.5), custom_call_target="tpu_custom_call" | custom-call | bytes 6000000 | tf_op jit(solution)/shard_map/pack_extra/pallas_call | solution.py:565
  11.6 6.0 %all-to-all-done.1.arrived = bf16[8,400,128]{2,1,0:T(8,128)(2,1)S(1)} async-done(((bf16[8,400,128]{2,1,0:T(8,128)(2,1)}), bf16[8,400,128]{2,1,0:T(8,128)(2,1)S(1)}, u32[]{:S(2)}, u32[]{:S(2)}) %all-to-all-start.1) | async-done | bytes 819232 | tf_op jit(solution)/shard_map/all_to_all | solution.py:531
  17.6 0.0 copy-start.5
  17.6 7.2 %all-to-all-start = ((bf16[8,400,128]{2,1,0:T(8,128)(2,1)}), bf16[8,400,128]{2,1,0:T(8,128)(2,1)S(1)}, u32[]{:S(2)}, u32[]{:S(2)}) async-start(bf16[8,400,128]{2,1,0:T(8,128)(2,1)} %pack_extra.1), calls=%async_computation | async-start | bytes 1638400 | tf_op jit(solution)/shard_map/all_to_all | solution.py:531
  24.9 1.4 %collective-permute-start = (bf16[6,320,128]{2,1,0:T(8,128)(2,1)}, bf16[6,320,128]{2,1,0:T(8,128)(2,1)}, u32[]{:S(2)}, u32[]{:S(2)}) collective-permute-start(bf16[6,320,128]{2,1,0:T(8,128)(2,1)} %get-tuple-element.12), channel_id=1, source_target_pairs={{0,1},{1,2},{2,3},{3,4},{4,5},{5,6},{6,7},{7,0},{8,9},{9,10},{10,1... | collective-permute-start | bytes 1474568 | tf_op jit(solution)/shard_map/ppermute | solution.py:562
  26.3 0.0 collective-permute-start.1
  26.3 0.0 copy-done.5
  26.3 12.4 %restore_main.1 = (bf16[8,6,48,128]{3,2,1,0:T(8,128)(2,1)}, bf16[2,64,64,128]{3,2,1,0:T(8,128)(2,1)}) custom-call(s32[7,8]{1,0:T(8,128)} %get-tuple-element.11.table, bf16[8,400,128]{2,1,0:T(8,128)(2,1)} %copy-done.5, bf16[3,3,128,128]{3,2,1,0:T(8,128)(2,1)} %bitcast.7, bf16[3,3,128,128]{3,2,1,0:T(8,128)(2,1)} %bitcast.14, ...), custom_call_target="tpu_custom_call" | custom-call | flops 7000000000 | bytes 8000000 | tf_op jit(solution)/shard_map/restore_main/pallas_call | solution.py:594
  38.8 0.0 all-to-all-done.arrived
  38.8 0.0 copy-start.4
  38.8 0.9 %copy-done.4 = bf16[8,400,128]{2,1,0:T(8,128)(2,1)} copy-done((bf16[8,400,128]{2,1,0:T(8,128)(2,1)}, bf16[8,400,128]{2,1,0:T(8,128)(2,1)S(1)}, u32[]{:S(2)}) %copy-start.4) | copy-done | bytes 819224
  39.7 4.8 %all-to-all-start.2 = ((bf16[8,6,48,128]{3,2,1,0:T(8,128)(2,1)}), bf16[8,6,48,128]{3,2,1,0:T(8,128)(2,1)S(1)}, u32[]{:S(2)}, u32[]{:S(2)}) async-start(bf16[8,6,48,128]{3,2,1,0:T(8,128)(2,1)} %get-tuple-element.18), calls=%async_computation.2 | async-start | bytes 1179648 | tf_op jit(solution)/shard_map/all_to_all | solution.py:531
  44.5 0.0 copy-start
  44.5 0.0 copy-start.2
  44.5 0.0 copy-start.3
  44.5 11.2 %restore_extra.1 = bf16[2,64,64,128]{3,2,1,0:T(8,128)(2,1)} custom-call(s32[7,8]{1,0:T(8,128)} %get-tuple-element.11.table, bf16[8,400,128]{2,1,0:T(8,128)(2,1)} %copy-done.4, bf16[3,3,128,128]{3,2,1,0:T(8,128)(2,1)} %bitcast.8, bf16[3,3,128,128]{3,2,1,0:T(8,128)(2,1)} %bitcast.15, ...), custom_call_target="tpu_custom_call", output_to_operand_aliasing={{}: (8, {})} | custom-call | flops 6000000000 | bytes 8000000 | tf_op jit(solution)/shard_map/restore_extra/pallas_call | solution.py:607
  55.6 0.0 copy-start.1
  55.7 0.0 collective-permute-done.above
  55.7 0.0 collective-permute-done.1.below
  55.7 0.0 copy-done
  55.7 0.0 copy-done.2
  55.7 0.0 copy-done.3
  55.7 5.7 %decode.1.decoded = bf16[12,320,128]{2,1,0:T(8,128)(2,1)S(1)} custom-call(bf16[6,2,320,128]{3,2,1,0:T(8,128)(2,1)S(1)} %copy-done, bf16[6,320,128]{2,1,0:T(8,128)(2,1)} %collective-permute-done.above, bf16[6,320,128]{2,1,0:T(8,128)(2,1)} %collective-permute-done.1.below, bf16[3,3,128,128]{3,2,1,0:T(8,128)(2,1)S(1)} %bitcast.9, f32[1,128]{1,0:T(1,128)S(1)} %bitcast.12), custom_call_target="tpu_custom_call" | custom-call | flops 3000000000 | bytes 6000000 | tf_op jit(solution)/shard_map/decode/pallas_call | solution.py:620
  61.4 0.0 all-to-all-done.2.back
  61.4 0.0 copy-done.1
  61.4 2.4 %paste.1 = bf16[12,320,128]{2,1,0:T(8,128)(2,1)} custom-call(s32[7,8]{1,0:T(8,128)S(1)} %copy-done.1, bf16[12,320,128]{2,1,0:T(8,128)(2,1)S(1)} %decode.1.decoded, bf16[8,6,48,128]{3,2,1,0:T(8,128)(2,1)S(1)} %all-to-all-done.2.back), custom_call_target="tpu_custom_call" | custom-call | bytes 6000000 | tf_op jit(solution)/shard_map/paste/pallas_call | solution.py:641
Async XLA Ops:
  3.9 13.7 %all-to-all-start.1 = ((bf16[8,400,128]{2,1,0:T(8,128)(2,1)}), bf16[8,400,128]{2,1,0:T(8,128)(2,1)S(1)}, u32[]{:S(2)}, u32[]{:S(2)}) async-start(bf16[8,400,128]{2,1,0:T(8,128)(2,1)} %get-tuple-element.14), calls=%async_computation.1 | async-start | bytes 1638400 | tf_op jit(solution)/shard_map/all_to_all | solution.py:531
  17.6 8.7 %copy-start.5 = (bf16[8,400,128]{2,1,0:T(8,128)(2,1)}, bf16[8,400,128]{2,1,0:T(8,128)(2,1)S(1)}, u32[]{:S(2)}) copy-start(bf16[8,400,128]{2,1,0:T(8,128)(2,1)S(1)} %all-to-all-done.1.arrived) | copy-start | bytes 2457604
  17.6 21.1 %all-to-all-start = ((bf16[8,400,128]{2,1,0:T(8,128)(2,1)}), bf16[8,400,128]{2,1,0:T(8,128)(2,1)S(1)}, u32[]{:S(2)}, u32[]{:S(2)}) async-start(bf16[8,400,128]{2,1,0:T(8,128)(2,1)} %pack_extra.1), calls=%async_computation | async-start | bytes 1638400 | tf_op jit(solution)/shard_map/all_to_all | solution.py:531
  24.9 30.8 %collective-permute-start = (bf16[6,320,128]{2,1,0:T(8,128)(2,1)}, bf16[6,320,128]{2,1,0:T(8,128)(2,1)}, u32[]{:S(2)}, u32[]{:S(2)}) collective-permute-start(bf16[6,320,128]{2,1,0:T(8,128)(2,1)} %get-tuple-element.12), channel_id=1, source_target_pairs={{0,1},{1,2},{2,3},{3,4},{4,5},{5,6},{6,7},{7,0},{8,9},{9,10},{10,1... | collective-permute-start | bytes 1474568 | tf_op jit(solution)/shard_map/ppermute | solution.py:562
  26.3 29.4 %collective-permute-start.1 = (bf16[6,320,128]{2,1,0:T(8,128)(2,1)}, bf16[6,320,128]{2,1,0:T(8,128)(2,1)}, u32[]{:S(2)}, u32[]{:S(2)}) collective-permute-start(bf16[6,320,128]{2,1,0:T(8,128)(2,1)} %get-tuple-element.13), channel_id=1, source_target_pairs={{1,0},{2,1},{3,2},{4,3},{5,4},{6,5},{7,6},{0,7},{9,8},{10,9},{11,1... | collective-permute-start | bytes 1474568 | tf_op jit(solution)/shard_map/ppermute | solution.py:563
  38.8 0.9 %copy-start.4 = (bf16[8,400,128]{2,1,0:T(8,128)(2,1)}, bf16[8,400,128]{2,1,0:T(8,128)(2,1)S(1)}, u32[]{:S(2)}) copy-start(bf16[8,400,128]{2,1,0:T(8,128)(2,1)S(1)} %all-to-all-done.arrived) | copy-start | bytes 2457604
  39.7 21.7 %all-to-all-start.2 = ((bf16[8,6,48,128]{3,2,1,0:T(8,128)(2,1)}), bf16[8,6,48,128]{3,2,1,0:T(8,128)(2,1)S(1)}, u32[]{:S(2)}, u32[]{:S(2)}) async-start(bf16[8,6,48,128]{3,2,1,0:T(8,128)(2,1)} %get-tuple-element.18), calls=%async_computation.2 | async-start | bytes 1179648 | tf_op jit(solution)/shard_map/all_to_all | solution.py:531
  44.5 11.2 %copy-start = (bf16[6,2,320,128]{3,2,1,0:T(8,128)(2,1)S(1)}, bf16[6,2,320,128]{3,2,1,0:T(8,128)(2,1)}, u32[]{:S(2)}) copy-start(bf16[6,2,320,128]{3,2,1,0:T(8,128)(2,1)} %feat.5) | copy-start | bytes 2949124
  44.5 11.2 %copy-start.2 = (bf16[9,128,128]{2,1,0:T(8,128)(2,1)S(1)}, bf16[9,128,128]{2,1,0:T(8,128)(2,1)}, u32[]{:S(2)}) copy-start(bf16[9,128,128]{2,1,0:T(8,128)(2,1)} %param.10) | copy-start | bytes 884740
  44.5 11.2 %copy-start.3 = (f32[128]{0:T(128)S(1)}, f32[128]{0:T(128)}, u32[]{:S(2)}) copy-start(f32[128]{0:T(128)} %param.11) | copy-start | bytes 1540
  55.6 5.7 %copy-start.1 = (s32[7,8]{1,0:T(8,128)S(1)}, s32[7,8]{1,0:T(8,128)}, u32[]{:S(2)}) copy-start(s32[7,8]{1,0:T(8,128)} %get-tuple-element.11.table) | copy-start | bytes 676

commit v5 on v4

--- a/solution.py
+++ b/solution.py
@@ -15,7 +15,7 @@
 BF16 = jnp.bfloat16
 F32 = jnp.float32
 I32 = jnp.int32
-FULL_GRANT = 62 * 1024 * 1024
+FULL_GRANT = 66500000
 SMALL_GRANT = 32 * 1024 * 1024
 ROW, COL, SIDE, ROW2, COL2, SIDE2, PLACE = range(7)
 
@@ -140,32 +140,30 @@
     return finish
 
 
-def pack_crops(dims, table, row_at, col_at, canvas, rim, staged, sent, sems):
+def pack_crops(dims, table, row_at, col_at, canvas, rim, staged, partner):
     me = lax.axis_index("tile")
     rim[...] = jnp.zeros_like(rim)
 
     @pl.loop(0, dims.tiles)
-    def _(w):
+    def _(s):
+        w = partner(s)
         row0 = table[row_at, w]
         col0 = table[col_at, w]
         start = first_local(jnp.maximum(row0 - 1, 0), me, dims)
         for i in range(dims.rows):
             row = jnp.minimum(start + i, dims.local_rows - 1)
-            staged[w, i * SPAN : (i + 1) * SPAN, :] = canvas[row, pl.ds(col0 + 8, SPAN), :].astype(BF16)
+            staged[s, i * SPAN : (i + 1) * SPAN, :] = canvas[row, pl.ds(col0 + 8, SPAN), :].astype(BF16)
             rim[2 * i : 2 * i + 1, :] = canvas[row, pl.ds(col0 + 7, 1), :]
             rim[2 * i + 1 : 2 * i + 2, :] = canvas[row, pl.ds(col0 + 8 + SPAN, 1), :]
-        staged[w, dims.rows * SPAN :, :] = rim[...].astype(BF16)
-        pltpu.make_async_copy(staged.at[w], sent.at[w], sems.at[w]).start()
-
-    @pl.loop(0, dims.tiles)
-    def _(w):
-        pltpu.make_async_copy(staged.at[w], sent.at[w], sems.at[w]).wait()
+        staged[s, dims.rows * SPAN :, :] = rim[...].astype(BF16)
 
 
 def pack_main_kernel(
-    dims, boxes_in, slots_in, feat, sent, table, last, leading,
-    boxes, slots, main, extra, seconds, held, canvas, rim, staged, sems, feat_sems, sent_sems,
+    dims, boxes_in, slots_in, feat, *refs
 ):
+    sent, refs = refs[: dims.tiles], refs[dims.tiles :]
+    table, last, leading, boxes, slots, main, extra, seconds, held, canvas, rim, staged, sems, feat_sems, sent_sems = refs
+    me = lax.axis_index("tile")
     copies = (
         pltpu.make_async_copy(boxes_in, boxes, sems.at[0]),
         pltpu.make_async_copy(slots_in, slots, sems.at[1]),
@@ -210,17 +208,27 @@
     )
     for edge in edges:
         edge.start()
-    pack_crops(dims, table, ROW, COL, canvas, rim, staged, sent, sent_sems)
+    pack_crops(dims, table, ROW, COL, canvas, rim, staged, lambda s: me ^ s)
+    copies = [pltpu.make_async_copy(staged.at[s], sent[s], sent_sems.at[s]) for s in range(dims.tiles)]
+    for copy in copies:
+        copy.start()
+    for copy in copies:
+        copy.wait()
     for edge in edges:
         edge.wait()
 
 
 def pack_extra_kernel(dims, table, feat, sent, held, canvas, rim, staged, sems, feat_sems, sent_sems):
     fill_canvas(dims, feat, held, canvas, feat_sems)()
-    pack_crops(dims, table, ROW2, COL2, canvas, rim, staged, sent, sent_sems)
-
-
-def restore(dims, row0, length, arrival, got, taps, biases, raw, decoded, wide, inner, mixed, delta):
+    pack_crops(dims, table, ROW2, COL2, canvas, rim, staged, lambda s: s)
+    copies = [pltpu.make_async_copy(staged.at[s], sent.at[s], sent_sems.at[s]) for s in range(dims.tiles)]
+    for copy in copies:
+        copy.start()
+    for copy in copies:
+        copy.wait()
+
+
+def restore(dims, row0, length, arrival, source, got, taps, biases, raw, decoded, wide, inner, mixed, delta, finish):
     chans = dims.chans
     above = row0 - 1
     pairs = SPAN // 2
@@ -234,16 +242,17 @@
         store[S + 1] = empty
 
     @pl.loop(0, dims.tiles)
-    def _(e):
-        arrival(e).wait()
+    def _(s):
+        arrival(s).wait()
+        e = source(s)
         start = first_local(jnp.maximum(above, 0), e, dims)
-        rim = got[e, dims.rows * SPAN :, :].astype(F32)
+        rim = got[s, dims.rows * SPAN :, :].astype(F32)
         at = lax.broadcasted_iota(I32, (SPAN, chans), 0)
         for i in range(dims.rows):
             local = start + i
             place = global_row(local, e, dims) - above
             place = jnp.where((local < dims.local_rows) & (place < SPAN + 2), place, SPAN + 2)
-            line = got[e, i * SPAN : (i + 1) * SPAN, :]
+            line = got[s, i * SPAN : (i + 1) * SPAN, :]
             wider = line.astype(F32)
             left = jnp.where(at == 0, rim[2 * i : 2 * i + 1], pltpu.roll(wider, 1, 0))
             right = jnp.where(at == SPAN - 1, rim[2 * i + 1 : 2 * i + 2], pltpu.roll(wider, SPAN - 1, 0))
@@ -271,7 +280,7 @@
     spots = jnp.clip((t.astype(F32) + 0.5) * lengthf / S - 0.5, 0.0, lengthf - 1.0)
     across = jnp.where((t >= 0) & (t < S), jnp.maximum(0.0, 1.0 - jnp.abs(spots - j)), 0.0)
     across = across.reshape(4 * half, SPAN).astype(BF16)
-    group = 4
+    group = 8
 
     @pl.loop(0, S // 2 // group)
     def _(step):
@@ -317,16 +326,17 @@
             mixed[k, pl.ds(0, half, stride=2), :] = total[k * half : (k + 1) * half, :chans]
             mixed[k, pl.ds(1, half, stride=2), :] = total[k * half : (k + 1) * half, chans:]
         delta[pl.ds(first, n)] = mixed[...].astype(BF16)
+        finish(step, pl.ds(first, n))
 
 
 def begin(dims, arrived, weights, scratch):
     got, row_store, column_store, got_sems, tap_sems = scratch
 
-    def arrival(e):
-        return pltpu.make_async_copy(arrived.at[e], got.at[e], got_sems.at[e])
-
-    for e in range(dims.tiles):
-        arrival(e).start()
+    def arrival(s):
+        return pltpu.make_async_copy(arrived[0], got.at[s], got_sems.at[s])
+
+    for s in range(dims.tiles):
+        pltpu.make_async_copy(arrived[s], got.at[s], got_sems.at[s]).start()
     taps = (
         RowTaps(weights[0], row_store, tap_sems.at[0]),
         ColumnTaps(weights[1], column_store.at[0], tap_sems.at[1]),
@@ -337,22 +347,25 @@
     return arrival, taps
 
 
-def main_kernel(
-    dims, table, arrived, dec_w, one_w, two_w, dec_b, one_b, two_b, sent, restored,
-    got, row_store, column_store, got_sems, tap_sems, raw, decoded, wide, inner, mixed, delta, sem, back, back_sems,
-):
+def main_kernel(dims, table, *refs):
     tiles, chans = dims.tiles, dims.chans
+    arrived, refs = refs[:tiles], refs[tiles:]
+    (dec_w, one_w, two_w, dec_b, one_b, two_b, sent, restored, got, row_store, column_store, got_sems, tap_sems) = refs[:13]
+    raw, decoded, wide, inner, mixed, delta, sem, back, back_sems = refs[13:]
     me = lax.axis_index("tile")
     row0 = table[ROW, me]
     length = table[SIDE, me]
     place = table[PLACE, me]
     scratch = (got, row_store, column_store, got_sems, tap_sems)
     arrival, taps = begin(dims, arrived, (dec_w, one_w, two_w), scratch)
-    restore(dims, row0, length, arrival, got, taps, (dec_b, one_b, two_b), raw, decoded, wide, inner, mixed, delta)
+    restore(
+        dims, row0, length, arrival, lambda s: me ^ s, got, taps, (dec_b, one_b, two_b),
+        raw, decoded, wide, inner, mixed, delta, lambda step, rows: None,
+    )
 
     @pl.when(place < CAP)
     def _():
-        pltpu.make_async_copy(delta, restored.at[place], sem).start()
+        pltpu.make_async_copy(delta, restored.at[place], sem.at[0]).start()
 
     lengthf = length.astype(F32)
     t = lax.broadcasted_iota(I32, (SPAN, S), 0).astype(F32)
@@ -362,7 +375,7 @@
     coarse = lift.astype(BF16)
     lift = jnp.concatenate([coarse, (lift - coarse.astype(F32)).astype(BF16)], 0)
     scale = 1.0 / (2.0 * lengthf)
-    group = 4
+    group = 8
 
     @pl.loop(0, SPAN // 2 // group)
     def _(step):
@@ -393,7 +406,7 @@
 
     @pl.when(place < CAP)
     def _():
-        pltpu.make_async_copy(delta, restored.at[place], sem).wait()
+        pltpu.make_async_copy(delta, restored.at[place], sem.at[0]).wait()
 
 
 def extra_kernel(
@@ -406,16 +419,24 @@
     place = table[PLACE, me]
 
     def write(slot):
-        copy = pltpu.make_async_copy(delta, restored.at[slot], sem)
+        copy = pltpu.make_async_copy(delta, restored.at[slot], sem.at[0])
         copy.start()
         copy.wait()
 
     @pl.when(length > 0)
     def _():
         scratch = (got, row_store, column_store, got_sems, tap_sems)
-        arrival, taps = begin(dims, arrived, (dec_w, one_w, two_w), scratch)
-        restore(dims, row0, length, arrival, got, taps, (dec_b, one_b, two_b), raw, decoded, wide, inner, mixed, delta)
-        write(1)
+        arrival, taps = begin(dims, [arrived.at[s] for s in range(dims.tiles)], (dec_w, one_w, two_w), scratch)
+
+        def leave(step, rows):
+            return pltpu.make_async_copy(delta.at[rows], restored.at[1, rows], sem.at[step])
+
+        restore(
+            dims, row0, length, arrival, lambda s: s, got, taps, (dec_b, one_b, two_b),
+            raw, decoded, wide, inner, mixed, delta, lambda step, rows: leave(step, rows).start(),
+        )
+        for step in range(2):
+            leave(step, pl.ds(step * (S // 2), S // 2)).wait()
 
     @pl.when(length == 0)
     def _():
@@ -443,23 +464,26 @@
             pltpu.make_async_copy(below.at[band], down.at[band], sems.at[2, band]),
         )
 
+    taps.start()
     for band in range(bands):
-        for copy in fetch(band):
+        for copy in fetch(band)[1:]:
             copy.start()
-    taps.start()
+    for band in range(bands):
+        fetch(band)[0].start()
     top = (me == 0).astype(I32)
     bottom = (me == dims.tiles - 1).astype(I32)
     edge = jnp.zeros((8, chans), F32)
     for a in range(4):
         lines[a, 0:8] = edge
         lines[a, 8 + cols :] = edge
+    taps.wait()
     for band in range(bands):
-        for copy in fetch(band):
+        for copy in fetch(band)[1:]:
             copy.wait()
-    taps.wait()
 
     @pl.loop(0, bands)
     def _(j):
+        fetch(j)[0].wait()
         no_top = (top == 1) & (j == 0)
         no_bottom = (bottom == 1) & (j == bands - 1)
         over = up[jnp.maximum(j - top, 0)].astype(F32)
@@ -483,28 +507,31 @@
 
 def paste_kernel(dims, table, decoded, back, finished, canvas, out, sems):
     me = lax.axis_index("tile")
-    for row in range(dims.local_rows):
-        canvas[row] = decoded[row].astype(F32)
-
-    @pl.loop(0, dims.tiles)
-    def _(e):
-        row0 = table[ROW, e]
-        col0 = table[COL, e]
-        length = table[SIDE, e]
-        start = first_local(row0, me, dims)
-        for i in range(dims.back_rows):
-            local = start + i
-
-            @pl.when((local < dims.local_rows) & (global_row(local, me, dims) - row0 < length))
+
+    def leave(row):
+        return pltpu.make_async_copy(out.at[row], finished.at[row], sems.at[row])
+
+    @pl.loop(0, dims.local_rows)
+    def _(row):
+        canvas[...] = decoded[row].astype(F32)
+        place = global_row(row, me, dims)
+
+        @pl.loop(0, dims.tiles)
+        def _(e):
+            row0 = table[ROW, e]
+            offset = place - row0
+
+            @pl.when((offset >= 0) & (offset < table[SIDE, e]))
             def _():
-                canvas[local, pl.ds(col0, SPAN), :] += back[e, i].astype(F32)
-
-    copies = [pltpu.make_async_copy(out.at[row], finished.at[row], sems.at[row]) for row in range(dims.local_rows)]
-    for row in range(dims.local_rows):
-        out[row] = canvas[row].astype(BF16)
-        copies[row].start()
-    for copy in copies:
-        copy.wait()
+                at = row - first_local(row0, me, dims)
+                canvas[pl.ds(table[COL, e], SPAN), :] += back[e, at].astype(F32)
+
+        out[row] = canvas[...].astype(BF16)
+        leave(row).start()
+
+    @pl.loop(0, dims.local_rows)
+    def _(row):
+        leave(row).wait()
 
 
 def shards(features, dec_weight, dec_bias, first_weight, first_bias, second_weight, second_bias, boxes, slots):
@@ -540,11 +567,12 @@
         dma((tiles,)),
     ]
     message = shaped(tiles, dims.message, chans)
-    sent_main, table, last, leading = pl.pallas_call(
+    *sent_main, table, last, leading = pl.pallas_call(
         functools.partial(pack_main_kernel, dims),
-        out_shape=[message, shaped(7, tiles, kind=I32), shaped(bands, cols, chans), shaped(bands, cols, chans)],
+        out_shape=[shaped(dims.message, chans)] * tiles
+        + [shaped(7, tiles, kind=I32), shaped(bands, cols, chans), shaped(bands, cols, chans)],
         in_specs=[hbm, hbm, hbm],
-        out_specs=[hbm, smem, hbm, hbm],
+        out_specs=[hbm] * tiles + [smem, hbm, hbm],
         scratch_shapes=[
             pltpu.SMEM(boxes.shape, I32),
             pltpu.SMEM(slots.shape, I32),
@@ -557,7 +585,9 @@
         cost_estimate=cost(0, 6e6),
         name="pack_main",
     )(boxes, slots, features)
-    got_main = swap(sent_main)
+    got_main = [sent_main[0]]
+    for s in range(1, tiles):
+        got_main.append(lax.ppermute(sent_main[s], "tile", [(i, i ^ s) for i in range(tiles)]))
     up = [(i, (i + 1) % tiles) for i in range(tiles)]
     above = lax.ppermute(last, "tile", up)
     below = lax.ppermute(leading, "tile", [(j, i) for i, j in up])
@@ -588,20 +618,20 @@
         pltpu.VMEM((S + 2, S // 2, 4 * chans), BF16),
         pltpu.VMEM((32, S, chans), F32),
         pltpu.VMEM((S, S, chans), BF16),
-        dma,
+        dma((2,)),
     ]
     restored_shape = shaped(CAP, S, S, chans)
     sent_back, partial = pl.pallas_call(
         functools.partial(main_kernel, dims),
         out_shape=[shaped(tiles, dims.back_rows, SPAN, chans), restored_shape],
-        in_specs=[smem] + [hbm] * 4 + [vmem] * 3,
+        in_specs=[smem] + [hbm] * (tiles + 3) + [vmem] * 3,
         out_specs=[hbm, hbm],
         scratch_shapes=restore_scratch
         + [pltpu.VMEM((tiles, dims.back_rows, SPAN, chans), BF16), dma((tiles,))],
         compiler_params=full,
         cost_estimate=cost(7e9, 8e6),
         name="restore_main",
-    )(table, got_main, *weights, *biases)
+    )(table, *got_main, *weights, *biases)
     got_back = swap(sent_back)
 
     restorations = pl.pallas_call(
@@ -644,7 +674,7 @@
         in_specs=[smem, vmem, vmem],
         out_specs=hbm,
         scratch_shapes=[
-            pltpu.VMEM((local_rows, cols, chans), F32),
+            pltpu.VMEM((cols, chans), F32),
             pltpu.VMEM((local_rows, cols, chans), BF16),
             dma((local_rows,)),
         ],

time: 65.1 us -> 61.6 us (0.946)
  the two profiles are of different devices: /device:TPU:13 before, /device:TPU:2 now
where the time goes in v5:
time: 61.6 us; the launch traced here: 60.4 us
  Pallas kernels  37.9 us (62%)
  starting transfers between devices  17.9 us (29%)
  local copies, waits for them, and re-layouts  2.79 us (5%)
  waiting for transfers between devices  1.04 us (2%)
  between operations  0.76 us (1%)
    pallas_call x1, Pallas kernels, shards(): pl.pallas_call(functools.partial(main_kernel, dims), out_shape=[shaped(ti...  11.4 us
    all_to_all x2, starting transfers between devices, swap(): lax.all_to_all(array, 'tile', split_axis=0, concat_axis=0, tiled=True)  10.7 us
    pallas_call x1, Pallas kernels, shards(): pl.pallas_call(functools.partial(extra_kernel, dims), out_shape=restored_...  10.4 us
    pallas_call x1, Pallas kernels, shards(): pl.pallas_call(functools.partial(decode_kernel, dims), out_shape=shaped(l...  5.45 us
    ppermute x7, starting transfers between devices, shards(): lax.ppermute(sent_main[s], 'tile', [(i, i ^ s) for i in range(tiles)])  5.42 us
    pallas_call x1, Pallas kernels, shards(): pl.pallas_call(functools.partial(paste_kernel, dims), out_shape=shaped(lo...  4.03 us
    pallas_call x1, Pallas kernels, shards(): pl.pallas_call(functools.partial(pack_extra_kernel, dims), out_shape=mess...  3.35 us
    pallas_call x1, Pallas kernels, shards(): pl.pallas_call(functools.partial(pack_main_kernel, dims), out_shape=[shap...  3.25 us
  transfers between devices with their start and end apart: 11, of which 1 were waited for; matrix products, arithmetic and copies ran while one was open for 0% of the time, Pallas kernels for 51%

profile of v5, /device:TPU:2, one launch (start us, length us, event | category | flops | bytes accessed | tf_op | source)
XLA Modules:
  0.0 60.4 jit_solution(3774478508953962935)
XLA Ops:
  0.6 3.2 %pack_main.1 = (bf16[400,128]{1,0:T(8,128)(2,1)}, bf16[400,128]{1,0:T(8,128)(2,1)}, bf16[400,128]{1,0:T(8,128)(2,1)}, bf16[400,128]{1,0:T(8,128)(2,1)}, bf16[400...) custom-call(s32[3,8]{1,0:T(4,128)} %boxes_in.1, ...), custom_call_target="tpu_custom_call" | custom-call | bytes 6000000 | tf_op jit(solution)/shard_map/pack_main/pallas_call | solution.py:570
  3.9 0.1 collective-permute-start.2
  4.0 0.1 collective-permute-start.3
  4.0 1.8 %collective-permute-start.4 = (bf16[400,128]{1,0:T(8,128)(2,1)}, bf16[400,128]{1,0:T(8,128)(2,1)S(1)}, u32[]{:S(2)}, u32[]{:S(2)}) collective-permute-start(bf16[400,128]{1,0:T(8,128)(2,1)} %get-tuple-element.24), channel_id=1, source_target_pairs={{0,3},{1,2},{2,1},{3,0},{4,7},{5,6},{6,5},{7,4},{8,11},{9,10},{10,... | collective-permute-start | bytes 307208 | tf_op jit(solution)/shard_map/ppermute | solution.py:590
  5.8 1.5 %collective-permute-start.5 = (bf16[400,128]{1,0:T(8,128)(2,1)}, bf16[400,128]{1,0:T(8,128)(2,1)}, u32[]{:S(2)}, u32[]{:S(2)}) collective-permute-start(bf16[400,128]{1,0:T(8,128)(2,1)} %get-tuple-element.25), channel_id=1, source_target_pairs={{0,4},{1,5},{2,6},{3,7},{4,0},{5,1},{6,2},{7,3},{8,12},{9,13},{10,... | collective-permute-start | bytes 307208 | tf_op jit(solution)/shard_map/ppermute | solution.py:590
  7.3 0.2 collective-permute-start.6
  7.5 0.0 collective-permute-done.2.refs_1_
  7.5 1.5 %collective-permute-start.7 = (bf16[400,128]{1,0:T(8,128)(2,1)}, bf16[400,128]{1,0:T(8,128)(2,1)}, u32[]{:S(2)}, u32[]{:S(2)}) collective-permute-start(bf16[400,128]{1,0:T(8,128)(2,1)} %get-tuple-element.27), channel_id=1, source_target_pairs={{0,6},{1,7},{2,4},{3,5},{4,2},{5,3},{6,0},{7,1},{8,14},{9,15},{10,... | collective-permute-start | bytes 307208 | tf_op jit(solution)/shard_map/ppermute | solution.py:590
  9.0 1.0 %collective-permute-done.3.refs_2_ = bf16[400,128]{1,0:T(8,128)(2,1)} collective-permute-done((bf16[400,128]{1,0:T(8,128)(2,1)}, bf16[400,128]{1,0:T(8,128)(2,1)}, u32[]{:S(2)}, u32[]{:S(2)}) %collective-permute-start.3) | collective-permute-done | bytes 102432 | tf_op jit(solution)/shard_map/ppermute | solution.py:590
  10.0 0.3 collective-permute-start.8
  10.3 3.4 %pack_extra.1 = bf16[8,400,128]{2,1,0:T(8,128)(2,1)} custom-call(s32[7,8]{1,0:T(8,128)} %get-tuple-element.18.table, bf16[6,2,320,128]{3,2,1,0:T(8,128)(2,1)} %feat.5), custom_call_target="tpu_custom_call" | custom-call | bytes 6000000 | tf_op jit(solution)/shard_map/pack_extra/pallas_call | solution.py:595
  13.7 5.6 %all-to-all-start = ((bf16[8,400,128]{2,1,0:T(8,128)(2,1)}), bf16[8,400,128]{2,1,0:T(8,128)(2,1)}, u32[]{:S(2)}, u32[]{:S(2)}) async-start(bf16[8,400,128]{2,1,0:T(8,128)(2,1)} %pack_extra.1), calls=%async_computation | async-start | bytes 1638400 | tf_op jit(solution)/shard_map/all_to_all | solution.py:558
  19.3 0.0 collective-permute-done.4.refs_3_
  19.3 0.0 copy-start.4
  19.3 0.6 %copy-done.4 = bf16[400,128]{1,0:T(8,128)(2,1)} copy-done((bf16[400,128]{1,0:T(8,128)(2,1)}, bf16[400,128]{1,0:T(8,128)(2,1)S(1)}, u32[]{:S(2)}) %copy-start.4) | copy-done | bytes 102424
  19.9 0.1 collective-permute-start
  20.1 0.0 collective-permute-done.5.refs_4_
  20.1 1.6 %collective-permute-start.1 = (bf16[6,320,128]{2,1,0:T(8,128)(2,1)}, bf16[6,320,128]{2,1,0:T(8,128)(2,1)}, u32[]{:S(2)}, u32[]{:S(2)}) collective-permute-start(bf16[6,320,128]{2,1,0:T(8,128)(2,1)} %get-tuple-element.20), channel_id=1, source_target_pairs={{1,0},{2,1},{3,2},{4,3},{5,4},{6,5},{7,6},{0,7},{9,8},{10,9},{11,1... | collective-permute-start | bytes 1474568 | tf_op jit(solution)/shard_map/ppermute | solution.py:593
  21.7 0.0 collective-permute-done.6.refs_5_
  21.7 0.0 collective-permute-done.7.refs_6_
  21.7 0.0 collective-permute-done.8.refs_7_
  21.7 11.4 %restore_main.1 = (bf16[8,6,48,128]{3,2,1,0:T(8,128)(2,1)}, bf16[2,64,64,128]{3,2,1,0:T(8,128)(2,1)}) custom-call(s32[7,8]{1,0:T(8,128)} %get-tuple-element.18.table, bf16[400,128]{1,0:T(8,128)(2,1)} %get-tuple-element.21.refs_0_, bf16[400,128]{1,0:T(8,128)(2,1)} %collective-permute-done.2.refs_1_, bf16[400,128]{1,0:T(8,128)(2,1)} %collective-permute-done.3.refs_2_, ...), custom_call_target="tpu_custom_call" | custom-call | flops 7000000000 | bytes 8000000 | tf_op jit(solution)/shard_map/restore_main/pallas_call | solution.py:624
  33.1 0.0 all-to-all-done.arrived
  33.1 5.1 %all-to-all-start.1 = ((bf16[8,6,48,128]{3,2,1,0:T(8,128)(2,1)}), bf16[8,6,48,128]{3,2,1,0:T(8,128)(2,1)}, u32[]{:S(2)}, u32[]{:S(2)}) async-start(bf16[8,6,48,128]{3,2,1,0:T(8,128)(2,1)} %get-tuple-element.32), calls=%async_computation.1 | async-start | bytes 1179648 | tf_op jit(solution)/shard_map/all_to_all | solution.py:558
  38.2 0.0 copy-start.3
  38.2 0.0 copy-start.1
  38.2 10.4 %restore_extra.1 = bf16[2,64,64,128]{3,2,1,0:T(8,128)(2,1)} custom-call(s32[7,8]{1,0:T(8,128)} %get-tuple-element.18.table, bf16[8,400,128]{2,1,0:T(8,128)(2,1)} %all-to-all-done.arrived, bf16[3,3,128,128]{3,2,1,0:T(8,128)(2,1)} %bitcast.8, bf16[3,3,128,128]{3,2,1,0:T(8,128)(2,1)} %bitcast.15, ...), custom_call_target="tpu_custom_call", output_to_operand_aliasing={{}: (8, {})} | custom-call | flops 6000000000 | bytes 8000000 | tf_op jit(solution)/shard_map/restore_extra/pallas_call | solution.py:637
  48.7 0.0 collective-permute-done.above
  48.7 0.0 collective-permute-done.1.below
  48.7 0.0 copy-done.3
  48.7 0.0 copy-start
  48.7 1.2 %copy-done = bf16[6,2,320,128]{3,2,1,0:T(8,128)(2,1)S(1)} copy-done((bf16[6,2,320,128]{3,2,1,0:T(8,128)(2,1)S(1)}, bf16[6,2,320,128]{3,2,1,0:T(8,128)(2,1)}, u32[]{:S(2)}) %copy-start) | copy-done | bytes 983064
  49.9 0.0 copy-start.2
  49.9 1.0 %copy-done.2 = bf16[9,128,128]{2,1,0:T(8,128)(2,1)S(1)} copy-done((bf16[9,128,128]{2,1,0:T(8,128)(2,1)S(1)}, bf16[9,128,128]{2,1,0:T(8,128)(2,1)}, u32[]{:S(2)}) %copy-start.2) | copy-done | bytes 294936
  50.9 5.4 %decode.1.decoded = bf16[12,320,128]{2,1,0:T(8,128)(2,1)S(1)} custom-call(bf16[6,2,320,128]{3,2,1,0:T(8,128)(2,1)S(1)} %copy-done, bf16[6,320,128]{2,1,0:T(8,128)(2,1)S(1)} %collective-permute-done.above, bf16[6,320,128]{2,1,0:T(8,128)(2,1)} %collective-permute-done.1.below, bf16[3,3,128,128]{3,2,1,0:T(8,128)(2,1)S(1)} %bitcast.9, f32[1,128]{1,0:T(1,128)S(1)} %bitcast.12), custom_call_target="tpu_custom_call" | custom-call | flops 3000000000 | bytes 6000000 | tf_op jit(solution)/shard_map/decode/pallas_call | solution.py:650
  56.3 0.0 all-to-all-done.1.back
  56.3 0.0 copy-done.1
  56.3 4.0 %paste.1 = bf16[12,320,128]{2,1,0:T(8,128)(2,1)} custom-call(s32[7,8]{1,0:T(8,128)S(1)} %copy-done.1, bf16[12,320,128]{2,1,0:T(8,128)(2,1)S(1)} %decode.1.decoded, bf16[8,6,48,128]{3,2,1,0:T(8,128)(2,1)} %all-to-all-done.1.back), custom_call_target="tpu_custom_call" | custom-call | bytes 6000000 | tf_op jit(solution)/shard_map/paste/pallas_call | solution.py:671
Async XLA Ops:
  3.9 3.6 %collective-permute-start.2 = (bf16[400,128]{1,0:T(8,128)(2,1)}, bf16[400,128]{1,0:T(8,128)(2,1)}, u32[]{:S(2)}, u32[]{:S(2)}) collective-permute-start(bf16[400,128]{1,0:T(8,128)(2,1)} %get-tuple-element.22), channel_id=1, source_target_pairs={{0,1},{1,0},{2,3},{3,2},{4,5},{5,4},{6,7},{7,6},{8,9},{9,8},{10,11... | collective-permute-start | bytes 307208 | tf_op jit(solution)/shard_map/ppermute | solution.py:590
  4.0 6.1 %collective-permute-start.3 = (bf16[400,128]{1,0:T(8,128)(2,1)}, bf16[400,128]{1,0:T(8,128)(2,1)}, u32[]{:S(2)}, u32[]{:S(2)}) collective-permute-start(bf16[400,128]{1,0:T(8,128)(2,1)} %get-tuple-element.23), channel_id=1, source_target_pairs={{0,2},{1,3},{2,0},{3,1},{4,6},{5,7},{6,4},{7,5},{8,10},{9,11},{10,... | collective-permute-start | bytes 307208 | tf_op jit(solution)/shard_map/ppermute | solution.py:590
  4.0 15.3 %collective-permute-start.4 = (bf16[400,128]{1,0:T(8,128)(2,1)}, bf16[400,128]{1,0:T(8,128)(2,1)S(1)}, u32[]{:S(2)}, u32[]{:S(2)}) collective-permute-start(bf16[400,128]{1,0:T(8,128)(2,1)} %get-tuple-element.24), channel_id=1, source_target_pairs={{0,3},{1,2},{2,1},{3,0},{4,7},{5,6},{6,5},{7,4},{8,11},{9,10},{10,... | collective-permute-start | bytes 307208 | tf_op jit(solution)/shard_map/ppermute | solution.py:590
  5.8 14.3 %collective-permute-start.5 = (bf16[400,128]{1,0:T(8,128)(2,1)}, bf16[400,128]{1,0:T(8,128)(2,1)}, u32[]{:S(2)}, u32[]{:S(2)}) collective-permute-start(bf16[400,128]{1,0:T(8,128)(2,1)} %get-tuple-element.25), channel_id=1, source_target_pairs={{0,4},{1,5},{2,6},{3,7},{4,0},{5,1},{6,2},{7,3},{8,12},{9,13},{10,... | collective-permute-start | bytes 307208 | tf_op jit(solution)/shard_map/ppermute | solution.py:590
  7.3 14.3 %collective-permute-start.6 = (bf16[400,128]{1,0:T(8,128)(2,1)}, bf16[400,128]{1,0:T(8,128)(2,1)}, u32[]{:S(2)}, u32[]{:S(2)}) collective-permute-start(bf16[400,128]{1,0:T(8,128)(2,1)} %get-tuple-element.26), channel_id=1, source_target_pairs={{0,5},{1,4},{2,7},{3,6},{4,1},{5,0},{6,3},{7,2},{8,13},{9,12},{10,... | collective-permute-start | bytes 307208 | tf_op jit(solution)/shard_map/ppermute | solution.py:590
  7.5 14.2 %collective-permute-start.7 = (bf16[400,128]{1,0:T(8,128)(2,1)}, bf16[400,128]{1,0:T(8,128)(2,1)}, u32[]{:S(2)}, u32[]{:S(2)}) collective-permute-start(bf16[400,128]{1,0:T(8,128)(2,1)} %get-tuple-element.27), channel_id=1, source_target_pairs={{0,6},{1,7},{2,4},{3,5},{4,2},{5,3},{6,0},{7,1},{8,14},{9,15},{10,... | collective-permute-start | bytes 307208 | tf_op jit(solution)/shard_map/ppermute | solution.py:590
  10.0 11.7 %collective-permute-start.8 = (bf16[400,128]{1,0:T(8,128)(2,1)}, bf16[400,128]{1,0:T(8,128)(2,1)}, u32[]{:S(2)}, u32[]{:S(2)}) collective-permute-start(bf16[400,128]{1,0:T(8,128)(2,1)} %get-tuple-element.28), channel_id=1, source_target_pairs={{0,7},{1,6},{2,5},{3,4},{4,3},{5,2},{6,1},{7,0},{8,15},{9,14},{10,... | collective-permute-start | bytes 307208 | tf_op jit(solution)/shard_map/ppermute | solution.py:590
  13.7 19.4 %all-to-all-start = ((bf16[8,400,128]{2,1,0:T(8,128)(2,1)}), bf16[8,400,128]{2,1,0:T(8,128)(2,1)}, u32[]{:S(2)}, u32[]{:S(2)}) async-start(bf16[8,400,128]{2,1,0:T(8,128)(2,1)} %pack_extra.1), calls=%async_computation | async-start | bytes 1638400 | tf_op jit(solution)/shard_map/all_to_all | solution.py:558
  19.3 0.6 %copy-start.4 = (bf16[400,128]{1,0:T(8,128)(2,1)}, bf16[400,128]{1,0:T(8,128)(2,1)S(1)}, u32[]{:S(2)}) copy-start(bf16[400,128]{1,0:T(8,128)(2,1)S(1)} %collective-permute-done.4.refs_3_) | copy-start | bytes 307204
  19.9 28.7 %collective-permute-start = (bf16[6,320,128]{2,1,0:T(8,128)(2,1)}, bf16[6,320,128]{2,1,0:T(8,128)(2,1)S(1)}, u32[]{:S(2)}, u32[]{:S(2)}) collective-permute-start(bf16[6,320,128]{2,1,0:T(8,128)(2,1)} %get-tuple-element.19), channel_id=1, source_target_pairs={{0,1},{1,2},{2,3},{3,4},{4,5},{5,6},{6,7},{7,0},{8,9},{9,10},{10,1... | collective-permute-start | bytes 1474568 | tf_op jit(solution)/shard_map/ppermute | solution.py:592
  20.1 28.6 %collective-permute-start.1 = (bf16[6,320,128]{2,1,0:T(8,128)(2,1)}, bf16[6,320,128]{2,1,0:T(8,128)(2,1)}, u32[]{:S(2)}, u32[]{:S(2)}) collective-permute-start(bf16[6,320,128]{2,1,0:T(8,128)(2,1)} %get-tuple-element.20), channel_id=1, source_target_pairs={{1,0},{2,1},{3,2},{4,3},{5,4},{6,5},{7,6},{0,7},{9,8},{10,9},{11,1... | collective-permute-start | bytes 1474568 | tf_op jit(solution)/shard_map/ppermute | solution.py:593
  33.1 23.2 %all-to-all-start.1 = ((bf16[8,6,48,128]{3,2,1,0:T(8,128)(2,1)}), bf16[8,6,48,128]{3,2,1,0:T(8,128)(2,1)}, u32[]{:S(2)}, u32[]{:S(2)}) async-start(bf16[8,6,48,128]{3,2,1,0:T(8,128)(2,1)} %get-tuple-element.32), calls=%async_computation.1 | async-start | bytes 1179648 | tf_op jit(solution)/shard_map/all_to_all | solution.py:558
  38.2 10.4 %copy-start.3 = (f32[128]{0:T(128)S(1)}, f32[128]{0:T(128)}, u32[]{:S(2)}) copy-start(f32[128]{0:T(128)} %param.11) | copy-start | bytes 1540
  38.2 18.1 %copy-start.1 = (s32[7,8]{1,0:T(8,128)S(1)}, s32[7,8]{1,0:T(8,128)}, u32[]{:S(2)}) copy-start(s32[7,8]{1,0:T(8,128)} %get-tuple-element.18.table) | copy-start | bytes 676
  48.7 1.2 %copy-start = (bf16[6,2,320,128]{3,2,1,0:T(8,128)(2,1)S(1)}, bf16[6,2,320,128]{3,2,1,0:T(8,128)(2,1)}, u32[]{:S(2)}) copy-start(bf16[6,2,320,128]{3,2,1,0:T(8,128)(2,1)} %feat.5) | copy-start | bytes 2949124
  49.9 1.0 %copy-start.2 = (bf16[9,128,128]{2,1,0:T(8,128)(2,1)S(1)}, bf16[9,128,128]{2,1,0:T(8,128)(2,1)}, u32[]{:S(2)}) copy-start(bf16[9,128,128]{2,1,0:T(8,128)(2,1)} %param.10) | copy-start | bytes 884740

commit v6 on v5

--- a/solution.py
+++ b/solution.py
@@ -16,7 +16,6 @@
 F32 = jnp.float32
 I32 = jnp.int32
 FULL_GRANT = 66500000
-SMALL_GRANT = 32 * 1024 * 1024
 ROW, COL, SIDE, ROW2, COL2, SIDE2, PLACE = range(7)
 
 
@@ -51,14 +50,16 @@
 
 
 def both(bias):
-    return jnp.concatenate([bias[...], bias[...]], -1)
+    return jnp.concatenate([bias, bias], -1)
 
 
 class RowTaps:
-    def __init__(self, source, store, sems):
+    def __init__(self, source, bias, store, held, sems):
         chans = source.shape[-1]
         self.store = store
+        self.held = held
         self.copies = (
+            pltpu.make_async_copy(bias, held, sems.at[2]),
             pltpu.make_async_copy(source, store.at[0:3, :, :, 0:chans], sems.at[0]),
             pltpu.make_async_copy(source, store.at[1:4, :, :, chans : 2 * chans], sems.at[1]),
         )
@@ -75,15 +76,20 @@
         for copy in self.copies:
             copy.wait()
 
+    def bias(self):
+        return both(self.held[...])
+
     def value(self):
         return self.store[...].reshape(-1, self.store.shape[-1])
 
 
 class ColumnTaps(RowTaps):
-    def __init__(self, source, store, sems):
+    def __init__(self, source, bias, store, held, sems):
         chans = source.shape[-1]
         self.store = store
+        self.held = held
         self.copies = (
+            pltpu.make_async_copy(bias, held, sems.at[2]),
             pltpu.make_async_copy(source, store.at[:, 0:3, :, 0:chans], sems.at[0]),
             pltpu.make_async_copy(source, store.at[:, 1:4, :, chans : 2 * chans], sems.at[1]),
         )
@@ -158,11 +164,11 @@
         staged[s, dims.rows * SPAN :, :] = rim[...].astype(BF16)
 
 
-def pack_main_kernel(
+def pack_kernel(
     dims, boxes_in, slots_in, feat, *refs
 ):
     sent, refs = refs[: dims.tiles], refs[dims.tiles :]
-    table, last, leading, boxes, slots, main, extra, seconds, held, canvas, rim, staged, sems, feat_sems, sent_sems = refs
+    sent_extra, table, last, leading, boxes, slots, main, extra, seconds, held, canvas, rim, staged, staged_extra, sems, feat_sems, sent_sems = refs
     me = lax.axis_index("tile")
     copies = (
         pltpu.make_async_copy(boxes_in, boxes, sems.at[0]),
@@ -212,23 +218,17 @@
     copies = [pltpu.make_async_copy(staged.at[s], sent[s], sent_sems.at[s]) for s in range(dims.tiles)]
     for copy in copies:
         copy.start()
+    pack_crops(dims, table, ROW2, COL2, canvas, rim, staged_extra, lambda s: s)
+    later = pltpu.make_async_copy(staged_extra, sent_extra, sems.at[0])
+    later.start()
     for copy in copies:
         copy.wait()
+    later.wait()
     for edge in edges:
         edge.wait()
 
 
-def pack_extra_kernel(dims, table, feat, sent, held, canvas, rim, staged, sems, feat_sems, sent_sems):
-    fill_canvas(dims, feat, held, canvas, feat_sems)()
-    pack_crops(dims, table, ROW2, COL2, canvas, rim, staged, lambda s: s)
-    copies = [pltpu.make_async_copy(staged.at[s], sent.at[s], sent_sems.at[s]) for s in range(dims.tiles)]
-    for copy in copies:
-        copy.start()
-    for copy in copies:
-        copy.wait()
-
-
-def restore(dims, row0, length, arrival, source, got, taps, biases, raw, decoded, wide, inner, mixed, delta, finish):
+def restore(dims, row0, length, arrival, source, got, taps, raw, decoded, wide, inner, mixed, delta, finish):
     chans = dims.chans
     above = row0 - 1
     pairs = SPAN // 2
@@ -264,7 +264,7 @@
     @pl.loop(0, pairs // n)
     def _(step):
         first = step * n
-        total = silu(row_pairs(raw, first, n, taps[0]) + both(biases[0]))
+        total = silu(row_pairs(raw, first, n, taps[0]) + taps[0].bias())
         for k in range(n):
             part = total[k * SPAN : (k + 1) * SPAN]
             at = 2 * (first + k)
@@ -280,7 +280,7 @@
     spots = jnp.clip((t.astype(F32) + 0.5) * lengthf / S - 0.5, 0.0, lengthf - 1.0)
     across = jnp.where((t >= 0) & (t < S), jnp.maximum(0.0, 1.0 - jnp.abs(spots - j)), 0.0)
     across = across.reshape(4 * half, SPAN).astype(BF16)
-    group = 8
+    group = 16
 
     @pl.loop(0, S // 2 // group)
     def _(step):
@@ -307,7 +307,7 @@
     @pl.loop(0, S // n)
     def _(step):
         first = step * n
-        total = silu(column_pairs(wide, first, n, taps[1]) + both(biases[1]))
+        total = silu(column_pairs(wide, first, n, taps[1]) + taps[1].bias())
         at = lax.broadcasted_iota(I32, (n, half, chans), 1)
         even = pltpu.roll(total[:, :chans], n * half - 1, 0).reshape(n, half, chans)
         odd = pltpu.roll(total[:, chans:], 1, 0).reshape(n, half, chans)
@@ -321,7 +321,7 @@
     @pl.loop(0, S // n)
     def _(step):
         first = step * n
-        total = column_pairs(inner, first, n, taps[2]) + both(biases[2])
+        total = column_pairs(inner, first, n, taps[2]) + taps[2].bias()
         for k in range(n):
             mixed[k, pl.ds(0, half, stride=2), :] = total[k * half : (k + 1) * half, :chans]
             mixed[k, pl.ds(1, half, stride=2), :] = total[k * half : (k + 1) * half, chans:]
@@ -329,8 +329,8 @@
         finish(step, pl.ds(first, n))
 
 
-def begin(dims, arrived, weights, scratch):
-    got, row_store, column_store, got_sems, tap_sems = scratch
+def begin(dims, arrived, weights, biases, scratch):
+    got, row_store, column_store, held, got_sems, tap_sems = scratch
 
     def arrival(s):
         return pltpu.make_async_copy(arrived[0], got.at[s], got_sems.at[s])
@@ -338,9 +338,9 @@
     for s in range(dims.tiles):
         pltpu.make_async_copy(arrived[s], got.at[s], got_sems.at[s]).start()
     taps = (
-        RowTaps(weights[0], row_store, tap_sems.at[0]),
-        ColumnTaps(weights[1], column_store.at[0], tap_sems.at[1]),
-        ColumnTaps(weights[2], column_store.at[1], tap_sems.at[2]),
+        RowTaps(weights[0], biases[0], row_store, held.at[0], tap_sems.at[0]),
+        ColumnTaps(weights[1], biases[1], column_store.at[0], held.at[1], tap_sems.at[1]),
+        ColumnTaps(weights[2], biases[2], column_store.at[1], held.at[2], tap_sems.at[2]),
     )
     for tap in taps:
         tap.start()
@@ -350,16 +350,16 @@
 def main_kernel(dims, table, *refs):
     tiles, chans = dims.tiles, dims.chans
     arrived, refs = refs[:tiles], refs[tiles:]
-    (dec_w, one_w, two_w, dec_b, one_b, two_b, sent, restored, got, row_store, column_store, got_sems, tap_sems) = refs[:13]
-    raw, decoded, wide, inner, mixed, delta, sem, back, back_sems = refs[13:]
+    (dec_w, one_w, two_w, dec_b, one_b, two_b, sent, restored, got, row_store, column_store, held) = refs[:12]
+    got_sems, tap_sems, raw, decoded, wide, inner, mixed, delta, sem, back, back_sems = refs[12:]
     me = lax.axis_index("tile")
     row0 = table[ROW, me]
     length = table[SIDE, me]
     place = table[PLACE, me]
-    scratch = (got, row_store, column_store, got_sems, tap_sems)
-    arrival, taps = begin(dims, arrived, (dec_w, one_w, two_w), scratch)
+    scratch = (got, row_store, column_store, held, got_sems, tap_sems)
+    arrival, taps = begin(dims, arrived, (dec_w, one_w, two_w), (dec_b, one_b, two_b), scratch)
     restore(
-        dims, row0, length, arrival, lambda s: me ^ s, got, taps, (dec_b, one_b, two_b),
+        dims, row0, length, arrival, lambda s: me ^ s, got, taps,
         raw, decoded, wide, inner, mixed, delta, lambda step, rows: None,
     )
 
@@ -375,7 +375,7 @@
     coarse = lift.astype(BF16)
     lift = jnp.concatenate([coarse, (lift - coarse.astype(F32)).astype(BF16)], 0)
     scale = 1.0 / (2.0 * lengthf)
-    group = 8
+    group = 12
 
     @pl.loop(0, SPAN // 2 // group)
     def _(step):
@@ -411,7 +411,7 @@
 
 def extra_kernel(
     dims, table, arrived, dec_w, one_w, two_w, dec_b, one_b, two_b, partial, restored,
-    got, row_store, column_store, got_sems, tap_sems, raw, decoded, wide, inner, mixed, delta, sem,
+    got, row_store, column_store, held, got_sems, tap_sems, raw, decoded, wide, inner, mixed, delta, sem,
 ):
     me = lax.axis_index("tile")
     row0 = table[ROW2, me]
@@ -425,14 +425,14 @@
 
     @pl.when(length > 0)
     def _():
-        scratch = (got, row_store, column_store, got_sems, tap_sems)
-        arrival, taps = begin(dims, [arrived.at[s] for s in range(dims.tiles)], (dec_w, one_w, two_w), scratch)
+        scratch = (got, row_store, column_store, held, got_sems, tap_sems)
+        arrival, taps = begin(dims, [arrived.at[s] for s in range(dims.tiles)], (dec_w, one_w, two_w), (dec_b, one_b, two_b), scratch)
 
         def leave(step, rows):
             return pltpu.make_async_copy(delta.at[rows], restored.at[1, rows], sem.at[step])
 
         restore(
-            dims, row0, length, arrival, lambda s: s, got, taps, (dec_b, one_b, two_b),
+            dims, row0, length, arrival, lambda s: s, got, taps,
             raw, decoded, wide, inner, mixed, delta, lambda step, rows: leave(step, rows).start(),
         )
         for step in range(2):
@@ -451,39 +451,56 @@
             write(1)
 
 
-def decode_kernel(dims, feat, above, below, weight, bias, decoded, held, up, down, store, lines, wide, mixed, sems, tap_sems):
+def finish_kernel(
+    dims, table, back, feat, above, below, weight, bias, finished,
+    got, held, up, down, store, held_bias, lines, wide, canvas, out, sems, tap_sems,
+):
     me = lax.axis_index("tile")
     bands, chans, cols = dims.bands, dims.chans, dims.cols
     half = cols // 2
-    taps = ColumnTaps(weight, store, tap_sems)
-
-    def fetch(band):
-        return (
-            pltpu.make_async_copy(feat.at[band], held.at[band], sems.at[0, band]),
-            pltpu.make_async_copy(above.at[band], up.at[band], sems.at[1, band]),
-            pltpu.make_async_copy(below.at[band], down.at[band], sems.at[2, band]),
-        )
-
+    taps = ColumnTaps(weight, bias, store, held_bias, tap_sems)
+    patches = pltpu.make_async_copy(back, got, sems.at[0])
+    patches.start()
+    loads = (
+        pltpu.make_async_copy(above, up, sems.at[1]),
+        pltpu.make_async_copy(below, down, sems.at[2]),
+        pltpu.make_async_copy(feat, held, sems.at[3]),
+    )
+    for load in loads:
+        load.start()
     taps.start()
-    for band in range(bands):
-        for copy in fetch(band)[1:]:
-            copy.start()
-    for band in range(bands):
-        fetch(band)[0].start()
+
+    def leave(band):
+        return pltpu.make_async_copy(out.at[band], finished.at[band], sems.at[4 + band])
+
     top = (me == 0).astype(I32)
     bottom = (me == dims.tiles - 1).astype(I32)
     edge = jnp.zeros((8, chans), F32)
-    for a in range(4):
-        lines[a, 0:8] = edge
-        lines[a, 8 + cols :] = edge
+    for k in range(lines.shape[0]):
+        for a in range(4):
+            lines[k, a, 0:8] = edge
+            lines[k, a, 8 + cols :] = edge
+    canvas[...] = jnp.zeros_like(canvas)
+    patches.wait()
+
+    @pl.loop(0, dims.tiles)
+    def _(e):
+        row0 = table[ROW, e]
+        col0 = table[COL, e]
+        length = table[SIDE, e]
+        start = first_local(row0, me, dims)
+        for i in range(dims.back_rows):
+            local = start + i
+
+            @pl.when((local < dims.local_rows) & (global_row(local, me, dims) - row0 < length))
+            def _():
+                canvas[local, pl.ds(col0, SPAN), :] += got[e, i].astype(F32)
+
+    for load in loads:
+        load.wait()
     taps.wait()
-    for band in range(bands):
-        for copy in fetch(band)[1:]:
-            copy.wait()
-
-    @pl.loop(0, bands)
-    def _(j):
-        fetch(j)[0].wait()
+
+    def band(j, lines, wide):
         no_top = (top == 1) & (j == 0)
         no_bottom = (bottom == 1) & (j == bands - 1)
         over = up[jnp.maximum(j - top, 0)].astype(F32)
@@ -496,42 +513,24 @@
         for a in range(4):
             for b in range(4):
                 wide[a, :, b * chans : (b + 1) * chans] = lines[a, pl.ds(7 + b, half, stride=2), :].astype(BF16)
-        total = silu(column_pairs(wide, 0, 2, taps) + both(bias))
+        total = silu(column_pairs(wide, 0, 2, taps) + taps.bias())
         for i in range(2):
             part = total[i * half : (i + 1) * half]
             for b in range(2):
                 here = lines[i + 1, pl.ds(8 + b, half, stride=2), :]
-                mixed[i, pl.ds(b, half, stride=2), :] = here + part[:, b * chans : (b + 1) * chans]
-            decoded[2 * j + i] = mixed[i].astype(BF16)
-
-
-def paste_kernel(dims, table, decoded, back, finished, canvas, out, sems):
-    me = lax.axis_index("tile")
-
-    def leave(row):
-        return pltpu.make_async_copy(out.at[row], finished.at[row], sems.at[row])
-
-    @pl.loop(0, dims.local_rows)
-    def _(row):
-        canvas[...] = decoded[row].astype(F32)
-        place = global_row(row, me, dims)
-
-        @pl.loop(0, dims.tiles)
-        def _(e):
-            row0 = table[ROW, e]
-            offset = place - row0
-
-            @pl.when((offset >= 0) & (offset < table[SIDE, e]))
-            def _():
-                at = row - first_local(row0, me, dims)
-                canvas[pl.ds(table[COL, e], SPAN), :] += back[e, at].astype(F32)
-
-        out[row] = canvas[...].astype(BF16)
-        leave(row).start()
-
-    @pl.loop(0, dims.local_rows)
-    def _(row):
-        leave(row).wait()
+                decoded = (here + part[:, b * chans : (b + 1) * chans]).astype(BF16).astype(F32)
+                at = pl.ds(b, half, stride=2)
+                canvas[2 * j + i, at, :] = canvas[2 * j + i, at, :] + decoded
+            out[j, i] = canvas[2 * j + i].astype(BF16)
+        leave(j).start()
+
+    @pl.loop(0, bands // 2)
+    def _(step):
+        for k in range(2):
+            band(2 * step + k, lines.at[k], wide.at[k])
+
+    for j in range(bands):
+        leave(j).wait()
 
 
 def shards(features, dec_weight, dec_bias, first_weight, first_bias, second_weight, second_bias, boxes, slots):
@@ -542,10 +541,8 @@
     assert tiles & (tiles - 1) == 0
 
     smem = pl.BlockSpec(memory_space=pltpu.SMEM)
-    vmem = pl.BlockSpec(memory_space=pltpu.VMEM)
     hbm = pl.BlockSpec(memory_space=pl.ANY)
     full = pltpu.CompilerParams(vmem_limit_bytes=FULL_GRANT)
-    small = pltpu.CompilerParams(vmem_limit_bytes=SMALL_GRANT)
     dma = pltpu.SemaphoreType.DMA
 
     def cost(flops, moved):
@@ -561,18 +558,19 @@
         pltpu.VMEM((bands, 2, cols, chans), BF16),
         pltpu.VMEM((local_rows, cols + 16, chans), F32),
         pltpu.VMEM((dims.rim, chans), F32),
+        pltpu.VMEM((tiles, dims.message, chans), BF16),
         pltpu.VMEM((tiles, dims.message, chans), BF16),
         dma((4,)),
         dma((bands,)),
         dma((tiles,)),
     ]
     message = shaped(tiles, dims.message, chans)
-    *sent_main, table, last, leading = pl.pallas_call(
-        functools.partial(pack_main_kernel, dims),
+    *sent_main, sent_extra, table, last, leading = pl.pallas_call(
+        functools.partial(pack_kernel, dims),
         out_shape=[shaped(dims.message, chans)] * tiles
-        + [shaped(7, tiles, kind=I32), shaped(bands, cols, chans), shaped(bands, cols, chans)],
+        + [message, shaped(7, tiles, kind=I32), shaped(bands, cols, chans), shaped(bands, cols, chans)],
         in_specs=[hbm, hbm, hbm],
-        out_specs=[hbm] * tiles + [smem, hbm, hbm],
+        out_specs=[hbm] * (tiles + 1) + [smem, hbm, hbm],
         scratch_shapes=[
             pltpu.SMEM(boxes.shape, I32),
             pltpu.SMEM(slots.shape, I32),
@@ -583,7 +581,7 @@
         + pack_scratch,
         compiler_params=full,
         cost_estimate=cost(0, 6e6),
-        name="pack_main",
+        name="pack",
     )(boxes, slots, features)
     got_main = [sent_main[0]]
     for s in range(1, tiles):
@@ -592,16 +590,6 @@
     above = lax.ppermute(last, "tile", up)
     below = lax.ppermute(leading, "tile", [(j, i) for i, j in up])
 
-    sent_extra = pl.pallas_call(
-        functools.partial(pack_extra_kernel, dims),
-        out_shape=message,
-        in_specs=[smem, hbm],
-        out_specs=hbm,
-        scratch_shapes=pack_scratch,
-        compiler_params=full,
-        cost_estimate=cost(0, 6e6),
-        name="pack_extra",
-    )(table, features)
     got_extra = swap(sent_extra)
 
     weights = tuple(w.reshape(3, 3, chans, chans) for w in (dec_weight, first_weight, second_weight))
@@ -610,8 +598,9 @@
         pltpu.VMEM((tiles, dims.message, chans), BF16),
         pltpu.VMEM((4, 3, chans, 2 * chans), BF16),
         pltpu.VMEM((2, 3, 4, chans, 2 * chans), BF16),
+        pltpu.VMEM((3, 1, chans), F32),
         dma((tiles,)),
-        dma((3, 2)),
+        dma((3, 3)),
         pltpu.VMEM((SPAN // 2 + 2, 2, SPAN, 3 * chans), BF16),
         pltpu.VMEM((SPAN, SPAN, chans), F32),
         pltpu.VMEM((S + 2, S // 2, 4 * chans), BF16),
@@ -624,7 +613,7 @@
     sent_back, partial = pl.pallas_call(
         functools.partial(main_kernel, dims),
         out_shape=[shaped(tiles, dims.back_rows, SPAN, chans), restored_shape],
-        in_specs=[smem] + [hbm] * (tiles + 3) + [vmem] * 3,
+        in_specs=[smem] + [hbm] * (tiles + 6),
         out_specs=[hbm, hbm],
         scratch_shapes=restore_scratch
         + [pltpu.VMEM((tiles, dims.back_rows, SPAN, chans), BF16), dma((tiles,))],
@@ -637,7 +626,7 @@
     restorations = pl.pallas_call(
         functools.partial(extra_kernel, dims),
         out_shape=restored_shape,
-        in_specs=[smem] + [hbm] * 4 + [vmem] * 3 + [hbm],
+        in_specs=[smem] + [hbm] * 8,
         out_specs=hbm,
         scratch_shapes=restore_scratch,
         input_output_aliases={8: 0},
@@ -647,42 +636,31 @@
     )(table, got_extra, *weights, *biases, partial)
 
     above, below, restorations = lax.optimization_barrier((above, below, restorations))
-    decoded = pl.pallas_call(
-        functools.partial(decode_kernel, dims),
-        out_shape=shaped(local_rows, cols, chans),
-        in_specs=[hbm] * 4 + [vmem],
-        out_specs=vmem,
+    assert bands % 2 == 0
+    finished = pl.pallas_call(
+        functools.partial(finish_kernel, dims),
+        out_shape=shaped(*features.shape),
+        in_specs=[smem] + [hbm] * 6,
+        out_specs=hbm,
         scratch_shapes=[
+            pltpu.VMEM((tiles, dims.back_rows, SPAN, chans), BF16),
             pltpu.VMEM((bands, 2, cols, chans), BF16),
             pltpu.VMEM((bands, cols, chans), BF16),
             pltpu.VMEM((bands, cols, chans), BF16),
             pltpu.VMEM((3, 4, chans, 2 * chans), BF16),
-            pltpu.VMEM((4, cols + 16, chans), F32),
-            pltpu.VMEM((4, cols // 2, 4 * chans), BF16),
-            pltpu.VMEM((2, cols, chans), F32),
-            dma((3, bands)),
-            dma((2,)),
+            pltpu.VMEM((1, chans), F32),
+            pltpu.VMEM((2, 4, cols + 16, chans), F32),
+            pltpu.VMEM((2, 4, cols // 2, 4 * chans), BF16),
+            pltpu.VMEM((local_rows, cols, chans), F32),
+            pltpu.VMEM((bands, 2, cols, chans), BF16),
+            dma((4 + bands,)),
+            dma((3,)),
         ],
-        compiler_params=small,
+        compiler_params=full,
         cost_estimate=cost(3e9, 6e6),
-        name="decode",
-    )(features, above, below, weights[0], biases[0])
-
-    finished = pl.pallas_call(
-        functools.partial(paste_kernel, dims),
-        out_shape=shaped(local_rows, cols, chans),
-        in_specs=[smem, vmem, vmem],
-        out_specs=hbm,
-        scratch_shapes=[
-            pltpu.VMEM((cols, chans), F32),
-            pltpu.VMEM((local_rows, cols, chans), BF16),
-            dma((local_rows,)),
-        ],
-        compiler_params=small,
-        cost_estimate=cost(0, 6e6),
-        name="paste",
-    )(table, decoded, got_back)
-    return finished.reshape(features.shape), restorations
+        name="finish",
+    )(table, got_back, features, above, below, weights[0], biases[0])
+    return finished, restorations
 
 
 def solution(mesh):

time: 61.6 us -> 53.8 us (0.87)
  the two profiles are of different devices: /device:TPU:2 before, /device:TPU:0 now
where the time goes in v6:
time: 53.8 us; the launch traced here: 53.4 us
  Pallas kernels  30.7 us (57%)
  starting transfers between devices  20 us (37%)
  waiting for transfers between devices  1.28 us (2%)
  between operations  0.72 us (1%)
  local copies, waits for them, and re-layouts  0.62 us (1%)
    pallas_call x1, Pallas kernels, shards(): pl.pallas_call(functools.partial(main_kernel, dims), out_shape=[shaped(ti...  10.8 us
    pallas_call x1, Pallas kernels, shards(): pl.pallas_call(functools.partial(extra_kernel, dims), out_shape=restored_...  10 us
    ppermute x7, starting transfers between devices, shards(): lax.ppermute(sent_main[s], 'tile', [(i, i ^ s) for i in range(tiles)])  8.84 us
    all_to_all x2, starting transfers between devices, swap(): lax.all_to_all(array, 'tile', split_axis=0, concat_axis=0, tiled=True)  8.54 us
    pallas_call x1, Pallas kernels, shards(): pl.pallas_call(functools.partial(finish_kernel, dims), out_shape=shaped(*...  6.3 us
    pallas_call x1, Pallas kernels, shards(): pl.pallas_call(functools.partial(pack_kernel, dims), out_shape=[shaped(di...  3.54 us
    ppermute x1, starting transfers between devices, shards(): below = lax.ppermute(leading, 'tile', [(j, i) for i, j in up])  1.39 us
    ppermute x1, starting transfers between devices, shards(): above = lax.ppermute(last, 'tile', up)  1.25 us
  transfers between devices with their start and end apart: 11, of which 1 were waited for; matrix products, arithmetic and copies ran while one was open for 0% of the time, Pallas kernels for 39%

profile of v6, /device:TPU:0, one launch (start us, length us, event | category | flops | bytes accessed | tf_op | source)
XLA Modules:
  0.0 53.4 jit_solution(11855566747690940381)
XLA Ops:
  0.6 3.5 %pack.1 = (bf16[400,128]{1,0:T(8,128)(2,1)}, bf16[400,128]{1,0:T(8,128)(2,1)}, bf16[400,128]{1,0:T(8,128)(2,1)}, bf16[400,128]{1,0:T(8,128)(2,1)}, bf16[400,128]...) custom-call(s32[3,8]{1,0:T(4,128)} %boxes_in.1, ...), custom_call_target="tpu_custom_call" | custom-call | bytes 6000000 | tf_op jit(solution)/shard_map/pack/pallas_call | solution.py:568
  4.2 0.5 collective-permute-start
  4.7 2.6 %collective-permute-start.1 = (bf16[400,128]{1,0:T(8,128)(2,1)}, bf16[400,128]{1,0:T(8,128)(2,1)}, u32[]{:S(2)}, u32[]{:S(2)}) collective-permute-start(bf16[400,128]{1,0:T(8,128)(2,1)} %get-tuple-element.22), channel_id=1, source_target_pairs={{0,2},{1,3},{2,0},{3,1},{4,6},{5,7},{6,4},{7,5},{8,10},{9,11},{10,... | collective-permute-start | bytes 307208 | tf_op jit(solution)/shard_map/ppermute | solution.py:588
  7.3 0.1 collective-permute-start.2
  7.3 1.8 %collective-permute-start.3 = (bf16[400,128]{1,0:T(8,128)(2,1)}, bf16[400,128]{1,0:T(8,128)(2,1)}, u32[]{:S(2)}, u32[]{:S(2)}) collective-permute-start(bf16[400,128]{1,0:T(8,128)(2,1)} %get-tuple-element.24), channel_id=1, source_target_pairs={{0,4},{1,5},{2,6},{3,7},{4,0},{5,1},{6,2},{7,3},{8,12},{9,13},{10,... | collective-permute-start | bytes 307208 | tf_op jit(solution)/shard_map/ppermute | solution.py:588
  9.1 0.0 collective-permute-start.4
  9.1 0.0 collective-permute-done.refs_1_
  9.1 2.6 %collective-permute-start.5 = (bf16[400,128]{1,0:T(8,128)(2,1)}, bf16[400,128]{1,0:T(8,128)(2,1)}, u32[]{:S(2)}, u32[]{:S(2)}) collective-permute-start(bf16[400,128]{1,0:T(8,128)(2,1)} %get-tuple-element.26), channel_id=1, source_target_pairs={{0,6},{1,7},{2,4},{3,5},{4,2},{5,3},{6,0},{7,1},{8,14},{9,15},{10,... | collective-permute-start | bytes 307208 | tf_op jit(solution)/shard_map/ppermute | solution.py:588
  11.7 0.0 collective-permute-done.1.refs_2_
  11.7 1.3 %collective-permute-start.6 = (bf16[400,128]{1,0:T(8,128)(2,1)}, bf16[400,128]{1,0:T(8,128)(2,1)}, u32[]{:S(2)}, u32[]{:S(2)}) collective-permute-start(bf16[400,128]{1,0:T(8,128)(2,1)} %get-tuple-element.27), channel_id=1, source_target_pairs={{0,7},{1,6},{2,5},{3,4},{4,3},{5,2},{6,1},{7,0},{8,15},{9,14},{10,... | collective-permute-start | bytes 307208 | tf_op jit(solution)/shard_map/ppermute | solution.py:588
  13.0 4.2 %all-to-all-start.1 = ((bf16[8,400,128]{2,1,0:T(8,128)(2,1)}), bf16[8,400,128]{2,1,0:T(8,128)(2,1)}, u32[]{:S(2)}, u32[]{:S(2)}) async-start(bf16[8,400,128]{2,1,0:T(8,128)(2,1)} %get-tuple-element.31), calls=%async_computation.1 | async-start | bytes 1638400 | tf_op jit(solution)/shard_map/all_to_all | solution.py:555
  17.3 0.0 collective-permute-done.2.refs_3_
  17.3 0.0 copy-start.1
  17.3 0.6 %copy-done.1 = bf16[400,128]{1,0:T(8,128)(2,1)} copy-done((bf16[400,128]{1,0:T(8,128)(2,1)}, bf16[400,128]{1,0:T(8,128)(2,1)S(1)}, u32[]{:S(2)}) %copy-start.1) | copy-done | bytes 102424
  17.9 1.3 %collective-permute-start.7 = (bf16[6,320,128]{2,1,0:T(8,128)(2,1)}, bf16[6,320,128]{2,1,0:T(8,128)(2,1)S(1)}, u32[]{:S(2)}, u32[]{:S(2)}) collective-permute-start(bf16[6,320,128]{2,1,0:T(8,128)(2,1)} %get-tuple-element.29), channel_id=1, source_target_pairs={{0,1},{1,2},{2,3},{3,4},{4,5},{5,6},{6,7},{7,0},{8,9},{9,10},{10,1... | collective-permute-start | bytes 1474568 | tf_op jit(solution)/shard_map/ppermute | solution.py:590
  19.1 0.0 collective-permute-done.3.refs_4_
  19.1 1.4 %collective-permute-start.8 = (bf16[6,320,128]{2,1,0:T(8,128)(2,1)}, bf16[6,320,128]{2,1,0:T(8,128)(2,1)}, u32[]{:S(2)}, u32[]{:S(2)}) collective-permute-start(bf16[6,320,128]{2,1,0:T(8,128)(2,1)} %get-tuple-element.30), channel_id=1, source_target_pairs={{1,0},{2,1},{3,2},{4,3},{5,4},{6,5},{7,6},{0,7},{9,8},{10,9},{11,1... | collective-permute-start | bytes 1474568 | tf_op jit(solution)/shard_map/ppermute | solution.py:591
  20.5 0.0 collective-permute-done.4.refs_5_
  20.5 0.0 collective-permute-done.5.refs_6_
  20.5 0.0 collective-permute-done.6.refs_7_
  20.6 10.8 %restore_main.1 = (bf16[8,6,48,128]{3,2,1,0:T(8,128)(2,1)}, bf16[2,64,64,128]{3,2,1,0:T(8,128)(2,1)}) custom-call(s32[7,8]{1,0:T(8,128)} %get-tuple-element.19.table, bf16[400,128]{1,0:T(8,128)(2,1)} %get-tuple-element.20.refs_0_, bf16[400,128]{1,0:T(8,128)(2,1)} %collective-permute-done.refs_1_, bf16[400,128]{1,0:T(8,128)(2,1)} %collective-permute-done.1.refs_2_, ...), custom_call_target="tpu_custom_call" | custom-call | flops 7000000000 | bytes 8000000 | tf_op jit(solution)/shard_map/restore_main/pallas_call | solution.py:613
  31.4 0.0 all-to-all-done.1.arrived
  31.4 4.3 %all-to-all-start = ((bf16[8,6,48,128]{3,2,1,0:T(8,128)(2,1)}), bf16[8,6,48,128]{3,2,1,0:T(8,128)(2,1)}, u32[]{:S(2)}, u32[]{:S(2)}) async-start(bf16[8,6,48,128]{3,2,1,0:T(8,128)(2,1)} %get-tuple-element.28), calls=%async_computation | async-start | bytes 1179648 | tf_op jit(solution)/shard_map/all_to_all | solution.py:555
  35.7 10.0 %restore_extra.1 = bf16[2,64,64,128]{3,2,1,0:T(8,128)(2,1)} custom-call(s32[7,8]{1,0:T(8,128)} %get-tuple-element.19.table, bf16[8,400,128]{2,1,0:T(8,128)(2,1)} %all-to-all-done.1.arrived, bf16[3,3,128,128]{3,2,1,0:T(8,128)(2,1)} %bitcast.11, bf16[3,3,128,128]{3,2,1,0:T(8,128)(2,1)} %bitcast.7, ...), custom_call_target="tpu_custom_call", output_to_operand_aliasing={{}: (8, {})} | custom-call | flops 6000000000 | bytes 8000000 | tf_op jit(solution)/shard_map/restore_extra/pallas_call | solution.py:626
  45.8 0.0 collective-permute-done.7.above
  45.8 0.0 copy-start
  45.8 0.0 collective-permute-done.8.below
  45.8 1.2 %all-to-all-done.back = bf16[8,6,48,128]{3,2,1,0:T(8,128)(2,1)} async-done(((bf16[8,6,48,128]{3,2,1,0:T(8,128)(2,1)}), bf16[8,6,48,128]{3,2,1,0:T(8,128)(2,1)}, u32[]{:S(2)}, u32[]{:S(2)}) %all-to-all-start) | async-done | bytes 589856 | tf_op jit(solution)/shard_map/all_to_all | solution.py:555
  47.1 0.0 copy-done
  47.1 6.3 %finish.1 = bf16[6,2,320,128]{3,2,1,0:T(8,128)(2,1)} custom-call(s32[7,8]{1,0:T(8,128)} %get-tuple-element.19.table, bf16[8,6,48,128]{3,2,1,0:T(8,128)(2,1)} %all-to-all-done.back, bf16[6,2,320,128]{3,2,1,0:T(8,128)(2,1)} %feat.3, bf16[6,320,128]{2,1,0:T(8,128)(2,1)} %copy-done, bf16[6,320,128]{2,1,0:T(8,128)(2,1)} %collective-permute-done.8.below, ...), custom_call_target="tpu_custom_call" | custom-call | flops 3000000000 | bytes 6000000 | tf_op jit(solution)/shard_map/finish/pallas_call | solution.py:640
Async XLA Ops:
  4.2 4.9 %collective-permute-start = (bf16[400,128]{1,0:T(8,128)(2,1)}, bf16[400,128]{1,0:T(8,128)(2,1)}, u32[]{:S(2)}, u32[]{:S(2)}) collective-permute-start(bf16[400,128]{1,0:T(8,128)(2,1)} %get-tuple-element.21), channel_id=1, source_target_pairs={{0,1},{1,0},{2,3},{3,2},{4,5},{5,4},{6,7},{7,6},{8,9},{9,8},{10,11... | collective-permute-start | bytes 307208 | tf_op jit(solution)/shard_map/ppermute | solution.py:588
  4.7 7.0 %collective-permute-start.1 = (bf16[400,128]{1,0:T(8,128)(2,1)}, bf16[400,128]{1,0:T(8,128)(2,1)}, u32[]{:S(2)}, u32[]{:S(2)}) collective-permute-start(bf16[400,128]{1,0:T(8,128)(2,1)} %get-tuple-element.22), channel_id=1, source_target_pairs={{0,2},{1,3},{2,0},{3,1},{4,6},{5,7},{6,4},{7,5},{8,10},{9,11},{10,... | collective-permute-start | bytes 307208 | tf_op jit(solution)/shard_map/ppermute | solution.py:588
  7.3 10.0 %collective-permute-start.2 = (bf16[400,128]{1,0:T(8,128)(2,1)}, bf16[400,128]{1,0:T(8,128)(2,1)S(1)}, u32[]{:S(2)}, u32[]{:S(2)}) collective-permute-start(bf16[400,128]{1,0:T(8,128)(2,1)} %get-tuple-element.23), channel_id=1, source_target_pairs={{0,3},{1,2},{2,1},{3,0},{4,7},{5,6},{6,5},{7,4},{8,11},{9,10},{10,... | collective-permute-start | bytes 307208 | tf_op jit(solution)/shard_map/ppermute | solution.py:588
  7.3 11.8 %collective-permute-start.3 = (bf16[400,128]{1,0:T(8,128)(2,1)}, bf16[400,128]{1,0:T(8,128)(2,1)}, u32[]{:S(2)}, u32[]{:S(2)}) collective-permute-start(bf16[400,128]{1,0:T(8,128)(2,1)} %get-tuple-element.24), channel_id=1, source_target_pairs={{0,4},{1,5},{2,6},{3,7},{4,0},{5,1},{6,2},{7,3},{8,12},{9,13},{10,... | collective-permute-start | bytes 307208 | tf_op jit(solution)/shard_map/ppermute | solution.py:588
  9.1 11.4 %collective-permute-start.4 = (bf16[400,128]{1,0:T(8,128)(2,1)}, bf16[400,128]{1,0:T(8,128)(2,1)}, u32[]{:S(2)}, u32[]{:S(2)}) collective-permute-start(bf16[400,128]{1,0:T(8,128)(2,1)} %get-tuple-element.25), channel_id=1, source_target_pairs={{0,5},{1,4},{2,7},{3,6},{4,1},{5,0},{6,3},{7,2},{8,13},{9,12},{10,... | collective-permute-start | bytes 307208 | tf_op jit(solution)/shard_map/ppermute | solution.py:588
  9.1 11.4 %collective-permute-start.5 = (bf16[400,128]{1,0:T(8,128)(2,1)}, bf16[400,128]{1,0:T(8,128)(2,1)}, u32[]{:S(2)}, u32[]{:S(2)}) collective-permute-start(bf16[400,128]{1,0:T(8,128)(2,1)} %get-tuple-element.26), channel_id=1, source_target_pairs={{0,6},{1,7},{2,4},{3,5},{4,2},{5,3},{6,0},{7,1},{8,14},{9,15},{10,... | collective-permute-start | bytes 307208 | tf_op jit(solution)/shard_map/ppermute | solution.py:588
  11.7 8.8 %collective-permute-start.6 = (bf16[400,128]{1,0:T(8,128)(2,1)}, bf16[400,128]{1,0:T(8,128)(2,1)}, u32[]{:S(2)}, u32[]{:S(2)}) collective-permute-start(bf16[400,128]{1,0:T(8,128)(2,1)} %get-tuple-element.27), channel_id=1, source_target_pairs={{0,7},{1,6},{2,5},{3,4},{4,3},{5,2},{6,1},{7,0},{8,15},{9,14},{10,... | collective-permute-start | bytes 307208 | tf_op jit(solution)/shard_map/ppermute | solution.py:588
  13.0 18.4 %all-to-all-start.1 = ((bf16[8,400,128]{2,1,0:T(8,128)(2,1)}), bf16[8,400,128]{2,1,0:T(8,128)(2,1)}, u32[]{:S(2)}, u32[]{:S(2)}) async-start(bf16[8,400,128]{2,1,0:T(8,128)(2,1)} %get-tuple-element.31), calls=%async_computation.1 | async-start | bytes 1638400 | tf_op jit(solution)/shard_map/all_to_all | solution.py:555
  17.3 0.6 %copy-start.1 = (bf16[400,128]{1,0:T(8,128)(2,1)}, bf16[400,128]{1,0:T(8,128)(2,1)S(1)}, u32[]{:S(2)}) copy-start(bf16[400,128]{1,0:T(8,128)(2,1)S(1)} %collective-permute-done.2.refs_3_) | copy-start | bytes 307204
  17.9 27.9 %collective-permute-start.7 = (bf16[6,320,128]{2,1,0:T(8,128)(2,1)}, bf16[6,320,128]{2,1,0:T(8,128)(2,1)S(1)}, u32[]{:S(2)}, u32[]{:S(2)}) collective-permute-start(bf16[6,320,128]{2,1,0:T(8,128)(2,1)} %get-tuple-element.29), channel_id=1, source_target_pairs={{0,1},{1,2},{2,3},{3,4},{4,5},{5,6},{6,7},{7,0},{8,9},{9,10},{10,1... | collective-permute-start | bytes 1474568 | tf_op jit(solution)/shard_map/ppermute | solution.py:590
  19.1 26.7 %collective-permute-start.8 = (bf16[6,320,128]{2,1,0:T(8,128)(2,1)}, bf16[6,320,128]{2,1,0:T(8,128)(2,1)}, u32[]{:S(2)}, u32[]{:S(2)}) collective-permute-start(bf16[6,320,128]{2,1,0:T(8,128)(2,1)} %get-tuple-element.30), channel_id=1, source_target_pairs={{1,0},{2,1},{3,2},{4,3},{5,4},{6,5},{7,6},{0,7},{9,8},{10,9},{11,1... | collective-permute-start | bytes 1474568 | tf_op jit(solution)/shard_map/ppermute | solution.py:591
  31.4 15.7 %all-to-all-start = ((bf16[8,6,48,128]{3,2,1,0:T(8,128)(2,1)}), bf16[8,6,48,128]{3,2,1,0:T(8,128)(2,1)}, u32[]{:S(2)}, u32[]{:S(2)}) async-start(bf16[8,6,48,128]{3,2,1,0:T(8,128)(2,1)} %get-tuple-element.28), calls=%async_computation | async-start | bytes 1179648 | tf_op jit(solution)/shard_map/all_to_all | solution.py:555
  45.8 1.3 %copy-start = (bf16[6,320,128]{2,1,0:T(8,128)(2,1)}, bf16[6,320,128]{2,1,0:T(8,128)(2,1)S(1)}, u32[]{:S(2)}) copy-start(bf16[6,320,128]{2,1,0:T(8,128)(2,1)S(1)} %collective-permute-done.7.above) | copy-start | bytes 1474564

commit v7 on v6

--- a/solution.py
+++ b/solution.py
@@ -11,6 +11,7 @@
 UNIT = 12
 NCLS = 3
 CAP = 2
+PIECE = 16
 SPAN = UNIT * (NCLS + 1)
 BF16 = jnp.bfloat16
 F32 = jnp.float32
@@ -258,6 +259,8 @@
             right = jnp.where(at == SPAN - 1, rim[2 * i + 1 : 2 * i + 2], pltpu.roll(wider, SPAN - 1, 0))
             raw[place >> 1, place & 1] = jnp.concatenate([left.astype(BF16), line, right.astype(BF16)], -1)
 
+    taps[1].start()
+    taps[2].start()
     taps[0].wait()
     n = 12
 
@@ -325,8 +328,10 @@
         for k in range(n):
             mixed[k, pl.ds(0, half, stride=2), :] = total[k * half : (k + 1) * half, :chans]
             mixed[k, pl.ds(1, half, stride=2), :] = total[k * half : (k + 1) * half, chans:]
-        delta[pl.ds(first, n)] = mixed[...].astype(BF16)
-        finish(step, pl.ds(first, n))
+            if k % PIECE == PIECE - 1:
+                at = pl.ds(first + k + 1 - PIECE, PIECE)
+                delta[at] = mixed[k + 1 - PIECE : k + 1].astype(BF16)
+                finish(step * (n // PIECE) + k // PIECE)
 
 
 def begin(dims, arrived, weights, biases, scratch):
@@ -342,8 +347,7 @@
         ColumnTaps(weights[1], biases[1], column_store.at[0], held.at[1], tap_sems.at[1]),
         ColumnTaps(weights[2], biases[2], column_store.at[1], held.at[2], tap_sems.at[2]),
     )
-    for tap in taps:
-        tap.start()
+    taps[0].start()
     return arrival, taps
 
 
@@ -360,7 +364,7 @@
     arrival, taps = begin(dims, arrived, (dec_w, one_w, two_w), (dec_b, one_b, two_b), scratch)
     restore(
         dims, row0, length, arrival, lambda s: me ^ s, got, taps,
-        raw, decoded, wide, inner, mixed, delta, lambda step, rows: None,
+        raw, decoded, wide, inner, mixed, delta, lambda piece: None,
     )
 
     @pl.when(place < CAP)
@@ -428,15 +432,16 @@
         scratch = (got, row_store, column_store, held, got_sems, tap_sems)
         arrival, taps = begin(dims, [arrived.at[s] for s in range(dims.tiles)], (dec_w, one_w, two_w), (dec_b, one_b, two_b), scratch)
 
-        def leave(step, rows):
-            return pltpu.make_async_copy(delta.at[rows], restored.at[1, rows], sem.at[step])
+        def leave(piece):
+            rows = pl.ds(piece * PIECE, PIECE)
+            return pltpu.make_async_copy(delta.at[rows], restored.at[1, rows], sem.at[piece])
 
         restore(
             dims, row0, length, arrival, lambda s: s, got, taps,
-            raw, decoded, wide, inner, mixed, delta, lambda step, rows: leave(step, rows).start(),
+            raw, decoded, wide, inner, mixed, delta, lambda piece: leave(piece).start(),
         )
-        for step in range(2):
-            leave(step, pl.ds(step * (S // 2), S // 2)).wait()
+        for piece in range(S // PIECE):
+            leave(piece).wait()
 
     @pl.when(length == 0)
     def _():
@@ -453,7 +458,7 @@
 
 def finish_kernel(
     dims, table, back, feat, above, below, weight, bias, finished,
-    got, held, up, down, store, held_bias, lines, wide, canvas, out, sems, tap_sems,
+    got, held, up, down, store, held_bias, lines, wide, canvas, out, sems, load_sems, tap_sems,
 ):
     me = lax.axis_index("tile")
     bands, chans, cols = dims.bands, dims.chans, dims.cols
@@ -461,17 +466,25 @@
     taps = ColumnTaps(weight, bias, store, held_bias, tap_sems)
     patches = pltpu.make_async_copy(back, got, sems.at[0])
     patches.start()
-    loads = (
-        pltpu.make_async_copy(above, up, sems.at[1]),
-        pltpu.make_async_copy(below, down, sems.at[2]),
-        pltpu.make_async_copy(feat, held, sems.at[3]),
-    )
-    for load in loads:
-        load.start()
+    def from_feat(band):
+        return pltpu.make_async_copy(feat.at[band], held.at[band], load_sems.at[0, band])
+
+    def from_above(band):
+        return pltpu.make_async_copy(above.at[band], up.at[band], load_sems.at[1, band])
+
+    def from_below(band):
+        return pltpu.make_async_copy(below.at[band], down.at[band], load_sems.at[2, band])
+
     taps.start()
+    from_below(0).start()
+    for j in range(bands):
+        from_feat(j).start()
+        from_above(j).start()
+        if j + 1 < bands:
+            from_below(j + 1).start()
 
     def leave(band):
-        return pltpu.make_async_copy(out.at[band], finished.at[band], sems.at[4 + band])
+        return pltpu.make_async_copy(out.at[band], finished.at[band], sems.at[1 + band])
 
     top = (me == 0).astype(I32)
     bottom = (me == dims.tiles - 1).astype(I32)
@@ -496,11 +509,17 @@
             def _():
                 canvas[local, pl.ds(col0, SPAN), :] += got[e, i].astype(F32)
 
-    for load in loads:
-        load.wait()
+    from_below(0).wait()
     taps.wait()
 
     def band(j, lines, wide):
+        from_feat(j).wait()
+        from_above(j).wait()
+
+        @pl.when(j + 1 < bands)
+        def _():
+            from_below(j + 1).wait()
+
         no_top = (top == 1) & (j == 0)
         no_bottom = (bottom == 1) & (j == bands - 1)
         over = up[jnp.maximum(j - top, 0)].astype(F32)
@@ -583,9 +602,9 @@
         cost_estimate=cost(0, 6e6),
         name="pack",
     )(boxes, slots, features)
-    got_main = [sent_main[0]]
-    for s in range(1, tiles):
-        got_main.append(lax.ppermute(sent_main[s], "tile", [(i, i ^ s) for i in range(tiles)]))
+    got_main = [sent_main[0]] + [None] * (tiles - 1)
+    for s in [1] + sorted(range(2, tiles), key=lambda s: (-(s >> 1).bit_count(), -(s >> 1), s)):
+        got_main[s] = lax.ppermute(sent_main[s], "tile", [(i, i ^ s) for i in range(tiles)])
     up = [(i, (i + 1) % tiles) for i in range(tiles)]
     above = lax.ppermute(last, "tile", up)
     below = lax.ppermute(leading, "tile", [(j, i) for i, j in up])
@@ -607,7 +626,7 @@
         pltpu.VMEM((S + 2, S // 2, 4 * chans), BF16),
         pltpu.VMEM((32, S, chans), F32),
         pltpu.VMEM((S, S, chans), BF16),
-        dma((2,)),
+        dma((S // PIECE,)),
     ]
     restored_shape = shaped(CAP, S, S, chans)
     sent_back, partial = pl.pallas_call(
@@ -653,7 +672,8 @@
             pltpu.VMEM((2, 4, cols // 2, 4 * chans), BF16),
             pltpu.VMEM((local_rows, cols, chans), F32),
             pltpu.VMEM((bands, 2, cols, chans), BF16),
-            dma((4 + bands,)),
+            dma((1 + bands,)),
+            dma((3, bands)),
             dma((3,)),
         ],
         compiler_params=full,

time: 53.8 us -> 55.3 us (1.028)
  waiting for transfers between devices: 1.28 us -> 8.42 us
  Pallas kernels: 30.7 us -> 25.2 us
    pallas_call x1, Pallas kernels: 10 us -> 3 us  [shards(): pl.pallas_call(functools.partial(extra_kernel, dims), out_shape=restored_...]
    all_to_all x2, waiting for transfers between devices: 1.25 us -> 6.9 us  [swap(): lax.all_to_all(array, 'tile', split_axis=0, concat_axis=0, tiled=True)]
    pallas_call x1, Pallas kernels: 6.3 us -> 7.85 us  [shards(): pl.pallas_call(functools.partial(finish_kernel, dims), out_shape=shaped(*...]
    ppermute x1, waiting for transfers between devices: 0.01 us -> 1.5 us  [shards(): above = lax.ppermute(last, 'tile', up)]
  transfers between devices with their start and end apart: 11 -> 11, of which waited for: 1 -> 2; matrix products, arithmetic and copies ran while one was open for 0% -> 0% of each run, Pallas kernels for 39% -> 25%
where the time goes in v7:
time: 55.3 us; the launch traced here: 54.9 us
  Pallas kernels  25.2 us (46%)
  starting transfers between devices  20 us (36%)
  waiting for transfers between devices  8.42 us (15%)
  between operations  0.7 us (1%)
  local copies, waits for them, and re-layouts  0.62 us (1%)
    pallas_call x1, Pallas kernels, shards(): pl.pallas_call(functools.partial(main_kernel, dims), out_shape=[shaped(ti...  10.8 us
    ppermute x7, starting transfers between devices, shards(): lax.ppermute(sent_main[s], 'tile', [(i, i ^ s) for i in range(tiles)])  8.84 us
    all_to_all x2, starting transfers between devices, swap(): lax.all_to_all(array, 'tile', split_axis=0, concat_axis=0, tiled=True)  8.52 us
    pallas_call x1, Pallas kernels, shards(): pl.pallas_call(functools.partial(finish_kernel, dims), out_shape=shaped(*...  7.85 us
    all_to_all x2, waiting for transfers between devices, swap(): lax.all_to_all(array, 'tile', split_axis=0, concat_axis=0, tiled=True)  6.9 us
    pallas_call x1, Pallas kernels, shards(): pl.pallas_call(functools.partial(pack_kernel, dims), out_shape=[shaped(di...  3.54 us
    pallas_call x1, Pallas kernels, shards(): pl.pallas_call(functools.partial(extra_kernel, dims), out_shape=restored_...  3 us
    ppermute x1, waiting for transfers between devices, shards(): above = lax.ppermute(last, 'tile', up)  1.5 us
  transfers between devices with their start and end apart: 11, of which 2 were waited for; matrix products, arithmetic and copies ran while one was open for 0% of the time, Pallas kernels for 25%

profile of v7, /device:TPU:0, one launch (start us, length us, event | category | flops | bytes accessed | tf_op | source)
XLA Modules:
  0.0 54.9 jit_solution(2087386577692850473)
XLA Ops:
  0.6 3.5 %pack.1 = (bf16[400,128]{1,0:T(8,128)(2,1)}, bf16[400,128]{1,0:T(8,128)(2,1)}, bf16[400,128]{1,0:T(8,128)(2,1)}, bf16[400,128]{1,0:T(8,128)(2,1)}, bf16[400,128]...) custom-call(s32[3,8]{1,0:T(4,128)} %boxes_in.1, ...), custom_call_target="tpu_custom_call" | custom-call | bytes 6000000 | tf_op jit(solution)/shard_map/pack/pallas_call | solution.py:587
  4.2 0.5 collective-permute-start
  4.7 2.6 %collective-permute-start.1 = (bf16[400,128]{1,0:T(8,128)(2,1)}, bf16[400,128]{1,0:T(8,128)(2,1)}, u32[]{:S(2)}, u32[]{:S(2)}) collective-permute-start(bf16[400,128]{1,0:T(8,128)(2,1)} %get-tuple-element.22), channel_id=1, source_target_pairs={{0,2},{1,3},{2,0},{3,1},{4,6},{5,7},{6,4},{7,5},{8,10},{9,11},{10,... | collective-permute-start | bytes 307208 | tf_op jit(solution)/shard_map/ppermute | solution.py:607
  7.3 0.1 collective-permute-start.2
  7.3 1.8 %collective-permute-start.3 = (bf16[400,128]{1,0:T(8,128)(2,1)}, bf16[400,128]{1,0:T(8,128)(2,1)}, u32[]{:S(2)}, u32[]{:S(2)}) collective-permute-start(bf16[400,128]{1,0:T(8,128)(2,1)} %get-tuple-element.24), channel_id=1, source_target_pairs={{0,4},{1,5},{2,6},{3,7},{4,0},{5,1},{6,2},{7,3},{8,12},{9,13},{10,... | collective-permute-start | bytes 307208 | tf_op jit(solution)/shard_map/ppermute | solution.py:607
  9.1 0.0 collective-permute-start.4
  9.1 0.0 collective-permute-done.refs_1_
  9.1 2.6 %collective-permute-start.5 = (bf16[400,128]{1,0:T(8,128)(2,1)}, bf16[400,128]{1,0:T(8,128)(2,1)}, u32[]{:S(2)}, u32[]{:S(2)}) collective-permute-start(bf16[400,128]{1,0:T(8,128)(2,1)} %get-tuple-element.26), channel_id=1, source_target_pairs={{0,6},{1,7},{2,4},{3,5},{4,2},{5,3},{6,0},{7,1},{8,14},{9,15},{10,... | collective-permute-start | bytes 307208 | tf_op jit(solution)/shard_map/ppermute | solution.py:607
  11.7 0.0 collective-permute-done.1.refs_2_
  11.7 1.3 %collective-permute-start.6 = (bf16[400,128]{1,0:T(8,128)(2,1)}, bf16[400,128]{1,0:T(8,128)(2,1)}, u32[]{:S(2)}, u32[]{:S(2)}) collective-permute-start(bf16[400,128]{1,0:T(8,128)(2,1)} %get-tuple-element.27), channel_id=1, source_target_pairs={{0,7},{1,6},{2,5},{3,4},{4,3},{5,2},{6,1},{7,0},{8,15},{9,14},{10,... | collective-permute-start | bytes 307208 | tf_op jit(solution)/shard_map/ppermute | solution.py:607
  13.0 4.2 %all-to-all-start.1 = ((bf16[8,400,128]{2,1,0:T(8,128)(2,1)}), bf16[8,400,128]{2,1,0:T(8,128)(2,1)}, u32[]{:S(2)}, u32[]{:S(2)}) async-start(bf16[8,400,128]{2,1,0:T(8,128)(2,1)} %get-tuple-element.31), calls=%async_computation.1 | async-start | bytes 1638400 | tf_op jit(solution)/shard_map/all_to_all | solution.py:574
  17.3 0.0 collective-permute-done.2.refs_3_
  17.3 0.0 copy-start.1
  17.3 0.6 %copy-done.1 = bf16[400,128]{1,0:T(8,128)(2,1)} copy-done((bf16[400,128]{1,0:T(8,128)(2,1)}, bf16[400,128]{1,0:T(8,128)(2,1)S(1)}, u32[]{:S(2)}) %copy-start.1) | copy-done | bytes 102424
  17.9 1.3 %collective-permute-start.7 = (bf16[6,320,128]{2,1,0:T(8,128)(2,1)}, bf16[6,320,128]{2,1,0:T(8,128)(2,1)S(1)}, u32[]{:S(2)}, u32[]{:S(2)}) collective-permute-start(bf16[6,320,128]{2,1,0:T(8,128)(2,1)} %get-tuple-element.29), channel_id=1, source_target_pairs={{0,1},{1,2},{2,3},{3,4},{4,5},{5,6},{6,7},{7,0},{8,9},{9,10},{10,1... | collective-permute-start | bytes 1474568 | tf_op jit(solution)/shard_map/ppermute | solution.py:609
  19.1 0.0 collective-permute-done.3.refs_4_
  19.1 1.4 %collective-permute-start.8 = (bf16[6,320,128]{2,1,0:T(8,128)(2,1)}, bf16[6,320,128]{2,1,0:T(8,128)(2,1)}, u32[]{:S(2)}, u32[]{:S(2)}) collective-permute-start(bf16[6,320,128]{2,1,0:T(8,128)(2,1)} %get-tuple-element.30), channel_id=1, source_target_pairs={{1,0},{2,1},{3,2},{4,3},{5,4},{6,5},{7,6},{0,7},{9,8},{10,9},{11,1... | collective-permute-start | bytes 1474568 | tf_op jit(solution)/shard_map/ppermute | solution.py:610
  20.5 0.0 collective-permute-done.4.refs_5_
  20.5 0.0 collective-permute-done.5.refs_6_
  20.5 0.0 collective-permute-done.6.refs_7_
  20.6 10.8 %restore_main.1 = (bf16[8,6,48,128]{3,2,1,0:T(8,128)(2,1)}, bf16[2,64,64,128]{3,2,1,0:T(8,128)(2,1)}) custom-call(s32[7,8]{1,0:T(8,128)} %get-tuple-element.19.table, bf16[400,128]{1,0:T(8,128)(2,1)} %get-tuple-element.20.refs_0_, bf16[400,128]{1,0:T(8,128)(2,1)} %collective-permute-done.refs_1_, bf16[400,128]{1,0:T(8,128)(2,1)} %collective-permute-done.1.refs_2_, ...), custom_call_target="tpu_custom_call" | custom-call | flops 7000000000 | bytes 8000000 | tf_op jit(solution)/shard_map/restore_main/pallas_call | solution.py:632
  31.3 0.0 all-to-all-done.1.arrived
  31.4 4.3 %all-to-all-start = ((bf16[8,6,48,128]{3,2,1,0:T(8,128)(2,1)}), bf16[8,6,48,128]{3,2,1,0:T(8,128)(2,1)}, u32[]{:S(2)}, u32[]{:S(2)}) async-start(bf16[8,6,48,128]{3,2,1,0:T(8,128)(2,1)} %get-tuple-element.28), calls=%async_computation | async-start | bytes 1179648 | tf_op jit(solution)/shard_map/all_to_all | solution.py:574
  35.7 3.0 %restore_extra.1 = bf16[2,64,64,128]{3,2,1,0:T(8,128)(2,1)} custom-call(s32[7,8]{1,0:T(8,128)} %get-tuple-element.19.table, bf16[8,400,128]{2,1,0:T(8,128)(2,1)} %all-to-all-done.1.arrived, bf16[3,3,128,128]{3,2,1,0:T(8,128)(2,1)} %bitcast.11, bf16[3,3,128,128]{3,2,1,0:T(8,128)(2,1)} %bitcast.7, ...), custom_call_target="tpu_custom_call", output_to_operand_aliasing={{}: (8, {})} | custom-call | flops 6000000000 | bytes 8000000 | tf_op jit(solution)/shard_map/restore_extra/pallas_call | solution.py:645
  38.7 1.5 %collective-permute-done.7.above = bf16[6,320,128]{2,1,0:T(8,128)(2,1)S(1)} collective-permute-done((bf16[6,320,128]{2,1,0:T(8,128)(2,1)}, bf16[6,320,128]{2,1,0:T(8,128)(2,1)S(1)}, u32[]{:S(2)}, u32[]{:S(2)}) %collective-permute-start.7) | collective-permute-done | bytes 491552 | tf_op jit(solution)/shard_map/ppermute | solution.py:609
  40.2 0.0 copy-start
  40.2 0.0 collective-permute-done.8.below
  40.2 6.9 %all-to-all-done.back = bf16[8,6,48,128]{3,2,1,0:T(8,128)(2,1)} async-done(((bf16[8,6,48,128]{3,2,1,0:T(8,128)(2,1)}), bf16[8,6,48,128]{3,2,1,0:T(8,128)(2,1)}, u32[]{:S(2)}, u32[]{:S(2)}) %all-to-all-start) | async-done | bytes 589856 | tf_op jit(solution)/shard_map/all_to_all | solution.py:574
  47.1 0.0 copy-done
  47.1 7.9 %finish.1 = bf16[6,2,320,128]{3,2,1,0:T(8,128)(2,1)} custom-call(s32[7,8]{1,0:T(8,128)} %get-tuple-element.19.table, bf16[8,6,48,128]{3,2,1,0:T(8,128)(2,1)} %all-to-all-done.back, bf16[6,2,320,128]{3,2,1,0:T(8,128)(2,1)} %feat.3, bf16[6,320,128]{2,1,0:T(8,128)(2,1)} %copy-done, bf16[6,320,128]{2,1,0:T(8,128)(2,1)} %collective-permute-done.8.below, ...), custom_call_target="tpu_custom_call" | custom-call | flops 3000000000 | bytes 6000000 | tf_op jit(solution)/shard_map/finish/pallas_call | solution.py:659
Async XLA Ops:
  4.2 4.9 %collective-permute-start = (bf16[400,128]{1,0:T(8,128)(2,1)}, bf16[400,128]{1,0:T(8,128)(2,1)}, u32[]{:S(2)}, u32[]{:S(2)}) collective-permute-start(bf16[400,128]{1,0:T(8,128)(2,1)} %get-tuple-element.21), channel_id=1, source_target_pairs={{0,1},{1,0},{2,3},{3,2},{4,5},{5,4},{6,7},{7,6},{8,9},{9,8},{10,11... | collective-permute-start | bytes 307208 | tf_op jit(solution)/shard_map/ppermute | solution.py:607
  4.7 7.0 %collective-permute-start.1 = (bf16[400,128]{1,0:T(8,128)(2,1)}, bf16[400,128]{1,0:T(8,128)(2,1)}, u32[]{:S(2)}, u32[]{:S(2)}) collective-permute-start(bf16[400,128]{1,0:T(8,128)(2,1)} %get-tuple-element.22), channel_id=1, source_target_pairs={{0,2},{1,3},{2,0},{3,1},{4,6},{5,7},{6,4},{7,5},{8,10},{9,11},{10,... | collective-permute-start | bytes 307208 | tf_op jit(solution)/shard_map/ppermute | solution.py:607
  7.3 10.0 %collective-permute-start.2 = (bf16[400,128]{1,0:T(8,128)(2,1)}, bf16[400,128]{1,0:T(8,128)(2,1)S(1)}, u32[]{:S(2)}, u32[]{:S(2)}) collective-permute-start(bf16[400,128]{1,0:T(8,128)(2,1)} %get-tuple-element.23), channel_id=1, source_target_pairs={{0,3},{1,2},{2,1},{3,0},{4,7},{5,6},{6,5},{7,4},{8,11},{9,10},{10,... | collective-permute-start | bytes 307208 | tf_op jit(solution)/shard_map/ppermute | solution.py:607
  7.3 11.8 %collective-permute-start.3 = (bf16[400,128]{1,0:T(8,128)(2,1)}, bf16[400,128]{1,0:T(8,128)(2,1)}, u32[]{:S(2)}, u32[]{:S(2)}) collective-permute-start(bf16[400,128]{1,0:T(8,128)(2,1)} %get-tuple-element.24), channel_id=1, source_target_pairs={{0,4},{1,5},{2,6},{3,7},{4,0},{5,1},{6,2},{7,3},{8,12},{9,13},{10,... | collective-permute-start | bytes 307208 | tf_op jit(solution)/shard_map/ppermute | solution.py:607
  9.1 11.4 %collective-permute-start.4 = (bf16[400,128]{1,0:T(8,128)(2,1)}, bf16[400,128]{1,0:T(8,128)(2,1)}, u32[]{:S(2)}, u32[]{:S(2)}) collective-permute-start(bf16[400,128]{1,0:T(8,128)(2,1)} %get-tuple-element.25), channel_id=1, source_target_pairs={{0,5},{1,4},{2,7},{3,6},{4,1},{5,0},{6,3},{7,2},{8,13},{9,12},{10,... | collective-permute-start | bytes 307208 | tf_op jit(solution)/shard_map/ppermute | solution.py:607
  9.1 11.4 %collective-permute-start.5 = (bf16[400,128]{1,0:T(8,128)(2,1)}, bf16[400,128]{1,0:T(8,128)(2,1)}, u32[]{:S(2)}, u32[]{:S(2)}) collective-permute-start(bf16[400,128]{1,0:T(8,128)(2,1)} %get-tuple-element.26), channel_id=1, source_target_pairs={{0,6},{1,7},{2,4},{3,5},{4,2},{5,3},{6,0},{7,1},{8,14},{9,15},{10,... | collective-permute-start | bytes 307208 | tf_op jit(solution)/shard_map/ppermute | solution.py:607
  11.7 8.8 %collective-permute-start.6 = (bf16[400,128]{1,0:T(8,128)(2,1)}, bf16[400,128]{1,0:T(8,128)(2,1)}, u32[]{:S(2)}, u32[]{:S(2)}) collective-permute-start(bf16[400,128]{1,0:T(8,128)(2,1)} %get-tuple-element.27), channel_id=1, source_target_pairs={{0,7},{1,6},{2,5},{3,4},{4,3},{5,2},{6,1},{7,0},{8,15},{9,14},{10,... | collective-permute-start | bytes 307208 | tf_op jit(solution)/shard_map/ppermute | solution.py:607
  13.0 18.3 %all-to-all-start.1 = ((bf16[8,400,128]{2,1,0:T(8,128)(2,1)}), bf16[8,400,128]{2,1,0:T(8,128)(2,1)}, u32[]{:S(2)}, u32[]{:S(2)}) async-start(bf16[8,400,128]{2,1,0:T(8,128)(2,1)} %get-tuple-element.31), calls=%async_computation.1 | async-start | bytes 1638400 | tf_op jit(solution)/shard_map/all_to_all | solution.py:574
  17.3 0.6 %copy-start.1 = (bf16[400,128]{1,0:T(8,128)(2,1)}, bf16[400,128]{1,0:T(8,128)(2,1)S(1)}, u32[]{:S(2)}) copy-start(bf16[400,128]{1,0:T(8,128)(2,1)S(1)} %collective-permute-done.2.refs_3_) | copy-start | bytes 307204
  17.9 22.3 %collective-permute-start.7 = (bf16[6,320,128]{2,1,0:T(8,128)(2,1)}, bf16[6,320,128]{2,1,0:T(8,128)(2,1)S(1)}, u32[]{:S(2)}, u32[]{:S(2)}) collective-permute-start(bf16[6,320,128]{2,1,0:T(8,128)(2,1)} %get-tuple-element.29), channel_id=1, source_target_pairs={{0,1},{1,2},{2,3},{3,4},{4,5},{5,6},{6,7},{7,0},{8,9},{9,10},{10,1... | collective-permute-start | bytes 1474568 | tf_op jit(solution)/shard_map/ppermute | solution.py:609
  19.1 21.0 %collective-permute-start.8 = (bf16[6,320,128]{2,1,0:T(8,128)(2,1)}, bf16[6,320,128]{2,1,0:T(8,128)(2,1)}, u32[]{:S(2)}, u32[]{:S(2)}) collective-permute-start(bf16[6,320,128]{2,1,0:T(8,128)(2,1)} %get-tuple-element.30), channel_id=1, source_target_pairs={{1,0},{2,1},{3,2},{4,3},{5,4},{6,5},{7,6},{0,7},{9,8},{10,9},{11,1... | collective-permute-start | bytes 1474568 | tf_op jit(solution)/shard_map/ppermute | solution.py:610
  31.4 15.7 %all-to-all-start = ((bf16[8,6,48,128]{3,2,1,0:T(8,128)(2,1)}), bf16[8,6,48,128]{3,2,1,0:T(8,128)(2,1)}, u32[]{:S(2)}, u32[]{:S(2)}) async-start(bf16[8,6,48,128]{3,2,1,0:T(8,128)(2,1)} %get-tuple-element.28), calls=%async_computation | async-start | bytes 1179648 | tf_op jit(solution)/shard_map/all_to_all | solution.py:574
  40.2 6.9 %copy-start = (bf16[6,320,128]{2,1,0:T(8,128)(2,1)}, bf16[6,320,128]{2,1,0:T(8,128)(2,1)S(1)}, u32[]{:S(2)}) copy-start(bf16[6,320,128]{2,1,0:T(8,128)(2,1)S(1)} %collective-permute-done.7.above) | copy-start | bytes 1474564

commit v8 on v7

--- a/solution.py
+++ b/solution.py
@@ -12,6 +12,7 @@
 NCLS = 3
 CAP = 2
 PIECE = 16
+BANDS_AT_ONCE = 3
 SPAN = UNIT * (NCLS + 1)
 BF16 = jnp.bfloat16
 F32 = jnp.float32
@@ -262,11 +263,8 @@
     taps[1].start()
     taps[2].start()
     taps[0].wait()
-    n = 12
-
-    @pl.loop(0, pairs // n)
-    def _(step):
-        first = step * n
+    n = 8
+    for first in range(0, pairs, n):
         total = silu(row_pairs(raw, first, n, taps[0]) + taps[0].bias())
         for k in range(n):
             part = total[k * SPAN : (k + 1) * SPAN]
@@ -283,33 +281,27 @@
     spots = jnp.clip((t.astype(F32) + 0.5) * lengthf / S - 0.5, 0.0, lengthf - 1.0)
     across = jnp.where((t >= 0) & (t < S), jnp.maximum(0.0, 1.0 - jnp.abs(spots - j)), 0.0)
     across = across.reshape(4 * half, SPAN).astype(BF16)
-    group = 16
-
-    @pl.loop(0, S // 2 // group)
-    def _(step):
-        for k in range(group):
-            lines = []
-            for parity in range(2):
-                s = 2 * (step * group + k) + parity
-                spot = jnp.clip((2 * s + 1) * length - S, 0, (length - 1) * 2 * S)
-                low = spot >> 7
-                part = (spot & 127).astype(F32) * (1.0 / (2 * S))
-                high = jnp.minimum(low + 1, SPAN - 1)
-                lines.append(((1.0 - part) * decoded[low] + part * decoded[high]).astype(BF16))
-            cells = jnp.dot(across, jnp.concatenate(lines, -1), preferred_element_type=F32).astype(BF16)
-            for parity in range(2):
-                at = 2 * (step * group + k) + parity + 1
-                for b in range(4):
-                    wide[at, :, b * chans : (b + 1) * chans] = cells[
-                        b * half : (b + 1) * half, parity * chans : (parity + 1) * chans
-                    ]
-
-    n = 32
     taps[1].wait()
-
-    @pl.loop(0, S // n)
-    def _(step):
-        first = step * n
+    taps[2].wait()
+    for m in range(S // 2):
+        lines = []
+        for parity in range(2):
+            s = 2 * m + parity
+            spot = jnp.clip((2 * s + 1) * length - S, 0, (length - 1) * 2 * S)
+            low = spot >> 7
+            part = (spot & 127).astype(F32) * (1.0 / (2 * S))
+            high = jnp.minimum(low + 1, SPAN - 1)
+            lines.append(((1.0 - part) * decoded[low] + part * decoded[high]).astype(BF16))
+        cells = jnp.dot(across, jnp.concatenate(lines, -1), preferred_element_type=F32).astype(BF16)
+        for parity in range(2):
+            at = 2 * m + parity + 1
+            for b in range(4):
+                wide[at, :, b * chans : (b + 1) * chans] = cells[
+                    b * half : (b + 1) * half, parity * chans : (parity + 1) * chans
+                ]
+
+    n = PIECE
+    for first in range(0, S, n):
         total = silu(column_pairs(wide, first, n, taps[1]) + taps[1].bias())
         at = lax.broadcasted_iota(I32, (n, half, chans), 1)
         even = pltpu.roll(total[:, :chans], n * half - 1, 0).reshape(n, half, chans)
@@ -319,19 +311,13 @@
         inner[rows, :, chans : 3 * chans] = total.astype(BF16).reshape(n, half, 2 * chans)
         inner[rows, :, 3 * chans :] = jnp.where(at == half - 1, 0.0, even).astype(BF16)
 
-    taps[2].wait()
-
-    @pl.loop(0, S // n)
-    def _(step):
-        first = step * n
+    for first in range(0, S, n):
         total = column_pairs(inner, first, n, taps[2]) + taps[2].bias()
         for k in range(n):
-            mixed[k, pl.ds(0, half, stride=2), :] = total[k * half : (k + 1) * half, :chans]
-            mixed[k, pl.ds(1, half, stride=2), :] = total[k * half : (k + 1) * half, chans:]
-            if k % PIECE == PIECE - 1:
-                at = pl.ds(first + k + 1 - PIECE, PIECE)
-                delta[at] = mixed[k + 1 - PIECE : k + 1].astype(BF16)
-                finish(step * (n // PIECE) + k // PIECE)
+            mixed[first + k, pl.ds(0, half, stride=2), :] = total[k * half : (k + 1) * half, :chans]
+            mixed[first + k, pl.ds(1, half, stride=2), :] = total[k * half : (k + 1) * half, chans:]
+        delta[first : first + n] = mixed[first : first + n].astype(BF16)
+        finish(first // PIECE)
 
 
 def begin(dims, arrived, weights, biases, scratch):
@@ -513,13 +499,6 @@
     taps.wait()
 
     def band(j, lines, wide):
-        from_feat(j).wait()
-        from_above(j).wait()
-
-        @pl.when(j + 1 < bands)
-        def _():
-            from_below(j + 1).wait()
-
         no_top = (top == 1) & (j == 0)
         no_bottom = (bottom == 1) & (j == bands - 1)
         over = up[jnp.maximum(j - top, 0)].astype(F32)
@@ -541,12 +520,24 @@
                 at = pl.ds(b, half, stride=2)
                 canvas[2 * j + i, at, :] = canvas[2 * j + i, at, :] + decoded
             out[j, i] = canvas[2 * j + i].astype(BF16)
-        leave(j).start()
-
-    @pl.loop(0, bands // 2)
+
+    @pl.loop(0, bands // BANDS_AT_ONCE)
     def _(step):
-        for k in range(2):
-            band(2 * step + k, lines.at[k], wide.at[k])
+        first = BANDS_AT_ONCE * step
+        for k in range(BANDS_AT_ONCE):
+            from_feat(first + k).wait()
+            from_above(first + k).wait()
+            if k + 1 < BANDS_AT_ONCE:
+                from_below(first + k + 1).wait()
+
+        @pl.when(first + BANDS_AT_ONCE < bands)
+        def _():
+            from_below(first + BANDS_AT_ONCE).wait()
+
+        for k in range(BANDS_AT_ONCE):
+            band(first + k, lines.at[k], wide.at[k])
+        for k in range(BANDS_AT_ONCE):
+            leave(first + k).start()
 
     for j in range(bands):
         leave(j).wait()
@@ -624,7 +615,7 @@
         pltpu.VMEM((SPAN, SPAN, chans), F32),
         pltpu.VMEM((S + 2, S // 2, 4 * chans), BF16),
         pltpu.VMEM((S + 2, S // 2, 4 * chans), BF16),
-        pltpu.VMEM((32, S, chans), F32),
+        pltpu.VMEM((S, S, chans), F32),
         pltpu.VMEM((S, S, chans), BF16),
         dma((S // PIECE,)),
     ]
@@ -655,7 +646,7 @@
     )(table, got_extra, *weights, *biases, partial)
 
     above, below, restorations = lax.optimization_barrier((above, below, restorations))
-    assert bands % 2 == 0
+    assert bands % BANDS_AT_ONCE == 0
     finished = pl.pallas_call(
         functools.partial(finish_kernel, dims),
         out_shape=shaped(*features.shape),
@@ -668,8 +659,8 @@
             pltpu.VMEM((bands, cols, chans), BF16),
             pltpu.VMEM((3, 4, chans, 2 * chans), BF16),
             pltpu.VMEM((1, chans), F32),
-            pltpu.VMEM((2, 4, cols + 16, chans), F32),
-            pltpu.VMEM((2, 4, cols // 2, 4 * chans), BF16),
+            pltpu.VMEM((BANDS_AT_ONCE, 4, cols + 16, chans), F32),
+            pltpu.VMEM((BANDS_AT_ONCE, 4, cols // 2, 4 * chans), BF16),
             pltpu.VMEM((local_rows, cols, chans), F32),
             pltpu.VMEM((bands, 2, cols, chans), BF16),
             dma((1 + bands,)),

time: 55.3 us -> 53.7 us (0.971)
  waiting for transfers between devices: 8.42 us -> 2.91 us
  Pallas kernels: 25.2 us -> 29 us
    pallas_call x1, Pallas kernels: 3 us -> 9.22 us  [shards(): pl.pallas_call(functools.partial(extra_kernel, dims), out_shape=restored_...]
    all_to_all x2, waiting for transfers between devices: 6.9 us -> 2.88 us  [swap(): lax.all_to_all(array, 'tile', split_axis=0, concat_axis=0, tiled=True)]
    pallas_call x1, Pallas kernels: 7.85 us -> 6.19 us  [shards(): pl.pallas_call(functools.partial(finish_kernel, dims), out_shape=shaped(*...]
    ppermute x1, waiting for transfers between devices: 1.5 us -> 0.01 us  [shards(): above = lax.ppermute(last, 'tile', up)]
    pallas_call x1, Pallas kernels: 10.8 us -> 10.1 us  [shards(): pl.pallas_call(functools.partial(main_kernel, dims), out_shape=[shaped(ti...]
  transfers between devices with their start and end apart: 11 -> 11, of which waited for: 2 -> 1; matrix products, arithmetic and copies ran while one was open for 0% -> 0% of each run, Pallas kernels for 25% -> 36%
where the time goes in v8:
time: 53.7 us; the launch traced here: 53.3 us
  Pallas kernels  29 us (54%)
  starting transfers between devices  20 us (37%)
  waiting for transfers between devices  2.91 us (5%)
  between operations  0.71 us (1%)
  local copies, waits for them, and re-layouts  0.62 us (1%)
    pallas_call x1, Pallas kernels, shards(): pl.pallas_call(functools.partial(main_kernel, dims), out_shape=[shaped(ti...  10.1 us
    pallas_call x1, Pallas kernels, shards(): pl.pallas_call(functools.partial(extra_kernel, dims), out_shape=restored_...  9.22 us
    ppermute x7, starting transfers between devices, shards(): lax.ppermute(sent_main[s], 'tile', [(i, i ^ s) for i in range(tiles)])  8.84 us
    all_to_all x2, starting transfers between devices, swap(): lax.all_to_all(array, 'tile', split_axis=0, concat_axis=0, tiled=True)  8.5 us
    pallas_call x1, Pallas kernels, shards(): pl.pallas_call(functools.partial(finish_kernel, dims), out_shape=shaped(*...  6.19 us
    pallas_call x1, Pallas kernels, shards(): pl.pallas_call(functools.partial(pack_kernel, dims), out_shape=[shaped(di...  3.54 us
    all_to_all x2, waiting for transfers between devices, swap(): lax.all_to_all(array, 'tile', split_axis=0, concat_axis=0, tiled=True)  2.88 us
    ppermute x1, starting transfers between devices, shards(): below = lax.ppermute(leading, 'tile', [(j, i) for i, j in up])  1.39 us
  transfers between devices with their start and end apart: 11, of which 1 were waited for; matrix products, arithmetic and copies ran while one was open for 0% of the time, Pallas kernels for 36%

profile of v8, /device:TPU:0, one launch (start us, length us, event | category | flops | bytes accessed | tf_op | source)
XLA Modules:
  0.0 53.3 jit_solution(9403154927591387651)
XLA Ops:
  0.6 3.5 %pack.1 = (bf16[400,128]{1,0:T(8,128)(2,1)}, bf16[400,128]{1,0:T(8,128)(2,1)}, bf16[400,128]{1,0:T(8,128)(2,1)}, bf16[400,128]{1,0:T(8,128)(2,1)}, bf16[400,128]...) custom-call(s32[3,8]{1,0:T(4,128)} %boxes_in.1, ...), custom_call_target="tpu_custom_call" | custom-call | bytes 6000000 | tf_op jit(solution)/shard_map/pack/pallas_call | solution.py:578
  4.2 0.5 collective-permute-start
  4.7 2.6 %collective-permute-start.1 = (bf16[400,128]{1,0:T(8,128)(2,1)}, bf16[400,128]{1,0:T(8,128)(2,1)}, u32[]{:S(2)}, u32[]{:S(2)}) collective-permute-start(bf16[400,128]{1,0:T(8,128)(2,1)} %get-tuple-element.22), channel_id=1, source_target_pairs={{0,2},{1,3},{2,0},{3,1},{4,6},{5,7},{6,4},{7,5},{8,10},{9,11},{10,... | collective-permute-start | bytes 307208 | tf_op jit(solution)/shard_map/ppermute | solution.py:598
  7.3 0.1 collective-permute-start.2
  7.3 1.8 %collective-permute-start.3 = (bf16[400,128]{1,0:T(8,128)(2,1)}, bf16[400,128]{1,0:T(8,128)(2,1)}, u32[]{:S(2)}, u32[]{:S(2)}) collective-permute-start(bf16[400,128]{1,0:T(8,128)(2,1)} %get-tuple-element.24), channel_id=1, source_target_pairs={{0,4},{1,5},{2,6},{3,7},{4,0},{5,1},{6,2},{7,3},{8,12},{9,13},{10,... | collective-permute-start | bytes 307208 | tf_op jit(solution)/shard_map/ppermute | solution.py:598
  9.1 0.0 collective-permute-start.4
  9.1 0.0 collective-permute-done.refs_1_
  9.1 2.6 %collective-permute-start.5 = (bf16[400,128]{1,0:T(8,128)(2,1)}, bf16[400,128]{1,0:T(8,128)(2,1)}, u32[]{:S(2)}, u32[]{:S(2)}) collective-permute-start(bf16[400,128]{1,0:T(8,128)(2,1)} %get-tuple-element.26), channel_id=1, source_target_pairs={{0,6},{1,7},{2,4},{3,5},{4,2},{5,3},{6,0},{7,1},{8,14},{9,15},{10,... | collective-permute-start | bytes 307208 | tf_op jit(solution)/shard_map/ppermute | solution.py:598
  11.7 0.0 collective-permute-done.1.refs_2_
  11.7 1.3 %collective-permute-start.6 = (bf16[400,128]{1,0:T(8,128)(2,1)}, bf16[400,128]{1,0:T(8,128)(2,1)}, u32[]{:S(2)}, u32[]{:S(2)}) collective-permute-start(bf16[400,128]{1,0:T(8,128)(2,1)} %get-tuple-element.27), channel_id=1, source_target_pairs={{0,7},{1,6},{2,5},{3,4},{4,3},{5,2},{6,1},{7,0},{8,15},{9,14},{10,... | collective-permute-start | bytes 307208 | tf_op jit(solution)/shard_map/ppermute | solution.py:598
  13.0 4.2 %all-to-all-start.1 = ((bf16[8,400,128]{2,1,0:T(8,128)(2,1)}), bf16[8,400,128]{2,1,0:T(8,128)(2,1)}, u32[]{:S(2)}, u32[]{:S(2)}) async-start(bf16[8,400,128]{2,1,0:T(8,128)(2,1)} %get-tuple-element.31), calls=%async_computation.1 | async-start | bytes 1638400 | tf_op jit(solution)/shard_map/all_to_all | solution.py:565
  17.3 0.0 collective-permute-done.2.refs_3_
  17.3 0.0 copy-start.1
  17.3 0.6 %copy-done.1 = bf16[400,128]{1,0:T(8,128)(2,1)} copy-done((bf16[400,128]{1,0:T(8,128)(2,1)}, bf16[400,128]{1,0:T(8,128)(2,1)S(1)}, u32[]{:S(2)}) %copy-start.1) | copy-done | bytes 102424
  17.9 1.3 %collective-permute-start.7 = (bf16[6,320,128]{2,1,0:T(8,128)(2,1)}, bf16[6,320,128]{2,1,0:T(8,128)(2,1)S(1)}, u32[]{:S(2)}, u32[]{:S(2)}) collective-permute-start(bf16[6,320,128]{2,1,0:T(8,128)(2,1)} %get-tuple-element.29), channel_id=1, source_target_pairs={{0,1},{1,2},{2,3},{3,4},{4,5},{5,6},{6,7},{7,0},{8,9},{9,10},{10,1... | collective-permute-start | bytes 1474568 | tf_op jit(solution)/shard_map/ppermute | solution.py:600
  19.1 0.0 collective-permute-done.3.refs_4_
  19.1 1.4 %collective-permute-start.8 = (bf16[6,320,128]{2,1,0:T(8,128)(2,1)}, bf16[6,320,128]{2,1,0:T(8,128)(2,1)}, u32[]{:S(2)}, u32[]{:S(2)}) collective-permute-start(bf16[6,320,128]{2,1,0:T(8,128)(2,1)} %get-tuple-element.30), channel_id=1, source_target_pairs={{1,0},{2,1},{3,2},{4,3},{5,4},{6,5},{7,6},{0,7},{9,8},{10,9},{11,1... | collective-permute-start | bytes 1474568 | tf_op jit(solution)/shard_map/ppermute | solution.py:601
  20.5 0.0 collective-permute-done.4.refs_5_
  20.5 0.0 collective-permute-done.5.refs_6_
  20.5 0.0 collective-permute-done.6.refs_7_
  20.6 10.1 %restore_main.1 = (bf16[8,6,48,128]{3,2,1,0:T(8,128)(2,1)}, bf16[2,64,64,128]{3,2,1,0:T(8,128)(2,1)}) custom-call(s32[7,8]{1,0:T(8,128)} %get-tuple-element.19.table, bf16[400,128]{1,0:T(8,128)(2,1)} %get-tuple-element.20.refs_0_, bf16[400,128]{1,0:T(8,128)(2,1)} %collective-permute-done.refs_1_, bf16[400,128]{1,0:T(8,128)(2,1)} %collective-permute-done.1.refs_2_, ...), custom_call_target="tpu_custom_call" | custom-call | flops 7000000000 | bytes 8000000 | tf_op jit(solution)/shard_map/restore_main/pallas_call | solution.py:623
  30.6 0.0 all-to-all-done.1.arrived
  30.7 4.3 %all-to-all-start = ((bf16[8,6,48,128]{3,2,1,0:T(8,128)(2,1)}), bf16[8,6,48,128]{3,2,1,0:T(8,128)(2,1)}, u32[]{:S(2)}, u32[]{:S(2)}) async-start(bf16[8,6,48,128]{3,2,1,0:T(8,128)(2,1)} %get-tuple-element.28), calls=%async_computation | async-start | bytes 1179648 | tf_op jit(solution)/shard_map/all_to_all | solution.py:565
  35.0 9.2 %restore_extra.1 = bf16[2,64,64,128]{3,2,1,0:T(8,128)(2,1)} custom-call(s32[7,8]{1,0:T(8,128)} %get-tuple-element.19.table, bf16[8,400,128]{2,1,0:T(8,128)(2,1)} %all-to-all-done.1.arrived, bf16[3,3,128,128]{3,2,1,0:T(8,128)(2,1)} %bitcast.11, bf16[3,3,128,128]{3,2,1,0:T(8,128)(2,1)} %bitcast.7, ...), custom_call_target="tpu_custom_call", output_to_operand_aliasing={{}: (8, {})} | custom-call | flops 6000000000 | bytes 8000000 | tf_op jit(solution)/shard_map/restore_extra/pallas_call | solution.py:636
  44.2 0.0 collective-permute-done.7.above
  44.2 0.0 copy-start
  44.2 0.0 collective-permute-done.8.below
  44.2 2.8 %all-to-all-done.back = bf16[8,6,48,128]{3,2,1,0:T(8,128)(2,1)} async-done(((bf16[8,6,48,128]{3,2,1,0:T(8,128)(2,1)}), bf16[8,6,48,128]{3,2,1,0:T(8,128)(2,1)}, u32[]{:S(2)}, u32[]{:S(2)}) %all-to-all-start) | async-done | bytes 589856 | tf_op jit(solution)/shard_map/all_to_all | solution.py:565
  47.1 0.0 copy-done
  47.1 6.2 %finish.1 = bf16[6,2,320,128]{3,2,1,0:T(8,128)(2,1)} custom-call(s32[7,8]{1,0:T(8,128)} %get-tuple-element.19.table, bf16[8,6,48,128]{3,2,1,0:T(8,128)(2,1)} %all-to-all-done.back, bf16[6,2,320,128]{3,2,1,0:T(8,128)(2,1)} %feat.3, bf16[6,320,128]{2,1,0:T(8,128)(2,1)} %copy-done, bf16[6,320,128]{2,1,0:T(8,128)(2,1)} %collective-permute-done.8.below, ...), custom_call_target="tpu_custom_call" | custom-call | flops 3000000000 | bytes 6000000 | tf_op jit(solution)/shard_map/finish/pallas_call | solution.py:650
Async XLA Ops:
  4.2 4.9 %collective-permute-start = (bf16[400,128]{1,0:T(8,128)(2,1)}, bf16[400,128]{1,0:T(8,128)(2,1)}, u32[]{:S(2)}, u32[]{:S(2)}) collective-permute-start(bf16[400,128]{1,0:T(8,128)(2,1)} %get-tuple-element.21), channel_id=1, source_target_pairs={{0,1},{1,0},{2,3},{3,2},{4,5},{5,4},{6,7},{7,6},{8,9},{9,8},{10,11... | collective-permute-start | bytes 307208 | tf_op jit(solution)/shard_map/ppermute | solution.py:598
  4.7 7.0 %collective-permute-start.1 = (bf16[400,128]{1,0:T(8,128)(2,1)}, bf16[400,128]{1,0:T(8,128)(2,1)}, u32[]{:S(2)}, u32[]{:S(2)}) collective-permute-start(bf16[400,128]{1,0:T(8,128)(2,1)} %get-tuple-element.22), channel_id=1, source_target_pairs={{0,2},{1,3},{2,0},{3,1},{4,6},{5,7},{6,4},{7,5},{8,10},{9,11},{10,... | collective-permute-start | bytes 307208 | tf_op jit(solution)/shard_map/ppermute | solution.py:598
  7.3 10.0 %collective-permute-start.2 = (bf16[400,128]{1,0:T(8,128)(2,1)}, bf16[400,128]{1,0:T(8,128)(2,1)S(1)}, u32[]{:S(2)}, u32[]{:S(2)}) collective-permute-start(bf16[400,128]{1,0:T(8,128)(2,1)} %get-tuple-element.23), channel_id=1, source_target_pairs={{0,3},{1,2},{2,1},{3,0},{4,7},{5,6},{6,5},{7,4},{8,11},{9,10},{10,... | collective-permute-start | bytes 307208 | tf_op jit(solution)/shard_map/ppermute | solution.py:598
  7.3 11.8 %collective-permute-start.3 = (bf16[400,128]{1,0:T(8,128)(2,1)}, bf16[400,128]{1,0:T(8,128)(2,1)}, u32[]{:S(2)}, u32[]{:S(2)}) collective-permute-start(bf16[400,128]{1,0:T(8,128)(2,1)} %get-tuple-element.24), channel_id=1, source_target_pairs={{0,4},{1,5},{2,6},{3,7},{4,0},{5,1},{6,2},{7,3},{8,12},{9,13},{10,... | collective-permute-start | bytes 307208 | tf_op jit(solution)/shard_map/ppermute | solution.py:598
  9.1 11.4 %collective-permute-start.4 = (bf16[400,128]{1,0:T(8,128)(2,1)}, bf16[400,128]{1,0:T(8,128)(2,1)}, u32[]{:S(2)}, u32[]{:S(2)}) collective-permute-start(bf16[400,128]{1,0:T(8,128)(2,1)} %get-tuple-element.25), channel_id=1, source_target_pairs={{0,5},{1,4},{2,7},{3,6},{4,1},{5,0},{6,3},{7,2},{8,13},{9,12},{10,... | collective-permute-start | bytes 307208 | tf_op jit(solution)/shard_map/ppermute | solution.py:598
  9.1 11.4 %collective-permute-start.5 = (bf16[400,128]{1,0:T(8,128)(2,1)}, bf16[400,128]{1,0:T(8,128)(2,1)}, u32[]{:S(2)}, u32[]{:S(2)}) collective-permute-start(bf16[400,128]{1,0:T(8,128)(2,1)} %get-tuple-element.26), channel_id=1, source_target_pairs={{0,6},{1,7},{2,4},{3,5},{4,2},{5,3},{6,0},{7,1},{8,14},{9,15},{10,... | collective-permute-start | bytes 307208 | tf_op jit(solution)/shard_map/ppermute | solution.py:598
  11.7 8.8 %collective-permute-start.6 = (bf16[400,128]{1,0:T(8,128)(2,1)}, bf16[400,128]{1,0:T(8,128)(2,1)}, u32[]{:S(2)}, u32[]{:S(2)}) collective-permute-start(bf16[400,128]{1,0:T(8,128)(2,1)} %get-tuple-element.27), channel_id=1, source_target_pairs={{0,7},{1,6},{2,5},{3,4},{4,3},{5,2},{6,1},{7,0},{8,15},{9,14},{10,... | collective-permute-start | bytes 307208 | tf_op jit(solution)/shard_map/ppermute | solution.py:598
  13.0 17.7 %all-to-all-start.1 = ((bf16[8,400,128]{2,1,0:T(8,128)(2,1)}), bf16[8,400,128]{2,1,0:T(8,128)(2,1)}, u32[]{:S(2)}, u32[]{:S(2)}) async-start(bf16[8,400,128]{2,1,0:T(8,128)(2,1)} %get-tuple-element.31), calls=%async_computation.1 | async-start | bytes 1638400 | tf_op jit(solution)/shard_map/all_to_all | solution.py:565
  17.3 0.6 %copy-start.1 = (bf16[400,128]{1,0:T(8,128)(2,1)}, bf16[400,128]{1,0:T(8,128)(2,1)S(1)}, u32[]{:S(2)}) copy-start(bf16[400,128]{1,0:T(8,128)(2,1)S(1)} %collective-permute-done.2.refs_3_) | copy-start | bytes 307204
  17.9 26.3 %collective-permute-start.7 = (bf16[6,320,128]{2,1,0:T(8,128)(2,1)}, bf16[6,320,128]{2,1,0:T(8,128)(2,1)S(1)}, u32[]{:S(2)}, u32[]{:S(2)}) collective-permute-start(bf16[6,320,128]{2,1,0:T(8,128)(2,1)} %get-tuple-element.29), channel_id=1, source_target_pairs={{0,1},{1,2},{2,3},{3,4},{4,5},{5,6},{6,7},{7,0},{8,9},{9,10},{10,1... | collective-permute-start | bytes 1474568 | tf_op jit(solution)/shard_map/ppermute | solution.py:600
  19.1 25.1 %collective-permute-start.8 = (bf16[6,320,128]{2,1,0:T(8,128)(2,1)}, bf16[6,320,128]{2,1,0:T(8,128)(2,1)}, u32[]{:S(2)}, u32[]{:S(2)}) collective-permute-start(bf16[6,320,128]{2,1,0:T(8,128)(2,1)} %get-tuple-element.30), channel_id=1, source_target_pairs={{1,0},{2,1},{3,2},{4,3},{5,4},{6,5},{7,6},{0,7},{9,8},{10,9},{11,1... | collective-permute-start | bytes 1474568 | tf_op jit(solution)/shard_map/ppermute | solution.py:601
  30.7 16.4 %all-to-all-start = ((bf16[8,6,48,128]{3,2,1,0:T(8,128)(2,1)}), bf16[8,6,48,128]{3,2,1,0:T(8,128)(2,1)}, u32[]{:S(2)}, u32[]{:S(2)}) async-start(bf16[8,6,48,128]{3,2,1,0:T(8,128)(2,1)} %get-tuple-element.28), calls=%async_computation | async-start | bytes 1179648 | tf_op jit(solution)/shard_map/all_to_all | solution.py:565
  44.2 2.9 %copy-start = (bf16[6,320,128]{2,1,0:T(8,128)(2,1)}, bf16[6,320,128]{2,1,0:T(8,128)(2,1)S(1)}, u32[]{:S(2)}) copy-start(bf16[6,320,128]{2,1,0:T(8,128)(2,1)S(1)} %collective-permute-done.7.above) | copy-start | bytes 1474564

commit v9 on v8

--- a/solution.py
+++ b/solution.py
@@ -148,22 +148,25 @@
     return finish
 
 
-def pack_crops(dims, table, row_at, col_at, canvas, rim, staged, partner):
+def pack_crops(dims, table, row_at, col_at, side_at, canvas, rim, staged, partner):
     me = lax.axis_index("tile")
     rim[...] = jnp.zeros_like(rim)
 
     @pl.loop(0, dims.tiles)
     def _(s):
         w = partner(s)
-        row0 = table[row_at, w]
-        col0 = table[col_at, w]
-        start = first_local(jnp.maximum(row0 - 1, 0), me, dims)
-        for i in range(dims.rows):
-            row = jnp.minimum(start + i, dims.local_rows - 1)
-            staged[s, i * SPAN : (i + 1) * SPAN, :] = canvas[row, pl.ds(col0 + 8, SPAN), :].astype(BF16)
-            rim[2 * i : 2 * i + 1, :] = canvas[row, pl.ds(col0 + 7, 1), :]
-            rim[2 * i + 1 : 2 * i + 2, :] = canvas[row, pl.ds(col0 + 8 + SPAN, 1), :]
-        staged[s, dims.rows * SPAN :, :] = rim[...].astype(BF16)
+
+        @pl.when(table[side_at, w] > 0)
+        def _():
+            row0 = table[row_at, w]
+            col0 = table[col_at, w]
+            start = first_local(jnp.maximum(row0 - 1, 0), me, dims)
+            for i in range(dims.rows):
+                row = jnp.minimum(start + i, dims.local_rows - 1)
+                staged[s, i * SPAN : (i + 1) * SPAN, :] = canvas[row, pl.ds(col0 + 8, SPAN), :].astype(BF16)
+                rim[2 * i : 2 * i + 1, :] = canvas[row, pl.ds(col0 + 7, 1), :]
+                rim[2 * i + 1 : 2 * i + 2, :] = canvas[row, pl.ds(col0 + 8 + SPAN, 1), :]
+            staged[s, dims.rows * SPAN :, :] = rim[...].astype(BF16)
 
 
 def pack_kernel(
@@ -216,11 +219,11 @@
     )
     for edge in edges:
         edge.start()
-    pack_crops(dims, table, ROW, COL, canvas, rim, staged, lambda s: me ^ s)
+    pack_crops(dims, table, ROW, COL, SIDE, canvas, rim, staged, lambda s: me ^ s)
     copies = [pltpu.make_async_copy(staged.at[s], sent[s], sent_sems.at[s]) for s in range(dims.tiles)]
     for copy in copies:
         copy.start()
-    pack_crops(dims, table, ROW2, COL2, canvas, rim, staged_extra, lambda s: s)
+    pack_crops(dims, table, ROW2, COL2, SIDE2, canvas, rim, staged_extra, lambda s: s)
     later = pltpu.make_async_copy(staged_extra, sent_extra, sems.at[0])
     later.start()
     for copy in copies:
@@ -243,22 +246,28 @@
         store[0] = empty
         store[S + 1] = empty
 
-    @pl.loop(0, dims.tiles)
-    def _(s):
-        arrival(s).wait()
+    column = lax.broadcasted_iota(I32, (SPAN, chans), 0)
+
+    def lay(s):
         e = source(s)
         start = first_local(jnp.maximum(above, 0), e, dims)
         rim = got[s, dims.rows * SPAN :, :].astype(F32)
-        at = lax.broadcasted_iota(I32, (SPAN, chans), 0)
         for i in range(dims.rows):
             local = start + i
             place = global_row(local, e, dims) - above
             place = jnp.where((local < dims.local_rows) & (place < SPAN + 2), place, SPAN + 2)
             line = got[s, i * SPAN : (i + 1) * SPAN, :]
             wider = line.astype(F32)
-            left = jnp.where(at == 0, rim[2 * i : 2 * i + 1], pltpu.roll(wider, 1, 0))
-            right = jnp.where(at == SPAN - 1, rim[2 * i + 1 : 2 * i + 2], pltpu.roll(wider, SPAN - 1, 0))
+            left = jnp.where(column == 0, rim[2 * i : 2 * i + 1], pltpu.roll(wider, 1, 0))
+            right = jnp.where(column == SPAN - 1, rim[2 * i + 1 : 2 * i + 2], pltpu.roll(wider, SPAN - 1, 0))
             raw[place >> 1, place & 1] = jnp.concatenate([left.astype(BF16), line, right.astype(BF16)], -1)
+
+    @pl.loop(0, dims.tiles // 4)
+    def _(step):
+        for k in range(4):
+            arrival(4 * step + k).wait()
+        for k in range(4):
+            lay(4 * step + k)
 
     taps[1].start()
     taps[2].start()
@@ -365,26 +374,22 @@
     coarse = lift.astype(BF16)
     lift = jnp.concatenate([coarse, (lift - coarse.astype(F32)).astype(BF16)], 0)
     scale = 1.0 / (2.0 * lengthf)
-    group = 12
-
-    @pl.loop(0, SPAN // 2 // group)
-    def _(step):
-        for k in range(group):
-            lines = []
-            for parity in range(2):
-                h = 2 * (step * group + k) + parity
-                spot = jnp.clip((2 * h + 1) * S - length, 0, (S - 1) * 2 * length)
-                low = ((spot.astype(F32) + 0.5) * scale).astype(I32)
-                part = (spot - low * 2 * length).astype(F32) * scale
-                high = jnp.minimum(low + 1, S - 1)
-                lines.append(((1.0 - part) * delta[low].astype(F32) + part * delta[high].astype(F32)).astype(BF16))
-            patch = jnp.dot(lift, jnp.concatenate(lines, -1), preferred_element_type=F32)
-            patch = (patch[:SPAN] + patch[SPAN:]).astype(BF16)
-            for parity in range(2):
-                row = row0 + 2 * (step * group + k) + parity
-                dest = (row & (dims.stride - 1)) >> 1
-                local = ((row >> dims.shift) << 1) + (row & 1)
-                back[dest, local - first_local(row0, dest, dims)] = patch[:, parity * chans : (parity + 1) * chans]
+    for m in range(SPAN // 2):
+        lines = []
+        for parity in range(2):
+            h = 2 * m + parity
+            spot = jnp.clip((2 * h + 1) * S - length, 0, (S - 1) * 2 * length)
+            low = ((spot.astype(F32) + 0.5) * scale).astype(I32)
+            part = (spot - low * 2 * length).astype(F32) * scale
+            high = jnp.minimum(low + 1, S - 1)
+            lines.append(((1.0 - part) * delta[low].astype(F32) + part * delta[high].astype(F32)).astype(BF16))
+        patch = jnp.dot(lift, jnp.concatenate(lines, -1), preferred_element_type=F32)
+        patch = (patch[:SPAN] + patch[SPAN:]).astype(BF16)
+        for parity in range(2):
+            row = row0 + 2 * m + parity
+            dest = (row & (dims.stride - 1)) >> 1
+            local = ((row >> dims.shift) << 1) + (row & 1)
+            back[dest, local - first_local(row0, dest, dims)] = patch[:, parity * chans : (parity + 1) * chans]
 
     def leave(e):
         return pltpu.make_async_copy(back.at[e], sent.at[e], back_sems.at[e])
@@ -627,7 +632,7 @@
         out_specs=[hbm, hbm],
         scratch_shapes=restore_scratch
         + [pltpu.VMEM((tiles, dims.back_rows, SPAN, chans), BF16), dma((tiles,))],
-        compiler_params=full,
+        compiler_params=pltpu.CompilerParams(vmem_limit_bytes=62 * 1024 * 1024),
         cost_estimate=cost(7e9, 8e6),
         name="restore_main",
     )(table, *got_main, *weights, *biases)

time: 53.7 us -> 54 us (level)
  Pallas kernels: 29 us -> 23.2 us
  waiting for transfers between devices: 2.91 us -> 7.57 us
  starting transfers between devices: 20 us -> 21.3 us
    pallas_call x1, Pallas kernels: 9.22 us -> 3.18 us  [shards(): pl.pallas_call(functools.partial(extra_kernel, dims), out_shape=restored_...]
    all_to_all x2, waiting for transfers between devices: 2.88 us -> 7.12 us  [swap(): lax.all_to_all(array, 'tile', split_axis=0, concat_axis=0, tiled=True)]
    all_to_all x2, starting transfers between devices: 8.5 us -> 9.84 us  [swap(): lax.all_to_all(array, 'tile', split_axis=0, concat_axis=0, tiled=True)]
  transfers between devices with their start and end apart: 11 -> 11, of which waited for: 1 -> 2; matrix products, arithmetic and copies ran while one was open for 0% -> 0% of each run, Pallas kernels for 36% -> 25%
where the time goes in v9:
time: 54 us; the launch traced here: 53.6 us
  Pallas kernels  23.2 us (43%)
  starting transfers between devices  21.3 us (39%)
  waiting for transfers between devices  7.57 us (14%)
  between operations  0.92 us (2%)
  local copies, waits for them, and re-layouts  0.65 us (1%)
    pallas_call x1, Pallas kernels, shards(): pl.pallas_call(functools.partial(main_kernel, dims), out_shape=[shaped(ti...  10.2 us
    all_to_all x2, starting transfers between devices, swap(): lax.all_to_all(array, 'tile', split_axis=0, concat_axis=0, tiled=True)  9.84 us
    ppermute x7, starting transfers between devices, shards(): lax.ppermute(sent_main[s], 'tile', [(i, i ^ s) for i in range(tiles)])  8.73 us
    all_to_all x2, waiting for transfers between devices, swap(): lax.all_to_all(array, 'tile', split_axis=0, concat_axis=0, tiled=True)  7.12 us
    pallas_call x1, Pallas kernels, shards(): pl.pallas_call(functools.partial(finish_kernel, dims), out_shape=shaped(*...  6.19 us
    pallas_call x1, Pallas kernels, shards(): pl.pallas_call(functools.partial(pack_kernel, dims), out_shape=[shaped(di...  3.58 us
    pallas_call x1, Pallas kernels, shards(): pl.pallas_call(functools.partial(extra_kernel, dims), out_shape=restored_...  3.18 us
    ppermute x1, starting transfers between devices, shards(): below = lax.ppermute(leading, 'tile', [(j, i) for i, j in up])  1.39 us
  transfers between devices with their start and end apart: 11, of which 2 were waited for; matrix products, arithmetic and copies ran while one was open for 0% of the time, Pallas kernels for 25%

profile of v9, /device:TPU:0, one launch (start us, length us, event | category | flops | bytes accessed | tf_op | source)
XLA Modules:
  0.0 53.6 jit_solution(4787718184069415845)
XLA Ops:
  0.6 3.6 %pack.1 = (bf16[400,128]{1,0:T(8,128)(2,1)}, bf16[400,128]{1,0:T(8,128)(2,1)}, bf16[400,128]{1,0:T(8,128)(2,1)}, bf16[400,128]{1,0:T(8,128)(2,1)}, bf16[400,128]...) custom-call(s32[3,8]{1,0:T(4,128)} %boxes_in.1, ...), custom_call_target="tpu_custom_call" | custom-call | bytes 6000000 | tf_op jit(solution)/shard_map/pack/pallas_call | solution.py:583
  4.2 0.5 collective-permute-start
  4.7 2.6 %collective-permute-start.1 = (bf16[400,128]{1,0:T(8,128)(2,1)}, bf16[400,128]{1,0:T(8,128)(2,1)S(1)}, u32[]{:S(2)}, u32[]{:S(2)}) collective-permute-start(bf16[400,128]{1,0:T(8,128)(2,1)} %get-tuple-element.22), channel_id=1, source_target_pairs={{0,2},{1,3},{2,0},{3,1},{4,6},{5,7},{6,4},{7,5},{8,10},{9,11},{10,... | collective-permute-start | bytes 307208 | tf_op jit(solution)/shard_map/ppermute | solution.py:603
  7.3 0.1 collective-permute-start.2
  7.4 1.8 %collective-permute-start.3 = (bf16[400,128]{1,0:T(8,128)(2,1)}, bf16[400,128]{1,0:T(8,128)(2,1)S(1)}, u32[]{:S(2)}, u32[]{:S(2)}) collective-permute-start(bf16[400,128]{1,0:T(8,128)(2,1)} %get-tuple-element.24), channel_id=1, source_target_pairs={{0,4},{1,5},{2,6},{3,7},{4,0},{5,1},{6,2},{7,3},{8,12},{9,13},{10,... | collective-permute-start | bytes 307208 | tf_op jit(solution)/shard_map/ppermute | solution.py:603
  9.1 0.0 collective-permute-start.4
  9.1 0.0 collective-permute-done.refs_1_
  9.2 0.0 copy-start.1
  9.2 2.6 %collective-permute-start.5 = (bf16[400,128]{1,0:T(8,128)(2,1)}, bf16[400,128]{1,0:T(8,128)(2,1)S(1)}, u32[]{:S(2)}, u32[]{:S(2)}) collective-permute-start(bf16[400,128]{1,0:T(8,128)(2,1)} %get-tuple-element.26), channel_id=1, source_target_pairs={{0,6},{1,7},{2,4},{3,5},{4,2},{5,3},{6,0},{7,1},{8,14},{9,15},{10,... | collective-permute-start | bytes 307208 | tf_op jit(solution)/shard_map/ppermute | solution.py:603
  11.8 0.0 collective-permute-done.1.refs_2_
  11.8 0.0 copy-start.2
  11.8 1.2 %collective-permute-start.6 = (bf16[400,128]{1,0:T(8,128)(2,1)}, bf16[400,128]{1,0:T(8,128)(2,1)S(1)}, u32[]{:S(2)}, u32[]{:S(2)}) collective-permute-start(bf16[400,128]{1,0:T(8,128)(2,1)} %get-tuple-element.27), channel_id=1, source_target_pairs={{0,7},{1,6},{2,5},{3,4},{4,3},{5,2},{6,1},{7,0},{8,15},{9,14},{10,... | collective-permute-start | bytes 307208 | tf_op jit(solution)/shard_map/ppermute | solution.py:603
  13.0 4.2 %all-to-all-start.1 = ((bf16[8,400,128]{2,1,0:T(8,128)(2,1)}), bf16[8,400,128]{2,1,0:T(8,128)(2,1)}, u32[]{:S(2)}, u32[]{:S(2)}) async-start(bf16[8,400,128]{2,1,0:T(8,128)(2,1)} %get-tuple-element.31), calls=%async_computation.1 | async-start | bytes 1638400 | tf_op jit(solution)/shard_map/all_to_all | solution.py:570
  17.2 0.0 collective-permute-done.2.refs_3_
  17.2 0.0 copy-start.3
  17.2 1.3 %collective-permute-start.7 = (bf16[6,320,128]{2,1,0:T(8,128)(2,1)}, bf16[6,320,128]{2,1,0:T(8,128)(2,1)S(1)}, u32[]{:S(2)}, u32[]{:S(2)}) collective-permute-start(bf16[6,320,128]{2,1,0:T(8,128)(2,1)} %get-tuple-element.29), channel_id=1, source_target_pairs={{0,1},{1,2},{2,3},{3,4},{4,5},{5,6},{6,7},{7,0},{8,9},{9,10},{10,1... | collective-permute-start | bytes 1474568 | tf_op jit(solution)/shard_map/ppermute | solution.py:605
  18.5 0.0 collective-permute-done.3.refs_4_
  18.5 0.0 copy-start.4
  18.5 1.4 %collective-permute-start.8 = (bf16[6,320,128]{2,1,0:T(8,128)(2,1)}, bf16[6,320,128]{2,1,0:T(8,128)(2,1)}, u32[]{:S(2)}, u32[]{:S(2)}) collective-permute-start(bf16[6,320,128]{2,1,0:T(8,128)(2,1)} %get-tuple-element.30), channel_id=1, source_target_pairs={{1,0},{2,1},{3,2},{4,3},{5,4},{6,5},{7,6},{0,7},{9,8},{10,9},{11,1... | collective-permute-start | bytes 1474568 | tf_op jit(solution)/shard_map/ppermute | solution.py:606
  19.9 0.0 collective-permute-done.4.refs_5_
  19.9 0.0 copy-start.5
  19.9 0.0 collective-permute-done.5.refs_6_
  19.9 0.0 copy-start.6
  19.9 0.0 collective-permute-done.6.refs_7_
  20.0 0.0 copy-start.7
  20.0 0.0 copy-done.1
  20.0 0.0 copy-done.2
  20.0 0.0 copy-done.3
  20.0 0.0 copy-done.4
  20.0 0.6 %copy-done.5 = bf16[400,128]{1,0:T(8,128)(2,1)} copy-done((bf16[400,128]{1,0:T(8,128)(2,1)}, bf16[400,128]{1,0:T(8,128)(2,1)S(1)}, u32[]{:S(2)}) %copy-start.5) | copy-done | bytes 102424
  20.6 0.0 copy-done.6
  20.6 0.0 copy-done.7
  20.6 10.2 %restore_main.1 = (bf16[8,6,48,128]{3,2,1,0:T(8,128)(2,1)}, bf16[2,64,64,128]{3,2,1,0:T(8,128)(2,1)}) custom-call(s32[7,8]{1,0:T(8,128)} %get-tuple-element.19.table, bf16[400,128]{1,0:T(8,128)(2,1)} %get-tuple-element.20.refs_0_, bf16[400,128]{1,0:T(8,128)(2,1)} %copy-done.1, bf16[400,128]{1,0:T(8,128)(2,1)} %copy-done.2, bf16[400,128]{1,0:T(8,128)(2,1)} %copy-done.3, ...), custom_call_target="tpu_custom_call" | custom-call | flops 7000000000 | bytes 8000000 | tf_op jit(solution)/shard_map/restore_main/pallas_call | solution.py:628
  30.9 0.0 all-to-all-done.1.arrived
  30.9 5.6 %all-to-all-start = ((bf16[8,6,48,128]{3,2,1,0:T(8,128)(2,1)}), bf16[8,6,48,128]{3,2,1,0:T(8,128)(2,1)}, u32[]{:S(2)}, u32[]{:S(2)}) async-start(bf16[8,6,48,128]{3,2,1,0:T(8,128)(2,1)} %get-tuple-element.28), calls=%async_computation | async-start | bytes 1179648 | tf_op jit(solution)/shard_map/all_to_all | solution.py:570
  36.5 3.2 %restore_extra.1 = bf16[2,64,64,128]{3,2,1,0:T(8,128)(2,1)} custom-call(s32[7,8]{1,0:T(8,128)} %get-tuple-element.19.table, bf16[8,400,128]{2,1,0:T(8,128)(2,1)} %all-to-all-done.1.arrived, bf16[3,3,128,128]{3,2,1,0:T(8,128)(2,1)} %bitcast.11, bf16[3,3,128,128]{3,2,1,0:T(8,128)(2,1)} %bitcast.7, ...), custom_call_target="tpu_custom_call", output_to_operand_aliasing={{}: (8, {})} | custom-call | flops 6000000000 | bytes 8000000 | tf_op jit(solution)/shard_map/restore_extra/pallas_call | solution.py:641
  39.7 0.4 collective-permute-done.7.above
  40.1 0.0 copy-start
  40.1 0.0 collective-permute-done.8.below
  40.1 7.1 %all-to-all-done.back = bf16[8,6,48,128]{3,2,1,0:T(8,128)(2,1)} async-done(((bf16[8,6,48,128]{3,2,1,0:T(8,128)(2,1)}), bf16[8,6,48,128]{3,2,1,0:T(8,128)(2,1)}, u32[]{:S(2)}, u32[]{:S(2)}) %all-to-all-start) | async-done | bytes 589856 | tf_op jit(solution)/shard_map/all_to_all | solution.py:570
  47.2 0.0 copy-done
  47.2 6.2 %finish.1 = bf16[6,2,320,128]{3,2,1,0:T(8,128)(2,1)} custom-call(s32[7,8]{1,0:T(8,128)} %get-tuple-element.19.table, bf16[8,6,48,128]{3,2,1,0:T(8,128)(2,1)} %all-to-all-done.back, bf16[6,2,320,128]{3,2,1,0:T(8,128)(2,1)} %feat.3, bf16[6,320,128]{2,1,0:T(8,128)(2,1)} %copy-done, bf16[6,320,128]{2,1,0:T(8,128)(2,1)} %collective-permute-done.8.below, ...), custom_call_target="tpu_custom_call" | custom-call | flops 3000000000 | bytes 6000000 | tf_op jit(solution)/shard_map/finish/pallas_call | solution.py:655
Async XLA Ops:
  4.2 4.9 %collective-permute-start = (bf16[400,128]{1,0:T(8,128)(2,1)}, bf16[400,128]{1,0:T(8,128)(2,1)S(1)}, u32[]{:S(2)}, u32[]{:S(2)}) collective-permute-start(bf16[400,128]{1,0:T(8,128)(2,1)} %get-tuple-element.21), channel_id=1, source_target_pairs={{0,1},{1,0},{2,3},{3,2},{4,5},{5,4},{6,7},{7,6},{8,9},{9,8},{10,11... | collective-permute-start | bytes 307208 | tf_op jit(solution)/shard_map/ppermute | solution.py:603
  4.7 7.0 %collective-permute-start.1 = (bf16[400,128]{1,0:T(8,128)(2,1)}, bf16[400,128]{1,0:T(8,128)(2,1)S(1)}, u32[]{:S(2)}, u32[]{:S(2)}) collective-permute-start(bf16[400,128]{1,0:T(8,128)(2,1)} %get-tuple-element.22), channel_id=1, source_target_pairs={{0,2},{1,3},{2,0},{3,1},{4,6},{5,7},{6,4},{7,5},{8,10},{9,11},{10,... | collective-permute-start | bytes 307208 | tf_op jit(solution)/shard_map/ppermute | solution.py:603
  7.3 9.9 %collective-permute-start.2 = (bf16[400,128]{1,0:T(8,128)(2,1)}, bf16[400,128]{1,0:T(8,128)(2,1)S(1)}, u32[]{:S(2)}, u32[]{:S(2)}) collective-permute-start(bf16[400,128]{1,0:T(8,128)(2,1)} %get-tuple-element.23), channel_id=1, source_target_pairs={{0,3},{1,2},{2,1},{3,0},{4,7},{5,6},{6,5},{7,4},{8,11},{9,10},{10,... | collective-permute-start | bytes 307208 | tf_op jit(solution)/shard_map/ppermute | solution.py:603
  7.4 11.2 %collective-permute-start.3 = (bf16[400,128]{1,0:T(8,128)(2,1)}, bf16[400,128]{1,0:T(8,128)(2,1)S(1)}, u32[]{:S(2)}, u32[]{:S(2)}) collective-permute-start(bf16[400,128]{1,0:T(8,128)(2,1)} %get-tuple-element.24), channel_id=1, source_target_pairs={{0,4},{1,5},{2,6},{3,7},{4,0},{5,1},{6,2},{7,3},{8,12},{9,13},{10,... | collective-permute-start | bytes 307208 | tf_op jit(solution)/shard_map/ppermute | solution.py:603
  9.1 10.8 %collective-permute-start.4 = (bf16[400,128]{1,0:T(8,128)(2,1)}, bf16[400,128]{1,0:T(8,128)(2,1)S(1)}, u32[]{:S(2)}, u32[]{:S(2)}) collective-permute-start(bf16[400,128]{1,0:T(8,128)(2,1)} %get-tuple-element.25), channel_id=1, source_target_pairs={{0,5},{1,4},{2,7},{3,6},{4,1},{5,0},{6,3},{7,2},{8,13},{9,12},{10,... | collective-permute-start | bytes 307208 | tf_op jit(solution)/shard_map/ppermute | solution.py:603
  9.2 10.8 %copy-start.1 = (bf16[400,128]{1,0:T(8,128)(2,1)}, bf16[400,128]{1,0:T(8,128)(2,1)S(1)}, u32[]{:S(2)}) copy-start(bf16[400,128]{1,0:T(8,128)(2,1)S(1)} %collective-permute-done.refs_1_) | copy-start | bytes 307204
  9.2 10.8 %collective-permute-start.5 = (bf16[400,128]{1,0:T(8,128)(2,1)}, bf16[400,128]{1,0:T(8,128)(2,1)S(1)}, u32[]{:S(2)}, u32[]{:S(2)}) collective-permute-start(bf16[400,128]{1,0:T(8,128)(2,1)} %get-tuple-element.26), channel_id=1, source_target_pairs={{0,6},{1,7},{2,4},{3,5},{4,2},{5,3},{6,0},{7,1},{8,14},{9,15},{10,... | collective-permute-start | bytes 307208 | tf_op jit(solution)/shard_map/ppermute | solution.py:603
  11.8 8.2 %copy-start.2 = (bf16[400,128]{1,0:T(8,128)(2,1)}, bf16[400,128]{1,0:T(8,128)(2,1)S(1)}, u32[]{:S(2)}) copy-start(bf16[400,128]{1,0:T(8,128)(2,1)S(1)} %collective-permute-done.1.refs_2_) | copy-start | bytes 307204
  11.8 8.2 %collective-permute-start.6 = (bf16[400,128]{1,0:T(8,128)(2,1)}, bf16[400,128]{1,0:T(8,128)(2,1)S(1)}, u32[]{:S(2)}, u32[]{:S(2)}) collective-permute-start(bf16[400,128]{1,0:T(8,128)(2,1)} %get-tuple-element.27), channel_id=1, source_target_pairs={{0,7},{1,6},{2,5},{3,4},{4,3},{5,2},{6,1},{7,0},{8,15},{9,14},{10,... | collective-permute-start | bytes 307208 | tf_op jit(solution)/shard_map/ppermute | solution.py:603
  13.0 17.9 %all-to-all-start.1 = ((bf16[8,400,128]{2,1,0:T(8,128)(2,1)}), bf16[8,400,128]{2,1,0:T(8,128)(2,1)}, u32[]{:S(2)}, u32[]{:S(2)}) async-start(bf16[8,400,128]{2,1,0:T(8,128)(2,1)} %get-tuple-element.31), calls=%async_computation.1 | async-start | bytes 1638400 | tf_op jit(solution)/shard_map/all_to_all | solution.py:570
  17.2 2.8 %copy-start.3 = (bf16[400,128]{1,0:T(8,128)(2,1)}, bf16[400,128]{1,0:T(8,128)(2,1)S(1)}, u32[]{:S(2)}) copy-start(bf16[400,128]{1,0:T(8,128)(2,1)S(1)} %collective-permute-done.2.refs_3_) | copy-start | bytes 307204
  17.2 22.9 %collective-permute-start.7 = (bf16[6,320,128]{2,1,0:T(8,128)(2,1)}, bf16[6,320,128]{2,1,0:T(8,128)(2,1)S(1)}, u32[]{:S(2)}, u32[]{:S(2)}) collective-permute-start(bf16[6,320,128]{2,1,0:T(8,128)(2,1)} %get-tuple-element.29), channel_id=1, source_target_pairs={{0,1},{1,2},{2,3},{3,4},{4,5},{5,6},{6,7},{7,0},{8,9},{9,10},{10,1... | collective-permute-start | bytes 1474568 | tf_op jit(solution)/shard_map/ppermute | solution.py:605
  18.5 1.5 %copy-start.4 = (bf16[400,128]{1,0:T(8,128)(2,1)}, bf16[400,128]{1,0:T(8,128)(2,1)S(1)}, u32[]{:S(2)}) copy-start(bf16[400,128]{1,0:T(8,128)(2,1)S(1)} %collective-permute-done.3.refs_4_) | copy-start | bytes 307204
  18.5 21.6 %collective-permute-start.8 = (bf16[6,320,128]{2,1,0:T(8,128)(2,1)}, bf16[6,320,128]{2,1,0:T(8,128)(2,1)}, u32[]{:S(2)}, u32[]{:S(2)}) collective-permute-start(bf16[6,320,128]{2,1,0:T(8,128)(2,1)} %get-tuple-element.30), channel_id=1, source_target_pairs={{1,0},{2,1},{3,2},{4,3},{5,4},{6,5},{7,6},{0,7},{9,8},{10,9},{11,1... | collective-permute-start | bytes 1474568 | tf_op jit(solution)/shard_map/ppermute | solution.py:606
  19.9 0.6 %copy-start.5 = (bf16[400,128]{1,0:T(8,128)(2,1)}, bf16[400,128]{1,0:T(8,128)(2,1)S(1)}, u32[]{:S(2)}) copy-start(bf16[400,128]{1,0:T(8,128)(2,1)S(1)} %collective-permute-done.4.refs_5_) | copy-start | bytes 307204
  19.9 0.7 %copy-start.6 = (bf16[400,128]{1,0:T(8,128)(2,1)}, bf16[400,128]{1,0:T(8,128)(2,1)S(1)}, u32[]{:S(2)}) copy-start(bf16[400,128]{1,0:T(8,128)(2,1)S(1)} %collective-permute-done.5.refs_6_) | copy-start | bytes 307204
  20.0 0.7 %copy-start.7 = (bf16[400,128]{1,0:T(8,128)(2,1)}, bf16[400,128]{1,0:T(8,128)(2,1)S(1)}, u32[]{:S(2)}) copy-start(bf16[400,128]{1,0:T(8,128)(2,1)S(1)} %collective-permute-done.6.refs_7_) | copy-start | bytes 307204
  30.9 16.4 %all-to-all-start = ((bf16[8,6,48,128]{3,2,1,0:T(8,128)(2,1)}), bf16[8,6,48,128]{3,2,1,0:T(8,128)(2,1)}, u32[]{:S(2)}, u32[]{:S(2)}) async-start(bf16[8,6,48,128]{3,2,1,0:T(8,128)(2,1)} %get-tuple-element.28), calls=%async_computation | async-start | bytes 1179648 | tf_op jit(solution)/shard_map/all_to_all | solution.py:570
  40.1 7.1 %copy-start = (bf16[6,320,128]{2,1,0:T(8,128)(2,1)}, bf16[6,320,128]{2,1,0:T(8,128)(2,1)S(1)}, u32[]{:S(2)}) copy-start(bf16[6,320,128]{2,1,0:T(8,128)(2,1)S(1)} %collective-permute-done.7.above) | copy-start | bytes 1474564

commit v10 on v8

--- a/solution.py
+++ b/solution.py
@@ -46,6 +46,19 @@
     return ((local >> 1) << dims.shift) + 2 * tile + (local & 1)
 
 
+def partner_order(tiles):
+    far = sorted(range(3, tiles), key=lambda s: (-(s >> 1).bit_count(), s))
+    return [0, 1, 2] + far
+
+
+def partner(place, tiles):
+    me = lax.axis_index("tile")
+    other = jnp.int32(0)
+    for k, s in enumerate(partner_order(tiles)):
+        other = jnp.where(place == k, s, other)
+    return me ^ other
+
+
 def silu(v):
     half = 0.5 * v
     return half + half * jnp.tanh(half)
@@ -148,13 +161,13 @@
     return finish
 
 
-def pack_crops(dims, table, row_at, col_at, canvas, rim, staged, partner):
+def pack_crops(dims, table, row_at, col_at, canvas, rim, staged, worker):
     me = lax.axis_index("tile")
     rim[...] = jnp.zeros_like(rim)
 
     @pl.loop(0, dims.tiles)
     def _(s):
-        w = partner(s)
+        w = worker(s)
         row0 = table[row_at, w]
         col0 = table[col_at, w]
         start = first_local(jnp.maximum(row0 - 1, 0), me, dims)
@@ -216,7 +229,7 @@
     )
     for edge in edges:
         edge.start()
-    pack_crops(dims, table, ROW, COL, canvas, rim, staged, lambda s: me ^ s)
+    pack_crops(dims, table, ROW, COL, canvas, rim, staged, lambda s: partner(s, dims.tiles))
     copies = [pltpu.make_async_copy(staged.at[s], sent[s], sent_sems.at[s]) for s in range(dims.tiles)]
     for copy in copies:
         copy.start()
@@ -349,7 +362,7 @@
     scratch = (got, row_store, column_store, held, got_sems, tap_sems)
     arrival, taps = begin(dims, arrived, (dec_w, one_w, two_w), (dec_b, one_b, two_b), scratch)
     restore(
-        dims, row0, length, arrival, lambda s: me ^ s, got, taps,
+        dims, row0, length, arrival, lambda s: partner(s, tiles), got, taps,
         raw, decoded, wide, inner, mixed, delta, lambda piece: None,
     )
 
@@ -593,9 +606,11 @@
         cost_estimate=cost(0, 6e6),
         name="pack",
     )(boxes, slots, features)
-    got_main = [sent_main[0]] + [None] * (tiles - 1)
-    for s in [1] + sorted(range(2, tiles), key=lambda s: (-(s >> 1).bit_count(), -(s >> 1), s)):
-        got_main[s] = lax.ppermute(sent_main[s], "tile", [(i, i ^ s) for i in range(tiles)])
+    got_main = [
+        lax.ppermute(message, "tile", [(i, i ^ s) for i in range(tiles)]) if s else message
+        for s, message in zip(partner_order(tiles), sent_main)
+    ]
+    *got_main, sent_extra, last, leading = lax.optimization_barrier((*got_main, sent_extra, last, leading))
     up = [(i, (i + 1) % tiles) for i in range(tiles)]
     above = lax.ppermute(last, "tile", up)
     below = lax.ppermute(leading, "tile", [(j, i) for i, j in up])

time: 53.7 us -> 61.7 us (1.15)
  waiting for transfers between devices: 2.91 us -> 19.7 us
  Pallas kernels: 29 us -> 21.9 us
  starting transfers between devices: 20 us -> 19 us
    ppermute x7, waiting for transfers between devices: 0.02 us -> 8.89 us  [shards(): lax.ppermute(message, 'tile', [(i, i ^ s) for i in range(tiles)])]
    pallas_call x1, Pallas kernels: 9.22 us -> 2.03 us  [shards(): pl.pallas_call(functools.partial(extra_kernel, dims), out_shape=restored_...]
    all_to_all x2, waiting for transfers between devices: 2.88 us -> 7.52 us  [swap(): lax.all_to_all(array, 'tile', split_axis=0, concat_axis=0, tiled=True)]
    ppermute x1, waiting for transfers between devices: 0.01 us -> 3.24 us  [shards(): above = lax.ppermute(last, 'tile', up)]
    ppermute x7, starting transfers between devices: 8.84 us -> 7.92 us  [shards(): lax.ppermute(message, 'tile', [(i, i ^ s) for i in range(tiles)])]
    ppermute x1, starting transfers between devices: 1.39 us -> 2.32 us  [shards(): below = lax.ppermute(leading, 'tile', [(j, i) for i, j in up])]
    ppermute x1, starting transfers between devices: 1.25 us -> 0.38 us  [shards(): above = lax.ppermute(last, 'tile', up)]
    unnamed x4 -> x2, local copies, waits for them, and re-layouts: 0.62 us -> 0.01 us
  transfers between devices with their start and end apart: 11 -> 11, of which waited for: 1 -> 8; matrix products, arithmetic and copies ran while one was open for 0% -> 0% of each run, Pallas kernels for 36% -> 20%
where the time goes in v10:
time: 61.7 us; the launch traced here: 61.2 us
  Pallas kernels  21.9 us (35%)
  waiting for transfers between devices  19.7 us (32%)
  starting transfers between devices  19 us (31%)
  between operations  0.68 us (1%)
    pallas_call x1, Pallas kernels, shards(): pl.pallas_call(functools.partial(main_kernel, dims), out_shape=[shaped(ti...  10.1 us
    ppermute x7, waiting for transfers between devices, shards(): lax.ppermute(message, 'tile', [(i, i ^ s) for i in range(tiles)])  8.89 us
    all_to_all x2, starting transfers between devices, swap(): lax.all_to_all(array, 'tile', split_axis=0, concat_axis=0, tiled=True)  8.4 us
    ppermute x7, starting transfers between devices, shards(): lax.ppermute(message, 'tile', [(i, i ^ s) for i in range(tiles)])  7.92 us
    all_to_all x2, waiting for transfers between devices, swap(): lax.all_to_all(array, 'tile', split_axis=0, concat_axis=0, tiled=True)  7.52 us
    pallas_call x1, Pallas kernels, shards(): pl.pallas_call(functools.partial(finish_kernel, dims), out_shape=shaped(*...  6.18 us
    pallas_call x1, Pallas kernels, shards(): pl.pallas_call(functools.partial(pack_kernel, dims), out_shape=[shaped(di...  3.57 us
    ppermute x1, waiting for transfers between devices, shards(): above = lax.ppermute(last, 'tile', up)  3.24 us
  transfers between devices with their start and end apart: 11, of which 8 were waited for; matrix products, arithmetic and copies ran while one was open for 0% of the time, Pallas kernels for 20%

profile of v10, /device:TPU:0, one launch (start us, length us, event | category | flops | bytes accessed | tf_op | source)
XLA Modules:
  0.0 61.2 jit_solution(14243396414229452843)
XLA Ops:
  0.6 3.6 %pack.1 = (bf16[400,128]{1,0:T(8,128)(2,1)}, bf16[400,128]{1,0:T(8,128)(2,1)}, bf16[400,128]{1,0:T(8,128)(2,1)}, bf16[400,128]{1,0:T(8,128)(2,1)}, bf16[400,128]...) custom-call(s32[3,8]{1,0:T(4,128)} %boxes_in.1, ...), custom_call_target="tpu_custom_call" | custom-call | bytes 6000000 | tf_op jit(solution)/shard_map/pack/pallas_call | solution.py:591
  4.2 0.5 collective-permute-start
  4.7 2.6 %collective-permute-start.1 = (bf16[400,128]{1,0:T(8,128)(2,1)}, bf16[400,128]{1,0:T(8,128)(2,1)}, u32[]{:S(2)}, u32[]{:S(2)}) collective-permute-start(bf16[400,128]{1,0:T(8,128)(2,1)} %get-tuple-element.33), channel_id=1, source_target_pairs={{0,2},{1,3},{2,0},{3,1},{4,6},{5,7},{6,4},{7,5},{8,10},{9,11},{10,... | collective-permute-start | bytes 307208 | tf_op jit(solution)/shard_map/ppermute | solution.py:610
  7.3 1.5 %collective-permute-start.2 = (bf16[400,128]{1,0:T(8,128)(2,1)}, bf16[400,128]{1,0:T(8,128)(2,1)}, u32[]{:S(2)}, u32[]{:S(2)}) collective-permute-start(bf16[400,128]{1,0:T(8,128)(2,1)} %get-tuple-element.34), channel_id=1, source_target_pairs={{0,6},{1,7},{2,4},{3,5},{4,2},{5,3},{6,0},{7,1},{8,14},{9,15},{10,... | collective-permute-start | bytes 307208 | tf_op jit(solution)/shard_map/ppermute | solution.py:610
  8.8 0.9 %collective-permute-start.3 = (bf16[400,128]{1,0:T(8,128)(2,1)}, bf16[400,128]{1,0:T(8,128)(2,1)}, u32[]{:S(2)}, u32[]{:S(2)}) collective-permute-start(bf16[400,128]{1,0:T(8,128)(2,1)} %get-tuple-element.35), channel_id=1, source_target_pairs={{0,7},{1,6},{2,5},{3,4},{4,3},{5,2},{6,1},{7,0},{8,15},{9,14},{10,... | collective-permute-start | bytes 307208 | tf_op jit(solution)/shard_map/ppermute | solution.py:610
  9.7 0.3 collective-permute-start.4
  10.0 0.0 collective-permute-done.refs_1_
  10.0 2.0 %collective-permute-start.5 = (bf16[400,128]{1,0:T(8,128)(2,1)}, bf16[400,128]{1,0:T(8,128)(2,1)}, u32[]{:S(2)}, u32[]{:S(2)}) collective-permute-start(bf16[400,128]{1,0:T(8,128)(2,1)} %get-tuple-element.37), channel_id=1, source_target_pairs={{0,4},{1,5},{2,6},{3,7},{4,0},{5,1},{6,2},{7,3},{8,12},{9,13},{10,... | collective-permute-start | bytes 307208 | tf_op jit(solution)/shard_map/ppermute | solution.py:610
  12.0 0.0 collective-permute-done.1.refs_2_
  12.0 0.1 collective-permute-start.6
  12.1 2.9 %collective-permute-done.2.refs_3_ = bf16[400,128]{1,0:T(8,128)(2,1)} collective-permute-done((bf16[400,128]{1,0:T(8,128)(2,1)}, bf16[400,128]{1,0:T(8,128)(2,1)}, u32[]{:S(2)}, u32[]{:S(2)}) %collective-permute-start.2) | collective-permute-done | bytes 102432 | tf_op jit(solution)/shard_map/ppermute | solution.py:610
  15.0 1.3 %collective-permute-done.3.refs_4_ = bf16[400,128]{1,0:T(8,128)(2,1)} collective-permute-done((bf16[400,128]{1,0:T(8,128)(2,1)}, bf16[400,128]{1,0:T(8,128)(2,1)}, u32[]{:S(2)}, u32[]{:S(2)}) %collective-permute-start.3) | collective-permute-done | bytes 102432 | tf_op jit(solution)/shard_map/ppermute | solution.py:610
  16.3 0.8 %collective-permute-done.4.refs_5_ = bf16[400,128]{1,0:T(8,128)(2,1)} collective-permute-done((bf16[400,128]{1,0:T(8,128)(2,1)}, bf16[400,128]{1,0:T(8,128)(2,1)}, u32[]{:S(2)}, u32[]{:S(2)}) %collective-permute-start.4) | collective-permute-done | bytes 102432 | tf_op jit(solution)/shard_map/ppermute | solution.py:610
  17.1 1.8 %collective-permute-done.5.refs_6_ = bf16[400,128]{1,0:T(8,128)(2,1)} collective-permute-done((bf16[400,128]{1,0:T(8,128)(2,1)}, bf16[400,128]{1,0:T(8,128)(2,1)}, u32[]{:S(2)}, u32[]{:S(2)}) %collective-permute-start.5) | collective-permute-done | bytes 102432 | tf_op jit(solution)/shard_map/ppermute | solution.py:610
  18.9 2.1 %collective-permute-done.6.refs_7_ = bf16[400,128]{1,0:T(8,128)(2,1)} collective-permute-done((bf16[400,128]{1,0:T(8,128)(2,1)}, bf16[400,128]{1,0:T(8,128)(2,1)}, u32[]{:S(2)}, u32[]{:S(2)}) %collective-permute-start.6) | collective-permute-done | bytes 102432 | tf_op jit(solution)/shard_map/ppermute | solution.py:610
  21.0 4.2 %all-to-all-start.1 = ((bf16[8,400,128]{2,1,0:T(8,128)(2,1)}), bf16[8,400,128]{2,1,0:T(8,128)(2,1)}, u32[]{:S(2)}, u32[]{:S(2)}) async-start(bf16[8,400,128]{2,1,0:T(8,128)(2,1)} %get-tuple-element.53), calls=%async_computation.1 | async-start | bytes 1638400 | tf_op jit(solution)/shard_map/all_to_all | solution.py:578
  25.2 0.4 collective-permute-start.7
  25.6 2.3 %collective-permute-start.8 = (bf16[6,320,128]{2,1,0:T(8,128)(2,1)}, bf16[6,320,128]{2,1,0:T(8,128)(2,1)}, u32[]{:S(2)}, u32[]{:S(2)}) collective-permute-start(bf16[6,320,128]{2,1,0:T(8,128)(2,1)} %get-tuple-element.52), channel_id=1, source_target_pairs={{1,0},{2,1},{3,2},{4,3},{5,4},{6,5},{7,6},{0,7},{9,8},{10,9},{11,1... | collective-permute-start | bytes 1474568 | tf_op jit(solution)/shard_map/ppermute | solution.py:616
  27.9 10.1 %restore_main.1 = (bf16[8,6,48,128]{3,2,1,0:T(8,128)(2,1)}, bf16[2,64,64,128]{3,2,1,0:T(8,128)(2,1)}) custom-call(s32[7,8]{1,0:T(8,128)} %get-tuple-element.30.table, bf16[400,128]{1,0:T(8,128)(2,1)} %get-tuple-element.42.refs_0_, bf16[400,128]{1,0:T(8,128)(2,1)} %collective-permute-done.refs_1_, bf16[400,128]{1,0:T(8,128)(2,1)} %collective-permute-done.1.refs_2_, ...), custom_call_target="tpu_custom_call" | custom-call | flops 7000000000 | bytes 8000000 | tf_op jit(solution)/shard_map/restore_main/pallas_call | solution.py:638
  38.0 0.6 %all-to-all-done.1.arrived = bf16[8,400,128]{2,1,0:T(8,128)(2,1)} async-done(((bf16[8,400,128]{2,1,0:T(8,128)(2,1)}), bf16[8,400,128]{2,1,0:T(8,128)(2,1)}, u32[]{:S(2)}, u32[]{:S(2)}) %all-to-all-start.1) | async-done | bytes 819232 | tf_op jit(solution)/shard_map/all_to_all | solution.py:578
  38.7 4.2 %all-to-all-start = ((bf16[8,6,48,128]{3,2,1,0:T(8,128)(2,1)}), bf16[8,6,48,128]{3,2,1,0:T(8,128)(2,1)}, u32[]{:S(2)}, u32[]{:S(2)}) async-start(bf16[8,6,48,128]{3,2,1,0:T(8,128)(2,1)} %get-tuple-element.50), calls=%async_computation | async-start | bytes 1179648 | tf_op jit(solution)/shard_map/all_to_all | solution.py:578
  42.9 2.0 %restore_extra.1 = bf16[2,64,64,128]{3,2,1,0:T(8,128)(2,1)} custom-call(s32[7,8]{1,0:T(8,128)} %get-tuple-element.30.table, bf16[8,400,128]{2,1,0:T(8,128)(2,1)} %all-to-all-done.1.arrived, bf16[3,3,128,128]{3,2,1,0:T(8,128)(2,1)} %bitcast.11, bf16[3,3,128,128]{3,2,1,0:T(8,128)(2,1)} %bitcast.7, ...), custom_call_target="tpu_custom_call", output_to_operand_aliasing={{}: (8, {})} | custom-call | flops 6000000000 | bytes 8000000 | tf_op jit(solution)/shard_map/restore_extra/pallas_call | solution.py:651
  44.9 3.2 %collective-permute-done.7.above = bf16[6,320,128]{2,1,0:T(8,128)(2,1)S(1)} collective-permute-done((bf16[6,320,128]{2,1,0:T(8,128)(2,1)}, bf16[6,320,128]{2,1,0:T(8,128)(2,1)S(1)}, u32[]{:S(2)}, u32[]{:S(2)}) %collective-permute-start.7) | collective-permute-done | bytes 491552 | tf_op jit(solution)/shard_map/ppermute | solution.py:615
  48.2 0.0 copy-start
  48.2 0.0 collective-permute-done.8.below
  48.2 6.9 %all-to-all-done.back = bf16[8,6,48,128]{3,2,1,0:T(8,128)(2,1)} async-done(((bf16[8,6,48,128]{3,2,1,0:T(8,128)(2,1)}), bf16[8,6,48,128]{3,2,1,0:T(8,128)(2,1)}, u32[]{:S(2)}, u32[]{:S(2)}) %all-to-all-start) | async-done | bytes 589856 | tf_op jit(solution)/shard_map/all_to_all | solution.py:578
  55.1 0.0 copy-done
  55.1 6.2 %finish.1 = bf16[6,2,320,128]{3,2,1,0:T(8,128)(2,1)} custom-call(s32[7,8]{1,0:T(8,128)} %get-tuple-element.30.table, bf16[8,6,48,128]{3,2,1,0:T(8,128)(2,1)} %all-to-all-done.back, bf16[6,2,320,128]{3,2,1,0:T(8,128)(2,1)} %feat.3, bf16[6,320,128]{2,1,0:T(8,128)(2,1)} %copy-done, bf16[6,320,128]{2,1,0:T(8,128)(2,1)} %collective-permute-done.8.below, ...), custom_call_target="tpu_custom_call" | custom-call | flops 3000000000 | bytes 6000000 | tf_op jit(solution)/shard_map/finish/pallas_call | solution.py:665
Async XLA Ops:
  4.2 5.8 %collective-permute-start = (bf16[400,128]{1,0:T(8,128)(2,1)}, bf16[400,128]{1,0:T(8,128)(2,1)}, u32[]{:S(2)}, u32[]{:S(2)}) collective-permute-start(bf16[400,128]{1,0:T(8,128)(2,1)} %get-tuple-element.32), channel_id=1, source_target_pairs={{0,1},{1,0},{2,3},{3,2},{4,5},{5,4},{6,7},{7,6},{8,9},{9,8},{10,11... | collective-permute-start | bytes 307208 | tf_op jit(solution)/shard_map/ppermute | solution.py:610
  4.7 7.3 %collective-permute-start.1 = (bf16[400,128]{1,0:T(8,128)(2,1)}, bf16[400,128]{1,0:T(8,128)(2,1)}, u32[]{:S(2)}, u32[]{:S(2)}) collective-permute-start(bf16[400,128]{1,0:T(8,128)(2,1)} %get-tuple-element.33), channel_id=1, source_target_pairs={{0,2},{1,3},{2,0},{3,1},{4,6},{5,7},{6,4},{7,5},{8,10},{9,11},{10,... | collective-permute-start | bytes 307208 | tf_op jit(solution)/shard_map/ppermute | solution.py:610
  7.3 7.8 %collective-permute-start.2 = (bf16[400,128]{1,0:T(8,128)(2,1)}, bf16[400,128]{1,0:T(8,128)(2,1)}, u32[]{:S(2)}, u32[]{:S(2)}) collective-permute-start(bf16[400,128]{1,0:T(8,128)(2,1)} %get-tuple-element.34), channel_id=1, source_target_pairs={{0,6},{1,7},{2,4},{3,5},{4,2},{5,3},{6,0},{7,1},{8,14},{9,15},{10,... | collective-permute-start | bytes 307208 | tf_op jit(solution)/shard_map/ppermute | solution.py:610
  8.8 7.6 %collective-permute-start.3 = (bf16[400,128]{1,0:T(8,128)(2,1)}, bf16[400,128]{1,0:T(8,128)(2,1)}, u32[]{:S(2)}, u32[]{:S(2)}) collective-permute-start(bf16[400,128]{1,0:T(8,128)(2,1)} %get-tuple-element.35), channel_id=1, source_target_pairs={{0,7},{1,6},{2,5},{3,4},{4,3},{5,2},{6,1},{7,0},{8,15},{9,14},{10,... | collective-permute-start | bytes 307208 | tf_op jit(solution)/shard_map/ppermute | solution.py:610
  9.7 7.4 %collective-permute-start.4 = (bf16[400,128]{1,0:T(8,128)(2,1)}, bf16[400,128]{1,0:T(8,128)(2,1)}, u32[]{:S(2)}, u32[]{:S(2)}) collective-permute-start(bf16[400,128]{1,0:T(8,128)(2,1)} %get-tuple-element.36), channel_id=1, source_target_pairs={{0,3},{1,2},{2,1},{3,0},{4,7},{5,6},{6,5},{7,4},{8,11},{9,10},{10,... | collective-permute-start | bytes 307208 | tf_op jit(solution)/shard_map/ppermute | solution.py:610
  10.0 8.9 %collective-permute-start.5 = (bf16[400,128]{1,0:T(8,128)(2,1)}, bf16[400,128]{1,0:T(8,128)(2,1)}, u32[]{:S(2)}, u32[]{:S(2)}) collective-permute-start(bf16[400,128]{1,0:T(8,128)(2,1)} %get-tuple-element.37), channel_id=1, source_target_pairs={{0,4},{1,5},{2,6},{3,7},{4,0},{5,1},{6,2},{7,3},{8,12},{9,13},{10,... | collective-permute-start | bytes 307208 | tf_op jit(solution)/shard_map/ppermute | solution.py:610
  12.0 9.0 %collective-permute-start.6 = (bf16[400,128]{1,0:T(8,128)(2,1)}, bf16[400,128]{1,0:T(8,128)(2,1)}, u32[]{:S(2)}, u32[]{:S(2)}) collective-permute-start(bf16[400,128]{1,0:T(8,128)(2,1)} %get-tuple-element.38), channel_id=1, source_target_pairs={{0,5},{1,4},{2,7},{3,6},{4,1},{5,0},{6,3},{7,2},{8,13},{9,12},{10,... | collective-permute-start | bytes 307208 | tf_op jit(solution)/shard_map/ppermute | solution.py:610
  21.0 17.7 %all-to-all-start.1 = ((bf16[8,400,128]{2,1,0:T(8,128)(2,1)}), bf16[8,400,128]{2,1,0:T(8,128)(2,1)}, u32[]{:S(2)}, u32[]{:S(2)}) async-start(bf16[8,400,128]{2,1,0:T(8,128)(2,1)} %get-tuple-element.53), calls=%async_computation.1 | async-start | bytes 1638400 | tf_op jit(solution)/shard_map/all_to_all | solution.py:578
  25.2 22.9 %collective-permute-start.7 = (bf16[6,320,128]{2,1,0:T(8,128)(2,1)}, bf16[6,320,128]{2,1,0:T(8,128)(2,1)S(1)}, u32[]{:S(2)}, u32[]{:S(2)}) collective-permute-start(bf16[6,320,128]{2,1,0:T(8,128)(2,1)} %get-tuple-element.51), channel_id=1, source_target_pairs={{0,1},{1,2},{2,3},{3,4},{4,5},{5,6},{6,7},{7,0},{8,9},{9,10},{10,1... | collective-permute-start | bytes 1474568 | tf_op jit(solution)/shard_map/ppermute | solution.py:615
  25.6 22.5 %collective-permute-start.8 = (bf16[6,320,128]{2,1,0:T(8,128)(2,1)}, bf16[6,320,128]{2,1,0:T(8,128)(2,1)}, u32[]{:S(2)}, u32[]{:S(2)}) collective-permute-start(bf16[6,320,128]{2,1,0:T(8,128)(2,1)} %get-tuple-element.52), channel_id=1, source_target_pairs={{1,0},{2,1},{3,2},{4,3},{5,4},{6,5},{7,6},{0,7},{9,8},{10,9},{11,1... | collective-permute-start | bytes 1474568 | tf_op jit(solution)/shard_map/ppermute | solution.py:616
  38.7 16.4 %all-to-all-start = ((bf16[8,6,48,128]{3,2,1,0:T(8,128)(2,1)}), bf16[8,6,48,128]{3,2,1,0:T(8,128)(2,1)}, u32[]{:S(2)}, u32[]{:S(2)}) async-start(bf16[8,6,48,128]{3,2,1,0:T(8,128)(2,1)} %get-tuple-element.50), calls=%async_computation | async-start | bytes 1179648 | tf_op jit(solution)/shard_map/all_to_all | solution.py:578
  48.2 6.9 %copy-start = (bf16[6,320,128]{2,1,0:T(8,128)(2,1)}, bf16[6,320,128]{2,1,0:T(8,128)(2,1)S(1)}, u32[]{:S(2)}) copy-start(bf16[6,320,128]{2,1,0:T(8,128)(2,1)S(1)} %collective-permute-done.7.above) | copy-start | bytes 1474564

commit v11 on v8

--- a/solution.py
+++ b/solution.py
@@ -105,13 +105,15 @@
         self.store[:, 0, :, chans : 2 * chans] = none
 
 
-def two_chains(wide, taps):
-    wide = wide.reshape(-1, wide.shape[-1])
+def chains(wide, taps, count):
     weight = taps.value()
-    middle = weight.shape[0] // 2
-    one = jnp.dot(wide[:, :middle], weight[:middle], preferred_element_type=F32)
-    two = jnp.dot(wide[:, middle:], weight[middle:], preferred_element_type=F32)
-    return one + two
+    depth = weight.shape[0] // count
+    total = None
+    for k in range(count):
+        part = slice(k * depth, (k + 1) * depth)
+        term = jnp.dot(wide[:, part], weight[part], preferred_element_type=F32)
+        total = term if total is None else total + term
+    return total
 
 
 def row_pairs(src, first, count, taps):
@@ -121,11 +123,13 @@
         src[pl.ds(first + 1, count), 0],
         src[pl.ds(first + 1, count), 1],
     ]
-    return two_chains(jnp.concatenate(parts, -1), taps)
+    wide = jnp.concatenate(parts, -1)
+    return chains(wide.reshape(-1, wide.shape[-1]), taps, 3)
 
 
 def column_pairs(src, first, count, taps):
-    return two_chains(jnp.concatenate([src[pl.ds(first + a, count)] for a in range(3)], -1), taps)
+    wide = jnp.concatenate([src[pl.ds(first + a, count)] for a in range(3)], -1)
+    return chains(wide.reshape(-1, wide.shape[-1]), taps, 3)
 
 
 def fill_canvas(dims, feat, held, canvas, sems):
@@ -260,20 +264,6 @@
             right = jnp.where(at == SPAN - 1, rim[2 * i + 1 : 2 * i + 2], pltpu.roll(wider, SPAN - 1, 0))
             raw[place >> 1, place & 1] = jnp.concatenate([left.astype(BF16), line, right.astype(BF16)], -1)
 
-    taps[1].start()
-    taps[2].start()
-    taps[0].wait()
-    n = 8
-    for first in range(0, pairs, n):
-        total = silu(row_pairs(raw, first, n, taps[0]) + taps[0].bias())
-        for k in range(n):
-            part = total[k * SPAN : (k + 1) * SPAN]
-            at = 2 * (first + k)
-            upper = raw[first + k, 1, :, chans : 2 * chans].astype(F32) + part[:, :chans]
-            lower = raw[first + k + 1, 0, :, chans : 2 * chans].astype(F32) + part[:, chans:]
-            decoded[at] = upper.astype(BF16).astype(F32)
-            decoded[at + 1] = lower.astype(BF16).astype(F32)
-
     lengthf = length.astype(F32)
     block = lax.broadcasted_iota(I32, (4, half, SPAN), 0)
     t = 2 * lax.broadcasted_iota(I32, (4, half, SPAN), 1) + block - 1
@@ -281,43 +271,67 @@
     spots = jnp.clip((t.astype(F32) + 0.5) * lengthf / S - 0.5, 0.0, lengthf - 1.0)
     across = jnp.where((t >= 0) & (t < S), jnp.maximum(0.0, 1.0 - jnp.abs(spots - j)), 0.0)
     across = across.reshape(4 * half, SPAN).astype(BF16)
-    taps[1].wait()
-    taps[2].wait()
-    for m in range(S // 2):
-        lines = []
-        for parity in range(2):
-            s = 2 * m + parity
-            spot = jnp.clip((2 * s + 1) * length - S, 0, (length - 1) * 2 * S)
-            low = spot >> 7
-            part = (spot & 127).astype(F32) * (1.0 / (2 * S))
-            high = jnp.minimum(low + 1, SPAN - 1)
-            lines.append(((1.0 - part) * decoded[low] + part * decoded[high]).astype(BF16))
-        cells = jnp.dot(across, jnp.concatenate(lines, -1), preferred_element_type=F32).astype(BF16)
-        for parity in range(2):
-            at = 2 * m + parity + 1
-            for b in range(4):
-                wide[at, :, b * chans : (b + 1) * chans] = cells[
-                    b * half : (b + 1) * half, parity * chans : (parity + 1) * chans
-                ]
-
+    for tap in taps:
+        tap.wait()
     n = PIECE
-    for first in range(0, S, n):
+
+    def region(piece):
+        first = piece * (n // 2)
+        total = silu(row_pairs(raw, first, n // 2, taps[0]) + taps[0].bias())
+        for k in range(n // 2):
+            part = total[k * SPAN : (k + 1) * SPAN]
+            at = 2 * (first + k)
+            upper = raw[first + k, 1, :, chans : 2 * chans].astype(F32) + part[:, :chans]
+            lower = raw[first + k + 1, 0, :, chans : 2 * chans].astype(F32) + part[:, chans:]
+            decoded[at] = upper.astype(BF16).astype(F32)
+            decoded[at + 1] = lower.astype(BF16).astype(F32)
+
+    def resample(piece):
+        for m in range(piece * (n // 2), (piece + 1) * (n // 2)):
+            lines = []
+            for parity in range(2):
+                s = 2 * m + parity
+                spot = jnp.clip((2 * s + 1) * length - S, 0, (length - 1) * 2 * S)
+                low = spot >> 7
+                part = (spot & 127).astype(F32) * (1.0 / (2 * S))
+                high = jnp.minimum(low + 1, SPAN - 1)
+                lines.append(((1.0 - part) * decoded[low] + part * decoded[high]).astype(BF16))
+            cells = jnp.dot(across, jnp.concatenate(lines, -1), preferred_element_type=F32).astype(BF16)
+            for parity in range(2):
+                at = 2 * m + parity + 1
+                for b in range(4):
+                    wide[at, :, b * chans : (b + 1) * chans] = cells[
+                        b * half : (b + 1) * half, parity * chans : (parity + 1) * chans
+                    ]
+
+    def first_conv(piece):
+        first = piece * n
         total = silu(column_pairs(wide, first, n, taps[1]) + taps[1].bias())
         at = lax.broadcasted_iota(I32, (n, half, chans), 1)
         even = pltpu.roll(total[:, :chans], n * half - 1, 0).reshape(n, half, chans)
         odd = pltpu.roll(total[:, chans:], 1, 0).reshape(n, half, chans)
-        rows = pl.ds(first + 1, n)
+        rows = slice(first + 1, first + 1 + n)
         inner[rows, :, 0:chans] = jnp.where(at == 0, 0.0, odd).astype(BF16)
         inner[rows, :, chans : 3 * chans] = total.astype(BF16).reshape(n, half, 2 * chans)
         inner[rows, :, 3 * chans :] = jnp.where(at == half - 1, 0.0, even).astype(BF16)
 
-    for first in range(0, S, n):
+    def second_conv(piece):
+        first = piece * n
         total = column_pairs(inner, first, n, taps[2]) + taps[2].bias()
         for k in range(n):
             mixed[first + k, pl.ds(0, half, stride=2), :] = total[k * half : (k + 1) * half, :chans]
             mixed[first + k, pl.ds(1, half, stride=2), :] = total[k * half : (k + 1) * half, chans:]
         delta[first : first + n] = mixed[first : first + n].astype(BF16)
-        finish(first // PIECE)
+
+    stages = (
+        [(region, 0), (resample, 0), (region, 1), (resample, 1), (first_conv, 0), (region, 2), (resample, 2)]
+        + [(first_conv, 1), (second_conv, 0), (resample, 3), (first_conv, 2), (second_conv, 1), (first_conv, 3)]
+        + [(second_conv, 2), (second_conv, 3)]
+    )
+    for stage, piece in stages:
+        stage(piece)
+        if stage is second_conv:
+            finish(piece)
 
 
 def begin(dims, arrived, weights, biases, scratch):
@@ -333,7 +347,8 @@
         ColumnTaps(weights[1], biases[1], column_store.at[0], held.at[1], tap_sems.at[1]),
         ColumnTaps(weights[2], biases[2], column_store.at[1], held.at[2], tap_sems.at[2]),
     )
-    taps[0].start()
+    for tap in taps:
+        tap.start()
     return arrival, taps
 
 

time: 53.7 us -> 55.1 us (1.026)
  Pallas kernels: 29 us -> 32.3 us
  waiting for transfers between devices: 2.91 us -> 0.03 us
  local copies, waits for them, and re-layouts: 0.62 us -> 1.37 us
    all_to_all x2, waiting for transfers between devices: 2.88 us -> 0.01 us  [swap(): lax.all_to_all(array, 'tile', split_axis=0, concat_axis=0, tiled=True)]
    pallas_call x1, Pallas kernels: 9.22 us -> 11 us  [shards(): pl.pallas_call(functools.partial(extra_kernel, dims), out_shape=restored_...]
    pallas_call x1, Pallas kernels: 10.1 us -> 11.6 us  [shards(): pl.pallas_call(functools.partial(main_kernel, dims), out_shape=[shaped(ti...]
    unnamed x4, local copies, waits for them, and re-layouts: 0.62 us -> 1.37 us
  transfers between devices with their start and end apart: 11 -> 11, of which waited for: 1 -> 0; matrix products, arithmetic and copies ran while one was open for 0% -> 0% of each run, Pallas kernels for 36% -> 41%
where the time goes in v11:
time: 55.1 us; the launch traced here: 54.6 us
  Pallas kernels  32.3 us (59%)
  starting transfers between devices  20 us (36%)
  local copies, waits for them, and re-layouts  1.37 us (2%)
  between operations  0.89 us (2%)
    pallas_call x1, Pallas kernels, shards(): pl.pallas_call(functools.partial(main_kernel, dims), out_shape=[shaped(ti...  11.6 us
    pallas_call x1, Pallas kernels, shards(): pl.pallas_call(functools.partial(extra_kernel, dims), out_shape=restored_...  11 us
    ppermute x7, starting transfers between devices, shards(): lax.ppermute(sent_main[s], 'tile', [(i, i ^ s) for i in range(tiles)])  8.84 us
    all_to_all x2, starting transfers between devices, swap(): lax.all_to_all(array, 'tile', split_axis=0, concat_axis=0, tiled=True)  8.55 us
    pallas_call x1, Pallas kernels, shards(): pl.pallas_call(functools.partial(finish_kernel, dims), out_shape=shaped(*...  6.14 us
    pallas_call x1, Pallas kernels, shards(): pl.pallas_call(functools.partial(pack_kernel, dims), out_shape=[shaped(di...  3.54 us
    ppermute x1, starting transfers between devices, shards(): below = lax.ppermute(leading, 'tile', [(j, i) for i, j in up])  1.39 us
    unnamed x4, local copies, waits for them, and re-layouts  1.37 us
  transfers between devices with their start and end apart: 11, of which 0 were waited for; matrix products, arithmetic and copies ran while one was open for 0% of the time, Pallas kernels for 41%

profile of v11, /device:TPU:0, one launch (start us, length us, event | category | flops | bytes accessed | tf_op | source)
XLA Modules:
  0.0 54.6 jit_solution(18385901073509129899)
XLA Ops:
  0.6 3.5 %pack.1 = (bf16[400,128]{1,0:T(8,128)(2,1)}, bf16[400,128]{1,0:T(8,128)(2,1)}, bf16[400,128]{1,0:T(8,128)(2,1)}, bf16[400,128]{1,0:T(8,128)(2,1)}, bf16[400,128]...) custom-call(s32[3,8]{1,0:T(4,128)} %boxes_in.1, ...), custom_call_target="tpu_custom_call" | custom-call | bytes 6000000 | tf_op jit(solution)/shard_map/pack/pallas_call | solution.py:593
  4.2 0.5 collective-permute-start
  4.7 2.6 %collective-permute-start.1 = (bf16[400,128]{1,0:T(8,128)(2,1)}, bf16[400,128]{1,0:T(8,128)(2,1)}, u32[]{:S(2)}, u32[]{:S(2)}) collective-permute-start(bf16[400,128]{1,0:T(8,128)(2,1)} %get-tuple-element.22), channel_id=1, source_target_pairs={{0,2},{1,3},{2,0},{3,1},{4,6},{5,7},{6,4},{7,5},{8,10},{9,11},{10,... | collective-permute-start | bytes 307208 | tf_op jit(solution)/shard_map/ppermute | solution.py:613
  7.3 0.1 collective-permute-start.2
  7.3 1.8 %collective-permute-start.3 = (bf16[400,128]{1,0:T(8,128)(2,1)}, bf16[400,128]{1,0:T(8,128)(2,1)}, u32[]{:S(2)}, u32[]{:S(2)}) collective-permute-start(bf16[400,128]{1,0:T(8,128)(2,1)} %get-tuple-element.24), channel_id=1, source_target_pairs={{0,4},{1,5},{2,6},{3,7},{4,0},{5,1},{6,2},{7,3},{8,12},{9,13},{10,... | collective-permute-start | bytes 307208 | tf_op jit(solution)/shard_map/ppermute | solution.py:613
  9.1 0.0 collective-permute-start.4
  9.1 0.0 collective-permute-done.refs_1_
  9.1 2.6 %collective-permute-start.5 = (bf16[400,128]{1,0:T(8,128)(2,1)}, bf16[400,128]{1,0:T(8,128)(2,1)}, u32[]{:S(2)}, u32[]{:S(2)}) collective-permute-start(bf16[400,128]{1,0:T(8,128)(2,1)} %get-tuple-element.26), channel_id=1, source_target_pairs={{0,6},{1,7},{2,4},{3,5},{4,2},{5,3},{6,0},{7,1},{8,14},{9,15},{10,... | collective-permute-start | bytes 307208 | tf_op jit(solution)/shard_map/ppermute | solution.py:613
  11.7 0.0 collective-permute-done.1.refs_2_
  11.7 1.3 %collective-permute-start.6 = (bf16[400,128]{1,0:T(8,128)(2,1)}, bf16[400,128]{1,0:T(8,128)(2,1)}, u32[]{:S(2)}, u32[]{:S(2)}) collective-permute-start(bf16[400,128]{1,0:T(8,128)(2,1)} %get-tuple-element.27), channel_id=1, source_target_pairs={{0,7},{1,6},{2,5},{3,4},{4,3},{5,2},{6,1},{7,0},{8,15},{9,14},{10,... | collective-permute-start | bytes 307208 | tf_op jit(solution)/shard_map/ppermute | solution.py:613
  13.0 4.2 %all-to-all-start.1 = ((bf16[8,400,128]{2,1,0:T(8,128)(2,1)}), bf16[8,400,128]{2,1,0:T(8,128)(2,1)}, u32[]{:S(2)}, u32[]{:S(2)}) async-start(bf16[8,400,128]{2,1,0:T(8,128)(2,1)} %get-tuple-element.31), calls=%async_computation.1 | async-start | bytes 1638400 | tf_op jit(solution)/shard_map/all_to_all | solution.py:580
  17.3 0.0 collective-permute-done.2.refs_3_
  17.3 0.0 copy-start.1
  17.3 0.6 %copy-done.1 = bf16[400,128]{1,0:T(8,128)(2,1)} copy-done((bf16[400,128]{1,0:T(8,128)(2,1)}, bf16[400,128]{1,0:T(8,128)(2,1)S(1)}, u32[]{:S(2)}) %copy-start.1) | copy-done | bytes 102424
  17.9 1.3 %collective-permute-start.7 = (bf16[6,320,128]{2,1,0:T(8,128)(2,1)}, bf16[6,320,128]{2,1,0:T(8,128)(2,1)S(1)}, u32[]{:S(2)}, u32[]{:S(2)}) collective-permute-start(bf16[6,320,128]{2,1,0:T(8,128)(2,1)} %get-tuple-element.29), channel_id=1, source_target_pairs={{0,1},{1,2},{2,3},{3,4},{4,5},{5,6},{6,7},{7,0},{8,9},{9,10},{10,1... | collective-permute-start | bytes 1474568 | tf_op jit(solution)/shard_map/ppermute | solution.py:615
  19.1 0.0 collective-permute-done.3.refs_4_
  19.1 1.4 %collective-permute-start.8 = (bf16[6,320,128]{2,1,0:T(8,128)(2,1)}, bf16[6,320,128]{2,1,0:T(8,128)(2,1)}, u32[]{:S(2)}, u32[]{:S(2)}) collective-permute-start(bf16[6,320,128]{2,1,0:T(8,128)(2,1)} %get-tuple-element.30), channel_id=1, source_target_pairs={{1,0},{2,1},{3,2},{4,3},{5,4},{6,5},{7,6},{0,7},{9,8},{10,9},{11,1... | collective-permute-start | bytes 1474568 | tf_op jit(solution)/shard_map/ppermute | solution.py:616
  20.5 0.0 collective-permute-done.4.refs_5_
  20.5 0.0 collective-permute-done.5.refs_6_
  20.5 0.0 collective-permute-done.6.refs_7_
  20.6 11.6 %restore_main.1 = (bf16[8,6,48,128]{3,2,1,0:T(8,128)(2,1)}, bf16[2,64,64,128]{3,2,1,0:T(8,128)(2,1)}) custom-call(s32[7,8]{1,0:T(8,128)} %get-tuple-element.19.table, bf16[400,128]{1,0:T(8,128)(2,1)} %get-tuple-element.20.refs_0_, bf16[400,128]{1,0:T(8,128)(2,1)} %collective-permute-done.refs_1_, bf16[400,128]{1,0:T(8,128)(2,1)} %collective-permute-done.1.refs_2_, ...), custom_call_target="tpu_custom_call" | custom-call | flops 7000000000 | bytes 8000000 | tf_op jit(solution)/shard_map/restore_main/pallas_call | solution.py:638
  32.2 0.0 all-to-all-done.1.arrived
  32.2 4.3 %all-to-all-start = ((bf16[8,6,48,128]{3,2,1,0:T(8,128)(2,1)}), bf16[8,6,48,128]{3,2,1,0:T(8,128)(2,1)}, u32[]{:S(2)}, u32[]{:S(2)}) async-start(bf16[8,6,48,128]{3,2,1,0:T(8,128)(2,1)} %get-tuple-element.28), calls=%async_computation | async-start | bytes 1179648 | tf_op jit(solution)/shard_map/all_to_all | solution.py:580
  36.5 11.0 %restore_extra.1 = bf16[2,64,64,128]{3,2,1,0:T(8,128)(2,1)} custom-call(s32[7,8]{1,0:T(8,128)} %get-tuple-element.19.table, bf16[8,400,128]{2,1,0:T(8,128)(2,1)} %all-to-all-done.1.arrived, bf16[3,3,128,128]{3,2,1,0:T(8,128)(2,1)} %bitcast.11, bf16[3,3,128,128]{3,2,1,0:T(8,128)(2,1)} %bitcast.7, ...), custom_call_target="tpu_custom_call", output_to_operand_aliasing={{}: (8, {})} | custom-call | flops 6000000000 | bytes 8000000 | tf_op jit(solution)/shard_map/restore_extra/pallas_call | solution.py:651
  47.5 0.0 collective-permute-done.7.above
  47.5 0.0 copy-start
  47.6 0.0 collective-permute-done.8.below
  47.6 0.0 all-to-all-done.back
  47.6 0.7 %copy-done = bf16[6,320,128]{2,1,0:T(8,128)(2,1)} copy-done((bf16[6,320,128]{2,1,0:T(8,128)(2,1)}, bf16[6,320,128]{2,1,0:T(8,128)(2,1)S(1)}, u32[]{:S(2)}) %copy-start) | copy-done | bytes 491544
  48.3 6.1 %finish.1 = bf16[6,2,320,128]{3,2,1,0:T(8,128)(2,1)} custom-call(s32[7,8]{1,0:T(8,128)} %get-tuple-element.19.table, bf16[8,6,48,128]{3,2,1,0:T(8,128)(2,1)} %all-to-all-done.back, bf16[6,2,320,128]{3,2,1,0:T(8,128)(2,1)} %feat.3, bf16[6,320,128]{2,1,0:T(8,128)(2,1)} %copy-done, bf16[6,320,128]{2,1,0:T(8,128)(2,1)} %collective-permute-done.8.below, ...), custom_call_target="tpu_custom_call" | custom-call | flops 3000000000 | bytes 6000000 | tf_op jit(solution)/shard_map/finish/pallas_call | solution.py:665
Async XLA Ops:
  4.2 4.9 %collective-permute-start = (bf16[400,128]{1,0:T(8,128)(2,1)}, bf16[400,128]{1,0:T(8,128)(2,1)}, u32[]{:S(2)}, u32[]{:S(2)}) collective-permute-start(bf16[400,128]{1,0:T(8,128)(2,1)} %get-tuple-element.21), channel_id=1, source_target_pairs={{0,1},{1,0},{2,3},{3,2},{4,5},{5,4},{6,7},{7,6},{8,9},{9,8},{10,11... | collective-permute-start | bytes 307208 | tf_op jit(solution)/shard_map/ppermute | solution.py:613
  4.7 7.0 %collective-permute-start.1 = (bf16[400,128]{1,0:T(8,128)(2,1)}, bf16[400,128]{1,0:T(8,128)(2,1)}, u32[]{:S(2)}, u32[]{:S(2)}) collective-permute-start(bf16[400,128]{1,0:T(8,128)(2,1)} %get-tuple-element.22), channel_id=1, source_target_pairs={{0,2},{1,3},{2,0},{3,1},{4,6},{5,7},{6,4},{7,5},{8,10},{9,11},{10,... | collective-permute-start | bytes 307208 | tf_op jit(solution)/shard_map/ppermute | solution.py:613
  7.3 10.0 %collective-permute-start.2 = (bf16[400,128]{1,0:T(8,128)(2,1)}, bf16[400,128]{1,0:T(8,128)(2,1)S(1)}, u32[]{:S(2)}, u32[]{:S(2)}) collective-permute-start(bf16[400,128]{1,0:T(8,128)(2,1)} %get-tuple-element.23), channel_id=1, source_target_pairs={{0,3},{1,2},{2,1},{3,0},{4,7},{5,6},{6,5},{7,4},{8,11},{9,10},{10,... | collective-permute-start | bytes 307208 | tf_op jit(solution)/shard_map/ppermute | solution.py:613
  7.3 11.8 %collective-permute-start.3 = (bf16[400,128]{1,0:T(8,128)(2,1)}, bf16[400,128]{1,0:T(8,128)(2,1)}, u32[]{:S(2)}, u32[]{:S(2)}) collective-permute-start(bf16[400,128]{1,0:T(8,128)(2,1)} %get-tuple-element.24), channel_id=1, source_target_pairs={{0,4},{1,5},{2,6},{3,7},{4,0},{5,1},{6,2},{7,3},{8,12},{9,13},{10,... | collective-permute-start | bytes 307208 | tf_op jit(solution)/shard_map/ppermute | solution.py:613
  9.1 11.4 %collective-permute-start.4 = (bf16[400,128]{1,0:T(8,128)(2,1)}, bf16[400,128]{1,0:T(8,128)(2,1)}, u32[]{:S(2)}, u32[]{:S(2)}) collective-permute-start(bf16[400,128]{1,0:T(8,128)(2,1)} %get-tuple-element.25), channel_id=1, source_target_pairs={{0,5},{1,4},{2,7},{3,6},{4,1},{5,0},{6,3},{7,2},{8,13},{9,12},{10,... | collective-permute-start | bytes 307208 | tf_op jit(solution)/shard_map/ppermute | solution.py:613
  9.1 11.4 %collective-permute-start.5 = (bf16[400,128]{1,0:T(8,128)(2,1)}, bf16[400,128]{1,0:T(8,128)(2,1)}, u32[]{:S(2)}, u32[]{:S(2)}) collective-permute-start(bf16[400,128]{1,0:T(8,128)(2,1)} %get-tuple-element.26), channel_id=1, source_target_pairs={{0,6},{1,7},{2,4},{3,5},{4,2},{5,3},{6,0},{7,1},{8,14},{9,15},{10,... | collective-permute-start | bytes 307208 | tf_op jit(solution)/shard_map/ppermute | solution.py:613
  11.7 8.8 %collective-permute-start.6 = (bf16[400,128]{1,0:T(8,128)(2,1)}, bf16[400,128]{1,0:T(8,128)(2,1)}, u32[]{:S(2)}, u32[]{:S(2)}) collective-permute-start(bf16[400,128]{1,0:T(8,128)(2,1)} %get-tuple-element.27), channel_id=1, source_target_pairs={{0,7},{1,6},{2,5},{3,4},{4,3},{5,2},{6,1},{7,0},{8,15},{9,14},{10,... | collective-permute-start | bytes 307208 | tf_op jit(solution)/shard_map/ppermute | solution.py:613
  13.0 19.2 %all-to-all-start.1 = ((bf16[8,400,128]{2,1,0:T(8,128)(2,1)}), bf16[8,400,128]{2,1,0:T(8,128)(2,1)}, u32[]{:S(2)}, u32[]{:S(2)}) async-start(bf16[8,400,128]{2,1,0:T(8,128)(2,1)} %get-tuple-element.31), calls=%async_computation.1 | async-start | bytes 1638400 | tf_op jit(solution)/shard_map/all_to_all | solution.py:580
  17.3 0.6 %copy-start.1 = (bf16[400,128]{1,0:T(8,128)(2,1)}, bf16[400,128]{1,0:T(8,128)(2,1)S(1)}, u32[]{:S(2)}) copy-start(bf16[400,128]{1,0:T(8,128)(2,1)S(1)} %collective-permute-done.2.refs_3_) | copy-start | bytes 307204
  17.9 29.6 %collective-permute-start.7 = (bf16[6,320,128]{2,1,0:T(8,128)(2,1)}, bf16[6,320,128]{2,1,0:T(8,128)(2,1)S(1)}, u32[]{:S(2)}, u32[]{:S(2)}) collective-permute-start(bf16[6,320,128]{2,1,0:T(8,128)(2,1)} %get-tuple-element.29), channel_id=1, source_target_pairs={{0,1},{1,2},{2,3},{3,4},{4,5},{5,6},{6,7},{7,0},{8,9},{9,10},{10,1... | collective-permute-start | bytes 1474568 | tf_op jit(solution)/shard_map/ppermute | solution.py:615
  19.1 28.4 %collective-permute-start.8 = (bf16[6,320,128]{2,1,0:T(8,128)(2,1)}, bf16[6,320,128]{2,1,0:T(8,128)(2,1)}, u32[]{:S(2)}, u32[]{:S(2)}) collective-permute-start(bf16[6,320,128]{2,1,0:T(8,128)(2,1)} %get-tuple-element.30), channel_id=1, source_target_pairs={{1,0},{2,1},{3,2},{4,3},{5,4},{6,5},{7,6},{0,7},{9,8},{10,9},{11,1... | collective-permute-start | bytes 1474568 | tf_op jit(solution)/shard_map/ppermute | solution.py:616
  32.2 15.4 %all-to-all-start = ((bf16[8,6,48,128]{3,2,1,0:T(8,128)(2,1)}), bf16[8,6,48,128]{3,2,1,0:T(8,128)(2,1)}, u32[]{:S(2)}, u32[]{:S(2)}) async-start(bf16[8,6,48,128]{3,2,1,0:T(8,128)(2,1)} %get-tuple-element.28), calls=%async_computation | async-start | bytes 1179648 | tf_op jit(solution)/shard_map/all_to_all | solution.py:580
  47.5 0.8 %copy-start = (bf16[6,320,128]{2,1,0:T(8,128)(2,1)}, bf16[6,320,128]{2,1,0:T(8,128)(2,1)S(1)}, u32[]{:S(2)}) copy-start(bf16[6,320,128]{2,1,0:T(8,128)(2,1)S(1)} %collective-permute-done.7.above) | copy-start | bytes 1474564

commit v12 on v8

--- a/solution.py
+++ b/solution.py
@@ -17,7 +17,7 @@
 BF16 = jnp.bfloat16
 F32 = jnp.float32
 I32 = jnp.int32
-FULL_GRANT = 66500000
+FULL_GRANT = 67000000
 ROW, COL, SIDE, ROW2, COL2, SIDE2, PLACE = range(7)
 
 
@@ -56,53 +56,44 @@
 
 
 class RowTaps:
-    def __init__(self, source, bias, store, held, sems):
-        chans = source.shape[-1]
-        self.store = store
-        self.held = held
+    def __init__(self, source, bias, fetched, store, held, sems):
+        self.fetched, self.store, self.held = fetched, store, held
         self.copies = (
-            pltpu.make_async_copy(bias, held, sems.at[2]),
-            pltpu.make_async_copy(source, store.at[0:3, :, :, 0:chans], sems.at[0]),
-            pltpu.make_async_copy(source, store.at[1:4, :, :, chans : 2 * chans], sems.at[1]),
+            pltpu.make_async_copy(source, fetched, sems.at[0]),
+            pltpu.make_async_copy(bias, held, sems.at[1]),
         )
 
     def start(self):
         for copy in self.copies:
             copy.start()
+
+    def wait(self):
+        for copy in self.copies:
+            copy.wait()
         chans = self.store.shape[2]
         none = jnp.zeros((3, chans, chans), BF16)
         self.store[3, :, :, 0:chans] = none
         self.store[0, :, :, chans : 2 * chans] = none
-
+        self.store[0:3, :, :, 0:chans] = self.fetched[...]
+        self.store[1:4, :, :, chans : 2 * chans] = self.fetched[...]
+
+    def bias(self):
+        return both(self.held[...])
+
+    def value(self):
+        return self.store[...].reshape(-1, self.store.shape[-1])
+
+
+class ColumnTaps(RowTaps):
     def wait(self):
         for copy in self.copies:
             copy.wait()
-
-    def bias(self):
-        return both(self.held[...])
-
-    def value(self):
-        return self.store[...].reshape(-1, self.store.shape[-1])
-
-
-class ColumnTaps(RowTaps):
-    def __init__(self, source, bias, store, held, sems):
-        chans = source.shape[-1]
-        self.store = store
-        self.held = held
-        self.copies = (
-            pltpu.make_async_copy(bias, held, sems.at[2]),
-            pltpu.make_async_copy(source, store.at[:, 0:3, :, 0:chans], sems.at[0]),
-            pltpu.make_async_copy(source, store.at[:, 1:4, :, chans : 2 * chans], sems.at[1]),
-        )
-
-    def start(self):
-        for copy in self.copies:
-            copy.start()
         chans = self.store.shape[2]
         none = jnp.zeros((3, chans, chans), BF16)
         self.store[:, 3, :, 0:chans] = none
         self.store[:, 0, :, chans : 2 * chans] = none
+        self.store[:, 0:3, :, 0:chans] = self.fetched[...]
+        self.store[:, 1:4, :, chans : 2 * chans] = self.fetched[...]
 
 
 def two_chains(wide, taps):
@@ -321,7 +312,7 @@
 
 
 def begin(dims, arrived, weights, biases, scratch):
-    got, row_store, column_store, held, got_sems, tap_sems = scratch
+    got, fetched, row_store, column_store, held, got_sems, tap_sems = scratch
 
     def arrival(s):
         return pltpu.make_async_copy(arrived[0], got.at[s], got_sems.at[s])
@@ -329,9 +320,9 @@
     for s in range(dims.tiles):
         pltpu.make_async_copy(arrived[s], got.at[s], got_sems.at[s]).start()
     taps = (
-        RowTaps(weights[0], biases[0], row_store, held.at[0], tap_sems.at[0]),
-        ColumnTaps(weights[1], biases[1], column_store.at[0], held.at[1], tap_sems.at[1]),
-        ColumnTaps(weights[2], biases[2], column_store.at[1], held.at[2], tap_sems.at[2]),
+        RowTaps(weights[0], biases[0], fetched.at[0], row_store, held.at[0], tap_sems.at[0]),
+        ColumnTaps(weights[1], biases[1], fetched.at[1], column_store.at[0], held.at[1], tap_sems.at[1]),
+        ColumnTaps(weights[2], biases[2], fetched.at[2], column_store.at[1], held.at[2], tap_sems.at[2]),
     )
     taps[0].start()
     return arrival, taps
@@ -340,13 +331,13 @@
 def main_kernel(dims, table, *refs):
     tiles, chans = dims.tiles, dims.chans
     arrived, refs = refs[:tiles], refs[tiles:]
-    (dec_w, one_w, two_w, dec_b, one_b, two_b, sent, restored, got, row_store, column_store, held) = refs[:12]
-    got_sems, tap_sems, raw, decoded, wide, inner, mixed, delta, sem, back, back_sems = refs[12:]
+    (dec_w, one_w, two_w, dec_b, one_b, two_b, sent, restored, got, fetched, row_store, column_store, held) = refs[:13]
+    got_sems, tap_sems, raw, decoded, wide, inner, mixed, delta, sem, back, back_sems = refs[13:]
     me = lax.axis_index("tile")
     row0 = table[ROW, me]
     length = table[SIDE, me]
     place = table[PLACE, me]
-    scratch = (got, row_store, column_store, held, got_sems, tap_sems)
+    scratch = (got, fetched, row_store, column_store, held, got_sems, tap_sems)
     arrival, taps = begin(dims, arrived, (dec_w, one_w, two_w), (dec_b, one_b, two_b), scratch)
     restore(
         dims, row0, length, arrival, lambda s: me ^ s, got, taps,
@@ -401,7 +392,7 @@
 
 def extra_kernel(
     dims, table, arrived, dec_w, one_w, two_w, dec_b, one_b, two_b, partial, restored,
-    got, row_store, column_store, held, got_sems, tap_sems, raw, decoded, wide, inner, mixed, delta, sem,
+    got, fetched, row_store, column_store, held, got_sems, tap_sems, raw, decoded, wide, inner, mixed, delta, sem,
 ):
     me = lax.axis_index("tile")
     row0 = table[ROW2, me]
@@ -415,7 +406,7 @@
 
     @pl.when(length > 0)
     def _():
-        scratch = (got, row_store, column_store, held, got_sems, tap_sems)
+        scratch = (got, fetched, row_store, column_store, held, got_sems, tap_sems)
         arrival, taps = begin(dims, [arrived.at[s] for s in range(dims.tiles)], (dec_w, one_w, two_w), (dec_b, one_b, two_b), scratch)
 
         def leave(piece):
@@ -444,12 +435,12 @@
 
 def finish_kernel(
     dims, table, back, feat, above, below, weight, bias, finished,
-    got, held, up, down, store, held_bias, lines, wide, canvas, out, sems, load_sems, tap_sems,
+    got, held, up, down, fetched, store, held_bias, lines, wide, canvas, out, sems, load_sems, tap_sems,
 ):
     me = lax.axis_index("tile")
     bands, chans, cols = dims.bands, dims.chans, dims.cols
     half = cols // 2
-    taps = ColumnTaps(weight, bias, store, held_bias, tap_sems)
+    taps = ColumnTaps(weight, bias, fetched, store, held_bias, tap_sems)
     patches = pltpu.make_async_copy(back, got, sems.at[0])
     patches.start()
     def from_feat(band):
@@ -606,11 +597,12 @@
     biases = (dec_bias[None], first_bias[None], second_bias[None])
     restore_scratch = [
         pltpu.VMEM((tiles, dims.message, chans), BF16),
+        pltpu.VMEM((3, 3, 3, chans, chans), BF16),
         pltpu.VMEM((4, 3, chans, 2 * chans), BF16),
         pltpu.VMEM((2, 3, 4, chans, 2 * chans), BF16),
         pltpu.VMEM((3, 1, chans), F32),
         dma((tiles,)),
-        dma((3, 3)),
+        dma((3, 2)),
         pltpu.VMEM((SPAN // 2 + 2, 2, SPAN, 3 * chans), BF16),
         pltpu.VMEM((SPAN, SPAN, chans), F32),
         pltpu.VMEM((S + 2, S // 2, 4 * chans), BF16),
@@ -657,6 +649,7 @@
             pltpu.VMEM((bands, 2, cols, chans), BF16),
             pltpu.VMEM((bands, cols, chans), BF16),
             pltpu.VMEM((bands, cols, chans), BF16),
+            pltpu.VMEM((3, 3, chans, chans), BF16),
             pltpu.VMEM((3, 4, chans, 2 * chans), BF16),
             pltpu.VMEM((1, chans), F32),
             pltpu.VMEM((BANDS_AT_ONCE, 4, cols + 16, chans), F32),
@@ -665,7 +658,7 @@
             pltpu.VMEM((bands, 2, cols, chans), BF16),
             dma((1 + bands,)),
             dma((3, bands)),
-            dma((3,)),
+            dma((2,)),
         ],
         compiler_params=full,
         cost_estimate=cost(3e9, 6e6),

time: 53.7 us -> 54.5 us (1.015)
  waiting for transfers between devices: 2.91 us -> 9.48 us
  Pallas kernels: 29 us -> 23.8 us
  local copies, waits for them, and re-layouts: 0.62 us -> 0 us
    pallas_call x1, Pallas kernels: 9.22 us -> 2.97 us  [shards(): pl.pallas_call(functools.partial(extra_kernel, dims), out_shape=restored_...]
    all_to_all x2, waiting for transfers between devices: 2.88 us -> 7.27 us  [swap(): lax.all_to_all(array, 'tile', split_axis=0, concat_axis=0, tiled=True)]
    ppermute x1, waiting for transfers between devices: 0.01 us -> 2.2 us  [shards(): above = lax.ppermute(last, 'tile', up)]
    pallas_call x1, Pallas kernels: 6.19 us -> 7.05 us  [shards(): pl.pallas_call(functools.partial(finish_kernel, dims), out_shape=shaped(*...]
    unnamed x4 -> x0, local copies, waits for them, and re-layouts: 0.62 us -> none
  transfers between devices with their start and end apart: 11 -> 11, of which waited for: 1 -> 3; matrix products, arithmetic and copies ran while one was open for 0% -> 0% of each run, Pallas kernels for 36% -> 24%
where the time goes in v12:
time: 54.5 us; the launch traced here: 54.1 us
  Pallas kernels  23.8 us (44%)
  starting transfers between devices  20.2 us (37%)
  waiting for transfers between devices  9.48 us (17%)
  between operations  0.68 us (1%)
    pallas_call x1, Pallas kernels, shards(): pl.pallas_call(functools.partial(main_kernel, dims), out_shape=[shaped(ti...  10.2 us
    ppermute x7, starting transfers between devices, shards(): lax.ppermute(sent_main[s], 'tile', [(i, i ^ s) for i in range(tiles)])  8.84 us
    all_to_all x2, starting transfers between devices, swap(): lax.all_to_all(array, 'tile', split_axis=0, concat_axis=0, tiled=True)  8.62 us
    all_to_all x2, waiting for transfers between devices, swap(): lax.all_to_all(array, 'tile', split_axis=0, concat_axis=0, tiled=True)  7.27 us
    pallas_call x1, Pallas kernels, shards(): pl.pallas_call(functools.partial(finish_kernel, dims), out_shape=shaped(*...  7.05 us
    pallas_call x1, Pallas kernels, shards(): pl.pallas_call(functools.partial(pack_kernel, dims), out_shape=[shaped(di...  3.54 us
    pallas_call x1, Pallas kernels, shards(): pl.pallas_call(functools.partial(extra_kernel, dims), out_shape=restored_...  2.97 us
    ppermute x1, waiting for transfers between devices, shards(): above = lax.ppermute(last, 'tile', up)  2.2 us
  transfers between devices with their start and end apart: 11, of which 3 were waited for; matrix products, arithmetic and copies ran while one was open for 0% of the time, Pallas kernels for 24%

profile of v12, /device:TPU:0, one launch (start us, length us, event | category | flops | bytes accessed | tf_op | source)
XLA Modules:
  0.0 54.1 jit_solution(4714973314963513895)
XLA Ops:
  0.6 3.5 %pack.1 = (bf16[400,128]{1,0:T(8,128)(2,1)}, bf16[400,128]{1,0:T(8,128)(2,1)}, bf16[400,128]{1,0:T(8,128)(2,1)}, bf16[400,128]{1,0:T(8,128)(2,1)}, bf16[400,128]...) custom-call(s32[3,8]{1,0:T(4,128)} %boxes_in.1, ...), custom_call_target="tpu_custom_call" | custom-call | bytes 6000000 | tf_op jit(solution)/shard_map/pack/pallas_call | solution.py:569
  4.2 0.5 collective-permute-start
  4.7 2.6 %collective-permute-start.1 = (bf16[400,128]{1,0:T(8,128)(2,1)}, bf16[400,128]{1,0:T(8,128)(2,1)}, u32[]{:S(2)}, u32[]{:S(2)}) collective-permute-start(bf16[400,128]{1,0:T(8,128)(2,1)} %get-tuple-element.22), channel_id=1, source_target_pairs={{0,2},{1,3},{2,0},{3,1},{4,6},{5,7},{6,4},{7,5},{8,10},{9,11},{10,... | collective-permute-start | bytes 307208 | tf_op jit(solution)/shard_map/ppermute | solution.py:589
  7.3 0.1 collective-permute-start.2
  7.3 1.8 %collective-permute-start.3 = (bf16[400,128]{1,0:T(8,128)(2,1)}, bf16[400,128]{1,0:T(8,128)(2,1)}, u32[]{:S(2)}, u32[]{:S(2)}) collective-permute-start(bf16[400,128]{1,0:T(8,128)(2,1)} %get-tuple-element.24), channel_id=1, source_target_pairs={{0,4},{1,5},{2,6},{3,7},{4,0},{5,1},{6,2},{7,3},{8,12},{9,13},{10,... | collective-permute-start | bytes 307208 | tf_op jit(solution)/shard_map/ppermute | solution.py:589
  9.1 0.0 collective-permute-start.4
  9.1 0.0 collective-permute-done.refs_1_
  9.1 2.6 %collective-permute-start.5 = (bf16[400,128]{1,0:T(8,128)(2,1)}, bf16[400,128]{1,0:T(8,128)(2,1)}, u32[]{:S(2)}, u32[]{:S(2)}) collective-permute-start(bf16[400,128]{1,0:T(8,128)(2,1)} %get-tuple-element.26), channel_id=1, source_target_pairs={{0,6},{1,7},{2,4},{3,5},{4,2},{5,3},{6,0},{7,1},{8,14},{9,15},{10,... | collective-permute-start | bytes 307208 | tf_op jit(solution)/shard_map/ppermute | solution.py:589
  11.7 0.0 collective-permute-done.1.refs_2_
  11.7 1.3 %collective-permute-start.6 = (bf16[400,128]{1,0:T(8,128)(2,1)}, bf16[400,128]{1,0:T(8,128)(2,1)}, u32[]{:S(2)}, u32[]{:S(2)}) collective-permute-start(bf16[400,128]{1,0:T(8,128)(2,1)} %get-tuple-element.27), channel_id=1, source_target_pairs={{0,7},{1,6},{2,5},{3,4},{4,3},{5,2},{6,1},{7,0},{8,15},{9,14},{10,... | collective-permute-start | bytes 307208 | tf_op jit(solution)/shard_map/ppermute | solution.py:589
  13.0 4.2 %all-to-all-start.1 = ((bf16[8,400,128]{2,1,0:T(8,128)(2,1)}), bf16[8,400,128]{2,1,0:T(8,128)(2,1)}, u32[]{:S(2)}, u32[]{:S(2)}) async-start(bf16[8,400,128]{2,1,0:T(8,128)(2,1)} %get-tuple-element.31), calls=%async_computation.1 | async-start | bytes 1638400 | tf_op jit(solution)/shard_map/all_to_all | solution.py:556
  17.2 0.0 collective-permute-done.2.refs_3_
  17.3 1.3 %collective-permute-start.7 = (bf16[6,320,128]{2,1,0:T(8,128)(2,1)}, bf16[6,320,128]{2,1,0:T(8,128)(2,1)}, u32[]{:S(2)}, u32[]{:S(2)}) collective-permute-start(bf16[6,320,128]{2,1,0:T(8,128)(2,1)} %get-tuple-element.29), channel_id=1, source_target_pairs={{0,1},{1,2},{2,3},{3,4},{4,5},{5,6},{6,7},{7,0},{8,9},{9,10},{10,1... | collective-permute-start | bytes 1474568 | tf_op jit(solution)/shard_map/ppermute | solution.py:591
  18.6 0.0 collective-permute-done.3.refs_4_
  18.6 1.4 %collective-permute-start.8 = (bf16[6,320,128]{2,1,0:T(8,128)(2,1)}, bf16[6,320,128]{2,1,0:T(8,128)(2,1)}, u32[]{:S(2)}, u32[]{:S(2)}) collective-permute-start(bf16[6,320,128]{2,1,0:T(8,128)(2,1)} %get-tuple-element.30), channel_id=1, source_target_pairs={{1,0},{2,1},{3,2},{4,3},{5,4},{6,5},{7,6},{0,7},{9,8},{10,9},{11,1... | collective-permute-start | bytes 1474568 | tf_op jit(solution)/shard_map/ppermute | solution.py:592
  20.0 0.0 collective-permute-done.4.refs_5_
  20.0 0.0 collective-permute-done.5.refs_6_
  20.0 0.0 collective-permute-done.6.refs_7_
  20.0 10.2 %restore_main.1 = (bf16[8,6,48,128]{3,2,1,0:T(8,128)(2,1)}, bf16[2,64,64,128]{3,2,1,0:T(8,128)(2,1)}) custom-call(s32[7,8]{1,0:T(8,128)} %get-tuple-element.19.table, bf16[400,128]{1,0:T(8,128)(2,1)} %get-tuple-element.20.refs_0_, bf16[400,128]{1,0:T(8,128)(2,1)} %collective-permute-done.refs_1_, bf16[400,128]{1,0:T(8,128)(2,1)} %collective-permute-done.1.refs_2_, ...), custom_call_target="tpu_custom_call" | custom-call | flops 7000000000 | bytes 8000000 | tf_op jit(solution)/shard_map/restore_main/pallas_call | solution.py:615
  30.2 0.5 all-to-all-done.1.arrived
  30.7 4.4 %all-to-all-start = ((bf16[8,6,48,128]{3,2,1,0:T(8,128)(2,1)}), bf16[8,6,48,128]{3,2,1,0:T(8,128)(2,1)}, u32[]{:S(2)}, u32[]{:S(2)}) async-start(bf16[8,6,48,128]{3,2,1,0:T(8,128)(2,1)} %get-tuple-element.28), calls=%async_computation | async-start | bytes 1179648 | tf_op jit(solution)/shard_map/all_to_all | solution.py:556
  35.1 3.0 %restore_extra.1 = bf16[2,64,64,128]{3,2,1,0:T(8,128)(2,1)} custom-call(s32[7,8]{1,0:T(8,128)} %get-tuple-element.19.table, bf16[8,400,128]{2,1,0:T(8,128)(2,1)} %all-to-all-done.1.arrived, bf16[3,3,128,128]{3,2,1,0:T(8,128)(2,1)} %bitcast.11, bf16[3,3,128,128]{3,2,1,0:T(8,128)(2,1)} %bitcast.7, ...), custom_call_target="tpu_custom_call", output_to_operand_aliasing={{}: (8, {})} | custom-call | flops 6000000000 | bytes 8000000 | tf_op jit(solution)/shard_map/restore_extra/pallas_call | solution.py:628
  38.1 2.2 %collective-permute-done.7.above = bf16[6,320,128]{2,1,0:T(8,128)(2,1)} collective-permute-done((bf16[6,320,128]{2,1,0:T(8,128)(2,1)}, bf16[6,320,128]{2,1,0:T(8,128)(2,1)}, u32[]{:S(2)}, u32[]{:S(2)}) %collective-permute-start.7) | collective-permute-done | bytes 491552 | tf_op jit(solution)/shard_map/ppermute | solution.py:591
  40.3 0.0 collective-permute-done.8.below
  40.3 6.8 %all-to-all-done.back = bf16[8,6,48,128]{3,2,1,0:T(8,128)(2,1)} async-done(((bf16[8,6,48,128]{3,2,1,0:T(8,128)(2,1)}), bf16[8,6,48,128]{3,2,1,0:T(8,128)(2,1)}, u32[]{:S(2)}, u32[]{:S(2)}) %all-to-all-start) | async-done | bytes 589856 | tf_op jit(solution)/shard_map/all_to_all | solution.py:556
  47.1 7.0 %finish.1 = bf16[6,2,320,128]{3,2,1,0:T(8,128)(2,1)} custom-call(s32[7,8]{1,0:T(8,128)} %get-tuple-element.19.table, bf16[8,6,48,128]{3,2,1,0:T(8,128)(2,1)} %all-to-all-done.back, bf16[6,2,320,128]{3,2,1,0:T(8,128)(2,1)} %feat.3, bf16[6,320,128]{2,1,0:T(8,128)(2,1)} %collective-permute-done.7.above, bf16[6,320,128]{2,1,0:T(8,128)(2,1)} %collective-permute-done.8.below, ...), custom_call_target="tpu_custom_call" | custom-call | flops 3000000000 | bytes 6000000 | tf_op jit(solution)/shard_map/finish/pallas_call | solution.py:642
Async XLA Ops:
  4.2 4.9 %collective-permute-start = (bf16[400,128]{1,0:T(8,128)(2,1)}, bf16[400,128]{1,0:T(8,128)(2,1)}, u32[]{:S(2)}, u32[]{:S(2)}) collective-permute-start(bf16[400,128]{1,0:T(8,128)(2,1)} %get-tuple-element.21), channel_id=1, source_target_pairs={{0,1},{1,0},{2,3},{3,2},{4,5},{5,4},{6,7},{7,6},{8,9},{9,8},{10,11... | collective-permute-start | bytes 307208 | tf_op jit(solution)/shard_map/ppermute | solution.py:589
  4.7 7.0 %collective-permute-start.1 = (bf16[400,128]{1,0:T(8,128)(2,1)}, bf16[400,128]{1,0:T(8,128)(2,1)}, u32[]{:S(2)}, u32[]{:S(2)}) collective-permute-start(bf16[400,128]{1,0:T(8,128)(2,1)} %get-tuple-element.22), channel_id=1, source_target_pairs={{0,2},{1,3},{2,0},{3,1},{4,6},{5,7},{6,4},{7,5},{8,10},{9,11},{10,... | collective-permute-start | bytes 307208 | tf_op jit(solution)/shard_map/ppermute | solution.py:589
  7.3 10.0 %collective-permute-start.2 = (bf16[400,128]{1,0:T(8,128)(2,1)}, bf16[400,128]{1,0:T(8,128)(2,1)}, u32[]{:S(2)}, u32[]{:S(2)}) collective-permute-start(bf16[400,128]{1,0:T(8,128)(2,1)} %get-tuple-element.23), channel_id=1, source_target_pairs={{0,3},{1,2},{2,1},{3,0},{4,7},{5,6},{6,5},{7,4},{8,11},{9,10},{10,... | collective-permute-start | bytes 307208 | tf_op jit(solution)/shard_map/ppermute | solution.py:589
  7.3 11.2 %collective-permute-start.3 = (bf16[400,128]{1,0:T(8,128)(2,1)}, bf16[400,128]{1,0:T(8,128)(2,1)}, u32[]{:S(2)}, u32[]{:S(2)}) collective-permute-start(bf16[400,128]{1,0:T(8,128)(2,1)} %get-tuple-element.24), channel_id=1, source_target_pairs={{0,4},{1,5},{2,6},{3,7},{4,0},{5,1},{6,2},{7,3},{8,12},{9,13},{10,... | collective-permute-start | bytes 307208 | tf_op jit(solution)/shard_map/ppermute | solution.py:589
  9.1 10.9 %collective-permute-start.4 = (bf16[400,128]{1,0:T(8,128)(2,1)}, bf16[400,128]{1,0:T(8,128)(2,1)}, u32[]{:S(2)}, u32[]{:S(2)}) collective-permute-start(bf16[400,128]{1,0:T(8,128)(2,1)} %get-tuple-element.25), channel_id=1, source_target_pairs={{0,5},{1,4},{2,7},{3,6},{4,1},{5,0},{6,3},{7,2},{8,13},{9,12},{10,... | collective-permute-start | bytes 307208 | tf_op jit(solution)/shard_map/ppermute | solution.py:589
  9.1 10.9 %collective-permute-start.5 = (bf16[400,128]{1,0:T(8,128)(2,1)}, bf16[400,128]{1,0:T(8,128)(2,1)}, u32[]{:S(2)}, u32[]{:S(2)}) collective-permute-start(bf16[400,128]{1,0:T(8,128)(2,1)} %get-tuple-element.26), channel_id=1, source_target_pairs={{0,6},{1,7},{2,4},{3,5},{4,2},{5,3},{6,0},{7,1},{8,14},{9,15},{10,... | collective-permute-start | bytes 307208 | tf_op jit(solution)/shard_map/ppermute | solution.py:589
  11.7 8.3 %collective-permute-start.6 = (bf16[400,128]{1,0:T(8,128)(2,1)}, bf16[400,128]{1,0:T(8,128)(2,1)}, u32[]{:S(2)}, u32[]{:S(2)}) collective-permute-start(bf16[400,128]{1,0:T(8,128)(2,1)} %get-tuple-element.27), channel_id=1, source_target_pairs={{0,7},{1,6},{2,5},{3,4},{4,3},{5,2},{6,1},{7,0},{8,15},{9,14},{10,... | collective-permute-start | bytes 307208 | tf_op jit(solution)/shard_map/ppermute | solution.py:589
  13.0 17.7 %all-to-all-start.1 = ((bf16[8,400,128]{2,1,0:T(8,128)(2,1)}), bf16[8,400,128]{2,1,0:T(8,128)(2,1)}, u32[]{:S(2)}, u32[]{:S(2)}) async-start(bf16[8,400,128]{2,1,0:T(8,128)(2,1)} %get-tuple-element.31), calls=%async_computation.1 | async-start | bytes 1638400 | tf_op jit(solution)/shard_map/all_to_all | solution.py:556
  17.3 23.0 %collective-permute-start.7 = (bf16[6,320,128]{2,1,0:T(8,128)(2,1)}, bf16[6,320,128]{2,1,0:T(8,128)(2,1)}, u32[]{:S(2)}, u32[]{:S(2)}) collective-permute-start(bf16[6,320,128]{2,1,0:T(8,128)(2,1)} %get-tuple-element.29), channel_id=1, source_target_pairs={{0,1},{1,2},{2,3},{3,4},{4,5},{5,6},{6,7},{7,0},{8,9},{9,10},{10,1... | collective-permute-start | bytes 1474568 | tf_op jit(solution)/shard_map/ppermute | solution.py:591
  18.6 21.7 %collective-permute-start.8 = (bf16[6,320,128]{2,1,0:T(8,128)(2,1)}, bf16[6,320,128]{2,1,0:T(8,128)(2,1)}, u32[]{:S(2)}, u32[]{:S(2)}) collective-permute-start(bf16[6,320,128]{2,1,0:T(8,128)(2,1)} %get-tuple-element.30), channel_id=1, source_target_pairs={{1,0},{2,1},{3,2},{4,3},{5,4},{6,5},{7,6},{0,7},{9,8},{10,9},{11,1... | collective-permute-start | bytes 1474568 | tf_op jit(solution)/shard_map/ppermute | solution.py:592
  30.7 16.4 %all-to-all-start = ((bf16[8,6,48,128]{3,2,1,0:T(8,128)(2,1)}), bf16[8,6,48,128]{3,2,1,0:T(8,128)(2,1)}, u32[]{:S(2)}, u32[]{:S(2)}) async-start(bf16[8,6,48,128]{3,2,1,0:T(8,128)(2,1)} %get-tuple-element.28), calls=%async_computation | async-start | bytes 1179648 | tf_op jit(solution)/shard_map/all_to_all | solution.py:556

commit v13 on v8

--- a/solution.py
+++ b/solution.py
@@ -17,7 +17,7 @@
 BF16 = jnp.bfloat16
 F32 = jnp.float32
 I32 = jnp.int32
-FULL_GRANT = 66500000
+FULL_GRANT = 67000000
 ROW, COL, SIDE, ROW2, COL2, SIDE2, PLACE = range(7)
 
 

time: 53.7 us -> 53.7 us (level)
  waiting for transfers between devices: 2.91 us -> 10.7 us
  Pallas kernels: 29 us -> 21.8 us
  local copies, waits for them, and re-layouts: 0.62 us -> 0 us
    pallas_call x1, Pallas kernels: 9.22 us -> 2.03 us  [shards(): pl.pallas_call(functools.partial(extra_kernel, dims), out_shape=restored_...]
    all_to_all x2, waiting for transfers between devices: 2.88 us -> 7.41 us  [swap(): lax.all_to_all(array, 'tile', split_axis=0, concat_axis=0, tiled=True)]
    ppermute x1, waiting for transfers between devices: 0.01 us -> 3.23 us  [shards(): above = lax.ppermute(last, 'tile', up)]
    unnamed x4 -> x0, local copies, waits for them, and re-layouts: 0.62 us -> none
  transfers between devices with their start and end apart: 11 -> 11, of which waited for: 1 -> 3; matrix products, arithmetic and copies ran while one was open for 0% -> 0% of each run, Pallas kernels for 36% -> 23%
where the time goes in v13:
time: 53.7 us; the launch traced here: 53.3 us
  Pallas kernels  21.8 us (41%)
  starting transfers between devices  20.1 us (37%)
  waiting for transfers between devices  10.7 us (20%)
  between operations  0.68 us (1%)
    pallas_call x1, Pallas kernels, shards(): pl.pallas_call(functools.partial(main_kernel, dims), out_shape=[shaped(ti...  10.1 us
    ppermute x7, starting transfers between devices, shards(): lax.ppermute(sent_main[s], 'tile', [(i, i ^ s) for i in range(tiles)])  8.84 us
    all_to_all x2, starting transfers between devices, swap(): lax.all_to_all(array, 'tile', split_axis=0, concat_axis=0, tiled=True)  8.53 us
    all_to_all x2, waiting for transfers between devices, swap(): lax.all_to_all(array, 'tile', split_axis=0, concat_axis=0, tiled=True)  7.41 us
    pallas_call x1, Pallas kernels, shards(): pl.pallas_call(functools.partial(finish_kernel, dims), out_shape=shaped(*...  6.19 us
    pallas_call x1, Pallas kernels, shards(): pl.pallas_call(functools.partial(pack_kernel, dims), out_shape=[shaped(di...  3.54 us
    ppermute x1, waiting for transfers between devices, shards(): above = lax.ppermute(last, 'tile', up)  3.23 us
    pallas_call x1, Pallas kernels, shards(): pl.pallas_call(functools.partial(extra_kernel, dims), out_shape=restored_...  2.03 us
  transfers between devices with their start and end apart: 11, of which 3 were waited for; matrix products, arithmetic and copies ran while one was open for 0% of the time, Pallas kernels for 23%

profile of v13, /device:TPU:0, one launch (start us, length us, event | category | flops | bytes accessed | tf_op | source)
XLA Modules:
  0.0 53.3 jit_solution(758959997212848462)
XLA Ops:
  0.6 3.5 %pack.1 = (bf16[400,128]{1,0:T(8,128)(2,1)}, bf16[400,128]{1,0:T(8,128)(2,1)}, bf16[400,128]{1,0:T(8,128)(2,1)}, bf16[400,128]{1,0:T(8,128)(2,1)}, bf16[400,128]...) custom-call(s32[3,8]{1,0:T(4,128)} %boxes_in.1, ...), custom_call_target="tpu_custom_call" | custom-call | bytes 6000000 | tf_op jit(solution)/shard_map/pack/pallas_call | solution.py:578
  4.2 0.5 collective-permute-start
  4.7 2.6 %collective-permute-start.1 = (bf16[400,128]{1,0:T(8,128)(2,1)}, bf16[400,128]{1,0:T(8,128)(2,1)}, u32[]{:S(2)}, u32[]{:S(2)}) collective-permute-start(bf16[400,128]{1,0:T(8,128)(2,1)} %get-tuple-element.22), channel_id=1, source_target_pairs={{0,2},{1,3},{2,0},{3,1},{4,6},{5,7},{6,4},{7,5},{8,10},{9,11},{10,... | collective-permute-start | bytes 307208 | tf_op jit(solution)/shard_map/ppermute | solution.py:598
  7.3 0.1 collective-permute-start.2
  7.3 1.8 %collective-permute-start.3 = (bf16[400,128]{1,0:T(8,128)(2,1)}, bf16[400,128]{1,0:T(8,128)(2,1)}, u32[]{:S(2)}, u32[]{:S(2)}) collective-permute-start(bf16[400,128]{1,0:T(8,128)(2,1)} %get-tuple-element.24), channel_id=1, source_target_pairs={{0,4},{1,5},{2,6},{3,7},{4,0},{5,1},{6,2},{7,3},{8,12},{9,13},{10,... | collective-permute-start | bytes 307208 | tf_op jit(solution)/shard_map/ppermute | solution.py:598
  9.1 0.0 collective-permute-start.4
  9.1 0.0 collective-permute-done.refs_1_
  9.1 2.6 %collective-permute-start.5 = (bf16[400,128]{1,0:T(8,128)(2,1)}, bf16[400,128]{1,0:T(8,128)(2,1)}, u32[]{:S(2)}, u32[]{:S(2)}) collective-permute-start(bf16[400,128]{1,0:T(8,128)(2,1)} %get-tuple-element.26), channel_id=1, source_target_pairs={{0,6},{1,7},{2,4},{3,5},{4,2},{5,3},{6,0},{7,1},{8,14},{9,15},{10,... | collective-permute-start | bytes 307208 | tf_op jit(solution)/shard_map/ppermute | solution.py:598
  11.7 0.0 collective-permute-done.1.refs_2_
  11.7 1.3 %collective-permute-start.6 = (bf16[400,128]{1,0:T(8,128)(2,1)}, bf16[400,128]{1,0:T(8,128)(2,1)}, u32[]{:S(2)}, u32[]{:S(2)}) collective-permute-start(bf16[400,128]{1,0:T(8,128)(2,1)} %get-tuple-element.27), channel_id=1, source_target_pairs={{0,7},{1,6},{2,5},{3,4},{4,3},{5,2},{6,1},{7,0},{8,15},{9,14},{10,... | collective-permute-start | bytes 307208 | tf_op jit(solution)/shard_map/ppermute | solution.py:598
  13.0 4.2 %all-to-all-start.1 = ((bf16[8,400,128]{2,1,0:T(8,128)(2,1)}), bf16[8,400,128]{2,1,0:T(8,128)(2,1)}, u32[]{:S(2)}, u32[]{:S(2)}) async-start(bf16[8,400,128]{2,1,0:T(8,128)(2,1)} %get-tuple-element.31), calls=%async_computation.1 | async-start | bytes 1638400 | tf_op jit(solution)/shard_map/all_to_all | solution.py:565
  17.2 0.0 collective-permute-done.2.refs_3_
  17.3 1.3 %collective-permute-start.7 = (bf16[6,320,128]{2,1,0:T(8,128)(2,1)}, bf16[6,320,128]{2,1,0:T(8,128)(2,1)}, u32[]{:S(2)}, u32[]{:S(2)}) collective-permute-start(bf16[6,320,128]{2,1,0:T(8,128)(2,1)} %get-tuple-element.29), channel_id=1, source_target_pairs={{0,1},{1,2},{2,3},{3,4},{4,5},{5,6},{6,7},{7,0},{8,9},{9,10},{10,1... | collective-permute-start | bytes 1474568 | tf_op jit(solution)/shard_map/ppermute | solution.py:600
  18.6 0.0 collective-permute-done.3.refs_4_
  18.6 1.4 %collective-permute-start.8 = (bf16[6,320,128]{2,1,0:T(8,128)(2,1)}, bf16[6,320,128]{2,1,0:T(8,128)(2,1)}, u32[]{:S(2)}, u32[]{:S(2)}) collective-permute-start(bf16[6,320,128]{2,1,0:T(8,128)(2,1)} %get-tuple-element.30), channel_id=1, source_target_pairs={{1,0},{2,1},{3,2},{4,3},{5,4},{6,5},{7,6},{0,7},{9,8},{10,9},{11,1... | collective-permute-start | bytes 1474568 | tf_op jit(solution)/shard_map/ppermute | solution.py:601
  20.0 0.0 collective-permute-done.4.refs_5_
  20.0 0.0 collective-permute-done.5.refs_6_
  20.0 0.0 collective-permute-done.6.refs_7_
  20.0 10.1 %restore_main.1 = (bf16[8,6,48,128]{3,2,1,0:T(8,128)(2,1)}, bf16[2,64,64,128]{3,2,1,0:T(8,128)(2,1)}) custom-call(s32[7,8]{1,0:T(8,128)} %get-tuple-element.19.table, bf16[400,128]{1,0:T(8,128)(2,1)} %get-tuple-element.20.refs_0_, bf16[400,128]{1,0:T(8,128)(2,1)} %collective-permute-done.refs_1_, bf16[400,128]{1,0:T(8,128)(2,1)} %collective-permute-done.1.refs_2_, ...), custom_call_target="tpu_custom_call" | custom-call | flops 7000000000 | bytes 8000000 | tf_op jit(solution)/shard_map/restore_main/pallas_call | solution.py:623
  30.1 0.6 %all-to-all-done.1.arrived = bf16[8,400,128]{2,1,0:T(8,128)(2,1)} async-done(((bf16[8,400,128]{2,1,0:T(8,128)(2,1)}), bf16[8,400,128]{2,1,0:T(8,128)(2,1)}, u32[]{:S(2)}, u32[]{:S(2)}) %all-to-all-start.1) | async-done | bytes 819232 | tf_op jit(solution)/shard_map/all_to_all | solution.py:565
  30.7 4.3 %all-to-all-start = ((bf16[8,6,48,128]{3,2,1,0:T(8,128)(2,1)}), bf16[8,6,48,128]{3,2,1,0:T(8,128)(2,1)}, u32[]{:S(2)}, u32[]{:S(2)}) async-start(bf16[8,6,48,128]{3,2,1,0:T(8,128)(2,1)} %get-tuple-element.28), calls=%async_computation | async-start | bytes 1179648 | tf_op jit(solution)/shard_map/all_to_all | solution.py:565
  35.0 2.0 %restore_extra.1 = bf16[2,64,64,128]{3,2,1,0:T(8,128)(2,1)} custom-call(s32[7,8]{1,0:T(8,128)} %get-tuple-element.19.table, bf16[8,400,128]{2,1,0:T(8,128)(2,1)} %all-to-all-done.1.arrived, bf16[3,3,128,128]{3,2,1,0:T(8,128)(2,1)} %bitcast.11, bf16[3,3,128,128]{3,2,1,0:T(8,128)(2,1)} %bitcast.7, ...), custom_call_target="tpu_custom_call", output_to_operand_aliasing={{}: (8, {})} | custom-call | flops 6000000000 | bytes 8000000 | tf_op jit(solution)/shard_map/restore_extra/pallas_call | solution.py:636
  37.0 3.2 %collective-permute-done.7.above = bf16[6,320,128]{2,1,0:T(8,128)(2,1)} collective-permute-done((bf16[6,320,128]{2,1,0:T(8,128)(2,1)}, bf16[6,320,128]{2,1,0:T(8,128)(2,1)}, u32[]{:S(2)}, u32[]{:S(2)}) %collective-permute-start.7) | collective-permute-done | bytes 491552 | tf_op jit(solution)/shard_map/ppermute | solution.py:600
  40.3 0.0 collective-permute-done.8.below
  40.3 6.8 %all-to-all-done.back = bf16[8,6,48,128]{3,2,1,0:T(8,128)(2,1)} async-done(((bf16[8,6,48,128]{3,2,1,0:T(8,128)(2,1)}), bf16[8,6,48,128]{3,2,1,0:T(8,128)(2,1)}, u32[]{:S(2)}, u32[]{:S(2)}) %all-to-all-start) | async-done | bytes 589856 | tf_op jit(solution)/shard_map/all_to_all | solution.py:565
  47.1 6.2 %finish.1 = bf16[6,2,320,128]{3,2,1,0:T(8,128)(2,1)} custom-call(s32[7,8]{1,0:T(8,128)} %get-tuple-element.19.table, bf16[8,6,48,128]{3,2,1,0:T(8,128)(2,1)} %all-to-all-done.back, bf16[6,2,320,128]{3,2,1,0:T(8,128)(2,1)} %feat.3, bf16[6,320,128]{2,1,0:T(8,128)(2,1)} %collective-permute-done.7.above, bf16[6,320,128]{2,1,0:T(8,128)(2,1)} %collective-permute-done.8.below, ...), custom_call_target="tpu_custom_call" | custom-call | flops 3000000000 | bytes 6000000 | tf_op jit(solution)/shard_map/finish/pallas_call | solution.py:650
Async XLA Ops:
  4.2 4.9 %collective-permute-start = (bf16[400,128]{1,0:T(8,128)(2,1)}, bf16[400,128]{1,0:T(8,128)(2,1)}, u32[]{:S(2)}, u32[]{:S(2)}) collective-permute-start(bf16[400,128]{1,0:T(8,128)(2,1)} %get-tuple-element.21), channel_id=1, source_target_pairs={{0,1},{1,0},{2,3},{3,2},{4,5},{5,4},{6,7},{7,6},{8,9},{9,8},{10,11... | collective-permute-start | bytes 307208 | tf_op jit(solution)/shard_map/ppermute | solution.py:598
  4.7 7.0 %collective-permute-start.1 = (bf16[400,128]{1,0:T(8,128)(2,1)}, bf16[400,128]{1,0:T(8,128)(2,1)}, u32[]{:S(2)}, u32[]{:S(2)}) collective-permute-start(bf16[400,128]{1,0:T(8,128)(2,1)} %get-tuple-element.22), channel_id=1, source_target_pairs={{0,2},{1,3},{2,0},{3,1},{4,6},{5,7},{6,4},{7,5},{8,10},{9,11},{10,... | collective-permute-start | bytes 307208 | tf_op jit(solution)/shard_map/ppermute | solution.py:598
  7.3 10.0 %collective-permute-start.2 = (bf16[400,128]{1,0:T(8,128)(2,1)}, bf16[400,128]{1,0:T(8,128)(2,1)}, u32[]{:S(2)}, u32[]{:S(2)}) collective-permute-start(bf16[400,128]{1,0:T(8,128)(2,1)} %get-tuple-element.23), channel_id=1, source_target_pairs={{0,3},{1,2},{2,1},{3,0},{4,7},{5,6},{6,5},{7,4},{8,11},{9,10},{10,... | collective-permute-start | bytes 307208 | tf_op jit(solution)/shard_map/ppermute | solution.py:598
  7.3 11.2 %collective-permute-start.3 = (bf16[400,128]{1,0:T(8,128)(2,1)}, bf16[400,128]{1,0:T(8,128)(2,1)}, u32[]{:S(2)}, u32[]{:S(2)}) collective-permute-start(bf16[400,128]{1,0:T(8,128)(2,1)} %get-tuple-element.24), channel_id=1, source_target_pairs={{0,4},{1,5},{2,6},{3,7},{4,0},{5,1},{6,2},{7,3},{8,12},{9,13},{10,... | collective-permute-start | bytes 307208 | tf_op jit(solution)/shard_map/ppermute | solution.py:598
  9.1 10.9 %collective-permute-start.4 = (bf16[400,128]{1,0:T(8,128)(2,1)}, bf16[400,128]{1,0:T(8,128)(2,1)}, u32[]{:S(2)}, u32[]{:S(2)}) collective-permute-start(bf16[400,128]{1,0:T(8,128)(2,1)} %get-tuple-element.25), channel_id=1, source_target_pairs={{0,5},{1,4},{2,7},{3,6},{4,1},{5,0},{6,3},{7,2},{8,13},{9,12},{10,... | collective-permute-start | bytes 307208 | tf_op jit(solution)/shard_map/ppermute | solution.py:598
  9.1 10.9 %collective-permute-start.5 = (bf16[400,128]{1,0:T(8,128)(2,1)}, bf16[400,128]{1,0:T(8,128)(2,1)}, u32[]{:S(2)}, u32[]{:S(2)}) collective-permute-start(bf16[400,128]{1,0:T(8,128)(2,1)} %get-tuple-element.26), channel_id=1, source_target_pairs={{0,6},{1,7},{2,4},{3,5},{4,2},{5,3},{6,0},{7,1},{8,14},{9,15},{10,... | collective-permute-start | bytes 307208 | tf_op jit(solution)/shard_map/ppermute | solution.py:598
  11.7 8.3 %collective-permute-start.6 = (bf16[400,128]{1,0:T(8,128)(2,1)}, bf16[400,128]{1,0:T(8,128)(2,1)}, u32[]{:S(2)}, u32[]{:S(2)}) collective-permute-start(bf16[400,128]{1,0:T(8,128)(2,1)} %get-tuple-element.27), channel_id=1, source_target_pairs={{0,7},{1,6},{2,5},{3,4},{4,3},{5,2},{6,1},{7,0},{8,15},{9,14},{10,... | collective-permute-start | bytes 307208 | tf_op jit(solution)/shard_map/ppermute | solution.py:598
  13.0 17.7 %all-to-all-start.1 = ((bf16[8,400,128]{2,1,0:T(8,128)(2,1)}), bf16[8,400,128]{2,1,0:T(8,128)(2,1)}, u32[]{:S(2)}, u32[]{:S(2)}) async-start(bf16[8,400,128]{2,1,0:T(8,128)(2,1)} %get-tuple-element.31), calls=%async_computation.1 | async-start | bytes 1638400 | tf_op jit(solution)/shard_map/all_to_all | solution.py:565
  17.3 23.0 %collective-permute-start.7 = (bf16[6,320,128]{2,1,0:T(8,128)(2,1)}, bf16[6,320,128]{2,1,0:T(8,128)(2,1)}, u32[]{:S(2)}, u32[]{:S(2)}) collective-permute-start(bf16[6,320,128]{2,1,0:T(8,128)(2,1)} %get-tuple-element.29), channel_id=1, source_target_pairs={{0,1},{1,2},{2,3},{3,4},{4,5},{5,6},{6,7},{7,0},{8,9},{9,10},{10,1... | collective-permute-start | bytes 1474568 | tf_op jit(solution)/shard_map/ppermute | solution.py:600
  18.6 21.7 %collective-permute-start.8 = (bf16[6,320,128]{2,1,0:T(8,128)(2,1)}, bf16[6,320,128]{2,1,0:T(8,128)(2,1)}, u32[]{:S(2)}, u32[]{:S(2)}) collective-permute-start(bf16[6,320,128]{2,1,0:T(8,128)(2,1)} %get-tuple-element.30), channel_id=1, source_target_pairs={{1,0},{2,1},{3,2},{4,3},{5,4},{6,5},{7,6},{0,7},{9,8},{10,9},{11,1... | collective-permute-start | bytes 1474568 | tf_op jit(solution)/shard_map/ppermute | solution.py:601
  30.7 16.4 %all-to-all-start = ((bf16[8,6,48,128]{3,2,1,0:T(8,128)(2,1)}), bf16[8,6,48,128]{3,2,1,0:T(8,128)(2,1)}, u32[]{:S(2)}, u32[]{:S(2)}) async-start(bf16[8,6,48,128]{3,2,1,0:T(8,128)(2,1)} %get-tuple-element.28), calls=%async_computation | async-start | bytes 1179648 | tf_op jit(solution)/shard_map/all_to_all | solution.py:565

commit v14 on v13

--- a/solution.py
+++ b/solution.py
@@ -148,22 +148,15 @@
     return finish
 
 
-def pack_crops(dims, table, row_at, col_at, canvas, rim, staged, partner):
+def pack_crop(dims, row0, col0, canvas, rim, staged):
     me = lax.axis_index("tile")
-    rim[...] = jnp.zeros_like(rim)
-
-    @pl.loop(0, dims.tiles)
-    def _(s):
-        w = partner(s)
-        row0 = table[row_at, w]
-        col0 = table[col_at, w]
-        start = first_local(jnp.maximum(row0 - 1, 0), me, dims)
-        for i in range(dims.rows):
-            row = jnp.minimum(start + i, dims.local_rows - 1)
-            staged[s, i * SPAN : (i + 1) * SPAN, :] = canvas[row, pl.ds(col0 + 8, SPAN), :].astype(BF16)
-            rim[2 * i : 2 * i + 1, :] = canvas[row, pl.ds(col0 + 7, 1), :]
-            rim[2 * i + 1 : 2 * i + 2, :] = canvas[row, pl.ds(col0 + 8 + SPAN, 1), :]
-        staged[s, dims.rows * SPAN :, :] = rim[...].astype(BF16)
+    start = first_local(jnp.maximum(row0 - 1, 0), me, dims)
+    for i in range(dims.rows):
+        row = jnp.minimum(start + i, dims.local_rows - 1)
+        staged[i * SPAN : (i + 1) * SPAN, :] = canvas[row, pl.ds(col0 + 8, SPAN), :].astype(BF16)
+        rim[2 * i : 2 * i + 1, :] = canvas[row, pl.ds(col0 + 7, 1), :]
+        rim[2 * i + 1 : 2 * i + 2, :] = canvas[row, pl.ds(col0 + 8 + SPAN, 1), :]
+    staged[dims.rows * SPAN :, :] = rim[...].astype(BF16)
 
 
 def pack_kernel(
@@ -210,24 +203,44 @@
 
     lax.fori_loop(0, dims.tiles, second_pass, jnp.int32(0))
     finish()
+    rim[...] = jnp.zeros_like(rim)
+    copies = [pltpu.make_async_copy(staged.at[s], sent[s], sent_sems.at[0, s]) for s in range(dims.tiles)]
+    half = dims.tiles // 2
+    for part in range(2):
+
+        @pl.loop(part * half, (part + 1) * half)
+        def _(s):
+            pack_crop(dims, table[ROW, me ^ s], table[COL, me ^ s], canvas, rim, staged.at[s])
+
+        for copy in copies[part * half : (part + 1) * half]:
+            copy.start()
     edges = (
         pltpu.make_async_copy(held.at[:, 1], last, sems.at[2]),
         pltpu.make_async_copy(held.at[:, 0], leading, sems.at[3]),
     )
     for edge in edges:
         edge.start()
-    pack_crops(dims, table, ROW, COL, canvas, rim, staged, lambda s: me ^ s)
-    copies = [pltpu.make_async_copy(staged.at[s], sent[s], sent_sems.at[s]) for s in range(dims.tiles)]
-    for copy in copies:
-        copy.start()
-    pack_crops(dims, table, ROW2, COL2, canvas, rim, staged_extra, lambda s: s)
-    later = pltpu.make_async_copy(staged_extra, sent_extra, sems.at[0])
-    later.start()
+
+    def later(w):
+        return pltpu.make_async_copy(staged_extra.at[w], sent_extra.at[w], sent_sems.at[1, w])
+
+    @pl.loop(0, dims.tiles)
+    def _(w):
+        @pl.when(table[SIDE2, w] > 0)
+        def _():
+            pack_crop(dims, table[ROW2, w], table[COL2, w], canvas, rim, staged_extra.at[w])
+            later(w).start()
+
     for copy in copies:
         copy.wait()
-    later.wait()
     for edge in edges:
         edge.wait()
+
+    @pl.loop(0, dims.tiles)
+    def _(w):
+        @pl.when(table[SIDE2, w] > 0)
+        def _():
+            later(w).wait()
 
 
 def restore(dims, row0, length, arrival, source, got, taps, raw, decoded, wide, inner, mixed, delta, finish):
@@ -572,7 +585,7 @@
         pltpu.VMEM((tiles, dims.message, chans), BF16),
         dma((4,)),
         dma((bands,)),
-        dma((tiles,)),
+        dma((2, tiles)),
     ]
     message = shaped(tiles, dims.message, chans)
     *sent_main, sent_extra, table, last, leading = pl.pallas_call(

time: 53.7 us -> 53.7 us (level)
  no operation moved by 1% of the time
where the time goes in v14:
time: 53.7 us; the launch traced here: 53.3 us
  Pallas kernels  21.9 us (41%)
  starting transfers between devices  20 us (37%)
  waiting for transfers between devices  10.7 us (20%)
  between operations  0.68 us (1%)
    pallas_call x1, Pallas kernels, shards(): pl.pallas_call(functools.partial(main_kernel, dims), out_shape=[shaped(ti...  10.1 us
    ppermute x7, starting transfers between devices, shards(): lax.ppermute(sent_main[s], 'tile', [(i, i ^ s) for i in range(tiles)])  8.84 us
    all_to_all x2, starting transfers between devices, swap(): lax.all_to_all(array, 'tile', split_axis=0, concat_axis=0, tiled=True)  8.5 us
    all_to_all x2, waiting for transfers between devices, swap(): lax.all_to_all(array, 'tile', split_axis=0, concat_axis=0, tiled=True)  7.4 us
    pallas_call x1, Pallas kernels, shards(): pl.pallas_call(functools.partial(finish_kernel, dims), out_shape=shaped(*...  6.17 us
    pallas_call x1, Pallas kernels, shards(): pl.pallas_call(functools.partial(pack_kernel, dims), out_shape=[shaped(di...  3.55 us
    ppermute x1, waiting for transfers between devices, shards(): above = lax.ppermute(last, 'tile', up)  3.26 us
    pallas_call x1, Pallas kernels, shards(): pl.pallas_call(functools.partial(extra_kernel, dims), out_shape=restored_...  2.03 us
  transfers between devices with their start and end apart: 11, of which 3 were waited for; matrix products, arithmetic and copies ran while one was open for 0% of the time, Pallas kernels for 23%

profile of v14, /device:TPU:0, one launch (start us, length us, event | category | flops | bytes accessed | tf_op | source)
XLA Modules:
  0.0 53.3 jit_solution(13443177540172735682)
XLA Ops:
  0.6 3.6 %pack.1 = (bf16[400,128]{1,0:T(8,128)(2,1)}, bf16[400,128]{1,0:T(8,128)(2,1)}, bf16[400,128]{1,0:T(8,128)(2,1)}, bf16[400,128]{1,0:T(8,128)(2,1)}, bf16[400,128]...) custom-call(s32[3,8]{1,0:T(4,128)} %boxes_in.1, ...), custom_call_target="tpu_custom_call" | custom-call | bytes 6000000 | tf_op jit(solution)/shard_map/pack/pallas_call | solution.py:591
  4.2 0.5 collective-permute-start
  4.7 2.6 %collective-permute-start.1 = (bf16[400,128]{1,0:T(8,128)(2,1)}, bf16[400,128]{1,0:T(8,128)(2,1)}, u32[]{:S(2)}, u32[]{:S(2)}) collective-permute-start(bf16[400,128]{1,0:T(8,128)(2,1)} %get-tuple-element.22), channel_id=1, source_target_pairs={{0,2},{1,3},{2,0},{3,1},{4,6},{5,7},{6,4},{7,5},{8,10},{9,11},{10,... | collective-permute-start | bytes 307208 | tf_op jit(solution)/shard_map/ppermute | solution.py:611
  7.3 0.1 collective-permute-start.2
  7.3 1.8 %collective-permute-start.3 = (bf16[400,128]{1,0:T(8,128)(2,1)}, bf16[400,128]{1,0:T(8,128)(2,1)}, u32[]{:S(2)}, u32[]{:S(2)}) collective-permute-start(bf16[400,128]{1,0:T(8,128)(2,1)} %get-tuple-element.24), channel_id=1, source_target_pairs={{0,4},{1,5},{2,6},{3,7},{4,0},{5,1},{6,2},{7,3},{8,12},{9,13},{10,... | collective-permute-start | bytes 307208 | tf_op jit(solution)/shard_map/ppermute | solution.py:611
  9.1 0.0 collective-permute-start.4
  9.1 0.0 collective-permute-done.refs_1_
  9.1 2.6 %collective-permute-start.5 = (bf16[400,128]{1,0:T(8,128)(2,1)}, bf16[400,128]{1,0:T(8,128)(2,1)}, u32[]{:S(2)}, u32[]{:S(2)}) collective-permute-start(bf16[400,128]{1,0:T(8,128)(2,1)} %get-tuple-element.26), channel_id=1, source_target_pairs={{0,6},{1,7},{2,4},{3,5},{4,2},{5,3},{6,0},{7,1},{8,14},{9,15},{10,... | collective-permute-start | bytes 307208 | tf_op jit(solution)/shard_map/ppermute | solution.py:611
  11.7 0.0 collective-permute-done.1.refs_2_
  11.7 1.3 %collective-permute-start.6 = (bf16[400,128]{1,0:T(8,128)(2,1)}, bf16[400,128]{1,0:T(8,128)(2,1)}, u32[]{:S(2)}, u32[]{:S(2)}) collective-permute-start(bf16[400,128]{1,0:T(8,128)(2,1)} %get-tuple-element.27), channel_id=1, source_target_pairs={{0,7},{1,6},{2,5},{3,4},{4,3},{5,2},{6,1},{7,0},{8,15},{9,14},{10,... | collective-permute-start | bytes 307208 | tf_op jit(solution)/shard_map/ppermute | solution.py:611
  13.0 4.2 %all-to-all-start.1 = ((bf16[8,400,128]{2,1,0:T(8,128)(2,1)}), bf16[8,400,128]{2,1,0:T(8,128)(2,1)}, u32[]{:S(2)}, u32[]{:S(2)}) async-start(bf16[8,400,128]{2,1,0:T(8,128)(2,1)} %get-tuple-element.31), calls=%async_computation.1 | async-start | bytes 1638400 | tf_op jit(solution)/shard_map/all_to_all | solution.py:578
  17.3 0.0 collective-permute-done.2.refs_3_
  17.3 1.3 %collective-permute-start.7 = (bf16[6,320,128]{2,1,0:T(8,128)(2,1)}, bf16[6,320,128]{2,1,0:T(8,128)(2,1)}, u32[]{:S(2)}, u32[]{:S(2)}) collective-permute-start(bf16[6,320,128]{2,1,0:T(8,128)(2,1)} %get-tuple-element.29), channel_id=1, source_target_pairs={{0,1},{1,2},{2,3},{3,4},{4,5},{5,6},{6,7},{7,0},{8,9},{9,10},{10,1... | collective-permute-start | bytes 1474568 | tf_op jit(solution)/shard_map/ppermute | solution.py:613
  18.6 0.0 collective-permute-done.3.refs_4_
  18.6 1.4 %collective-permute-start.8 = (bf16[6,320,128]{2,1,0:T(8,128)(2,1)}, bf16[6,320,128]{2,1,0:T(8,128)(2,1)}, u32[]{:S(2)}, u32[]{:S(2)}) collective-permute-start(bf16[6,320,128]{2,1,0:T(8,128)(2,1)} %get-tuple-element.30), channel_id=1, source_target_pairs={{1,0},{2,1},{3,2},{4,3},{5,4},{6,5},{7,6},{0,7},{9,8},{10,9},{11,1... | collective-permute-start | bytes 1474568 | tf_op jit(solution)/shard_map/ppermute | solution.py:614
  20.0 0.0 collective-permute-done.4.refs_5_
  20.0 0.0 collective-permute-done.5.refs_6_
  20.0 0.0 collective-permute-done.6.refs_7_
  20.0 10.1 %restore_main.1 = (bf16[8,6,48,128]{3,2,1,0:T(8,128)(2,1)}, bf16[2,64,64,128]{3,2,1,0:T(8,128)(2,1)}) custom-call(s32[7,8]{1,0:T(8,128)} %get-tuple-element.19.table, bf16[400,128]{1,0:T(8,128)(2,1)} %get-tuple-element.20.refs_0_, bf16[400,128]{1,0:T(8,128)(2,1)} %collective-permute-done.refs_1_, bf16[400,128]{1,0:T(8,128)(2,1)} %collective-permute-done.1.refs_2_, ...), custom_call_target="tpu_custom_call" | custom-call | flops 7000000000 | bytes 8000000 | tf_op jit(solution)/shard_map/restore_main/pallas_call | solution.py:636
  30.1 0.6 %all-to-all-done.1.arrived = bf16[8,400,128]{2,1,0:T(8,128)(2,1)} async-done(((bf16[8,400,128]{2,1,0:T(8,128)(2,1)}), bf16[8,400,128]{2,1,0:T(8,128)(2,1)}, u32[]{:S(2)}, u32[]{:S(2)}) %all-to-all-start.1) | async-done | bytes 819232 | tf_op jit(solution)/shard_map/all_to_all | solution.py:578
  30.7 4.3 %all-to-all-start = ((bf16[8,6,48,128]{3,2,1,0:T(8,128)(2,1)}), bf16[8,6,48,128]{3,2,1,0:T(8,128)(2,1)}, u32[]{:S(2)}, u32[]{:S(2)}) async-start(bf16[8,6,48,128]{3,2,1,0:T(8,128)(2,1)} %get-tuple-element.28), calls=%async_computation | async-start | bytes 1179648 | tf_op jit(solution)/shard_map/all_to_all | solution.py:578
  35.0 2.0 %restore_extra.1 = bf16[2,64,64,128]{3,2,1,0:T(8,128)(2,1)} custom-call(s32[7,8]{1,0:T(8,128)} %get-tuple-element.19.table, bf16[8,400,128]{2,1,0:T(8,128)(2,1)} %all-to-all-done.1.arrived, bf16[3,3,128,128]{3,2,1,0:T(8,128)(2,1)} %bitcast.11, bf16[3,3,128,128]{3,2,1,0:T(8,128)(2,1)} %bitcast.7, ...), custom_call_target="tpu_custom_call", output_to_operand_aliasing={{}: (8, {})} | custom-call | flops 6000000000 | bytes 8000000 | tf_op jit(solution)/shard_map/restore_extra/pallas_call | solution.py:649
  37.0 3.3 %collective-permute-done.7.above = bf16[6,320,128]{2,1,0:T(8,128)(2,1)} collective-permute-done((bf16[6,320,128]{2,1,0:T(8,128)(2,1)}, bf16[6,320,128]{2,1,0:T(8,128)(2,1)}, u32[]{:S(2)}, u32[]{:S(2)}) %collective-permute-start.7) | collective-permute-done | bytes 491552 | tf_op jit(solution)/shard_map/ppermute | solution.py:613
  40.3 0.0 collective-permute-done.8.below
  40.3 6.8 %all-to-all-done.back = bf16[8,6,48,128]{3,2,1,0:T(8,128)(2,1)} async-done(((bf16[8,6,48,128]{3,2,1,0:T(8,128)(2,1)}), bf16[8,6,48,128]{3,2,1,0:T(8,128)(2,1)}, u32[]{:S(2)}, u32[]{:S(2)}) %all-to-all-start) | async-done | bytes 589856 | tf_op jit(solution)/shard_map/all_to_all | solution.py:578
  47.1 6.2 %finish.1 = bf16[6,2,320,128]{3,2,1,0:T(8,128)(2,1)} custom-call(s32[7,8]{1,0:T(8,128)} %get-tuple-element.19.table, bf16[8,6,48,128]{3,2,1,0:T(8,128)(2,1)} %all-to-all-done.back, bf16[6,2,320,128]{3,2,1,0:T(8,128)(2,1)} %feat.3, bf16[6,320,128]{2,1,0:T(8,128)(2,1)} %collective-permute-done.7.above, bf16[6,320,128]{2,1,0:T(8,128)(2,1)} %collective-permute-done.8.below, ...), custom_call_target="tpu_custom_call" | custom-call | flops 3000000000 | bytes 6000000 | tf_op jit(solution)/shard_map/finish/pallas_call | solution.py:663
Async XLA Ops:
  4.2 4.9 %collective-permute-start = (bf16[400,128]{1,0:T(8,128)(2,1)}, bf16[400,128]{1,0:T(8,128)(2,1)}, u32[]{:S(2)}, u32[]{:S(2)}) collective-permute-start(bf16[400,128]{1,0:T(8,128)(2,1)} %get-tuple-element.21), channel_id=1, source_target_pairs={{0,1},{1,0},{2,3},{3,2},{4,5},{5,4},{6,7},{7,6},{8,9},{9,8},{10,11... | collective-permute-start | bytes 307208 | tf_op jit(solution)/shard_map/ppermute | solution.py:611
  4.7 7.0 %collective-permute-start.1 = (bf16[400,128]{1,0:T(8,128)(2,1)}, bf16[400,128]{1,0:T(8,128)(2,1)}, u32[]{:S(2)}, u32[]{:S(2)}) collective-permute-start(bf16[400,128]{1,0:T(8,128)(2,1)} %get-tuple-element.22), channel_id=1, source_target_pairs={{0,2},{1,3},{2,0},{3,1},{4,6},{5,7},{6,4},{7,5},{8,10},{9,11},{10,... | collective-permute-start | bytes 307208 | tf_op jit(solution)/shard_map/ppermute | solution.py:611
  7.3 10.0 %collective-permute-start.2 = (bf16[400,128]{1,0:T(8,128)(2,1)}, bf16[400,128]{1,0:T(8,128)(2,1)}, u32[]{:S(2)}, u32[]{:S(2)}) collective-permute-start(bf16[400,128]{1,0:T(8,128)(2,1)} %get-tuple-element.23), channel_id=1, source_target_pairs={{0,3},{1,2},{2,1},{3,0},{4,7},{5,6},{6,5},{7,4},{8,11},{9,10},{10,... | collective-permute-start | bytes 307208 | tf_op jit(solution)/shard_map/ppermute | solution.py:611
  7.3 11.2 %collective-permute-start.3 = (bf16[400,128]{1,0:T(8,128)(2,1)}, bf16[400,128]{1,0:T(8,128)(2,1)}, u32[]{:S(2)}, u32[]{:S(2)}) collective-permute-start(bf16[400,128]{1,0:T(8,128)(2,1)} %get-tuple-element.24), channel_id=1, source_target_pairs={{0,4},{1,5},{2,6},{3,7},{4,0},{5,1},{6,2},{7,3},{8,12},{9,13},{10,... | collective-permute-start | bytes 307208 | tf_op jit(solution)/shard_map/ppermute | solution.py:611
  9.1 10.9 %collective-permute-start.4 = (bf16[400,128]{1,0:T(8,128)(2,1)}, bf16[400,128]{1,0:T(8,128)(2,1)}, u32[]{:S(2)}, u32[]{:S(2)}) collective-permute-start(bf16[400,128]{1,0:T(8,128)(2,1)} %get-tuple-element.25), channel_id=1, source_target_pairs={{0,5},{1,4},{2,7},{3,6},{4,1},{5,0},{6,3},{7,2},{8,13},{9,12},{10,... | collective-permute-start | bytes 307208 | tf_op jit(solution)/shard_map/ppermute | solution.py:611
  9.1 10.9 %collective-permute-start.5 = (bf16[400,128]{1,0:T(8,128)(2,1)}, bf16[400,128]{1,0:T(8,128)(2,1)}, u32[]{:S(2)}, u32[]{:S(2)}) collective-permute-start(bf16[400,128]{1,0:T(8,128)(2,1)} %get-tuple-element.26), channel_id=1, source_target_pairs={{0,6},{1,7},{2,4},{3,5},{4,2},{5,3},{6,0},{7,1},{8,14},{9,15},{10,... | collective-permute-start | bytes 307208 | tf_op jit(solution)/shard_map/ppermute | solution.py:611
  11.7 8.3 %collective-permute-start.6 = (bf16[400,128]{1,0:T(8,128)(2,1)}, bf16[400,128]{1,0:T(8,128)(2,1)}, u32[]{:S(2)}, u32[]{:S(2)}) collective-permute-start(bf16[400,128]{1,0:T(8,128)(2,1)} %get-tuple-element.27), channel_id=1, source_target_pairs={{0,7},{1,6},{2,5},{3,4},{4,3},{5,2},{6,1},{7,0},{8,15},{9,14},{10,... | collective-permute-start | bytes 307208 | tf_op jit(solution)/shard_map/ppermute | solution.py:611
  13.0 17.7 %all-to-all-start.1 = ((bf16[8,400,128]{2,1,0:T(8,128)(2,1)}), bf16[8,400,128]{2,1,0:T(8,128)(2,1)}, u32[]{:S(2)}, u32[]{:S(2)}) async-start(bf16[8,400,128]{2,1,0:T(8,128)(2,1)} %get-tuple-element.31), calls=%async_computation.1 | async-start | bytes 1638400 | tf_op jit(solution)/shard_map/all_to_all | solution.py:578
  17.3 23.0 %collective-permute-start.7 = (bf16[6,320,128]{2,1,0:T(8,128)(2,1)}, bf16[6,320,128]{2,1,0:T(8,128)(2,1)}, u32[]{:S(2)}, u32[]{:S(2)}) collective-permute-start(bf16[6,320,128]{2,1,0:T(8,128)(2,1)} %get-tuple-element.29), channel_id=1, source_target_pairs={{0,1},{1,2},{2,3},{3,4},{4,5},{5,6},{6,7},{7,0},{8,9},{9,10},{10,1... | collective-permute-start | bytes 1474568 | tf_op jit(solution)/shard_map/ppermute | solution.py:613
  18.6 21.7 %collective-permute-start.8 = (bf16[6,320,128]{2,1,0:T(8,128)(2,1)}, bf16[6,320,128]{2,1,0:T(8,128)(2,1)}, u32[]{:S(2)}, u32[]{:S(2)}) collective-permute-start(bf16[6,320,128]{2,1,0:T(8,128)(2,1)} %get-tuple-element.30), channel_id=1, source_target_pairs={{1,0},{2,1},{3,2},{4,3},{5,4},{6,5},{7,6},{0,7},{9,8},{10,9},{11,1... | collective-permute-start | bytes 1474568 | tf_op jit(solution)/shard_map/ppermute | solution.py:614
  30.7 16.4 %all-to-all-start = ((bf16[8,6,48,128]{3,2,1,0:T(8,128)(2,1)}), bf16[8,6,48,128]{3,2,1,0:T(8,128)(2,1)}, u32[]{:S(2)}, u32[]{:S(2)}) async-start(bf16[8,6,48,128]{3,2,1,0:T(8,128)(2,1)} %get-tuple-element.28), calls=%async_computation | async-start | bytes 1179648 | tf_op jit(solution)/shard_map/all_to_all | solution.py:578

commit v15 on v14

--- a/solution.py
+++ b/solution.py
@@ -18,6 +18,7 @@
 F32 = jnp.float32
 I32 = jnp.int32
 FULL_GRANT = 67000000
+LAST_GRANT = 32 * 1024 * 1024
 ROW, COL, SIDE, ROW2, COL2, SIDE2, PLACE = range(7)
 
 
@@ -680,7 +681,7 @@
             dma((3, bands)),
             dma((3,)),
         ],
-        compiler_params=full,
+        compiler_params=pltpu.CompilerParams(vmem_limit_bytes=LAST_GRANT),
         cost_estimate=cost(3e9, 6e6),
         name="finish",
     )(table, got_back, features, above, below, weights[0], biases[0])

time: 53.7 us -> 56.3 us (1.048)
  Pallas kernels: 21.9 us -> 29.6 us
  waiting for transfers between devices: 10.7 us -> 3.36 us
  local copies, waits for them, and re-layouts: 0 us -> 2.17 us
    pallas_call x1, Pallas kernels: 2.03 us -> 9.36 us  [shards(): pl.pallas_call(functools.partial(extra_kernel, dims), out_shape=restored_...]
    all_to_all x2, waiting for transfers between devices: 7.4 us -> 3.34 us  [swap(): lax.all_to_all(array, 'tile', split_axis=0, concat_axis=0, tiled=True)]
    ppermute x1, waiting for transfers between devices: 3.26 us -> 0.01 us  [shards(): above = lax.ppermute(last, 'tile', up)]
    unnamed x0 -> x8, local copies, waits for them, and re-layouts: none -> 2.17 us
  transfers between devices with their start and end apart: 11 -> 11, of which waited for: 3 -> 2; matrix products, arithmetic and copies ran while one was open for 0% -> 0% of each run, Pallas kernels for 23% -> 35%
where the time goes in v15:
time: 56.3 us; the launch traced here: 55.8 us
  Pallas kernels  29.6 us (53%)
  starting transfers between devices  20 us (36%)
  waiting for transfers between devices  3.36 us (6%)
  local copies, waits for them, and re-layouts  2.17 us (4%)
  between operations  0.71 us (1%)
    pallas_call x1, Pallas kernels, shards(): pl.pallas_call(functools.partial(main_kernel, dims), out_shape=[shaped(ti...  10.1 us
    pallas_call x1, Pallas kernels, shards(): pl.pallas_call(functools.partial(extra_kernel, dims), out_shape=restored_...  9.36 us
    ppermute x7, starting transfers between devices, shards(): lax.ppermute(sent_main[s], 'tile', [(i, i ^ s) for i in range(tiles)])  8.84 us
    all_to_all x2, starting transfers between devices, swap(): lax.all_to_all(array, 'tile', split_axis=0, concat_axis=0, tiled=True)  8.47 us
    pallas_call x1, Pallas kernels, shards(): pl.pallas_call(functools.partial(finish_kernel, dims), out_shape=shaped(*...  6.57 us
    pallas_call x1, Pallas kernels, shards(): pl.pallas_call(functools.partial(pack_kernel, dims), out_shape=[shaped(di...  3.55 us
    all_to_all x2, waiting for transfers between devices, swap(): lax.all_to_all(array, 'tile', split_axis=0, concat_axis=0, tiled=True)  3.34 us
    unnamed x8, local copies, waits for them, and re-layouts  2.17 us
  transfers between devices with their start and end apart: 11, of which 2 were waited for; matrix products, arithmetic and copies ran while one was open for 0% of the time, Pallas kernels for 35%

profile of v15, /device:TPU:0, one launch (start us, length us, event | category | flops | bytes accessed | tf_op | source)
XLA Modules:
  0.0 55.8 jit_solution(1694560132614594336)
XLA Ops:
  0.6 3.6 %pack.1 = (bf16[400,128]{1,0:T(8,128)(2,1)}, bf16[400,128]{1,0:T(8,128)(2,1)}, bf16[400,128]{1,0:T(8,128)(2,1)}, bf16[400,128]{1,0:T(8,128)(2,1)}, bf16[400,128]...) custom-call(s32[3,8]{1,0:T(4,128)} %boxes_in.1, ...), custom_call_target="tpu_custom_call" | custom-call | bytes 6000000 | tf_op jit(solution)/shard_map/pack/pallas_call | solution.py:592
  4.2 0.5 collective-permute-start
  4.7 2.6 %collective-permute-start.1 = (bf16[400,128]{1,0:T(8,128)(2,1)}, bf16[400,128]{1,0:T(8,128)(2,1)}, u32[]{:S(2)}, u32[]{:S(2)}) collective-permute-start(bf16[400,128]{1,0:T(8,128)(2,1)} %get-tuple-element.22), channel_id=1, source_target_pairs={{0,2},{1,3},{2,0},{3,1},{4,6},{5,7},{6,4},{7,5},{8,10},{9,11},{10,... | collective-permute-start | bytes 307208 | tf_op jit(solution)/shard_map/ppermute | solution.py:612
  7.3 0.1 collective-permute-start.2
  7.3 1.8 %collective-permute-start.3 = (bf16[400,128]{1,0:T(8,128)(2,1)}, bf16[400,128]{1,0:T(8,128)(2,1)}, u32[]{:S(2)}, u32[]{:S(2)}) collective-permute-start(bf16[400,128]{1,0:T(8,128)(2,1)} %get-tuple-element.24), channel_id=1, source_target_pairs={{0,4},{1,5},{2,6},{3,7},{4,0},{5,1},{6,2},{7,3},{8,12},{9,13},{10,... | collective-permute-start | bytes 307208 | tf_op jit(solution)/shard_map/ppermute | solution.py:612
  9.1 0.0 collective-permute-start.4
  9.1 0.0 collective-permute-done.refs_1_
  9.1 2.6 %collective-permute-start.5 = (bf16[400,128]{1,0:T(8,128)(2,1)}, bf16[400,128]{1,0:T(8,128)(2,1)}, u32[]{:S(2)}, u32[]{:S(2)}) collective-permute-start(bf16[400,128]{1,0:T(8,128)(2,1)} %get-tuple-element.26), channel_id=1, source_target_pairs={{0,6},{1,7},{2,4},{3,5},{4,2},{5,3},{6,0},{7,1},{8,14},{9,15},{10,... | collective-permute-start | bytes 307208 | tf_op jit(solution)/shard_map/ppermute | solution.py:612
  11.7 0.0 collective-permute-done.1.refs_2_
  11.7 1.3 %collective-permute-start.6 = (bf16[400,128]{1,0:T(8,128)(2,1)}, bf16[400,128]{1,0:T(8,128)(2,1)}, u32[]{:S(2)}, u32[]{:S(2)}) collective-permute-start(bf16[400,128]{1,0:T(8,128)(2,1)} %get-tuple-element.27), channel_id=1, source_target_pairs={{0,7},{1,6},{2,5},{3,4},{4,3},{5,2},{6,1},{7,0},{8,15},{9,14},{10,... | collective-permute-start | bytes 307208 | tf_op jit(solution)/shard_map/ppermute | solution.py:612
  13.0 4.2 %all-to-all-start.1 = ((bf16[8,400,128]{2,1,0:T(8,128)(2,1)}), bf16[8,400,128]{2,1,0:T(8,128)(2,1)}, u32[]{:S(2)}, u32[]{:S(2)}) async-start(bf16[8,400,128]{2,1,0:T(8,128)(2,1)} %get-tuple-element.31), calls=%async_computation.1 | async-start | bytes 1638400 | tf_op jit(solution)/shard_map/all_to_all | solution.py:579
  17.3 0.0 collective-permute-done.2.refs_3_
  17.3 1.3 %collective-permute-start.7 = (bf16[6,320,128]{2,1,0:T(8,128)(2,1)}, bf16[6,320,128]{2,1,0:T(8,128)(2,1)}, u32[]{:S(2)}, u32[]{:S(2)}) collective-permute-start(bf16[6,320,128]{2,1,0:T(8,128)(2,1)} %get-tuple-element.29), channel_id=1, source_target_pairs={{0,1},{1,2},{2,3},{3,4},{4,5},{5,6},{6,7},{7,0},{8,9},{9,10},{10,1... | collective-permute-start | bytes 1474568 | tf_op jit(solution)/shard_map/ppermute | solution.py:614
  18.6 0.0 collective-permute-done.3.refs_4_
  18.6 1.4 %collective-permute-start.8 = (bf16[6,320,128]{2,1,0:T(8,128)(2,1)}, bf16[6,320,128]{2,1,0:T(8,128)(2,1)}, u32[]{:S(2)}, u32[]{:S(2)}) collective-permute-start(bf16[6,320,128]{2,1,0:T(8,128)(2,1)} %get-tuple-element.30), channel_id=1, source_target_pairs={{1,0},{2,1},{3,2},{4,3},{5,4},{6,5},{7,6},{0,7},{9,8},{10,9},{11,1... | collective-permute-start | bytes 1474568 | tf_op jit(solution)/shard_map/ppermute | solution.py:615
  20.0 0.0 collective-permute-done.4.refs_5_
  20.0 0.0 collective-permute-done.5.refs_6_
  20.0 0.0 collective-permute-done.6.refs_7_
  20.0 10.1 %restore_main.1 = (bf16[8,6,48,128]{3,2,1,0:T(8,128)(2,1)}, bf16[2,64,64,128]{3,2,1,0:T(8,128)(2,1)}) custom-call(s32[7,8]{1,0:T(8,128)} %get-tuple-element.19.table, bf16[400,128]{1,0:T(8,128)(2,1)} %get-tuple-element.20.refs_0_, bf16[400,128]{1,0:T(8,128)(2,1)} %collective-permute-done.refs_1_, bf16[400,128]{1,0:T(8,128)(2,1)} %collective-permute-done.1.refs_2_, ...), custom_call_target="tpu_custom_call" | custom-call | flops 7000000000 | bytes 8000000 | tf_op jit(solution)/shard_map/restore_main/pallas_call | solution.py:637
  30.1 0.6 %all-to-all-done.1.arrived = bf16[8,400,128]{2,1,0:T(8,128)(2,1)} async-done(((bf16[8,400,128]{2,1,0:T(8,128)(2,1)}), bf16[8,400,128]{2,1,0:T(8,128)(2,1)}, u32[]{:S(2)}, u32[]{:S(2)}) %all-to-all-start.1) | async-done | bytes 819232 | tf_op jit(solution)/shard_map/all_to_all | solution.py:579
  30.7 4.2 %all-to-all-start = ((bf16[8,6,48,128]{3,2,1,0:T(8,128)(2,1)}), bf16[8,6,48,128]{3,2,1,0:T(8,128)(2,1)}, u32[]{:S(2)}, u32[]{:S(2)}) async-start(bf16[8,6,48,128]{3,2,1,0:T(8,128)(2,1)} %get-tuple-element.28), calls=%async_computation | async-start | bytes 1179648 | tf_op jit(solution)/shard_map/all_to_all | solution.py:579
  35.0 0.0 copy-start.2
  35.0 0.0 copy-start.3
  35.0 9.4 %restore_extra.1 = bf16[2,64,64,128]{3,2,1,0:T(8,128)(2,1)} custom-call(s32[7,8]{1,0:T(8,128)} %get-tuple-element.19.table, bf16[8,400,128]{2,1,0:T(8,128)(2,1)} %all-to-all-done.1.arrived, bf16[3,3,128,128]{3,2,1,0:T(8,128)(2,1)} %bitcast.7, bf16[3,3,128,128]{3,2,1,0:T(8,128)(2,1)} %bitcast.13, ...), custom_call_target="tpu_custom_call", output_to_operand_aliasing={{}: (8, {})} | custom-call | flops 6000000000 | bytes 8000000 | tf_op jit(solution)/shard_map/restore_extra/pallas_call | solution.py:650
  44.3 0.0 collective-permute-done.7.above
  44.4 0.0 collective-permute-done.8.below
  44.4 2.7 %all-to-all-done.back = bf16[8,6,48,128]{3,2,1,0:T(8,128)(2,1)} async-done(((bf16[8,6,48,128]{3,2,1,0:T(8,128)(2,1)}), bf16[8,6,48,128]{3,2,1,0:T(8,128)(2,1)}, u32[]{:S(2)}, u32[]{:S(2)}) %all-to-all-start) | async-done | bytes 589856 | tf_op jit(solution)/shard_map/all_to_all | solution.py:579
  47.1 0.0 copy-done.2
  47.1 0.0 copy-done.3
  47.1 0.0 copy-start
  47.1 1.2 %copy-done = bf16[6,2,320,128]{3,2,1,0:T(8,128)(2,1)S(1)} copy-done((bf16[6,2,320,128]{3,2,1,0:T(8,128)(2,1)S(1)}, bf16[6,2,320,128]{3,2,1,0:T(8,128)(2,1)}, u32[]{:S(2)}) %copy-start) | copy-done | bytes 983064
  48.3 0.0 copy-start.1
  48.3 1.0 %copy-done.1 = bf16[9,128,128]{2,1,0:T(8,128)(2,1)S(1)} copy-done((bf16[9,128,128]{2,1,0:T(8,128)(2,1)S(1)}, bf16[9,128,128]{2,1,0:T(8,128)(2,1)}, u32[]{:S(2)}) %copy-start.1) | copy-done | bytes 294936
  49.3 6.6 %finish.1 = bf16[6,2,320,128]{3,2,1,0:T(8,128)(2,1)} custom-call(s32[7,8]{1,0:T(8,128)S(1)} %copy-done.2, bf16[8,6,48,128]{3,2,1,0:T(8,128)(2,1)} %all-to-all-done.back, bf16[6,2,320,128]{3,2,1,0:T(8,128)(2,1)S(1)} %copy-done, bf16[6,320,128]{2,1,0:T(8,128)(2,1)} %collective-permute-done.7.above, bf16[6,320,128]{2,1,0:T(8,128)(2,1)} %collective-permute-done.8.below, ...), custom_call_target="tpu_custom_call" | custom-call | flops 3000000000 | bytes 6000000 | tf_op jit(solution)/shard_map/finish/pallas_call | solution.py:664
Async XLA Ops:
  4.2 4.9 %collective-permute-start = (bf16[400,128]{1,0:T(8,128)(2,1)}, bf16[400,128]{1,0:T(8,128)(2,1)}, u32[]{:S(2)}, u32[]{:S(2)}) collective-permute-start(bf16[400,128]{1,0:T(8,128)(2,1)} %get-tuple-element.21), channel_id=1, source_target_pairs={{0,1},{1,0},{2,3},{3,2},{4,5},{5,4},{6,7},{7,6},{8,9},{9,8},{10,11... | collective-permute-start | bytes 307208 | tf_op jit(solution)/shard_map/ppermute | solution.py:612
  4.7 7.0 %collective-permute-start.1 = (bf16[400,128]{1,0:T(8,128)(2,1)}, bf16[400,128]{1,0:T(8,128)(2,1)}, u32[]{:S(2)}, u32[]{:S(2)}) collective-permute-start(bf16[400,128]{1,0:T(8,128)(2,1)} %get-tuple-element.22), channel_id=1, source_target_pairs={{0,2},{1,3},{2,0},{3,1},{4,6},{5,7},{6,4},{7,5},{8,10},{9,11},{10,... | collective-permute-start | bytes 307208 | tf_op jit(solution)/shard_map/ppermute | solution.py:612
  7.3 10.0 %collective-permute-start.2 = (bf16[400,128]{1,0:T(8,128)(2,1)}, bf16[400,128]{1,0:T(8,128)(2,1)}, u32[]{:S(2)}, u32[]{:S(2)}) collective-permute-start(bf16[400,128]{1,0:T(8,128)(2,1)} %get-tuple-element.23), channel_id=1, source_target_pairs={{0,3},{1,2},{2,1},{3,0},{4,7},{5,6},{6,5},{7,4},{8,11},{9,10},{10,... | collective-permute-start | bytes 307208 | tf_op jit(solution)/shard_map/ppermute | solution.py:612
  7.3 11.2 %collective-permute-start.3 = (bf16[400,128]{1,0:T(8,128)(2,1)}, bf16[400,128]{1,0:T(8,128)(2,1)}, u32[]{:S(2)}, u32[]{:S(2)}) collective-permute-start(bf16[400,128]{1,0:T(8,128)(2,1)} %get-tuple-element.24), channel_id=1, source_target_pairs={{0,4},{1,5},{2,6},{3,7},{4,0},{5,1},{6,2},{7,3},{8,12},{9,13},{10,... | collective-permute-start | bytes 307208 | tf_op jit(solution)/shard_map/ppermute | solution.py:612
  9.1 10.9 %collective-permute-start.4 = (bf16[400,128]{1,0:T(8,128)(2,1)}, bf16[400,128]{1,0:T(8,128)(2,1)}, u32[]{:S(2)}, u32[]{:S(2)}) collective-permute-start(bf16[400,128]{1,0:T(8,128)(2,1)} %get-tuple-element.25), channel_id=1, source_target_pairs={{0,5},{1,4},{2,7},{3,6},{4,1},{5,0},{6,3},{7,2},{8,13},{9,12},{10,... | collective-permute-start | bytes 307208 | tf_op jit(solution)/shard_map/ppermute | solution.py:612
  9.1 10.9 %collective-permute-start.5 = (bf16[400,128]{1,0:T(8,128)(2,1)}, bf16[400,128]{1,0:T(8,128)(2,1)}, u32[]{:S(2)}, u32[]{:S(2)}) collective-permute-start(bf16[400,128]{1,0:T(8,128)(2,1)} %get-tuple-element.26), channel_id=1, source_target_pairs={{0,6},{1,7},{2,4},{3,5},{4,2},{5,3},{6,0},{7,1},{8,14},{9,15},{10,... | collective-permute-start | bytes 307208 | tf_op jit(solution)/shard_map/ppermute | solution.py:612
  11.7 8.3 %collective-permute-start.6 = (bf16[400,128]{1,0:T(8,128)(2,1)}, bf16[400,128]{1,0:T(8,128)(2,1)}, u32[]{:S(2)}, u32[]{:S(2)}) collective-permute-start(bf16[400,128]{1,0:T(8,128)(2,1)} %get-tuple-element.27), channel_id=1, source_target_pairs={{0,7},{1,6},{2,5},{3,4},{4,3},{5,2},{6,1},{7,0},{8,15},{9,14},{10,... | collective-permute-start | bytes 307208 | tf_op jit(solution)/shard_map/ppermute | solution.py:612
  13.0 17.7 %all-to-all-start.1 = ((bf16[8,400,128]{2,1,0:T(8,128)(2,1)}), bf16[8,400,128]{2,1,0:T(8,128)(2,1)}, u32[]{:S(2)}, u32[]{:S(2)}) async-start(bf16[8,400,128]{2,1,0:T(8,128)(2,1)} %get-tuple-element.31), calls=%async_computation.1 | async-start | bytes 1638400 | tf_op jit(solution)/shard_map/all_to_all | solution.py:579
  17.3 27.1 %collective-permute-start.7 = (bf16[6,320,128]{2,1,0:T(8,128)(2,1)}, bf16[6,320,128]{2,1,0:T(8,128)(2,1)}, u32[]{:S(2)}, u32[]{:S(2)}) collective-permute-start(bf16[6,320,128]{2,1,0:T(8,128)(2,1)} %get-tuple-element.29), channel_id=1, source_target_pairs={{0,1},{1,2},{2,3},{3,4},{4,5},{5,6},{6,7},{7,0},{8,9},{9,10},{10,1... | collective-permute-start | bytes 1474568 | tf_op jit(solution)/shard_map/ppermute | solution.py:614
  18.6 25.8 %collective-permute-start.8 = (bf16[6,320,128]{2,1,0:T(8,128)(2,1)}, bf16[6,320,128]{2,1,0:T(8,128)(2,1)}, u32[]{:S(2)}, u32[]{:S(2)}) collective-permute-start(bf16[6,320,128]{2,1,0:T(8,128)(2,1)} %get-tuple-element.30), channel_id=1, source_target_pairs={{1,0},{2,1},{3,2},{4,3},{5,4},{6,5},{7,6},{0,7},{9,8},{10,9},{11,1... | collective-permute-start | bytes 1474568 | tf_op jit(solution)/shard_map/ppermute | solution.py:615
  30.7 16.4 %all-to-all-start = ((bf16[8,6,48,128]{3,2,1,0:T(8,128)(2,1)}), bf16[8,6,48,128]{3,2,1,0:T(8,128)(2,1)}, u32[]{:S(2)}, u32[]{:S(2)}) async-start(bf16[8,6,48,128]{3,2,1,0:T(8,128)(2,1)} %get-tuple-element.28), calls=%async_computation | async-start | bytes 1179648 | tf_op jit(solution)/shard_map/all_to_all | solution.py:579
  35.0 12.1 %copy-start.2 = (s32[7,8]{1,0:T(8,128)S(1)}, s32[7,8]{1,0:T(8,128)}, u32[]{:S(2)}) copy-start(s32[7,8]{1,0:T(8,128)} %get-tuple-element.19.table) | copy-start | bytes 676
  35.0 12.1 %copy-start.3 = (f32[128]{0:T(128)S(1)}, f32[128]{0:T(128)}, u32[]{:S(2)}) copy-start(f32[128]{0:T(128)} %param.11) | copy-start | bytes 1540
  47.1 1.2 %copy-start = (bf16[6,2,320,128]{3,2,1,0:T(8,128)(2,1)S(1)}, bf16[6,2,320,128]{3,2,1,0:T(8,128)(2,1)}, u32[]{:S(2)}) copy-start(bf16[6,2,320,128]{3,2,1,0:T(8,128)(2,1)} %feat.3) | copy-start | bytes 2949124
  48.3 1.0 %copy-start.1 = (bf16[9,128,128]{2,1,0:T(8,128)(2,1)S(1)}, bf16[9,128,128]{2,1,0:T(8,128)(2,1)}, u32[]{:S(2)}) copy-start(bf16[9,128,128]{2,1,0:T(8,128)(2,1)} %param.10) | copy-start | bytes 884740
